TPU v7x, 32 devices: a whole 2x2x4 slice. The times are simulated.
32 devices in a mesh: band: 8 (over z, core), dom: 4 (over y, x).
Axes of the slice: x: 2, y: 2, z: 4, core: 2. Of those that a mesh axis runs over, the one named last changes fastest.
Arguments:
- orbitals: bfloat16 [512, 24576], P('band', 'dom'), may hold values from -6 to 6
- rotation: bfloat16 [512, 256], P('band'), may hold values from -0.375 to 0.375
- projectors: bfloat16 [32, 16, 24576], P(None, None, 'dom'), may hold values from -0.078125 to 0.078125
- coupling: float32 [64, 16, 16], P('dom'), may hold values from -5 to 5
- slot_atom: int32 [4, 32], replicated, may hold values from 0 to 63, as said below
Outputs:
- updated_orbitals: bfloat16 [512, 24576], P('band', 'dom')
Inputs may be any that keep to these rules, and one draw needn't show every extreme that they name: `slot_atom`: the atoms of one row are distinct. Atom a is owned by domain a // 16. A row names at most 16 atoms of any one owner; domain 4 - 1 is named exactly 16 times by every row. Other owners are named between 0 and 16 times, unevenly.
All inputs are finite; a program needn't handle non-finite values.
Results may differ from a plain program's by a relative error of at most 0.0057.
Values may be sent and summed in bfloat16 or wider, within the bound.
No kernel may reach another device: no remote copies, remote signals or barrier semaphores. Data moves between devices by JAX's collectives and lax.ppermute only.
A program may use at most 64 MiB of HBM per device.

v0:
```python
import functools

import jax
import jax.numpy as jnp
from jax import lax
from jax.experimental import pallas as pl
from jax.experimental.pallas import tpu as pltpu
from jax.sharding import PartitionSpec as P

TURN = 3 * 10**9
COUPLE = 2 * 10**9
APPLY = 2 * 10**9
F32 = jnp.float32
BF16 = jnp.bfloat16
ROOM = pltpu.CompilerParams(vmem_limit_bytes=8 * 2**20)
NT = (((1,), (1,)), ((), ()))
VMEM = pl.BlockSpec(memory_space=pltpu.VMEM)
SMEM = pl.BlockSpec(memory_space=pltpu.SMEM)


def flops(count):
    return pl.CostEstimate(flops=count, bytes_accessed=0, transcendentals=0)


def call(kernel, name, outs, args, scratch=(), first=VMEM, cost=0):
    shapes = [jax.ShapeDtypeStruct(*o) for o in outs]
    return pl.pallas_call(
        kernel,
        in_specs=[first] + [VMEM] * (len(args) - 1),
        out_specs=[VMEM] * len(outs),
        out_shape=shapes,
        scratch_shapes=list(scratch),
        compiler_params=ROOM,
        cost_estimate=flops(cost),
        name=name,
    )(*args)


def along_bands(block, distance, senders=(0, 1)):
    count = lax.axis_size("band")
    route = [(i, (i + distance) % count if i % 2 in senders else i) for i in range(count)]
    return lax.ppermute(block, "band", route)


def swapped(block):
    count = lax.axis_size("band")
    return lax.ppermute(block, "band", [(i, i ^ 1) for i in range(count)])


def on_even():
    return lax.axis_index("band") % 2 == 0


def by_permutes():
    count = lax.axis_size("dom")
    return count <= 8 and count & (count - 1) == 0


def from_all_domains(block):
    count = lax.axis_size("dom")
    if by_permutes():
        routes = [[(i, i ^ mask) for i in range(count)] for mask in range(1, count)]
        return [block] + [lax.ppermute(block, "dom", route) for route in routes]
    whole = lax.all_gather(block, "dom")
    return [whole[d] for d in range(count)]


def domain_at(place):
    return lax.axis_index("dom") ^ place if by_permutes() else place


def tile_of(extent, most):
    return max(w for w in range(128, most + 1, 128) if extent % w == 0)


def parts_of(points):
    part = points // 3
    return (points - part, part) if part % 128 == 0 else (points // 2, points // 2)


def turn_kernel(coupling_ref, out_ref):
    owned, rank = coupling_ref.shape
    whole = coupling_ref[...]
    high = whole.astype(BF16)
    unit = lax.broadcasted_iota(jnp.int32, (rank, rank), 0) == lax.broadcasted_iota(
        jnp.int32, (rank, rank), 1
    )
    unit = jnp.where(unit, 1.0, 0.0).astype(BF16)
    for i, piece in enumerate((high, (whole - high.astype(F32)).astype(BF16))):
        turned = lax.dot_general(unit, piece, NT, preferred_element_type=F32)
        out_ref[:, i * owned : (i + 1) * owned] = turned.astype(BF16)


def project_kernel(orb_ref, proj_ref, turned_ref, out_ref, *own_refs):
    width, points = orb_ref.shape
    out_ref[width:, : turned_ref.shape[1]] = turned_ref[...]
    at = 0
    for own_ref in own_refs:
        own_ref[...] = orb_ref[:, at : at + own_ref.shape[1]]
        at += own_ref.shape[1]
    tile = tile_of(points, 1024)
    total = None
    for at in range(0, points, tile):
        term = lax.dot_general(
            proj_ref[:, at : at + tile], orb_ref[:, at : at + tile], NT, preferred_element_type=F32
        )
        total = term if total is None else total + term
    out_ref[:width, :] = total.T.astype(BF16)


def project(orbitals, proj, coupling):
    width, points = orbitals.shape
    owned, rank = coupling.shape
    turned = call(
        turn_kernel, "turn", [((rank, 2 * owned), BF16)], [coupling], cost=TURN
    )[0]
    outs = [((width + rank, proj.shape[0]), BF16)]
    outs += [((width, extent), BF16) for extent in parts_of(points)]
    return call(project_kernel, "project", outs, [orbitals, proj, turned])


def couple_kernel(count, slots, owned, slot_ref, *refs):
    loads, pass_ref = refs[:count], refs[count]
    out_ref, passed_ref, pick, high_ref, low_ref = refs[count + 1 :]
    passed_ref[...] = pass_ref[...]
    width, flat = out_ref.shape
    rank = flat // slots
    me = lax.axis_index("dom")
    lanes = lax.broadcasted_iota(jnp.int32, (rank, flat), 1)
    unit = lanes % rank == lax.broadcasted_iota(jnp.int32, (rank, flat), 0)
    lane_slot = lanes // rank

    atoms = jnp.zeros((rank, flat), jnp.int32)
    for k in range(slots):
        atoms = jnp.where(lane_slot == k, slot_ref[me, k], atoms)

    columns = None
    for place in range(count):
        owner = domain_at(place)
        for a in range(owned):
            hit = unit & (atoms == owner * owned + a)
            pick[a * rank : (a + 1) * rank, :] = jnp.where(hit, 1.0, 0.0).astype(BF16)
        parts = [loads[place][width:, i * owned * rank : (i + 1) * owned * rank] for i in (0, 1)]
        term = jnp.dot(jnp.concatenate(parts, 0), pick[...], preferred_element_type=F32)
        columns = term if columns is None else columns + term
    high, low = columns[:rank], columns[rank:]

    total = None
    for place in range(count):
        domain = domain_at(place)
        for k in range(slots):
            hit = atoms == slot_ref[domain, k]
            rows = slice(k * rank, (k + 1) * rank)
            high_ref[rows, :] = jnp.where(hit, high, 0.0).astype(BF16)
            low_ref[rows, :] = jnp.where(hit, low, 0.0).astype(BF16)
        block = loads[place][:width, :]
        term = jnp.dot(block, high_ref[...], preferred_element_type=F32)
        term += jnp.dot(block, low_ref[...], preferred_element_type=F32)
        total = term if total is None else total + term
    out_ref[...] = total.astype(BF16)


def couple(slot_atom, loads, width, owned, passed):
    flat = loads[0].shape[1]
    slots = slot_atom.shape[1]
    return call(
        functools.partial(couple_kernel, len(loads), slots, owned),
        "couple",
        [((width, flat), BF16), (passed.shape, passed.dtype)],
        [slot_atom, *loads, passed],
        [
            pltpu.VMEM((owned * (flat // slots), flat), BF16),
            pltpu.VMEM((flat, flat), BF16),
            pltpu.VMEM((flat, flat), BF16),
        ],
        first=SMEM,
        cost=COUPLE,
    )


def choose_kernel(count, *refs):
    evens, odd_ref, out_ref = refs[:count], refs[count], refs[-1]

    @pl.when(on_even())
    def _():
        at = 0
        for even_ref in evens:
            out_ref[:, at : at + even_ref.shape[1]] = even_ref[...]
            at += even_ref.shape[1]

    @pl.when(jnp.logical_not(on_even()))
    def _():
        out_ref[...] = odd_ref[...]


def choose(evens, odd, *after):
    outs = [(odd.shape, odd.dtype)]
    return call(
        functools.partial(choose_kernel, len(evens)), "choose", outs, [*evens, odd, *after]
    )[0]


def by_distance(rot_ref, width):
    tiles = [rot_ref[:, s * width : (s + 1) * width] for s in range(4)]
    even = on_even()
    one, three = tiles[1].astype(F32), tiles[3].astype(F32)
    by_swap = jnp.where(even, one, three).astype(BF16)
    by_ring = jnp.where(even, three, one).astype(BF16)
    return [tiles[0], by_swap, tiles[2], by_ring]


def apply_kernel(rot_ref, mine, one, two, three, proj_ref, out_ref):
    width, flat = mine.shape
    points = proj_ref.shape[1]
    mixed = None
    blocks = [mine, one, two, three]
    for s, block in enumerate(blocks):
        term = jnp.dot(
            rot_ref[:, s * width : (s + 1) * width], block[...], preferred_element_type=F32
        )
        mixed = term if mixed is None else mixed + term
    mixed = mixed.astype(BF16)
    tile = tile_of(points, 1024)
    for at in range(0, points, tile):
        out_ref[:, at : at + tile] = jnp.dot(
            mixed, proj_ref[:, at : at + tile], preferred_element_type=F32
        )


def finish_kernel(rot_ref, own, swap, two, ring, applied, out_hbm, stack, out_ref, sems):
    width, points = own.shape
    turn = jnp.concatenate(by_distance(rot_ref, width), axis=1)
    pieces = sems.shape[0]
    tile = points // pieces
    copies = []
    for i in range(pieces):
        here = slice(i * tile, (i + 1) * tile)
        for s, ref in enumerate((own, swap, two, ring)):
            stack[s * width : (s + 1) * width, here] = ref[:, here]
        rotated = jnp.dot(turn, stack[:, here], preferred_element_type=F32)
        added = rotated.astype(BF16).astype(F32) + applied[:, here]
        out_ref[:, here] = added.astype(out_ref.dtype)
        part = (slice(None), pl.ds(i * tile, tile))
        copies.append(pltpu.make_async_copy(out_ref.at[part], out_hbm.at[part], sems.at[i]))
        copies[-1].start()
    for copy in copies:
        copy.wait()


def finish(*args):
    width, points = args[-1].shape
    pieces = points // tile_of(points, 1024)
    return pl.pallas_call(
        finish_kernel,
        in_specs=[VMEM] * len(args),
        out_specs=pl.BlockSpec(memory_space=pl.ANY),
        out_shape=jax.ShapeDtypeStruct((width, points), BF16),
        scratch_shapes=[
            pltpu.VMEM((4 * width, points), BF16),
            pltpu.VMEM((width, points), BF16),
            pltpu.SemaphoreType.DMA((pieces,)),
        ],
        compiler_params=ROOM,
        cost_estimate=flops(0),
        name="finish",
    )(*args)


def on_device(orbitals, rotation, projectors, coupling, slot_atom):
    width, points = orbitals.shape
    slot_count, rank, _ = projectors.shape
    owned = coupling.shape[0]
    proj = projectors.reshape(slot_count * rank, points)

    mixed = along_bands(orbitals, 2, (1,))
    load, *own = project(orbitals, proj, coupling.reshape(owned * rank, rank))
    loads = from_all_domains(load)
    two_even = [along_bands(own[0], 2, (0,))]
    mine, own[1] = couple(slot_atom, loads, width, owned, own[1])
    mine_two = along_bands(mine, 2)
    two_even.append(along_bands(own[1], 2, (0,)))
    mixed = choose([mixed], mixed, mine)
    ring = along_bands(mixed, 1)
    mine_three = along_bands(mine_two, 1)
    mine_one = swapped(choose([mine], mine_two, mixed))
    applied = call(
        apply_kernel,
        "apply",
        [((width, points), F32)],
        [rotation, mine, mine_one, mine_two, mine_three, proj],
        cost=APPLY,
    )[0]
    two = choose(two_even, mixed, applied)
    swap = swapped(two)
    return finish(rotation, orbitals, swap, two, ring, applied)


def solution(mesh):
    in_specs = (P("band", "dom"), P("band", None), P(None, None, "dom"), P("dom", None, None), P())
    out_specs = P("band", "dom")
    return jax.shard_map(
        on_device, mesh=mesh, in_specs=in_specs, out_specs=out_specs, check_vma=False
    )
```

profile of v0, /device:TPU:0, one launch (start us, length us, event | category | flops | bytes accessed | tf_op | source)
XLA Modules:
  0.0 39.6 jit_solution(11944492056610887777)
XLA Ops:
  0.0 0.0 copy-start.1
  0.0 0.0 copy-start
  0.0 2.2 %collective-permute-start.5 = (bf16[64,6144]{1,0:T(8,128)(2,1)}, bf16[64,6144]{1,0:T(8,128)(2,1)S(1)}, u32[]{:S(2)}, u32[]{:S(2)}) collective-permute-start(bf16[64,6144]{1,0:T(8,128)(2,1)} %own.1), channel_id=1, source_target_pairs={{0,0},{4,12},{8,8},{12,20},{16,16},{20,28},{24,24},{28,4},{1,1},{5... | collective-permute-start | bytes 2359304 | tf_op jit(solution)/shard_map/ppermute | solution.py:42
  2.3 0.0 copy-start.3
  2.3 0.9 %copy-done.3 = f32[16,16,16]{2,1,0:T(8,128)S(1)} copy-done((f32[16,16,16]{2,1,0:T(8,128)S(1)}, f32[16,16,16]{2,1,0:T(8,128)}, u32[]{:S(2)}) %copy-start.3) | copy-done | bytes 16408
  3.2 0.1 turn.1.turned_ref
  3.3 0.0 copy-start.4
  3.3 0.0 copy-done.1
  3.3 0.0 copy-done
  3.3 1.9 %project.1 = (bf16[80,512]{1,0:T(8,128)(2,1)S(1)}, bf16[64,4096]{1,0:T(8,128)(2,1)S(1)}, bf16[64,2048]{1,0:T(8,128)(2,1)S(1)}) custom-call(bf16[64,6144]{1,0:T(8,128)(2,1)S(1)} %copy-done.1, bf16[512,6144]{1,0:T(8,128)(2,1)S(1)} %bitcast.2, bf16[16,512]{1,0:T(8,128)(2,1)S(1)} %turn.1.turned_ref), custom_call_target="tpu_custom_call" | custom-call | tf_op jit(solution)/shard_map/project/pallas_call | solution.py:27
  5.2 0.0 copy-start.2
  5.2 4.0 %collective-permute-start.3 = (bf16[80,512]{1,0:T(8,128)(2,1)S(1)}, bf16[80,512]{1,0:T(8,128)(2,1)S(1)}, u32[]{:S(2)}, u32[]{:S(2)}) collective-permute-start(bf16[80,512]{1,0:T(8,128)(2,1)S(1)} %get-tuple-element.11.refs_0_), channel_id=1, source_target_pairs={{0,3},{1,2},{2,1},{3,0},{4,7},{5,6},{6,5},{7,4},{8,11},{9,10},{10,... | collective-permute-start | bytes 245768 | tf_op jit(solution)/shard_map/ppermute | solution.py:63
  9.2 0.5 %collective-permute-start.2 = (bf16[80,512]{1,0:T(8,128)(2,1)S(1)}, bf16[80,512]{1,0:T(8,128)(2,1)S(1)}, u32[]{:S(2)}, u32[]{:S(2)}) collective-permute-start(bf16[80,512]{1,0:T(8,128)(2,1)S(1)} %get-tuple-element.11.refs_0_), channel_id=1, source_target_pairs={{0,2},{1,3},{2,0},{3,1},{4,6},{5,7},{6,4},{7,5},{8,10},{9,11},{10,... | collective-permute-start | bytes 245768 | tf_op jit(solution)/shard_map/ppermute | solution.py:63
  9.7 0.1 collective-permute-start.1
  9.8 3.9 %collective-permute-start = (bf16[64,4096]{1,0:T(8,128)(2,1)S(1)}, bf16[64,4096]{1,0:T(8,128)(2,1)S(1)}, u32[]{:S(2)}, u32[]{:S(2)}) collective-permute-start(bf16[64,4096]{1,0:T(8,128)(2,1)S(1)} %get-tuple-element.10), channel_id=1, source_target_pairs={{0,8},{4,4},{8,16},{12,12},{16,24},{20,20},{24,0},{28,28},{1,9},{5... | collective-permute-start | bytes 1572872 | tf_op jit(solution)/shard_map/ppermute | solution.py:42
  13.7 0.0 collective-permute-done.3.refs_3_
  13.7 0.6 %collective-permute-done.2.refs_2_ = bf16[80,512]{1,0:T(8,128)(2,1)S(1)} collective-permute-done((bf16[80,512]{1,0:T(8,128)(2,1)S(1)}, bf16[80,512]{1,0:T(8,128)(2,1)S(1)}, u32[]{:S(2)}, u32[]{:S(2)}) %collective-permute-start.2) | collective-permute-done | bytes 81952 | tf_op jit(solution)/shard_map/ppermute | solution.py:63
  14.3 0.5 %collective-permute-done.1.refs_1_ = bf16[80,512]{1,0:T(8,128)(2,1)S(1)} collective-permute-done((bf16[80,512]{1,0:T(8,128)(2,1)S(1)}, bf16[80,512]{1,0:T(8,128)(2,1)S(1)}, u32[]{:S(2)}, u32[]{:S(2)}) %collective-permute-start.1) | collective-permute-done | bytes 81952 | tf_op jit(solution)/shard_map/ppermute | solution.py:63
  14.8 0.0 copy-done.4
  14.8 1.5 %couple.1 = (bf16[64,512]{1,0:T(8,128)(2,1)S(1)}, bf16[64,2048]{1,0:T(8,128)(2,1)S(1)}) custom-call(s32[4,32]{1,0:T(4,128)S(1)} %copy-done.4, bf16[80,512]{1,0:T(8,128)(2,1)S(1)} %get-tuple-element.11.refs_0_, bf16[80,512]{1,0:T(8,128)(2,1)S(1)} %collective-permute-done.1.refs_1_, bf16[80,512]{1,0:T(8,128)(2,1)S(1)} %collective-permute-done.2.refs_2_, ...), custom_call_target="tpu_custom_call" | custom-call | flops 2000000000 | tf_op jit(solution)/shard_map/couple/pallas_call | solution.py:27
  16.3 1.6 %collective-permute-start.6 = (bf16[64,512]{1,0:T(8,128)(2,1)S(1)}, bf16[64,512]{1,0:T(8,128)(2,1)S(1)}, u32[]{:S(2)}, u32[]{:S(2)}) collective-permute-start(bf16[64,512]{1,0:T(8,128)(2,1)S(1)} %get-tuple-element.14.refs_2_.refs_0_.mine), channel_id=1, source_target_pairs={{0,8},{4,12},{8,16},{12,20},{16,24},{20,28},{24,0},{28,4},{1,9},{5... | collective-permute-start | bytes 196616 | tf_op jit(solution)/shard_map/ppermute | solution.py:42
  17.9 3.5 %collective-permute-start.4 = (bf16[64,2048]{1,0:T(8,128)(2,1)S(1)}, bf16[64,2048]{1,0:T(8,128)(2,1)S(1)}, u32[]{:S(2)}, u32[]{:S(2)}) collective-permute-start(bf16[64,2048]{1,0:T(8,128)(2,1)S(1)} %get-tuple-element.13), channel_id=1, source_target_pairs={{0,8},{4,4},{8,16},{12,12},{16,24},{20,20},{24,0},{28,28},{1,9},{5... | collective-permute-start | bytes 786440 | tf_op jit(solution)/shard_map/ppermute | solution.py:42
  21.4 2.9 %collective-permute-done.6.refs_1_.two = bf16[64,512]{1,0:T(8,128)(2,1)S(1)} collective-permute-done((bf16[64,512]{1,0:T(8,128)(2,1)S(1)}, bf16[64,512]{1,0:T(8,128)(2,1)S(1)}, u32[]{:S(2)}, u32[]{:S(2)}) %collective-permute-start.6) | collective-permute-done | bytes 65568 | tf_op jit(solution)/shard_map/ppermute | solution.py:42
  24.3 0.0 collective-permute-start.8
  24.3 0.0 collective-permute-done.5.refs_0_.refs_1_
  24.3 0.1 choose.3.refs_2_
  24.4 0.2 collective-permute-start.7
  24.5 0.4 %collective-permute-start.10 = (bf16[64,6144]{1,0:T(8,128)(2,1)S(1)}, bf16[64,6144]{1,0:T(8,128)(2,1)S(1)}, u32[]{:S(2)}, u32[]{:S(2)}) collective-permute-start(bf16[64,6144]{1,0:T(8,128)(2,1)S(1)} %choose.3.refs_2_), channel_id=1, source_target_pairs={{0,4},{4,8},{8,12},{12,16},{16,20},{20,24},{24,28},{28,0},{1,5},{5... | collective-permute-start | bytes 2359304 | tf_op jit(solution)/shard_map/ppermute | solution.py:42
  25.0 4.8 %collective-permute-done.8.three = bf16[64,512]{1,0:T(8,128)(2,1)S(1)} collective-permute-done((bf16[64,512]{1,0:T(8,128)(2,1)S(1)}, bf16[64,512]{1,0:T(8,128)(2,1)S(1)}, u32[]{:S(2)}, u32[]{:S(2)}) %collective-permute-start.8) | collective-permute-done | bytes 65568 | tf_op jit(solution)/shard_map/ppermute | solution.py:42
  29.8 0.0 collective-permute-done.7.one
  29.8 0.0 copy-done.2
  29.8 1.4 %apply.1.refs_3_.applied = f32[64,6144]{1,0:T(8,128)S(1)} custom-call(bf16[64,256]{1,0:T(8,128)(2,1)S(1)} %copy-done.2, bf16[64,512]{1,0:T(8,128)(2,1)S(1)} %get-tuple-element.14.refs_2_.refs_0_.mine, bf16[64,512]{1,0:T(8,128)(2,1)S(1)} %collective-permute-done.7.one, bf16[64,512]{1,0:T(8,128)(2,1)S(1)} %collective-permute-done.6.refs_1_.two, ...), custom_call_target="tpu_custom_call" | custom-call | flops 2000000000 | tf_op jit(solution)/shard_map/apply/pallas_call | solution.py:27
  31.2 0.0 collective-permute-done.4.refs_1_
  31.2 0.0 collective-permute-done.refs_0_
  31.2 0.1 choose.5.two
  31.3 0.1 collective-permute-start.9
  31.4 6.8 %collective-permute-done.10.ring = bf16[64,6144]{1,0:T(8,128)(2,1)S(1)} collective-permute-done((bf16[64,6144]{1,0:T(8,128)(2,1)S(1)}, bf16[64,6144]{1,0:T(8,128)(2,1)S(1)}, u32[]{:S(2)}, u32[]{:S(2)}) %collective-permute-start.10) | collective-permute-done | bytes 786464 | tf_op jit(solution)/shard_map/ppermute | solution.py:42
  38.2 0.0 collective-permute-done.9.swap
  38.2 1.4 %finish.1 = bf16[64,6144]{1,0:T(8,128)(2,1)} custom-call(bf16[64,256]{1,0:T(8,128)(2,1)S(1)} %copy-done.2, bf16[64,6144]{1,0:T(8,128)(2,1)S(1)} %copy-done.1, bf16[64,6144]{1,0:T(8,128)(2,1)S(1)} %collective-permute-done.9.swap, bf16[64,6144]{1,0:T(8,128)(2,1)S(1)} %choose.5.two, bf16[64,6144]{1,0:T(8,128)(2,1)S(1)} %collective-permute-done.10.ring, ...), custom_call_target="tpu_custom_call" | custom-call | tf_op jit(solution)/shard_map/finish/pallas_call | solution.py:253
  (1 shorter events, 0.0 us)
Async XLA Ops:
  0.0 3.3 %copy-start.1 = (bf16[64,6144]{1,0:T(8,128)(2,1)S(1)}, bf16[64,6144]{1,0:T(8,128)(2,1)}, u32[]{:S(2)}) copy-start(bf16[64,6144]{1,0:T(8,128)(2,1)} %own.1) | copy-start | bytes 2359300
  0.0 3.3 %copy-start = (bf16[32,16,6144]{2,1,0:T(8,128)(2,1)S(1)}, bf16[32,16,6144]{2,1,0:T(8,128)(2,1)}, u32[]{:S(2)}) copy-start(bf16[32,16,6144]{2,1,0:T(8,128)(2,1)} %param.7) | copy-start | bytes 18874372
  0.0 24.3 %collective-permute-start.5 = (bf16[64,6144]{1,0:T(8,128)(2,1)}, bf16[64,6144]{1,0:T(8,128)(2,1)S(1)}, u32[]{:S(2)}, u32[]{:S(2)}) collective-permute-start(bf16[64,6144]{1,0:T(8,128)(2,1)} %own.1), channel_id=1, source_target_pairs={{0,0},{4,12},{8,8},{12,20},{16,16},{20,28},{24,24},{28,4},{1,1},{5... | collective-permute-start | bytes 2359304 | tf_op jit(solution)/shard_map/ppermute | solution.py:42
  2.3 0.9 %copy-start.3 = (f32[16,16,16]{2,1,0:T(8,128)S(1)}, f32[16,16,16]{2,1,0:T(8,128)}, u32[]{:S(2)}) copy-start(f32[16,16,16]{2,1,0:T(8,128)} %param.8) | copy-start | bytes 49156
  3.3 11.5 %copy-start.4 = (s32[4,32]{1,0:T(4,128)S(1)}, s32[4,32]{1,0:T(4,128)}, u32[]{:S(2)}) copy-start(s32[4,32]{1,0:T(4,128)} %slot_ref.1) | copy-start | bytes 1540
  5.2 24.6 %copy-start.2 = (bf16[64,256]{1,0:T(8,128)(2,1)S(1)}, bf16[64,256]{1,0:T(8,128)(2,1)}, u32[]{:S(2)}) copy-start(bf16[64,256]{1,0:T(8,128)(2,1)} %rot_ref.3) | copy-start | bytes 98308
  5.2 8.5 %collective-permute-start.3 = (bf16[80,512]{1,0:T(8,128)(2,1)S(1)}, bf16[80,512]{1,0:T(8,128)(2,1)S(1)}, u32[]{:S(2)}, u32[]{:S(2)}) collective-permute-start(bf16[80,512]{1,0:T(8,128)(2,1)S(1)} %get-tuple-element.11.refs_0_), channel_id=1, source_target_pairs={{0,3},{1,2},{2,1},{3,0},{4,7},{5,6},{6,5},{7,4},{8,11},{9,10},{10,... | collective-permute-start | bytes 245768 | tf_op jit(solution)/shard_map/ppermute | solution.py:63
  9.2 5.1 %collective-permute-start.2 = (bf16[80,512]{1,0:T(8,128)(2,1)S(1)}, bf16[80,512]{1,0:T(8,128)(2,1)S(1)}, u32[]{:S(2)}, u32[]{:S(2)}) collective-permute-start(bf16[80,512]{1,0:T(8,128)(2,1)S(1)} %get-tuple-element.11.refs_0_), channel_id=1, source_target_pairs={{0,2},{1,3},{2,0},{3,1},{4,6},{5,7},{6,4},{7,5},{8,10},{9,11},{10,... | collective-permute-start | bytes 245768 | tf_op jit(solution)/shard_map/ppermute | solution.py:63
  9.7 5.1 %collective-permute-start.1 = (bf16[80,512]{1,0:T(8,128)(2,1)S(1)}, bf16[80,512]{1,0:T(8,128)(2,1)S(1)}, u32[]{:S(2)}, u32[]{:S(2)}) collective-permute-start(bf16[80,512]{1,0:T(8,128)(2,1)S(1)} %get-tuple-element.11.refs_0_), channel_id=1, source_target_pairs={{0,1},{1,0},{2,3},{3,2},{4,5},{5,4},{6,7},{7,6},{8,9},{9,8},{10,11... | collective-permute-start | bytes 245768 | tf_op jit(solution)/shard_map/ppermute | solution.py:63
  9.8 21.4 %collective-permute-start = (bf16[64,4096]{1,0:T(8,128)(2,1)S(1)}, bf16[64,4096]{1,0:T(8,128)(2,1)S(1)}, u32[]{:S(2)}, u32[]{:S(2)}) collective-permute-start(bf16[64,4096]{1,0:T(8,128)(2,1)S(1)} %get-tuple-element.10), channel_id=1, source_target_pairs={{0,8},{4,4},{8,16},{12,12},{16,24},{20,20},{24,0},{28,28},{1,9},{5... | collective-permute-start | bytes 1572872 | tf_op jit(solution)/shard_map/ppermute | solution.py:42
  16.3 8.0 %collective-permute-start.6 = (bf16[64,512]{1,0:T(8,128)(2,1)S(1)}, bf16[64,512]{1,0:T(8,128)(2,1)S(1)}, u32[]{:S(2)}, u32[]{:S(2)}) collective-permute-start(bf16[64,512]{1,0:T(8,128)(2,1)S(1)} %get-tuple-element.14.refs_2_.refs_0_.mine), channel_id=1, source_target_pairs={{0,8},{4,12},{8,16},{12,20},{16,24},{20,28},{24,0},{28,4},{1,9},{5... | collective-permute-start | bytes 196616 | tf_op jit(solution)/shard_map/ppermute | solution.py:42
  17.9 13.3 %collective-permute-start.4 = (bf16[64,2048]{1,0:T(8,128)(2,1)S(1)}, bf16[64,2048]{1,0:T(8,128)(2,1)S(1)}, u32[]{:S(2)}, u32[]{:S(2)}) collective-permute-start(bf16[64,2048]{1,0:T(8,128)(2,1)S(1)} %get-tuple-element.13), channel_id=1, source_target_pairs={{0,8},{4,4},{8,16},{12,12},{16,24},{20,20},{24,0},{28,28},{1,9},{5... | collective-permute-start | bytes 786440 | tf_op jit(solution)/shard_map/ppermute | solution.py:42
  24.3 5.5 %collective-permute-start.8 = (bf16[64,512]{1,0:T(8,128)(2,1)S(1)}, bf16[64,512]{1,0:T(8,128)(2,1)S(1)}, u32[]{:S(2)}, u32[]{:S(2)}) collective-permute-start(bf16[64,512]{1,0:T(8,128)(2,1)S(1)} %collective-permute-done.6.refs_1_.two), channel_id=1, source_target_pairs={{0,4},{4,8},{8,12},{12,16},{16,20},{20,24},{24,28},{28,0},{1,5},{5... | collective-permute-start | bytes 196616 | tf_op jit(solution)/shard_map/ppermute | solution.py:42
  24.4 5.4 %collective-permute-start.7 = (bf16[64,512]{1,0:T(8,128)(2,1)S(1)}, bf16[64,512]{1,0:T(8,128)(2,1)S(1)}, u32[]{:S(2)}, u32[]{:S(2)}) collective-permute-start(bf16[64,512]{1,0:T(8,128)(2,1)S(1)} %choose.4), channel_id=1, source_target_pairs={{0,4},{4,0},{8,12},{12,8},{16,20},{20,16},{24,28},{28,24},{1,5},{5... | collective-permute-start | bytes 196616 | tf_op jit(solution)/shard_map/ppermute | solution.py:47
  24.5 13.7 %collective-permute-start.10 = (bf16[64,6144]{1,0:T(8,128)(2,1)S(1)}, bf16[64,6144]{1,0:T(8,128)(2,1)S(1)}, u32[]{:S(2)}, u32[]{:S(2)}) collective-permute-start(bf16[64,6144]{1,0:T(8,128)(2,1)S(1)} %choose.3.refs_2_), channel_id=1, source_target_pairs={{0,4},{4,8},{8,12},{12,16},{16,20},{20,24},{24,28},{28,0},{1,5},{5... | collective-permute-start | bytes 2359304 | tf_op jit(solution)/shard_map/ppermute | solution.py:42
  31.3 6.9 %collective-permute-start.9 = (bf16[64,6144]{1,0:T(8,128)(2,1)S(1)}, bf16[64,6144]{1,0:T(8,128)(2,1)S(1)}, u32[]{:S(2)}, u32[]{:S(2)}) collective-permute-start(bf16[64,6144]{1,0:T(8,128)(2,1)S(1)} %choose.5.two), channel_id=1, source_target_pairs={{0,4},{4,0},{8,12},{12,8},{16,20},{20,16},{24,28},{28,24},{1,5},{5... | collective-permute-start | bytes 2359304 | tf_op jit(solution)/shard_map/ppermute | solution.py:47
where the time goes:
time: 39.8 us; the launch traced here: 39.6 us
  starting transfers between devices  16.5 us (41%)
  waiting for transfers between devices  15.5 us (39%)
  Pallas kernels  6.51 us (16%)
  local copies, waits for them, and re-layouts  0.94 us (2%)
    ppermute x6, waiting for transfers between devices, along_bands(): return lax.ppermute(block, 'band', route)  14.5 us
    ppermute x6, starting transfers between devices, along_bands(): return lax.ppermute(block, 'band', route)  11.6 us
    pallas_call x7, Pallas kernels, call(): pl.pallas_call(kernel, in_specs=[first] + [VMEM] * (len(args) - 1), out_s...  5.13 us
    ppermute x3, starting transfers between devices, from_all_domains(): return [block] + [lax.ppermute(block, 'dom', route) for route in routes]  4.6 us
    pallas_call x1, Pallas kernels, finish(): pl.pallas_call(finish_kernel, in_specs=[VMEM] * len(args), out_specs=pl.B...  1.38 us
    ppermute x3, waiting for transfers between devices, from_all_domains(): return [block] + [lax.ppermute(block, 'dom', route) for route in routes]  1.05 us
    unnamed x10, local copies, waits for them, and re-layouts  0.94 us
  transfers between devices with their start and end apart: 11, of which 5 were waited for; matrix products, arithmetic and copies ran while one was open for 0% of the time, Pallas kernels for 13%

commit v1 on v0

--- a/solution.py
+++ b/solution.py
@@ -9,7 +9,7 @@
 
 TURN = 3 * 10**9
 COUPLE = 2 * 10**9
-APPLY = 2 * 10**9
+APPLY = 5 * 10**9
 F32 = jnp.float32
 BF16 = jnp.bfloat16
 ROOM = pltpu.CompilerParams(vmem_limit_bytes=8 * 2**20)
@@ -36,10 +36,9 @@
     )(*args)
 
 
-def along_bands(block, distance, senders=(0, 1)):
+def along_bands(block, distance):
     count = lax.axis_size("band")
-    route = [(i, (i + distance) % count if i % 2 in senders else i) for i in range(count)]
-    return lax.ppermute(block, "band", route)
+    return lax.ppermute(block, "band", [(i, (i + distance) % count) for i in range(count)])
 
 
 def swapped(block):
@@ -71,11 +70,6 @@
 
 def tile_of(extent, most):
     return max(w for w in range(128, most + 1, 128) if extent % w == 0)
-
-
-def parts_of(points):
-    part = points // 3
-    return (points - part, part) if part % 128 == 0 else (points // 2, points // 2)
 
 
 def turn_kernel(coupling_ref, out_ref):
@@ -91,13 +85,9 @@
         out_ref[:, i * owned : (i + 1) * owned] = turned.astype(BF16)
 
 
-def project_kernel(orb_ref, proj_ref, turned_ref, out_ref, *own_refs):
+def project_kernel(orb_ref, proj_ref, turned_ref, out_ref):
     width, points = orb_ref.shape
     out_ref[width:, : turned_ref.shape[1]] = turned_ref[...]
-    at = 0
-    for own_ref in own_refs:
-        own_ref[...] = orb_ref[:, at : at + own_ref.shape[1]]
-        at += own_ref.shape[1]
     tile = tile_of(points, 1024)
     total = None
     for at in range(0, points, tile):
@@ -115,14 +105,12 @@
         turn_kernel, "turn", [((rank, 2 * owned), BF16)], [coupling], cost=TURN
     )[0]
     outs = [((width + rank, proj.shape[0]), BF16)]
-    outs += [((width, extent), BF16) for extent in parts_of(points)]
-    return call(project_kernel, "project", outs, [orbitals, proj, turned])
+    return call(project_kernel, "project", outs, [orbitals, proj, turned])[0]
 
 
 def couple_kernel(count, slots, owned, slot_ref, *refs):
-    loads, pass_ref = refs[:count], refs[count]
-    out_ref, passed_ref, pick, high_ref, low_ref = refs[count + 1 :]
-    passed_ref[...] = pass_ref[...]
+    loads = refs[:count]
+    out_ref, pick, high_ref, low_ref = refs[count:]
     width, flat = out_ref.shape
     rank = flat // slots
     me = lax.axis_index("dom")
@@ -160,14 +148,14 @@
     out_ref[...] = total.astype(BF16)
 
 
-def couple(slot_atom, loads, width, owned, passed):
+def couple(slot_atom, loads, width, owned):
     flat = loads[0].shape[1]
     slots = slot_atom.shape[1]
     return call(
         functools.partial(couple_kernel, len(loads), slots, owned),
         "couple",
-        [((width, flat), BF16), (passed.shape, passed.dtype)],
-        [slot_atom, *loads, passed],
+        [((width, flat), BF16)],
+        [slot_atom, *loads],
         [
             pltpu.VMEM((owned * (flat // slots), flat), BF16),
             pltpu.VMEM((flat, flat), BF16),
@@ -175,38 +163,41 @@
         ],
         first=SMEM,
         cost=COUPLE,
-    )
-
-
-def choose_kernel(count, *refs):
-    evens, odd_ref, out_ref = refs[:count], refs[count], refs[-1]
+    )[0]
+
+
+def hold_kernel(block_ref, after_ref, out_ref):
+    out_ref[...] = block_ref[...]
+
+
+def hold(block, after):
+    return call(hold_kernel, "hold", [(block.shape, block.dtype)], [block, after])[0]
+
+
+def choose_kernel(mine, mine_two, own, two_a, two_b, coef_ref, upper_ref, lower_ref, held_ref):
+    cut, half = two_a.shape[0], upper_ref.shape[0]
 
     @pl.when(on_even())
     def _():
-        at = 0
-        for even_ref in evens:
-            out_ref[:, at : at + even_ref.shape[1]] = even_ref[...]
-            at += even_ref.shape[1]
+        coef_ref[...] = mine[...]
+        upper_ref[...] = own[:half, :]
+        lower_ref[...] = own[half:, :]
 
     @pl.when(jnp.logical_not(on_even()))
     def _():
-        out_ref[...] = odd_ref[...]
-
-
-def choose(evens, odd, *after):
-    outs = [(odd.shape, odd.dtype)]
-    return call(
-        functools.partial(choose_kernel, len(evens)), "choose", outs, [*evens, odd, *after]
-    )[0]
-
-
-def by_distance(rot_ref, width):
-    tiles = [rot_ref[:, s * width : (s + 1) * width] for s in range(4)]
-    even = on_even()
-    one, three = tiles[1].astype(F32), tiles[3].astype(F32)
-    by_swap = jnp.where(even, one, three).astype(BF16)
-    by_ring = jnp.where(even, three, one).astype(BF16)
-    return [tiles[0], by_swap, tiles[2], by_ring]
+        coef_ref[...] = mine_two[...]
+        upper_ref[...] = two_a[:half, :]
+        lower_ref[: cut - half, :] = two_a[half:, :]
+        lower_ref[cut - half :, :] = two_b[...]
+
+    held_ref[...] = two_b[...]
+
+
+def choose(mine, mine_two, own, two_a, two_b):
+    args = [mine, mine_two, own, two_a, two_b]
+    half = ((own.shape[0] // 2, own.shape[1]), own.dtype)
+    outs = [(mine.shape, mine.dtype), half, half, (two_b.shape, two_b.dtype)]
+    return call(choose_kernel, "choose", outs, args)
 
 
 def apply_kernel(rot_ref, mine, one, two, three, proj_ref, out_ref):
@@ -227,17 +218,20 @@
         )
 
 
-def finish_kernel(rot_ref, own, swap, two, ring, applied, out_hbm, stack, out_ref, sems):
+def finish_kernel(
+    rot_ref, own, one_a, one_b, two_a, two_b, three_a, three_b, applied, out_hbm, stack, out_ref, sems
+):
     width, points = own.shape
-    turn = jnp.concatenate(by_distance(rot_ref, width), axis=1)
     pieces = sems.shape[0]
     tile = points // pieces
     copies = []
     for i in range(pieces):
         here = slice(i * tile, (i + 1) * tile)
-        for s, ref in enumerate((own, swap, two, ring)):
-            stack[s * width : (s + 1) * width, here] = ref[:, here]
-        rotated = jnp.dot(turn, stack[:, here], preferred_element_type=F32)
+        at = 0
+        for ref in (own, one_a, one_b, two_a, two_b, three_a, three_b):
+            stack[at : at + ref.shape[0], here] = ref[:, here]
+            at += ref.shape[0]
+        rotated = jnp.dot(rot_ref[...], stack[:, here], preferred_element_type=F32)
         added = rotated.astype(BF16).astype(F32) + applied[:, here]
         out_ref[:, here] = added.astype(out_ref.dtype)
         part = (slice(None), pl.ds(i * tile, tile))
@@ -272,17 +266,18 @@
     owned = coupling.shape[0]
     proj = projectors.reshape(slot_count * rank, points)
 
-    mixed = along_bands(orbitals, 2, (1,))
-    load, *own = project(orbitals, proj, coupling.reshape(owned * rank, rank))
-    loads = from_all_domains(load)
-    two_even = [along_bands(own[0], 2, (0,))]
-    mine, own[1] = couple(slot_atom, loads, width, owned, own[1])
+    cut = width * 3 // 4
+    two_a = along_bands(orbitals[:cut], 2)
+    two_b = along_bands(orbitals[cut:], 2)
+    loads = from_all_domains(project(orbitals, proj, coupling.reshape(owned * rank, rank)))
+    mine = couple(slot_atom, loads, width, owned)
     mine_two = along_bands(mine, 2)
-    two_even.append(along_bands(own[1], 2, (0,)))
-    mixed = choose([mixed], mixed, mine)
-    ring = along_bands(mixed, 1)
+    three_a = along_bands(hold(two_a, mine), 1)
+    other, upper, lower, held = choose(mine, mine_two, orbitals, two_a, two_b)
     mine_three = along_bands(mine_two, 1)
-    mine_one = swapped(choose([mine], mine_two, mixed))
+    mine_one = swapped(other)
+    three_b = along_bands(held, 1)
+    one_a, one_b = swapped(upper), swapped(lower)
     applied = call(
         apply_kernel,
         "apply",
@@ -290,9 +285,7 @@
         [rotation, mine, mine_one, mine_two, mine_three, proj],
         cost=APPLY,
     )[0]
-    two = choose(two_even, mixed, applied)
-    swap = swapped(two)
-    return finish(rotation, orbitals, swap, two, ring, applied)
+    return finish(rotation, orbitals, one_a, one_b, two_a, two_b, three_a, three_b, applied)
 
 
 def solution(mesh):

time: 39.8 us -> 36.1 us (0.907)
  starting transfers between devices: 16.5 us -> 12.7 us
  local copies, waits for them, and re-layouts: 0.94 us -> 3.61 us
  waiting for transfers between devices: 15.5 us -> 13.1 us
    ppermute x6, starting transfers between devices: 11.6 us -> 6.46 us  [along_bands(): lax.ppermute(block, 'band', [(i, (i + distance) % count) for i in range(c...]
    ppermute x6, waiting for transfers between devices: 14.5 us -> 10.9 us  [along_bands(): lax.ppermute(block, 'band', [(i, (i + distance) % count) for i in range(c...]
    ppermute x2 -> x3, starting transfers between devices: 0.23 us -> 2.66 us  [swapped(): return lax.ppermute(block, 'band', [(i, i ^ 1) for i in range(count)])]
    unnamed x10 -> x12, local copies, waits for them, and re-layouts: 0.94 us -> 2.35 us
    slice x0 -> x2, local copies, waits for them, and re-layouts: none -> 1.27 us  [the longest x1 1.25 us: on_device(): two_a = along_bands(orbitals[:cut], 2)]
    ppermute x3, waiting for transfers between devices: 1.05 us -> 2.26 us  [from_all_domains(): return [block] + [lax.ppermute(block, 'dom', route) for route in routes]]
    ppermute x3, starting transfers between devices: 4.6 us -> 3.55 us  [from_all_domains(): return [block] + [lax.ppermute(block, 'dom', route) for route in routes]]
    pallas_call x7 -> x6, Pallas kernels: 5.13 us -> 5.03 us  [call(): pl.pallas_call(kernel, in_specs=[first] + [VMEM] * (len(args) - 1), out_s...]
  transfers between devices with their start and end apart: 11 -> 12, of which waited for: 5 -> 7; matrix products, arithmetic and copies ran while one was open for 0% -> 0% of each run, Pallas kernels for 13% -> 14%
where the time goes in v1:
time: 36.1 us; the launch traced here: 35.9 us
  waiting for transfers between devices  13.1 us (36%)
  starting transfers between devices  12.7 us (35%)
  Pallas kernels  6.43 us (18%)
  local copies, waits for them, and re-layouts  3.61 us (10%)
    ppermute x6, waiting for transfers between devices, along_bands(): lax.ppermute(block, 'band', [(i, (i + distance) % count) for i in range(c...  10.9 us
    ppermute x6, starting transfers between devices, along_bands(): lax.ppermute(block, 'band', [(i, (i + distance) % count) for i in range(c...  6.46 us
    pallas_call x6, Pallas kernels, call(): pl.pallas_call(kernel, in_specs=[first] + [VMEM] * (len(args) - 1), out_s...  5.03 us
    ppermute x3, starting transfers between devices, from_all_domains(): return [block] + [lax.ppermute(block, 'dom', route) for route in routes]  3.55 us
    ppermute x3, starting transfers between devices, swapped(): return lax.ppermute(block, 'band', [(i, i ^ 1) for i in range(count)])  2.66 us
    unnamed x12, local copies, waits for them, and re-layouts  2.35 us
    ppermute x3, waiting for transfers between devices, from_all_domains(): return [block] + [lax.ppermute(block, 'dom', route) for route in routes]  2.26 us
    pallas_call x1, Pallas kernels, finish(): pl.pallas_call(finish_kernel, in_specs=[VMEM] * len(args), out_specs=pl.B...  1.4 us
  transfers between devices with their start and end apart: 12, of which 7 were waited for; matrix products, arithmetic and copies ran while one was open for 0% of the time, Pallas kernels for 14%

profile of v1, /device:TPU:0, one launch (start us, length us, event | category | flops | bytes accessed | tf_op | source)
XLA Modules:
  0.0 35.9 jit_solution(18394802336974178468)
XLA Ops:
  0.0 0.0 copy-start
  0.0 0.0 slice-start
  0.0 1.3 %slice.6 = bf16[48,6144]{1,0:T(8,128)(2,1)S(1)} slice(bf16[64,6144]{1,0:T(8,128)(2,1)} %own.3), slice={[0:48], [0:6144]} | slice | bytes 1179648 | tf_op jit(solution)/shard_map/slice | solution.py:270
  1.3 3.1 %collective-permute-start.4 = (bf16[48,6144]{1,0:T(8,128)(2,1)S(1)}, bf16[48,6144]{1,0:T(8,128)(2,1)S(1)}, u32[]{:S(2)}, u32[]{:S(2)}) collective-permute-start(bf16[48,6144]{1,0:T(8,128)(2,1)S(1)} %slice.6), channel_id=1, source_target_pairs={{0,8},{4,12},{8,16},{12,20},{16,24},{20,28},{24,0},{28,4},{1,9},{5... | collective-permute-start | bytes 1769480 | tf_op jit(solution)/shard_map/ppermute | solution.py:41
  4.3 0.0 copy-start.2
  4.3 0.9 %copy-done.2 = f32[16,16,16]{2,1,0:T(8,128)S(1)} copy-done((f32[16,16,16]{2,1,0:T(8,128)S(1)}, f32[16,16,16]{2,1,0:T(8,128)}, u32[]{:S(2)}) %copy-start.2) | copy-done | bytes 16408
  5.2 0.0 slice-start.1
  5.2 0.1 turn.1.turned_ref
  5.4 0.0 copy-start.3
  5.4 0.0 copy-done
  5.4 0.0 slice-done
  5.4 1.4 %slice-done.1 = s8[2097152]{0:T(1024)(128)(4,1)S(1)} async-done(((s8[6291456]{0:T(1024)(128)(4,1)}), s8[2097152]{0:T(1024)(128)(4,1)S(1)}, s32[]{:S(2)}) %slice-start.1) | async-done | bytes 2097176
  6.8 1.8 %project.1.refs_0_ = bf16[80,512]{1,0:T(8,128)(2,1)S(1)} custom-call(bf16[64,6144]{1,0:T(8,128)(2,1)S(1)} %copy-done, bf16[512,6144]{1,0:T(8,128)(2,1)S(1)} %bitcast.4, bf16[16,512]{1,0:T(8,128)(2,1)S(1)} %turn.1.turned_ref), custom_call_target="tpu_custom_call" | custom-call | tf_op jit(solution)/shard_map/project/pallas_call | solution.py:27
  8.7 0.0 copy-start.1
  8.7 2.5 %collective-permute-start.2 = (bf16[80,512]{1,0:T(8,128)(2,1)S(1)}, bf16[80,512]{1,0:T(8,128)(2,1)S(1)}, u32[]{:S(2)}, u32[]{:S(2)}) collective-permute-start(bf16[80,512]{1,0:T(8,128)(2,1)S(1)} %project.1.refs_0_), channel_id=1, source_target_pairs={{0,3},{1,2},{2,1},{3,0},{4,7},{5,6},{6,5},{7,4},{8,11},{9,10},{10,... | collective-permute-start | bytes 245768 | tf_op jit(solution)/shard_map/ppermute | solution.py:62
  11.2 0.5 %collective-permute-start.1 = (bf16[80,512]{1,0:T(8,128)(2,1)S(1)}, bf16[80,512]{1,0:T(8,128)(2,1)S(1)}, u32[]{:S(2)}, u32[]{:S(2)}) collective-permute-start(bf16[80,512]{1,0:T(8,128)(2,1)S(1)} %project.1.refs_0_), channel_id=1, source_target_pairs={{0,2},{1,3},{2,0},{3,1},{4,6},{5,7},{6,4},{7,5},{8,10},{9,11},{10,... | collective-permute-start | bytes 245768 | tf_op jit(solution)/shard_map/ppermute | solution.py:62
  11.7 0.5 %collective-permute-start = (bf16[80,512]{1,0:T(8,128)(2,1)S(1)}, bf16[80,512]{1,0:T(8,128)(2,1)S(1)}, u32[]{:S(2)}, u32[]{:S(2)}) collective-permute-start(bf16[80,512]{1,0:T(8,128)(2,1)S(1)} %project.1.refs_0_), channel_id=1, source_target_pairs={{0,1},{1,0},{2,3},{3,2},{4,5},{5,4},{6,7},{7,6},{8,9},{9,8},{10,11... | collective-permute-start | bytes 245768 | tf_op jit(solution)/shard_map/ppermute | solution.py:62
  12.2 1.6 %collective-permute-start.5 = (bf16[16,6144]{1,0:T(8,128)(2,1)S(1)}, bf16[16,6144]{1,0:T(8,128)(2,1)S(1)}, u32[]{:S(2)}, u32[]{:S(2)}) collective-permute-start(bf16[16,6144]{1,0:T(8,128)(2,1)S(1)} %slice.7), channel_id=1, source_target_pairs={{0,8},{4,12},{8,16},{12,20},{16,24},{20,28},{24,0},{28,4},{1,9},{5... | collective-permute-start | bytes 589832 | tf_op jit(solution)/shard_map/ppermute | solution.py:41
  13.9 0.3 collective-permute-done.2.refs_3_
  14.2 1.5 %collective-permute-done.1.refs_2_ = bf16[80,512]{1,0:T(8,128)(2,1)S(1)} collective-permute-done((bf16[80,512]{1,0:T(8,128)(2,1)S(1)}, bf16[80,512]{1,0:T(8,128)(2,1)S(1)}, u32[]{:S(2)}, u32[]{:S(2)}) %collective-permute-start.1) | collective-permute-done | bytes 81952 | tf_op jit(solution)/shard_map/ppermute | solution.py:62
  15.7 0.5 %collective-permute-done.refs_1_ = bf16[80,512]{1,0:T(8,128)(2,1)S(1)} collective-permute-done((bf16[80,512]{1,0:T(8,128)(2,1)S(1)}, bf16[80,512]{1,0:T(8,128)(2,1)S(1)}, u32[]{:S(2)}, u32[]{:S(2)}) %collective-permute-start) | collective-permute-done | bytes 81952 | tf_op jit(solution)/shard_map/ppermute | solution.py:62
  16.1 0.0 copy-done.3
  16.1 1.5 %couple.1.mine.after_ref = bf16[64,512]{1,0:T(8,128)(2,1)S(1)} custom-call(s32[4,32]{1,0:T(4,128)S(1)} %copy-done.3, bf16[80,512]{1,0:T(8,128)(2,1)S(1)} %project.1.refs_0_, bf16[80,512]{1,0:T(8,128)(2,1)S(1)} %collective-permute-done.refs_1_, bf16[80,512]{1,0:T(8,128)(2,1)S(1)} %collective-permute-done.1.refs_2_, ...), custom_call_target="tpu_custom_call" | custom-call | flops 2000000000 | tf_op jit(solution)/shard_map/couple/pallas_call | solution.py:27
  17.7 1.6 %collective-permute-start.3 = (bf16[64,512]{1,0:T(8,128)(2,1)S(1)}, bf16[64,512]{1,0:T(8,128)(2,1)S(1)}, u32[]{:S(2)}, u32[]{:S(2)}) collective-permute-start(bf16[64,512]{1,0:T(8,128)(2,1)S(1)} %couple.1.mine.after_ref), channel_id=1, source_target_pairs={{0,8},{4,12},{8,16},{12,20},{16,24},{20,28},{24,0},{28,4},{1,9},{5... | collective-permute-start | bytes 196616 | tf_op jit(solution)/shard_map/ppermute | solution.py:41
  19.3 1.2 %collective-permute-done.4.two_a.block_ref = bf16[48,6144]{1,0:T(8,128)(2,1)S(1)} collective-permute-done((bf16[48,6144]{1,0:T(8,128)(2,1)S(1)}, bf16[48,6144]{1,0:T(8,128)(2,1)S(1)}, u32[]{:S(2)}, u32[]{:S(2)}) %collective-permute-start.4) | collective-permute-done | bytes 589856 | tf_op jit(solution)/shard_map/ppermute | solution.py:41
  20.6 0.1 collective-permute-start.8
  20.6 4.7 %collective-permute-done.3.mine_two.two = bf16[64,512]{1,0:T(8,128)(2,1)S(1)} collective-permute-done((bf16[64,512]{1,0:T(8,128)(2,1)S(1)}, bf16[64,512]{1,0:T(8,128)(2,1)S(1)}, u32[]{:S(2)}, u32[]{:S(2)}) %collective-permute-start.3) | collective-permute-done | bytes 65568 | tf_op jit(solution)/shard_map/ppermute | solution.py:41
  25.3 0.0 collective-permute-start.11
  25.3 0.0 collective-permute-done.5.two_b
  25.3 0.1 choose.1
  25.4 0.9 %collective-permute-start.10 = (bf16[64,512]{1,0:T(8,128)(2,1)S(1)}, bf16[64,512]{1,0:T(8,128)(2,1)S(1)}, u32[]{:S(2)}, u32[]{:S(2)}) collective-permute-start(bf16[64,512]{1,0:T(8,128)(2,1)S(1)} %get-tuple-element.12), channel_id=1, source_target_pairs={{0,4},{4,0},{8,12},{12,8},{16,20},{20,16},{24,28},{28,24},{1,5},{5... | collective-permute-start | bytes 196616 | tf_op jit(solution)/shard_map/ppermute | solution.py:46
  26.3 0.1 collective-permute-start.9
  26.3 1.8 %collective-permute-start.6 = (bf16[32,6144]{1,0:T(8,128)(2,1)S(1)}, bf16[32,6144]{1,0:T(8,128)(2,1)S(1)}, u32[]{:S(2)}, u32[]{:S(2)}) collective-permute-start(bf16[32,6144]{1,0:T(8,128)(2,1)S(1)} %get-tuple-element.9), channel_id=1, source_target_pairs={{0,4},{4,0},{8,12},{12,8},{16,20},{20,16},{24,28},{28,24},{1,5},{5... | collective-permute-start | bytes 1179656 | tf_op jit(solution)/shard_map/ppermute | solution.py:46
  28.1 4.3 %collective-permute-done.11.three = bf16[64,512]{1,0:T(8,128)(2,1)S(1)} collective-permute-done((bf16[64,512]{1,0:T(8,128)(2,1)S(1)}, bf16[64,512]{1,0:T(8,128)(2,1)S(1)}, u32[]{:S(2)}, u32[]{:S(2)}) %collective-permute-start.11) | collective-permute-done | bytes 65568 | tf_op jit(solution)/shard_map/ppermute | solution.py:41
  32.4 0.0 collective-permute-start.7
  32.4 0.0 collective-permute-done.10.one
  32.4 0.0 copy-done.1
  32.4 1.4 %apply.1.applied = f32[64,6144]{1,0:T(8,128)S(1)} custom-call(bf16[64,256]{1,0:T(8,128)(2,1)S(1)} %copy-done.1, bf16[64,512]{1,0:T(8,128)(2,1)S(1)} %couple.1.mine.after_ref, bf16[64,512]{1,0:T(8,128)(2,1)S(1)} %collective-permute-done.10.one, bf16[64,512]{1,0:T(8,128)(2,1)S(1)} %collective-permute-done.3.mine_two.two, ...), custom_call_target="tpu_custom_call" | custom-call | flops 5000000000 | tf_op jit(solution)/shard_map/apply/pallas_call | solution.py:27
  33.9 0.7 %collective-permute-done.9.three_b = bf16[16,6144]{1,0:T(8,128)(2,1)S(1)} collective-permute-done((bf16[16,6144]{1,0:T(8,128)(2,1)S(1)}, bf16[16,6144]{1,0:T(8,128)(2,1)S(1)}, u32[]{:S(2)}, u32[]{:S(2)}) %collective-permute-start.9) | collective-permute-done | bytes 196640 | tf_op jit(solution)/shard_map/ppermute | solution.py:41
  34.5 0.0 collective-permute-done.6.one_a
  34.5 0.0 collective-permute-done.7.one_b
  34.5 0.0 collective-permute-done.8.three_a
  34.5 1.4 %finish.1 = bf16[64,6144]{1,0:T(8,128)(2,1)} custom-call(bf16[64,256]{1,0:T(8,128)(2,1)S(1)} %copy-done.1, bf16[64,6144]{1,0:T(8,128)(2,1)S(1)} %copy-done, bf16[32,6144]{1,0:T(8,128)(2,1)S(1)} %collective-permute-done.6.one_a, bf16[32,6144]{1,0:T(8,128)(2,1)S(1)} %collective-permute-done.7.one_b, ...), custom_call_target="tpu_custom_call" | custom-call | tf_op jit(solution)/shard_map/finish/pallas_call | solution.py:247
  (3 shorter events, 0.1 us)
Async XLA Ops:
  0.0 5.4 %copy-start = (bf16[64,6144]{1,0:T(8,128)(2,1)S(1)}, bf16[64,6144]{1,0:T(8,128)(2,1)}, u32[]{:S(2)}) copy-start(bf16[64,6144]{1,0:T(8,128)(2,1)} %own.3) | copy-start | bytes 2359300
  0.0 5.4 %slice-start = ((s8[6291456]{0:T(1024)(128)(4,1)}), s8[4194304]{0:T(1024)(128)(4,1)S(1)}, s32[]{:S(2)}) async-start(s8[6291456]{0:T(1024)(128)(4,1)} %bitcast.2), calls=%async_computation | async-start | bytes 8388608
  1.3 19.3 %collective-permute-start.4 = (bf16[48,6144]{1,0:T(8,128)(2,1)S(1)}, bf16[48,6144]{1,0:T(8,128)(2,1)S(1)}, u32[]{:S(2)}, u32[]{:S(2)}) collective-permute-start(bf16[48,6144]{1,0:T(8,128)(2,1)S(1)} %slice.6), channel_id=1, source_target_pairs={{0,8},{4,12},{8,16},{12,20},{16,24},{20,28},{24,0},{28,4},{1,9},{5... | collective-permute-start | bytes 1769480 | tf_op jit(solution)/shard_map/ppermute | solution.py:41
  4.3 0.9 %copy-start.2 = (f32[16,16,16]{2,1,0:T(8,128)S(1)}, f32[16,16,16]{2,1,0:T(8,128)}, u32[]{:S(2)}) copy-start(f32[16,16,16]{2,1,0:T(8,128)} %param.8) | copy-start | bytes 49156
  5.2 1.6 %slice-start.1 = ((s8[6291456]{0:T(1024)(128)(4,1)}), s8[2097152]{0:T(1024)(128)(4,1)S(1)}, s32[]{:S(2)}) async-start(s8[6291456]{0:T(1024)(128)(4,1)} %bitcast.2), calls=%async_computation.1 | async-start | bytes 4194304
  5.4 10.8 %copy-start.3 = (s32[4,32]{1,0:T(4,128)S(1)}, s32[4,32]{1,0:T(4,128)}, u32[]{:S(2)}) copy-start(s32[4,32]{1,0:T(4,128)} %slot_ref.1) | copy-start | bytes 1540
  8.7 23.8 %copy-start.1 = (bf16[64,256]{1,0:T(8,128)(2,1)S(1)}, bf16[64,256]{1,0:T(8,128)(2,1)}, u32[]{:S(2)}) copy-start(bf16[64,256]{1,0:T(8,128)(2,1)} %rot_ref.3) | copy-start | bytes 98308
  8.7 5.5 %collective-permute-start.2 = (bf16[80,512]{1,0:T(8,128)(2,1)S(1)}, bf16[80,512]{1,0:T(8,128)(2,1)S(1)}, u32[]{:S(2)}, u32[]{:S(2)}) collective-permute-start(bf16[80,512]{1,0:T(8,128)(2,1)S(1)} %project.1.refs_0_), channel_id=1, source_target_pairs={{0,3},{1,2},{2,1},{3,0},{4,7},{5,6},{6,5},{7,4},{8,11},{9,10},{10,... | collective-permute-start | bytes 245768 | tf_op jit(solution)/shard_map/ppermute | solution.py:62
  11.2 4.5 %collective-permute-start.1 = (bf16[80,512]{1,0:T(8,128)(2,1)S(1)}, bf16[80,512]{1,0:T(8,128)(2,1)S(1)}, u32[]{:S(2)}, u32[]{:S(2)}) collective-permute-start(bf16[80,512]{1,0:T(8,128)(2,1)S(1)} %project.1.refs_0_), channel_id=1, source_target_pairs={{0,2},{1,3},{2,0},{3,1},{4,6},{5,7},{6,4},{7,5},{8,10},{9,11},{10,... | collective-permute-start | bytes 245768 | tf_op jit(solution)/shard_map/ppermute | solution.py:62
  11.7 4.4 %collective-permute-start = (bf16[80,512]{1,0:T(8,128)(2,1)S(1)}, bf16[80,512]{1,0:T(8,128)(2,1)S(1)}, u32[]{:S(2)}, u32[]{:S(2)}) collective-permute-start(bf16[80,512]{1,0:T(8,128)(2,1)S(1)} %project.1.refs_0_), channel_id=1, source_target_pairs={{0,1},{1,0},{2,3},{3,2},{4,5},{5,4},{6,7},{7,6},{8,9},{9,8},{10,11... | collective-permute-start | bytes 245768 | tf_op jit(solution)/shard_map/ppermute | solution.py:62
  12.2 13.1 %collective-permute-start.5 = (bf16[16,6144]{1,0:T(8,128)(2,1)S(1)}, bf16[16,6144]{1,0:T(8,128)(2,1)S(1)}, u32[]{:S(2)}, u32[]{:S(2)}) collective-permute-start(bf16[16,6144]{1,0:T(8,128)(2,1)S(1)} %slice.7), channel_id=1, source_target_pairs={{0,8},{4,12},{8,16},{12,20},{16,24},{20,28},{24,0},{28,4},{1,9},{5... | collective-permute-start | bytes 589832 | tf_op jit(solution)/shard_map/ppermute | solution.py:41
  17.7 7.6 %collective-permute-start.3 = (bf16[64,512]{1,0:T(8,128)(2,1)S(1)}, bf16[64,512]{1,0:T(8,128)(2,1)S(1)}, u32[]{:S(2)}, u32[]{:S(2)}) collective-permute-start(bf16[64,512]{1,0:T(8,128)(2,1)S(1)} %couple.1.mine.after_ref), channel_id=1, source_target_pairs={{0,8},{4,12},{8,16},{12,20},{16,24},{20,28},{24,0},{28,4},{1,9},{5... | collective-permute-start | bytes 196616 | tf_op jit(solution)/shard_map/ppermute | solution.py:41
  20.6 14.0 %collective-permute-start.8 = (bf16[48,6144]{1,0:T(8,128)(2,1)S(1)}, bf16[48,6144]{1,0:T(8,128)(2,1)S(1)}, u32[]{:S(2)}, u32[]{:S(2)}) collective-permute-start(bf16[48,6144]{1,0:T(8,128)(2,1)S(1)} %hold.1), channel_id=1, source_target_pairs={{0,4},{4,8},{8,12},{12,16},{16,20},{20,24},{24,28},{28,0},{1,5},{5... | collective-permute-start | bytes 1769480 | tf_op jit(solution)/shard_map/ppermute | solution.py:41
  25.3 7.1 %collective-permute-start.11 = (bf16[64,512]{1,0:T(8,128)(2,1)S(1)}, bf16[64,512]{1,0:T(8,128)(2,1)S(1)}, u32[]{:S(2)}, u32[]{:S(2)}) collective-permute-start(bf16[64,512]{1,0:T(8,128)(2,1)S(1)} %collective-permute-done.3.mine_two.two), channel_id=1, source_target_pairs={{0,4},{4,8},{8,12},{12,16},{16,20},{20,24},{24,28},{28,0},{1,5},{5... | collective-permute-start | bytes 196616 | tf_op jit(solution)/shard_map/ppermute | solution.py:41
  25.4 7.0 %collective-permute-start.10 = (bf16[64,512]{1,0:T(8,128)(2,1)S(1)}, bf16[64,512]{1,0:T(8,128)(2,1)S(1)}, u32[]{:S(2)}, u32[]{:S(2)}) collective-permute-start(bf16[64,512]{1,0:T(8,128)(2,1)S(1)} %get-tuple-element.12), channel_id=1, source_target_pairs={{0,4},{4,0},{8,12},{12,8},{16,20},{20,16},{24,28},{28,24},{1,5},{5... | collective-permute-start | bytes 196616 | tf_op jit(solution)/shard_map/ppermute | solution.py:46
  26.3 8.3 %collective-permute-start.9 = (bf16[16,6144]{1,0:T(8,128)(2,1)S(1)}, bf16[16,6144]{1,0:T(8,128)(2,1)S(1)}, u32[]{:S(2)}, u32[]{:S(2)}) collective-permute-start(bf16[16,6144]{1,0:T(8,128)(2,1)S(1)} %get-tuple-element.11), channel_id=1, source_target_pairs={{0,4},{4,8},{8,12},{12,16},{16,20},{20,24},{24,28},{28,0},{1,5},{5... | collective-permute-start | bytes 589832 | tf_op jit(solution)/shard_map/ppermute | solution.py:41
  26.3 8.2 %collective-permute-start.6 = (bf16[32,6144]{1,0:T(8,128)(2,1)S(1)}, bf16[32,6144]{1,0:T(8,128)(2,1)S(1)}, u32[]{:S(2)}, u32[]{:S(2)}) collective-permute-start(bf16[32,6144]{1,0:T(8,128)(2,1)S(1)} %get-tuple-element.9), channel_id=1, source_target_pairs={{0,4},{4,0},{8,12},{12,8},{16,20},{20,16},{24,28},{28,24},{1,5},{5... | collective-permute-start | bytes 1179656 | tf_op jit(solution)/shard_map/ppermute | solution.py:46
  32.4 2.1 %collective-permute-start.7 = (bf16[32,6144]{1,0:T(8,128)(2,1)S(1)}, bf16[32,6144]{1,0:T(8,128)(2,1)S(1)}, u32[]{:S(2)}, u32[]{:S(2)}) collective-permute-start(bf16[32,6144]{1,0:T(8,128)(2,1)S(1)} %get-tuple-element.10), channel_id=1, source_target_pairs={{0,4},{4,0},{8,12},{12,8},{16,20},{20,16},{24,28},{28,24},{1,5},{5... | collective-permute-start | bytes 1179656 | tf_op jit(solution)/shard_map/ppermute | solution.py:46

commit v2 on v1

--- a/solution.py
+++ b/solution.py
@@ -9,7 +9,9 @@
 
 TURN = 3 * 10**9
 COUPLE = 2 * 10**9
-APPLY = 5 * 10**9
+APPLY = 50 * 10**8
+GATHER = 45 * 10**8
+
 F32 = jnp.float32
 BF16 = jnp.bfloat16
 ROOM = pltpu.CompilerParams(vmem_limit_bytes=8 * 2**20)
@@ -174,42 +176,78 @@
     return call(hold_kernel, "hold", [(block.shape, block.dtype)], [block, after])[0]
 
 
-def choose_kernel(mine, mine_two, own, two_a, two_b, coef_ref, upper_ref, lower_ref, held_ref):
-    cut, half = two_a.shape[0], upper_ref.shape[0]
+def packed(coef_shape, rows):
+    width, flat = coef_shape
+    return [
+        (slice(i * flat, (i + 1) * flat), slice(i * rows, (i + 1) * rows))
+        for i in range(width // rows)
+    ]
+
+
+def choose_kernel(mine, mine_two, own, two_a, two_b, swap_ref, *held_refs):
+    width, cut = own.shape[0], two_a.shape[0]
+    parts = packed(mine.shape, two_b.shape[0])
 
     @pl.when(on_even())
     def _():
-        coef_ref[...] = mine[...]
-        upper_ref[...] = own[:half, :]
-        lower_ref[...] = own[half:, :]
+        swap_ref[:width, :] = own[...]
+        for columns, rows in parts:
+            swap_ref[width:, columns] = mine[rows, :]
 
     @pl.when(jnp.logical_not(on_even()))
     def _():
-        coef_ref[...] = mine_two[...]
-        upper_ref[...] = two_a[:half, :]
-        lower_ref[: cut - half, :] = two_a[half:, :]
-        lower_ref[cut - half :, :] = two_b[...]
-
-    held_ref[...] = two_b[...]
+        swap_ref[:cut, :] = two_a[...]
+        swap_ref[cut:width, :] = two_b[...]
+        for columns, rows in parts:
+            swap_ref[width:, columns] = mine_two[rows, :]
+
+    at = 0
+    for ref in held_refs:
+        ref[...] = two_b[:, at : at + ref.shape[1]]
+        at += ref.shape[1]
 
 
 def choose(mine, mine_two, own, two_a, two_b):
     args = [mine, mine_two, own, two_a, two_b]
-    half = ((own.shape[0] // 2, own.shape[1]), own.dtype)
-    outs = [(mine.shape, mine.dtype), half, half, (two_b.shape, two_b.dtype)]
+    rows, points = two_b.shape
+    last = points * 7 // 12 // 128 * 128
+    outs = [((own.shape[0] + rows, points), own.dtype)]
+    outs += [((rows, extent), own.dtype) for extent in (points - last, last)]
     return call(choose_kernel, "choose", outs, args)
 
 
-def apply_kernel(rot_ref, mine, one, two, three, proj_ref, out_ref):
+def gather_kernel(rot_ref, own, two_a, two_b, three_a, out_ref, stack):
+    width, points = own.shape
+    depth = stack.shape[0]
+    turn = jnp.concatenate([rot_ref[:, :width], rot_ref[:, 2 * width : width + depth]], axis=1)
+    tile = tile_of(points, 1024)
+    for i in range(points // tile):
+        here = slice(i * tile, (i + 1) * tile)
+        at = 0
+        for ref in (own, two_a, two_b, three_a):
+            stack[at : at + ref.shape[0], here] = ref[:, here]
+            at += ref.shape[0]
+        out_ref[:, here] = jnp.dot(turn, stack[:, here], preferred_element_type=F32)
+
+
+def gather(rotation, *blocks):
+    width, points = blocks[0].shape
+    depth = sum(block.shape[0] for block in blocks)
+    scratch = [pltpu.VMEM((depth, points), BF16)]
+    return call(
+        gather_kernel, "gather", [((width, points), F32)], [rotation, *blocks], scratch, cost=GATHER
+    )[0]
+
+
+def apply_kernel(rot_ref, mine, swap_ref, two, three, proj_ref, after_ref, out_ref):
     width, flat = mine.shape
     points = proj_ref.shape[1]
-    mixed = None
-    blocks = [mine, one, two, three]
-    for s, block in enumerate(blocks):
-        term = jnp.dot(
-            rot_ref[:, s * width : (s + 1) * width], block[...], preferred_element_type=F32
-        )
-        mixed = term if mixed is None else mixed + term
+    one = [swap_ref[width:, columns] for columns, _ in packed(mine.shape, swap_ref.shape[0] - width)]
+    blocks = (mine[...], jnp.concatenate(one, axis=0), two[...], three[...])
+    mixed = sum(
+        jnp.dot(rot_ref[:, s * width : (s + 1) * width], block, preferred_element_type=F32)
+        for s, block in enumerate(blocks)
+    )
     mixed = mixed.astype(BF16)
     tile = tile_of(points, 1024)
     for at in range(0, points, tile):
@@ -218,42 +256,53 @@
         )
 
 
-def finish_kernel(
-    rot_ref, own, one_a, one_b, two_a, two_b, three_a, three_b, applied, out_hbm, stack, out_ref, sems
-):
-    width, points = own.shape
+def finish_kernel(start, rot_ref, partial_ref, swap_ref, last_ref, applied, *refs):
+    out_hbm, out_ref, sems = refs[-3:]
+    width, extent = out_ref.shape
+    rows = last_ref.shape[0]
     pieces = sems.shape[0]
-    tile = points // pieces
+    tile = extent // pieces
+    turn = jnp.concatenate(
+        [rot_ref[:, width : 2 * width], rot_ref[:, rot_ref.shape[1] - rows :]], axis=1
+    )
     copies = []
     for i in range(pieces):
         here = slice(i * tile, (i + 1) * tile)
-        at = 0
-        for ref in (own, one_a, one_b, two_a, two_b, three_a, three_b):
-            stack[at : at + ref.shape[0], here] = ref[:, here]
-            at += ref.shape[0]
-        rotated = jnp.dot(rot_ref[...], stack[:, here], preferred_element_type=F32)
-        added = rotated.astype(BF16).astype(F32) + applied[:, here]
+        there = slice(start + i * tile, start + (i + 1) * tile)
+        last = jnp.concatenate([swap_ref[:width, there], last_ref[:, here]], axis=0)
+        rotated = partial_ref[:, there] + jnp.dot(turn, last, preferred_element_type=F32)
+        added = rotated.astype(BF16).astype(F32) + applied[:, there]
         out_ref[:, here] = added.astype(out_ref.dtype)
-        part = (slice(None), pl.ds(i * tile, tile))
-        copies.append(pltpu.make_async_copy(out_ref.at[part], out_hbm.at[part], sems.at[i]))
+        copies.append(
+            pltpu.make_async_copy(
+                out_ref.at[:, pl.ds(i * tile, tile)],
+                out_hbm.at[:, pl.ds(start + i * tile, tile)],
+                sems.at[i],
+            )
+        )
         copies[-1].start()
     for copy in copies:
         copy.wait()
 
 
-def finish(*args):
-    width, points = args[-1].shape
-    pieces = points // tile_of(points, 1024)
+def finish(start, rotation, partial, swap, last, applied, so_far):
+    width, points = applied.shape
+    extent = last.shape[1]
+    pieces = extent // tile_of(extent, 1024)
+    args = [rotation, partial, swap, last, applied]
+    specs = [VMEM] * len(args)
+    alias = {}
+    if so_far is not None:
+        alias = {len(args): 0}
+        args.append(so_far)
+        specs.append(pl.BlockSpec(memory_space=pl.ANY))
     return pl.pallas_call(
-        finish_kernel,
-        in_specs=[VMEM] * len(args),
+        functools.partial(finish_kernel, start),
+        in_specs=specs,
         out_specs=pl.BlockSpec(memory_space=pl.ANY),
         out_shape=jax.ShapeDtypeStruct((width, points), BF16),
-        scratch_shapes=[
-            pltpu.VMEM((4 * width, points), BF16),
-            pltpu.VMEM((width, points), BF16),
-            pltpu.SemaphoreType.DMA((pieces,)),
-        ],
+        scratch_shapes=[pltpu.VMEM((width, extent), BF16), pltpu.SemaphoreType.DMA((pieces,))],
+        input_output_aliases=alias,
         compiler_params=ROOM,
         cost_estimate=flops(0),
         name="finish",
@@ -273,19 +322,23 @@
     mine = couple(slot_atom, loads, width, owned)
     mine_two = along_bands(mine, 2)
     three_a = along_bands(hold(two_a, mine), 1)
-    other, upper, lower, held = choose(mine, mine_two, orbitals, two_a, two_b)
+    swap, *held = choose(mine, mine_two, orbitals, two_a, two_b)
     mine_three = along_bands(mine_two, 1)
-    mine_one = swapped(other)
-    three_b = along_bands(held, 1)
-    one_a, one_b = swapped(upper), swapped(lower)
+    swap = swapped(swap)
+    three_b = [along_bands(block, 1) for block in held]
+    partial = gather(rotation, orbitals, two_a, two_b, three_a)
     applied = call(
         apply_kernel,
         "apply",
         [((width, points), F32)],
-        [rotation, mine, mine_one, mine_two, mine_three, proj],
+        [rotation, mine, swap, mine_two, mine_three, proj, partial],
         cost=APPLY,
     )[0]
-    return finish(rotation, orbitals, one_a, one_b, two_a, two_b, three_a, three_b, applied)
+    out, start = None, 0
+    for last in three_b:
+        out = finish(start, rotation, partial, swap, last, applied, out)
+        start += last.shape[1]
+    return out
 
 
 def solution(mesh):

time: 36.1 us -> 36.1 us (level)
  starting transfers between devices: 12.7 us -> 11.1 us
  Pallas kernels: 6.43 us -> 7.62 us
    ppermute x3 -> x1, starting transfers between devices: 2.66 us -> 0.07 us  [swapped(): return lax.ppermute(block, 'band', [(i, i ^ 1) for i in range(count)])]
    ppermute x6 -> x7, starting transfers between devices: 6.46 us -> 7.45 us  [along_bands(): lax.ppermute(block, 'band', [(i, (i + distance) % count) for i in range(c...]
    pallas_call x1 -> x2, Pallas kernels: 1.4 us -> 2.01 us  [finish(): pl.pallas_call(functools.partial(finish_kernel, start), in_specs=specs, o...]
    pallas_call x6 -> x7, Pallas kernels: 5.03 us -> 5.61 us  [call(): pl.pallas_call(kernel, in_specs=[first] + [VMEM] * (len(args) - 1), out_s...]
    ppermute x6 -> x7, waiting for transfers between devices: 10.9 us -> 11 us  [along_bands(): lax.ppermute(block, 'band', [(i, (i + distance) % count) for i in range(c...]
  transfers between devices with their start and end apart: 12 -> 11, of which waited for: 7 -> 7; matrix products, arithmetic and copies ran while one was open for 0% -> 0% of each run, Pallas kernels for 14% -> 18%
where the time goes in v2:
time: 36.1 us; the launch traced here: 35.9 us
  waiting for transfers between devices  13.2 us (37%)
  starting transfers between devices  11.1 us (31%)
  Pallas kernels  7.62 us (21%)
  local copies, waits for them, and re-layouts  3.88 us (11%)
    ppermute x7, waiting for transfers between devices, along_bands(): lax.ppermute(block, 'band', [(i, (i + distance) % count) for i in range(c...  11 us
    ppermute x7, starting transfers between devices, along_bands(): lax.ppermute(block, 'band', [(i, (i + distance) % count) for i in range(c...  7.45 us
    pallas_call x7, Pallas kernels, call(): pl.pallas_call(kernel, in_specs=[first] + [VMEM] * (len(args) - 1), out_s...  5.61 us
    ppermute x3, starting transfers between devices, from_all_domains(): return [block] + [lax.ppermute(block, 'dom', route) for route in routes]  3.55 us
    unnamed x12, local copies, waits for them, and re-layouts  2.61 us
    ppermute x3, waiting for transfers between devices, from_all_domains(): return [block] + [lax.ppermute(block, 'dom', route) for route in routes]  2.26 us
    pallas_call x2, Pallas kernels, finish(): pl.pallas_call(functools.partial(finish_kernel, start), in_specs=specs, o...  2.01 us
    slice x1, local copies, waits for them, and re-layouts, on_device(): two_a = along_bands(orbitals[:cut], 2)  1.25 us
  transfers between devices with their start and end apart: 11, of which 7 were waited for; matrix products, arithmetic and copies ran while one was open for 0% of the time, Pallas kernels for 18%

profile of v2, /device:TPU:0, one launch (start us, length us, event | category | flops | bytes accessed | tf_op | source)
XLA Modules:
  0.0 35.9 jit_solution(4095479078813302561)
XLA Ops:
  0.0 0.0 slice-start
  0.0 1.3 %slice.6 = bf16[48,6144]{1,0:T(8,128)(2,1)S(1)} slice(bf16[64,6144]{1,0:T(8,128)(2,1)} %own.3), slice={[0:48], [0:6144]} | slice | bytes 1179648 | tf_op jit(solution)/shard_map/slice | solution.py:319
  1.3 3.1 %collective-permute-start = (bf16[48,6144]{1,0:T(8,128)(2,1)S(1)}, bf16[48,6144]{1,0:T(8,128)(2,1)S(1)}, u32[]{:S(2)}, u32[]{:S(2)}) collective-permute-start(bf16[48,6144]{1,0:T(8,128)(2,1)S(1)} %slice.6), channel_id=1, source_target_pairs={{0,8},{4,12},{8,16},{12,20},{16,24},{20,28},{24,0},{28,4},{1,9},{5... | collective-permute-start | bytes 1769480 | tf_op jit(solution)/shard_map/ppermute | solution.py:43
  4.3 0.0 copy-start.2
  4.3 0.9 %copy-done.2 = f32[16,16,16]{2,1,0:T(8,128)S(1)} copy-done((f32[16,16,16]{2,1,0:T(8,128)S(1)}, f32[16,16,16]{2,1,0:T(8,128)}, u32[]{:S(2)}) %copy-start.2) | copy-done | bytes 16408
  5.2 0.0 copy-start
  5.2 0.0 slice-start.1
  5.2 0.1 turn.1.turned_ref
  5.4 0.0 slice-done
  5.4 1.0 %copy-done = bf16[64,6144]{1,0:T(8,128)(2,1)S(1)} copy-done((bf16[64,6144]{1,0:T(8,128)(2,1)S(1)}, bf16[64,6144]{1,0:T(8,128)(2,1)}, u32[]{:S(2)}) %copy-start) | copy-done | bytes 786456
  6.4 0.7 %slice-done.1 = s8[2097152]{0:T(1024)(128)(4,1)S(1)} async-done(((s8[6291456]{0:T(1024)(128)(4,1)}), s8[2097152]{0:T(1024)(128)(4,1)S(1)}, s32[]{:S(2)}) %slice-start.1) | async-done | bytes 2097176
  7.1 0.0 copy-start.3
  7.1 1.8 %project.1.refs_0_ = bf16[80,512]{1,0:T(8,128)(2,1)S(1)} custom-call(bf16[64,6144]{1,0:T(8,128)(2,1)S(1)} %copy-done, bf16[512,6144]{1,0:T(8,128)(2,1)S(1)} %bitcast.4, bf16[16,512]{1,0:T(8,128)(2,1)S(1)} %turn.1.turned_ref), custom_call_target="tpu_custom_call" | custom-call | tf_op jit(solution)/shard_map/project/pallas_call | solution.py:29
  8.9 2.5 %collective-permute-start.4 = (bf16[80,512]{1,0:T(8,128)(2,1)S(1)}, bf16[80,512]{1,0:T(8,128)(2,1)S(1)}, u32[]{:S(2)}, u32[]{:S(2)}) collective-permute-start(bf16[80,512]{1,0:T(8,128)(2,1)S(1)} %project.1.refs_0_), channel_id=1, source_target_pairs={{0,3},{1,2},{2,1},{3,0},{4,7},{5,6},{6,5},{7,4},{8,11},{9,10},{10,... | collective-permute-start | bytes 245768 | tf_op jit(solution)/shard_map/ppermute | solution.py:64
  11.4 0.5 %collective-permute-start.3 = (bf16[80,512]{1,0:T(8,128)(2,1)S(1)}, bf16[80,512]{1,0:T(8,128)(2,1)S(1)}, u32[]{:S(2)}, u32[]{:S(2)}) collective-permute-start(bf16[80,512]{1,0:T(8,128)(2,1)S(1)} %project.1.refs_0_), channel_id=1, source_target_pairs={{0,2},{1,3},{2,0},{3,1},{4,6},{5,7},{6,4},{7,5},{8,10},{9,11},{10,... | collective-permute-start | bytes 245768 | tf_op jit(solution)/shard_map/ppermute | solution.py:64
  11.9 0.5 %collective-permute-start.2 = (bf16[80,512]{1,0:T(8,128)(2,1)S(1)}, bf16[80,512]{1,0:T(8,128)(2,1)S(1)}, u32[]{:S(2)}, u32[]{:S(2)}) collective-permute-start(bf16[80,512]{1,0:T(8,128)(2,1)S(1)} %project.1.refs_0_), channel_id=1, source_target_pairs={{0,1},{1,0},{2,3},{3,2},{4,5},{5,4},{6,7},{7,6},{8,9},{9,8},{10,11... | collective-permute-start | bytes 245768 | tf_op jit(solution)/shard_map/ppermute | solution.py:64
  12.5 1.6 %collective-permute-start.1 = (bf16[16,6144]{1,0:T(8,128)(2,1)S(1)}, bf16[16,6144]{1,0:T(8,128)(2,1)S(1)}, u32[]{:S(2)}, u32[]{:S(2)}) collective-permute-start(bf16[16,6144]{1,0:T(8,128)(2,1)S(1)} %slice.7), channel_id=1, source_target_pairs={{0,8},{4,12},{8,16},{12,20},{16,24},{20,28},{24,0},{28,4},{1,9},{5... | collective-permute-start | bytes 589832 | tf_op jit(solution)/shard_map/ppermute | solution.py:43
  14.1 0.3 collective-permute-done.4.refs_3_
  14.4 1.5 %collective-permute-done.3.refs_2_ = bf16[80,512]{1,0:T(8,128)(2,1)S(1)} collective-permute-done((bf16[80,512]{1,0:T(8,128)(2,1)S(1)}, bf16[80,512]{1,0:T(8,128)(2,1)S(1)}, u32[]{:S(2)}, u32[]{:S(2)}) %collective-permute-start.3) | collective-permute-done | bytes 81952 | tf_op jit(solution)/shard_map/ppermute | solution.py:64
  15.9 0.5 %collective-permute-done.2.refs_1_ = bf16[80,512]{1,0:T(8,128)(2,1)S(1)} collective-permute-done((bf16[80,512]{1,0:T(8,128)(2,1)S(1)}, bf16[80,512]{1,0:T(8,128)(2,1)S(1)}, u32[]{:S(2)}, u32[]{:S(2)}) %collective-permute-start.2) | collective-permute-done | bytes 81952 | tf_op jit(solution)/shard_map/ppermute | solution.py:64
  16.4 0.0 copy-done.3
  16.4 1.5 %couple.1.after_ref.mine = bf16[64,512]{1,0:T(8,128)(2,1)S(1)} custom-call(s32[4,32]{1,0:T(4,128)S(1)} %copy-done.3, bf16[80,512]{1,0:T(8,128)(2,1)S(1)} %project.1.refs_0_, bf16[80,512]{1,0:T(8,128)(2,1)S(1)} %collective-permute-done.2.refs_1_, bf16[80,512]{1,0:T(8,128)(2,1)S(1)} %collective-permute-done.3.refs_2_, ...), custom_call_target="tpu_custom_call" | custom-call | flops 2000000000 | tf_op jit(solution)/shard_map/couple/pallas_call | solution.py:29
  17.9 0.0 copy-start.1
  17.9 1.6 %collective-permute-start.6 = (bf16[64,512]{1,0:T(8,128)(2,1)S(1)}, bf16[64,512]{1,0:T(8,128)(2,1)S(1)}, u32[]{:S(2)}, u32[]{:S(2)}) collective-permute-start(bf16[64,512]{1,0:T(8,128)(2,1)S(1)} %couple.1.after_ref.mine), channel_id=1, source_target_pairs={{0,8},{4,12},{8,16},{12,20},{16,24},{20,28},{24,0},{28,4},{1,9},{5... | collective-permute-start | bytes 196616 | tf_op jit(solution)/shard_map/ppermute | solution.py:43
  19.6 1.0 %collective-permute-done.block_ref.two_a = bf16[48,6144]{1,0:T(8,128)(2,1)S(1)} collective-permute-done((bf16[48,6144]{1,0:T(8,128)(2,1)S(1)}, bf16[48,6144]{1,0:T(8,128)(2,1)S(1)}, u32[]{:S(2)}, u32[]{:S(2)}) %collective-permute-start) | collective-permute-done | bytes 589856 | tf_op jit(solution)/shard_map/ppermute | solution.py:43
  20.6 0.1 collective-permute-start.5
  20.6 4.7 %collective-permute-done.6.mine_two.two = bf16[64,512]{1,0:T(8,128)(2,1)S(1)} collective-permute-done((bf16[64,512]{1,0:T(8,128)(2,1)S(1)}, bf16[64,512]{1,0:T(8,128)(2,1)S(1)}, u32[]{:S(2)}, u32[]{:S(2)}) %collective-permute-start.6) | collective-permute-done | bytes 65568 | tf_op jit(solution)/shard_map/ppermute | solution.py:43
  25.3 0.0 collective-permute-done.1.two_b
  25.3 0.1 choose.1
  25.4 0.1 collective-permute-start.7
  25.5 0.5 %collective-permute-start.9 = (bf16[64,512]{1,0:T(8,128)(2,1)S(1)}, bf16[64,512]{1,0:T(8,128)(2,1)S(1)}, u32[]{:S(2)}, u32[]{:S(2)}) collective-permute-start(bf16[64,512]{1,0:T(8,128)(2,1)S(1)} %collective-permute-done.6.mine_two.two), channel_id=1, source_target_pairs={{0,4},{4,8},{8,12},{12,16},{16,20},{20,24},{24,28},{28,0},{1,5},{5... | collective-permute-start | bytes 196616 | tf_op jit(solution)/shard_map/ppermute | solution.py:43
  26.0 0.1 collective-permute-start.10
  26.1 0.4 %collective-permute-start.8 = (bf16[16,3584]{1,0:T(8,128)(2,1)S(1)}, bf16[16,3584]{1,0:T(8,128)(2,1)S(1)}, u32[]{:S(2)}, u32[]{:S(2)}) collective-permute-start(bf16[16,3584]{1,0:T(8,128)(2,1)S(1)} %get-tuple-element.9), channel_id=1, source_target_pairs={{0,4},{4,8},{8,12},{12,16},{16,20},{20,24},{24,28},{28,0},{1,5},{5... | collective-permute-start | bytes 344072 | tf_op jit(solution)/shard_map/ppermute | solution.py:43
  26.5 5.2 %collective-permute-done.5.three_a = bf16[48,6144]{1,0:T(8,128)(2,1)S(1)} collective-permute-done((bf16[48,6144]{1,0:T(8,128)(2,1)S(1)}, bf16[48,6144]{1,0:T(8,128)(2,1)S(1)}, u32[]{:S(2)}, u32[]{:S(2)}) %collective-permute-start.5) | collective-permute-done | bytes 589856 | tf_op jit(solution)/shard_map/ppermute | solution.py:43
  31.7 0.0 copy-done.1
  31.7 0.6 %gather.1.after_ref.partial_ref = f32[64,6144]{1,0:T(8,128)S(1)} custom-call(bf16[64,256]{1,0:T(8,128)(2,1)S(1)} %copy-done.1, bf16[64,6144]{1,0:T(8,128)(2,1)S(1)} %copy-done, bf16[48,6144]{1,0:T(8,128)(2,1)S(1)} %collective-permute-done.block_ref.two_a, bf16[16,6144]{1,0:T(8,128)(2,1)S(1)} %collective-permute-done.1.two_b, ...), custom_call_target="tpu_custom_call" | custom-call | flops 4499999744 | tf_op jit(solution)/shard_map/gather/pallas_call | solution.py:29
  32.3 0.1 collective-permute-done.9.three
  32.4 0.0 collective-permute-done.7.swap_ref
  32.4 1.4 %apply.1.applied = f32[64,6144]{1,0:T(8,128)S(1)} custom-call(bf16[64,256]{1,0:T(8,128)(2,1)S(1)} %copy-done.1, bf16[64,512]{1,0:T(8,128)(2,1)S(1)} %couple.1.after_ref.mine, bf16[80,6144]{1,0:T(8,128)(2,1)S(1)} %collective-permute-done.7.swap_ref, bf16[64,512]{1,0:T(8,128)(2,1)S(1)} %collective-permute-done.6.mine_two.two, ...), custom_call_target="tpu_custom_call" | custom-call | flops 5000000000 | tf_op jit(solution)/shard_map/apply/pallas_call | solution.py:29
  33.9 0.0 collective-permute-done.10.last_ref
  33.9 1.0 %finish.2.refs_0_ = bf16[64,6144]{1,0:T(8,128)(2,1)} custom-call(bf16[64,256]{1,0:T(8,128)(2,1)S(1)} %copy-done.1, f32[64,6144]{1,0:T(8,128)S(1)} %gather.1.after_ref.partial_ref, bf16[80,6144]{1,0:T(8,128)(2,1)S(1)} %collective-permute-done.7.swap_ref, bf16[16,2560]{1,0:T(8,128)(2,1)S(1)} %collective-permute-done.10.last_ref, f32[64,6144]{1,0:T(8,128)S(1)} %apply.1.applied), custom_call_target="tpu_custom_call" | custom-call | tf_op jit(solution)/shard_map/finish/pallas_call | solution.py:299
  34.9 0.0 collective-permute-done.8.last_ref
  34.9 1.0 %finish.3 = bf16[64,6144]{1,0:T(8,128)(2,1)} custom-call(bf16[64,256]{1,0:T(8,128)(2,1)S(1)} %copy-done.1, f32[64,6144]{1,0:T(8,128)S(1)} %gather.1.after_ref.partial_ref, bf16[80,6144]{1,0:T(8,128)(2,1)S(1)} %collective-permute-done.7.swap_ref, bf16[16,3584]{1,0:T(8,128)(2,1)S(1)} %collective-permute-done.8.last_ref, ...), custom_call_target="tpu_custom_call", output_to_operand_aliasing={{}: (5, {})} | custom-call | tf_op jit(solution)/shard_map/finish/pallas_call | solution.py:299
  (3 shorter events, 0.1 us)
Async XLA Ops:
  0.0 5.4 %slice-start = ((s8[6291456]{0:T(1024)(128)(4,1)}), s8[4194304]{0:T(1024)(128)(4,1)S(1)}, s32[]{:S(2)}) async-start(s8[6291456]{0:T(1024)(128)(4,1)} %bitcast.2), calls=%async_computation | async-start | bytes 8388608
  1.3 19.3 %collective-permute-start = (bf16[48,6144]{1,0:T(8,128)(2,1)S(1)}, bf16[48,6144]{1,0:T(8,128)(2,1)S(1)}, u32[]{:S(2)}, u32[]{:S(2)}) collective-permute-start(bf16[48,6144]{1,0:T(8,128)(2,1)S(1)} %slice.6), channel_id=1, source_target_pairs={{0,8},{4,12},{8,16},{12,20},{16,24},{20,28},{24,0},{28,4},{1,9},{5... | collective-permute-start | bytes 1769480 | tf_op jit(solution)/shard_map/ppermute | solution.py:43
  4.3 0.9 %copy-start.2 = (f32[16,16,16]{2,1,0:T(8,128)S(1)}, f32[16,16,16]{2,1,0:T(8,128)}, u32[]{:S(2)}) copy-start(f32[16,16,16]{2,1,0:T(8,128)} %param.8) | copy-start | bytes 49156
  5.2 1.1 %copy-start = (bf16[64,6144]{1,0:T(8,128)(2,1)S(1)}, bf16[64,6144]{1,0:T(8,128)(2,1)}, u32[]{:S(2)}) copy-start(bf16[64,6144]{1,0:T(8,128)(2,1)} %own.3) | copy-start | bytes 2359300
  5.2 1.8 %slice-start.1 = ((s8[6291456]{0:T(1024)(128)(4,1)}), s8[2097152]{0:T(1024)(128)(4,1)S(1)}, s32[]{:S(2)}) async-start(s8[6291456]{0:T(1024)(128)(4,1)} %bitcast.2), calls=%async_computation.1 | async-start | bytes 4194304
  7.1 9.3 %copy-start.3 = (s32[4,32]{1,0:T(4,128)S(1)}, s32[4,32]{1,0:T(4,128)}, u32[]{:S(2)}) copy-start(s32[4,32]{1,0:T(4,128)} %slot_ref.1) | copy-start | bytes 1540
  8.9 5.5 %collective-permute-start.4 = (bf16[80,512]{1,0:T(8,128)(2,1)S(1)}, bf16[80,512]{1,0:T(8,128)(2,1)S(1)}, u32[]{:S(2)}, u32[]{:S(2)}) collective-permute-start(bf16[80,512]{1,0:T(8,128)(2,1)S(1)} %project.1.refs_0_), channel_id=1, source_target_pairs={{0,3},{1,2},{2,1},{3,0},{4,7},{5,6},{6,5},{7,4},{8,11},{9,10},{10,... | collective-permute-start | bytes 245768 | tf_op jit(solution)/shard_map/ppermute | solution.py:64
  11.4 4.5 %collective-permute-start.3 = (bf16[80,512]{1,0:T(8,128)(2,1)S(1)}, bf16[80,512]{1,0:T(8,128)(2,1)S(1)}, u32[]{:S(2)}, u32[]{:S(2)}) collective-permute-start(bf16[80,512]{1,0:T(8,128)(2,1)S(1)} %project.1.refs_0_), channel_id=1, source_target_pairs={{0,2},{1,3},{2,0},{3,1},{4,6},{5,7},{6,4},{7,5},{8,10},{9,11},{10,... | collective-permute-start | bytes 245768 | tf_op jit(solution)/shard_map/ppermute | solution.py:64
  11.9 4.4 %collective-permute-start.2 = (bf16[80,512]{1,0:T(8,128)(2,1)S(1)}, bf16[80,512]{1,0:T(8,128)(2,1)S(1)}, u32[]{:S(2)}, u32[]{:S(2)}) collective-permute-start(bf16[80,512]{1,0:T(8,128)(2,1)S(1)} %project.1.refs_0_), channel_id=1, source_target_pairs={{0,1},{1,0},{2,3},{3,2},{4,5},{5,4},{6,7},{7,6},{8,9},{9,8},{10,11... | collective-permute-start | bytes 245768 | tf_op jit(solution)/shard_map/ppermute | solution.py:64
  12.5 12.8 %collective-permute-start.1 = (bf16[16,6144]{1,0:T(8,128)(2,1)S(1)}, bf16[16,6144]{1,0:T(8,128)(2,1)S(1)}, u32[]{:S(2)}, u32[]{:S(2)}) collective-permute-start(bf16[16,6144]{1,0:T(8,128)(2,1)S(1)} %slice.7), channel_id=1, source_target_pairs={{0,8},{4,12},{8,16},{12,20},{16,24},{20,28},{24,0},{28,4},{1,9},{5... | collective-permute-start | bytes 589832 | tf_op jit(solution)/shard_map/ppermute | solution.py:43
  17.9 13.8 %copy-start.1 = (bf16[64,256]{1,0:T(8,128)(2,1)S(1)}, bf16[64,256]{1,0:T(8,128)(2,1)}, u32[]{:S(2)}) copy-start(bf16[64,256]{1,0:T(8,128)(2,1)} %rot_ref.7) | copy-start | bytes 98308
  17.9 7.4 %collective-permute-start.6 = (bf16[64,512]{1,0:T(8,128)(2,1)S(1)}, bf16[64,512]{1,0:T(8,128)(2,1)S(1)}, u32[]{:S(2)}, u32[]{:S(2)}) collective-permute-start(bf16[64,512]{1,0:T(8,128)(2,1)S(1)} %couple.1.after_ref.mine), channel_id=1, source_target_pairs={{0,8},{4,12},{8,16},{12,20},{16,24},{20,28},{24,0},{28,4},{1,9},{5... | collective-permute-start | bytes 196616 | tf_op jit(solution)/shard_map/ppermute | solution.py:43
  20.6 11.2 %collective-permute-start.5 = (bf16[48,6144]{1,0:T(8,128)(2,1)S(1)}, bf16[48,6144]{1,0:T(8,128)(2,1)S(1)}, u32[]{:S(2)}, u32[]{:S(2)}) collective-permute-start(bf16[48,6144]{1,0:T(8,128)(2,1)S(1)} %hold.1), channel_id=1, source_target_pairs={{0,4},{4,8},{8,12},{12,16},{16,20},{20,24},{24,28},{28,0},{1,5},{5... | collective-permute-start | bytes 1769480 | tf_op jit(solution)/shard_map/ppermute | solution.py:43
  25.4 7.0 %collective-permute-start.7 = (bf16[80,6144]{1,0:T(8,128)(2,1)S(1)}, bf16[80,6144]{1,0:T(8,128)(2,1)S(1)}, u32[]{:S(2)}, u32[]{:S(2)}) collective-permute-start(bf16[80,6144]{1,0:T(8,128)(2,1)S(1)} %get-tuple-element.8), channel_id=1, source_target_pairs={{0,4},{4,0},{8,12},{12,8},{16,20},{20,16},{24,28},{28,24},{1,5},{5... | collective-permute-start | bytes 2949128 | tf_op jit(solution)/shard_map/ppermute | solution.py:48
  25.5 7.0 %collective-permute-start.9 = (bf16[64,512]{1,0:T(8,128)(2,1)S(1)}, bf16[64,512]{1,0:T(8,128)(2,1)S(1)}, u32[]{:S(2)}, u32[]{:S(2)}) collective-permute-start(bf16[64,512]{1,0:T(8,128)(2,1)S(1)} %collective-permute-done.6.mine_two.two), channel_id=1, source_target_pairs={{0,4},{4,8},{8,12},{12,16},{16,20},{20,24},{24,28},{28,0},{1,5},{5... | collective-permute-start | bytes 196616 | tf_op jit(solution)/shard_map/ppermute | solution.py:43
  26.0 7.9 %collective-permute-start.10 = (bf16[16,2560]{1,0:T(8,128)(2,1)S(1)}, bf16[16,2560]{1,0:T(8,128)(2,1)S(1)}, u32[]{:S(2)}, u32[]{:S(2)}) collective-permute-start(bf16[16,2560]{1,0:T(8,128)(2,1)S(1)} %get-tuple-element.10), channel_id=1, source_target_pairs={{0,4},{4,8},{8,12},{12,16},{16,20},{20,24},{24,28},{28,0},{1,5},{5... | collective-permute-start | bytes 245768 | tf_op jit(solution)/shard_map/ppermute | solution.py:43
  26.1 8.8 %collective-permute-start.8 = (bf16[16,3584]{1,0:T(8,128)(2,1)S(1)}, bf16[16,3584]{1,0:T(8,128)(2,1)S(1)}, u32[]{:S(2)}, u32[]{:S(2)}) collective-permute-start(bf16[16,3584]{1,0:T(8,128)(2,1)S(1)} %get-tuple-element.9), channel_id=1, source_target_pairs={{0,4},{4,8},{8,12},{12,16},{16,20},{20,24},{24,28},{28,0},{1,5},{5... | collective-permute-start | bytes 344072 | tf_op jit(solution)/shard_map/ppermute | solution.py:43

commit v3 on v2

--- a/solution.py
+++ b/solution.py
@@ -10,7 +10,7 @@
 TURN = 3 * 10**9
 COUPLE = 2 * 10**9
 APPLY = 50 * 10**8
-GATHER = 45 * 10**8
+GATHER = 66 * 10**8
 
 F32 = jnp.float32
 BF16 = jnp.bfloat16
@@ -168,6 +168,14 @@
     )[0]
 
 
+def lower_kernel(block_ref, out_ref):
+    out_ref[...] = block_ref[block_ref.shape[0] - out_ref.shape[0] :, :]
+
+
+def lower(block, rows):
+    return call(lower_kernel, "lower", [((rows, block.shape[1]), block.dtype)], [block])[0]
+
+
 def hold_kernel(block_ref, after_ref, out_ref):
     out_ref[...] = block_ref[...]
 
@@ -184,9 +192,9 @@
     ]
 
 
-def choose_kernel(mine, mine_two, own, two_a, two_b, swap_ref, *held_refs):
+def choose_kernel(mine, mine_two, own, two_a, two_b, swap_ref, held_ref):
     width, cut = own.shape[0], two_a.shape[0]
-    parts = packed(mine.shape, two_b.shape[0])
+    parts = packed(mine.shape, swap_ref.shape[0] - width)
 
     @pl.when(on_even())
     def _():
@@ -201,18 +209,13 @@
         for columns, rows in parts:
             swap_ref[width:, columns] = mine_two[rows, :]
 
-    at = 0
-    for ref in held_refs:
-        ref[...] = two_b[:, at : at + ref.shape[1]]
-        at += ref.shape[1]
+    held_ref[...] = two_b[...]
 
 
 def choose(mine, mine_two, own, two_a, two_b):
     args = [mine, mine_two, own, two_a, two_b]
-    rows, points = two_b.shape
-    last = points * 7 // 12 // 128 * 128
-    outs = [((own.shape[0] + rows, points), own.dtype)]
-    outs += [((rows, extent), own.dtype) for extent in (points - last, last)]
+    width, points = own.shape
+    outs = [((width + width // 4, points), own.dtype), (two_b.shape, own.dtype)]
     return call(choose_kernel, "choose", outs, args)
 
 
@@ -256,53 +259,39 @@
         )
 
 
-def finish_kernel(start, rot_ref, partial_ref, swap_ref, last_ref, applied, *refs):
-    out_hbm, out_ref, sems = refs[-3:]
-    width, extent = out_ref.shape
+def finish_kernel(
+    rot_ref, partial_ref, swap_ref, last_ref, applied, out_hbm, out_ref, sems
+):
+    width, points = out_ref.shape
     rows = last_ref.shape[0]
     pieces = sems.shape[0]
-    tile = extent // pieces
+    tile = points // pieces
     turn = jnp.concatenate(
         [rot_ref[:, width : 2 * width], rot_ref[:, rot_ref.shape[1] - rows :]], axis=1
     )
     copies = []
     for i in range(pieces):
         here = slice(i * tile, (i + 1) * tile)
-        there = slice(start + i * tile, start + (i + 1) * tile)
-        last = jnp.concatenate([swap_ref[:width, there], last_ref[:, here]], axis=0)
-        rotated = partial_ref[:, there] + jnp.dot(turn, last, preferred_element_type=F32)
-        added = rotated.astype(BF16).astype(F32) + applied[:, there]
+        last = jnp.concatenate([swap_ref[:width, here], last_ref[:, here]], axis=0)
+        rotated = partial_ref[:, here] + jnp.dot(turn, last, preferred_element_type=F32)
+        added = rotated.astype(BF16).astype(F32) + applied[:, here]
         out_ref[:, here] = added.astype(out_ref.dtype)
-        copies.append(
-            pltpu.make_async_copy(
-                out_ref.at[:, pl.ds(i * tile, tile)],
-                out_hbm.at[:, pl.ds(start + i * tile, tile)],
-                sems.at[i],
-            )
-        )
+        part = (slice(None), pl.ds(i * tile, tile))
+        copies.append(pltpu.make_async_copy(out_ref.at[part], out_hbm.at[part], sems.at[i]))
         copies[-1].start()
     for copy in copies:
         copy.wait()
 
 
-def finish(start, rotation, partial, swap, last, applied, so_far):
-    width, points = applied.shape
-    extent = last.shape[1]
-    pieces = extent // tile_of(extent, 1024)
-    args = [rotation, partial, swap, last, applied]
-    specs = [VMEM] * len(args)
-    alias = {}
-    if so_far is not None:
-        alias = {len(args): 0}
-        args.append(so_far)
-        specs.append(pl.BlockSpec(memory_space=pl.ANY))
+def finish(*args):
+    width, points = args[-1].shape
+    pieces = points // tile_of(points, 1024)
     return pl.pallas_call(
-        functools.partial(finish_kernel, start),
-        in_specs=specs,
+        finish_kernel,
+        in_specs=[VMEM] * len(args),
         out_specs=pl.BlockSpec(memory_space=pl.ANY),
         out_shape=jax.ShapeDtypeStruct((width, points), BF16),
-        scratch_shapes=[pltpu.VMEM((width, extent), BF16), pltpu.SemaphoreType.DMA((pieces,))],
-        input_output_aliases=alias,
+        scratch_shapes=[pltpu.VMEM((width, points), BF16), pltpu.SemaphoreType.DMA((pieces,))],
         compiler_params=ROOM,
         cost_estimate=flops(0),
         name="finish",
@@ -315,17 +304,17 @@
     owned = coupling.shape[0]
     proj = projectors.reshape(slot_count * rank, points)
 
-    cut = width * 3 // 4
+    cut = width // 2
     two_a = along_bands(orbitals[:cut], 2)
-    two_b = along_bands(orbitals[cut:], 2)
+    two_b = along_bands(lower(orbitals, width - cut), 2)
     loads = from_all_domains(project(orbitals, proj, coupling.reshape(owned * rank, rank)))
     mine = couple(slot_atom, loads, width, owned)
     mine_two = along_bands(mine, 2)
     three_a = along_bands(hold(two_a, mine), 1)
-    swap, *held = choose(mine, mine_two, orbitals, two_a, two_b)
+    swap, held = choose(mine, mine_two, orbitals, two_a, two_b)
     mine_three = along_bands(mine_two, 1)
     swap = swapped(swap)
-    three_b = [along_bands(block, 1) for block in held]
+    three_b = along_bands(held, 1)
     partial = gather(rotation, orbitals, two_a, two_b, three_a)
     applied = call(
         apply_kernel,
@@ -334,11 +323,7 @@
         [rotation, mine, swap, mine_two, mine_three, proj, partial],
         cost=APPLY,
     )[0]
-    out, start = None, 0
-    for last in three_b:
-        out = finish(start, rotation, partial, swap, last, applied, out)
-        start += last.shape[1]
-    return out
+    return finish(rotation, partial, swap, three_b, applied)
 
 
 def solution(mesh):

time: 36.1 us -> 37.2 us (1.030)
  waiting for transfers between devices: 13.2 us -> 15.6 us
  Pallas kernels: 7.62 us -> 6.73 us
  starting transfers between devices: 11.1 us -> 10.5 us
    ppermute x3, waiting for transfers between devices: 2.26 us -> 3.91 us  [from_all_domains(): return [block] + [lax.ppermute(block, 'dom', route) for route in routes]]
    pallas_call x2 -> x1, Pallas kernels: 2.01 us -> 1.2 us  [finish(): pl.pallas_call(finish_kernel, in_specs=[VMEM] * len(args), out_specs=pl.B...]
    ppermute x7 -> x6, waiting for transfers between devices: 11 us -> 11.7 us  [along_bands(): lax.ppermute(block, 'band', [(i, (i + distance) % count) for i in range(c...]
    ppermute x7 -> x6, starting transfers between devices: 7.45 us -> 6.89 us  [along_bands(): lax.ppermute(block, 'band', [(i, (i + distance) % count) for i in range(c...]
    unnamed x12 -> x14, local copies, waits for them, and re-layouts: 2.61 us -> 2.96 us
    pallas_call x7 -> x8, Pallas kernels: 5.61 us -> 5.53 us  [call(): pl.pallas_call(kernel, in_specs=[first] + [VMEM] * (len(args) - 1), out_s...]
  transfers between devices with their start and end apart: 11 -> 10, of which waited for: 7 -> 7; matrix products, arithmetic and copies ran while one was open for 0% -> 0% of each run, Pallas kernels for 18% -> 15%
where the time goes in v3:
time: 37.2 us; the launch traced here: 37 us
  waiting for transfers between devices  15.6 us (42%)
  starting transfers between devices  10.5 us (28%)
  Pallas kernels  6.73 us (18%)
  local copies, waits for them, and re-layouts  4.01 us (11%)
    ppermute x6, waiting for transfers between devices, along_bands(): lax.ppermute(block, 'band', [(i, (i + distance) % count) for i in range(c...  11.7 us
    ppermute x6, starting transfers between devices, along_bands(): lax.ppermute(block, 'band', [(i, (i + distance) % count) for i in range(c...  6.89 us
    pallas_call x8, Pallas kernels, call(): pl.pallas_call(kernel, in_specs=[first] + [VMEM] * (len(args) - 1), out_s...  5.53 us
    ppermute x3, waiting for transfers between devices, from_all_domains(): return [block] + [lax.ppermute(block, 'dom', route) for route in routes]  3.91 us
    ppermute x3, starting transfers between devices, from_all_domains(): return [block] + [lax.ppermute(block, 'dom', route) for route in routes]  3.55 us
    unnamed x14, local copies, waits for them, and re-layouts  2.96 us
    pallas_call x1, Pallas kernels, finish(): pl.pallas_call(finish_kernel, in_specs=[VMEM] * len(args), out_specs=pl.B...  1.2 us
    slice x1, local copies, waits for them, and re-layouts, on_device(): two_a = along_bands(orbitals[:cut], 2)  1.06 us
  transfers between devices with their start and end apart: 10, of which 7 were waited for; matrix products, arithmetic and copies ran while one was open for 0% of the time, Pallas kernels for 15%

profile of v3, /device:TPU:0, one launch (start us, length us, event | category | flops | bytes accessed | tf_op | source)
XLA Modules:
  0.0 37.0 jit_solution(570968442703187639)
XLA Ops:
  0.0 0.0 copy-start.3
  0.0 1.1 %slice.3 = bf16[32,6144]{1,0:T(8,128)(2,1)S(1)} slice(bf16[64,6144]{1,0:T(8,128)(2,1)} %own.3), slice={[0:32], [0:6144]} | slice | bytes 786432 | tf_op jit(solution)/shard_map/slice | solution.py:308
  1.1 3.1 %collective-permute-start = (bf16[32,6144]{1,0:T(8,128)(2,1)S(1)}, bf16[32,6144]{1,0:T(8,128)(2,1)S(1)}, u32[]{:S(2)}, u32[]{:S(2)}) collective-permute-start(bf16[32,6144]{1,0:T(8,128)(2,1)S(1)} %slice.3), channel_id=1, source_target_pairs={{0,8},{4,12},{8,16},{12,20},{16,24},{20,28},{24,0},{28,4},{1,9},{5... | collective-permute-start | bytes 1179656 | tf_op jit(solution)/shard_map/ppermute | solution.py:43
  4.1 0.0 copy-start
  4.1 1.1 %copy-done = bf16[64,6144]{1,0:T(8,128)(2,1)S(1)} copy-done((bf16[64,6144]{1,0:T(8,128)(2,1)S(1)}, bf16[64,6144]{1,0:T(8,128)(2,1)}, u32[]{:S(2)}) %copy-start) | copy-done | bytes 786456
  5.3 0.0 slice-start
  5.3 1.6 %collective-permute-start.1 = (bf16[32,6144]{1,0:T(8,128)(2,1)S(1)}, bf16[32,6144]{1,0:T(8,128)(2,1)S(1)}, u32[]{:S(2)}, u32[]{:S(2)}) collective-permute-start(bf16[32,6144]{1,0:T(8,128)(2,1)S(1)} %lower.1), channel_id=1, source_target_pairs={{0,8},{4,12},{8,16},{12,20},{16,24},{20,28},{24,0},{28,4},{1,9},{5... | collective-permute-start | bytes 1179656 | tf_op jit(solution)/shard_map/ppermute | solution.py:43
  6.9 0.0 copy-done.3
  6.9 0.0 copy-start.1
  6.9 0.0 slice-start.1
  6.9 0.1 turn.1.turned_ref
  7.1 0.4 %slice-done = s8[4194304]{0:T(1024)(128)(4,1)S(1)} async-done(((s8[6291456]{0:T(1024)(128)(4,1)}), s8[4194304]{0:T(1024)(128)(4,1)S(1)}, s32[]{:S(2)}) %slice-start) | async-done | bytes 4194328
  7.5 0.7 %copy-done.1 = bf16[64,6144]{1,0:T(8,128)(2,1)S(1)} copy-done((bf16[64,6144]{1,0:T(8,128)(2,1)S(1)}, bf16[64,6144]{1,0:T(8,128)(2,1)}, u32[]{:S(2)}) %copy-start.1) | copy-done | bytes 786456
  8.2 0.7 %slice-done.1 = s8[2097152]{0:T(1024)(128)(4,1)S(1)} async-done(((s8[6291456]{0:T(1024)(128)(4,1)}), s8[2097152]{0:T(1024)(128)(4,1)S(1)}, s32[]{:S(2)}) %slice-start.1) | async-done | bytes 2097176
  8.9 0.0 copy-start.4
  8.9 1.8 %project.1.refs_0_ = bf16[80,512]{1,0:T(8,128)(2,1)S(1)} custom-call(bf16[64,6144]{1,0:T(8,128)(2,1)S(1)} %copy-done.1, bf16[512,6144]{1,0:T(8,128)(2,1)S(1)} %bitcast.4, bf16[16,512]{1,0:T(8,128)(2,1)S(1)} %turn.1.turned_ref), custom_call_target="tpu_custom_call" | custom-call | tf_op jit(solution)/shard_map/project/pallas_call | solution.py:29
  10.7 2.5 %collective-permute-start.4 = (bf16[80,512]{1,0:T(8,128)(2,1)S(1)}, bf16[80,512]{1,0:T(8,128)(2,1)S(1)}, u32[]{:S(2)}, u32[]{:S(2)}) collective-permute-start(bf16[80,512]{1,0:T(8,128)(2,1)S(1)} %project.1.refs_0_), channel_id=1, source_target_pairs={{0,3},{1,2},{2,1},{3,0},{4,7},{5,6},{6,5},{7,4},{8,11},{9,10},{10,... | collective-permute-start | bytes 245768 | tf_op jit(solution)/shard_map/ppermute | solution.py:64
  13.2 0.5 %collective-permute-start.3 = (bf16[80,512]{1,0:T(8,128)(2,1)S(1)}, bf16[80,512]{1,0:T(8,128)(2,1)S(1)}, u32[]{:S(2)}, u32[]{:S(2)}) collective-permute-start(bf16[80,512]{1,0:T(8,128)(2,1)S(1)} %project.1.refs_0_), channel_id=1, source_target_pairs={{0,2},{1,3},{2,0},{3,1},{4,6},{5,7},{6,4},{7,5},{8,10},{9,11},{10,... | collective-permute-start | bytes 245768 | tf_op jit(solution)/shard_map/ppermute | solution.py:64
  13.7 0.5 %collective-permute-start.2 = (bf16[80,512]{1,0:T(8,128)(2,1)S(1)}, bf16[80,512]{1,0:T(8,128)(2,1)S(1)}, u32[]{:S(2)}, u32[]{:S(2)}) collective-permute-start(bf16[80,512]{1,0:T(8,128)(2,1)S(1)} %project.1.refs_0_), channel_id=1, source_target_pairs={{0,1},{1,0},{2,3},{3,2},{4,5},{5,4},{6,7},{7,6},{8,9},{9,8},{10,11... | collective-permute-start | bytes 245768 | tf_op jit(solution)/shard_map/ppermute | solution.py:64
  14.3 2.0 %collective-permute-done.4.refs_3_ = bf16[80,512]{1,0:T(8,128)(2,1)S(1)} collective-permute-done((bf16[80,512]{1,0:T(8,128)(2,1)S(1)}, bf16[80,512]{1,0:T(8,128)(2,1)S(1)}, u32[]{:S(2)}, u32[]{:S(2)}) %collective-permute-start.4) | collective-permute-done | bytes 81952 | tf_op jit(solution)/shard_map/ppermute | solution.py:64
  16.2 1.4 %collective-permute-done.3.refs_2_ = bf16[80,512]{1,0:T(8,128)(2,1)S(1)} collective-permute-done((bf16[80,512]{1,0:T(8,128)(2,1)S(1)}, bf16[80,512]{1,0:T(8,128)(2,1)S(1)}, u32[]{:S(2)}, u32[]{:S(2)}) %collective-permute-start.3) | collective-permute-done | bytes 81952 | tf_op jit(solution)/shard_map/ppermute | solution.py:64
  17.7 0.5 %collective-permute-done.2.refs_1_ = bf16[80,512]{1,0:T(8,128)(2,1)S(1)} collective-permute-done((bf16[80,512]{1,0:T(8,128)(2,1)S(1)}, bf16[80,512]{1,0:T(8,128)(2,1)S(1)}, u32[]{:S(2)}, u32[]{:S(2)}) %collective-permute-start.2) | collective-permute-done | bytes 81952 | tf_op jit(solution)/shard_map/ppermute | solution.py:64
  18.2 0.0 copy-done.4
  18.2 1.5 %couple.1.after_ref.mine = bf16[64,512]{1,0:T(8,128)(2,1)S(1)} custom-call(s32[4,32]{1,0:T(4,128)S(1)} %copy-done.4, bf16[80,512]{1,0:T(8,128)(2,1)S(1)} %project.1.refs_0_, bf16[80,512]{1,0:T(8,128)(2,1)S(1)} %collective-permute-done.2.refs_1_, bf16[80,512]{1,0:T(8,128)(2,1)S(1)} %collective-permute-done.3.refs_2_, ...), custom_call_target="tpu_custom_call" | custom-call | flops 2000000000 | tf_op jit(solution)/shard_map/couple/pallas_call | solution.py:29
  19.7 0.0 copy-start.2
  19.7 1.6 %collective-permute-start.6 = (bf16[64,512]{1,0:T(8,128)(2,1)S(1)}, bf16[64,512]{1,0:T(8,128)(2,1)S(1)}, u32[]{:S(2)}, u32[]{:S(2)}) collective-permute-start(bf16[64,512]{1,0:T(8,128)(2,1)S(1)} %couple.1.after_ref.mine), channel_id=1, source_target_pairs={{0,8},{4,12},{8,16},{12,20},{16,24},{20,28},{24,0},{28,4},{1,9},{5... | collective-permute-start | bytes 196616 | tf_op jit(solution)/shard_map/ppermute | solution.py:43
  21.4 0.0 collective-permute-done.block_ref.two_a
  21.4 0.1 collective-permute-start.5
  21.5 4.4 %collective-permute-done.6.mine_two.two = bf16[64,512]{1,0:T(8,128)(2,1)S(1)} collective-permute-done((bf16[64,512]{1,0:T(8,128)(2,1)S(1)}, bf16[64,512]{1,0:T(8,128)(2,1)S(1)}, u32[]{:S(2)}, u32[]{:S(2)}) %collective-permute-start.6) | collective-permute-done | bytes 65568 | tf_op jit(solution)/shard_map/ppermute | solution.py:43
  25.9 0.0 collective-permute-done.1.two_b
  25.9 0.1 choose.1
  26.0 0.1 collective-permute-start.7
  26.0 0.5 %collective-permute-start.9 = (bf16[64,512]{1,0:T(8,128)(2,1)S(1)}, bf16[64,512]{1,0:T(8,128)(2,1)S(1)}, u32[]{:S(2)}, u32[]{:S(2)}) collective-permute-start(bf16[64,512]{1,0:T(8,128)(2,1)S(1)} %collective-permute-done.6.mine_two.two), channel_id=1, source_target_pairs={{0,4},{4,8},{8,12},{12,16},{16,20},{20,24},{24,28},{28,0},{1,5},{5... | collective-permute-start | bytes 196616 | tf_op jit(solution)/shard_map/ppermute | solution.py:43
  26.5 0.0 collective-permute-start.8
  26.5 3.9 %collective-permute-done.5.three_a = bf16[32,6144]{1,0:T(8,128)(2,1)S(1)} collective-permute-done((bf16[32,6144]{1,0:T(8,128)(2,1)S(1)}, bf16[32,6144]{1,0:T(8,128)(2,1)S(1)}, u32[]{:S(2)}, u32[]{:S(2)}) %collective-permute-start.5) | collective-permute-done | bytes 393248 | tf_op jit(solution)/shard_map/ppermute | solution.py:43
  30.4 0.0 copy-done.2
  30.5 0.5 %gather.1.after_ref.partial_ref = f32[64,6144]{1,0:T(8,128)S(1)} custom-call(bf16[64,256]{1,0:T(8,128)(2,1)S(1)} %copy-done.2, bf16[64,6144]{1,0:T(8,128)(2,1)S(1)} %copy-done.1, bf16[32,6144]{1,0:T(8,128)(2,1)S(1)} %collective-permute-done.block_ref.two_a, bf16[32,6144]{1,0:T(8,128)(2,1)S(1)} %collective-permute-done.1.two_b, ...), custom_call_target="tpu_custom_call" | custom-call | flops 6600000000 | tf_op jit(solution)/shard_map/gather/pallas_call | solution.py:29
  30.9 0.7 %collective-permute-done.9.three = bf16[64,512]{1,0:T(8,128)(2,1)S(1)} collective-permute-done((bf16[64,512]{1,0:T(8,128)(2,1)S(1)}, bf16[64,512]{1,0:T(8,128)(2,1)S(1)}, u32[]{:S(2)}, u32[]{:S(2)}) %collective-permute-start.9) | collective-permute-done | bytes 65568 | tf_op jit(solution)/shard_map/ppermute | solution.py:43
  31.6 0.0 collective-permute-done.7.swap_ref
  31.6 1.4 %apply.1.applied = f32[64,6144]{1,0:T(8,128)S(1)} custom-call(bf16[64,256]{1,0:T(8,128)(2,1)S(1)} %copy-done.2, bf16[64,512]{1,0:T(8,128)(2,1)S(1)} %couple.1.after_ref.mine, bf16[80,6144]{1,0:T(8,128)(2,1)S(1)} %collective-permute-done.7.swap_ref, bf16[64,512]{1,0:T(8,128)(2,1)S(1)} %collective-permute-done.6.mine_two.two, ...), custom_call_target="tpu_custom_call" | custom-call | flops 5000000000 | tf_op jit(solution)/shard_map/apply/pallas_call | solution.py:29
  33.0 2.8 %collective-permute-done.8.last_ref = bf16[32,6144]{1,0:T(8,128)(2,1)S(1)} collective-permute-done((bf16[32,6144]{1,0:T(8,128)(2,1)S(1)}, bf16[32,6144]{1,0:T(8,128)(2,1)S(1)}, u32[]{:S(2)}, u32[]{:S(2)}) %collective-permute-start.8) | collective-permute-done | bytes 393248 | tf_op jit(solution)/shard_map/ppermute | solution.py:43
  35.8 1.2 %finish.1 = bf16[64,6144]{1,0:T(8,128)(2,1)} custom-call(bf16[64,256]{1,0:T(8,128)(2,1)S(1)} %copy-done.2, f32[64,6144]{1,0:T(8,128)S(1)} %gather.1.after_ref.partial_ref, bf16[80,6144]{1,0:T(8,128)(2,1)S(1)} %collective-permute-done.7.swap_ref, bf16[32,6144]{1,0:T(8,128)(2,1)S(1)} %collective-permute-done.8.last_ref, f32[64,6144]{1,0:T(8,128)S(1)} %apply.1.applied), custom_call_target="tpu_custom_call" | custom-call | tf_op jit(solution)/shard_map/finish/pallas_call | solution.py:289
  (3 shorter events, 0.1 us)
Async XLA Ops:
  0.0 6.9 %copy-start.3 = (f32[16,16,16]{2,1,0:T(8,128)S(1)}, f32[16,16,16]{2,1,0:T(8,128)}, u32[]{:S(2)}) copy-start(f32[16,16,16]{2,1,0:T(8,128)} %param.8) | copy-start | bytes 49156
  1.1 20.3 %collective-permute-start = (bf16[32,6144]{1,0:T(8,128)(2,1)S(1)}, bf16[32,6144]{1,0:T(8,128)(2,1)S(1)}, u32[]{:S(2)}, u32[]{:S(2)}) collective-permute-start(bf16[32,6144]{1,0:T(8,128)(2,1)S(1)} %slice.3), channel_id=1, source_target_pairs={{0,8},{4,12},{8,16},{12,20},{16,24},{20,28},{24,0},{28,4},{1,9},{5... | collective-permute-start | bytes 1179656 | tf_op jit(solution)/shard_map/ppermute | solution.py:43
  4.1 1.1 %copy-start = (bf16[64,6144]{1,0:T(8,128)(2,1)S(1)}, bf16[64,6144]{1,0:T(8,128)(2,1)}, u32[]{:S(2)}) copy-start(bf16[64,6144]{1,0:T(8,128)(2,1)} %own.3) | copy-start | bytes 2359300
  5.3 2.2 %slice-start = ((s8[6291456]{0:T(1024)(128)(4,1)}), s8[4194304]{0:T(1024)(128)(4,1)S(1)}, s32[]{:S(2)}) async-start(s8[6291456]{0:T(1024)(128)(4,1)} %bitcast.2), calls=%async_computation | async-start | bytes 8388608
  5.3 20.6 %collective-permute-start.1 = (bf16[32,6144]{1,0:T(8,128)(2,1)S(1)}, bf16[32,6144]{1,0:T(8,128)(2,1)S(1)}, u32[]{:S(2)}, u32[]{:S(2)}) collective-permute-start(bf16[32,6144]{1,0:T(8,128)(2,1)S(1)} %lower.1), channel_id=1, source_target_pairs={{0,8},{4,12},{8,16},{12,20},{16,24},{20,28},{24,0},{28,4},{1,9},{5... | collective-permute-start | bytes 1179656 | tf_op jit(solution)/shard_map/ppermute | solution.py:43
  6.9 1.3 %copy-start.1 = (bf16[64,6144]{1,0:T(8,128)(2,1)S(1)}, bf16[64,6144]{1,0:T(8,128)(2,1)}, u32[]{:S(2)}) copy-start(bf16[64,6144]{1,0:T(8,128)(2,1)} %own.3) | copy-start | bytes 2359300
  6.9 2.0 %slice-start.1 = ((s8[6291456]{0:T(1024)(128)(4,1)}), s8[2097152]{0:T(1024)(128)(4,1)S(1)}, s32[]{:S(2)}) async-start(s8[6291456]{0:T(1024)(128)(4,1)} %bitcast.2), calls=%async_computation.1 | async-start | bytes 4194304
  8.9 9.3 %copy-start.4 = (s32[4,32]{1,0:T(4,128)S(1)}, s32[4,32]{1,0:T(4,128)}, u32[]{:S(2)}) copy-start(s32[4,32]{1,0:T(4,128)} %slot_ref.1) | copy-start | bytes 1540
  10.7 5.5 %collective-permute-start.4 = (bf16[80,512]{1,0:T(8,128)(2,1)S(1)}, bf16[80,512]{1,0:T(8,128)(2,1)S(1)}, u32[]{:S(2)}, u32[]{:S(2)}) collective-permute-start(bf16[80,512]{1,0:T(8,128)(2,1)S(1)} %project.1.refs_0_), channel_id=1, source_target_pairs={{0,3},{1,2},{2,1},{3,0},{4,7},{5,6},{6,5},{7,4},{8,11},{9,10},{10,... | collective-permute-start | bytes 245768 | tf_op jit(solution)/shard_map/ppermute | solution.py:64
  13.2 4.4 %collective-permute-start.3 = (bf16[80,512]{1,0:T(8,128)(2,1)S(1)}, bf16[80,512]{1,0:T(8,128)(2,1)S(1)}, u32[]{:S(2)}, u32[]{:S(2)}) collective-permute-start(bf16[80,512]{1,0:T(8,128)(2,1)S(1)} %project.1.refs_0_), channel_id=1, source_target_pairs={{0,2},{1,3},{2,0},{3,1},{4,6},{5,7},{6,4},{7,5},{8,10},{9,11},{10,... | collective-permute-start | bytes 245768 | tf_op jit(solution)/shard_map/ppermute | solution.py:64
  13.7 4.4 %collective-permute-start.2 = (bf16[80,512]{1,0:T(8,128)(2,1)S(1)}, bf16[80,512]{1,0:T(8,128)(2,1)S(1)}, u32[]{:S(2)}, u32[]{:S(2)}) collective-permute-start(bf16[80,512]{1,0:T(8,128)(2,1)S(1)} %project.1.refs_0_), channel_id=1, source_target_pairs={{0,1},{1,0},{2,3},{3,2},{4,5},{5,4},{6,7},{7,6},{8,9},{9,8},{10,11... | collective-permute-start | bytes 245768 | tf_op jit(solution)/shard_map/ppermute | solution.py:64
  19.7 10.7 %copy-start.2 = (bf16[64,256]{1,0:T(8,128)(2,1)S(1)}, bf16[64,256]{1,0:T(8,128)(2,1)}, u32[]{:S(2)}) copy-start(bf16[64,256]{1,0:T(8,128)(2,1)} %rot_ref.5) | copy-start | bytes 98308
  19.7 6.1 %collective-permute-start.6 = (bf16[64,512]{1,0:T(8,128)(2,1)S(1)}, bf16[64,512]{1,0:T(8,128)(2,1)S(1)}, u32[]{:S(2)}, u32[]{:S(2)}) collective-permute-start(bf16[64,512]{1,0:T(8,128)(2,1)S(1)} %couple.1.after_ref.mine), channel_id=1, source_target_pairs={{0,8},{4,12},{8,16},{12,20},{16,24},{20,28},{24,0},{28,4},{1,9},{5... | collective-permute-start | bytes 196616 | tf_op jit(solution)/shard_map/ppermute | solution.py:43
  21.4 9.1 %collective-permute-start.5 = (bf16[32,6144]{1,0:T(8,128)(2,1)S(1)}, bf16[32,6144]{1,0:T(8,128)(2,1)S(1)}, u32[]{:S(2)}, u32[]{:S(2)}) collective-permute-start(bf16[32,6144]{1,0:T(8,128)(2,1)S(1)} %hold.1), channel_id=1, source_target_pairs={{0,4},{4,8},{8,12},{12,16},{16,20},{20,24},{24,28},{28,0},{1,5},{5... | collective-permute-start | bytes 1179656 | tf_op jit(solution)/shard_map/ppermute | solution.py:43
  26.0 5.6 %collective-permute-start.7 = (bf16[80,6144]{1,0:T(8,128)(2,1)S(1)}, bf16[80,6144]{1,0:T(8,128)(2,1)S(1)}, u32[]{:S(2)}, u32[]{:S(2)}) collective-permute-start(bf16[80,6144]{1,0:T(8,128)(2,1)S(1)} %get-tuple-element.7), channel_id=1, source_target_pairs={{0,4},{4,0},{8,12},{12,8},{16,20},{20,16},{24,28},{28,24},{1,5},{5... | collective-permute-start | bytes 2949128 | tf_op jit(solution)/shard_map/ppermute | solution.py:48
  26.0 5.5 %collective-permute-start.9 = (bf16[64,512]{1,0:T(8,128)(2,1)S(1)}, bf16[64,512]{1,0:T(8,128)(2,1)S(1)}, u32[]{:S(2)}, u32[]{:S(2)}) collective-permute-start(bf16[64,512]{1,0:T(8,128)(2,1)S(1)} %collective-permute-done.6.mine_two.two), channel_id=1, source_target_pairs={{0,4},{4,8},{8,12},{12,16},{16,20},{20,24},{24,28},{28,0},{1,5},{5... | collective-permute-start | bytes 196616 | tf_op jit(solution)/shard_map/ppermute | solution.py:43
  26.5 9.3 %collective-permute-start.8 = (bf16[32,6144]{1,0:T(8,128)(2,1)S(1)}, bf16[32,6144]{1,0:T(8,128)(2,1)S(1)}, u32[]{:S(2)}, u32[]{:S(2)}) collective-permute-start(bf16[32,6144]{1,0:T(8,128)(2,1)S(1)} %get-tuple-element.8), channel_id=1, source_target_pairs={{0,4},{4,8},{8,12},{12,16},{16,20},{20,24},{24,28},{28,0},{1,5},{5... | collective-permute-start | bytes 1179656 | tf_op jit(solution)/shard_map/ppermute | solution.py:43

commit v4 on v3

--- a/solution.py
+++ b/solution.py
@@ -10,7 +10,7 @@
 TURN = 3 * 10**9
 COUPLE = 2 * 10**9
 APPLY = 50 * 10**8
-GATHER = 66 * 10**8
+GATHER = 45 * 10**8
 
 F32 = jnp.float32
 BF16 = jnp.bfloat16
@@ -166,14 +166,6 @@
         first=SMEM,
         cost=COUPLE,
     )[0]
-
-
-def lower_kernel(block_ref, out_ref):
-    out_ref[...] = block_ref[block_ref.shape[0] - out_ref.shape[0] :, :]
-
-
-def lower(block, rows):
-    return call(lower_kernel, "lower", [((rows, block.shape[1]), block.dtype)], [block])[0]
 
 
 def hold_kernel(block_ref, after_ref, out_ref):
@@ -304,9 +296,9 @@
     owned = coupling.shape[0]
     proj = projectors.reshape(slot_count * rank, points)
 
-    cut = width // 2
+    cut = width * 3 // 4
     two_a = along_bands(orbitals[:cut], 2)
-    two_b = along_bands(lower(orbitals, width - cut), 2)
+    two_b = along_bands(orbitals[cut:], 2)
     loads = from_all_domains(project(orbitals, proj, coupling.reshape(owned * rank, rank)))
     mine = couple(slot_atom, loads, width, owned)
     mine_two = along_bands(mine, 2)

time: 37.2 us -> 35.9 us (0.965)
  waiting for transfers between devices: 15.6 us -> 14.3 us
    ppermute x3, waiting for transfers between devices: 3.91 us -> 2.26 us  [from_all_domains(): return [block] + [lax.ppermute(block, 'dom', route) for route in routes]]
    unnamed x14 -> x12, local copies, waits for them, and re-layouts: 2.96 us -> 2.61 us
    pallas_call x8 -> x7, Pallas kernels: 5.53 us -> 5.61 us  [call(): pl.pallas_call(kernel, in_specs=[first] + [VMEM] * (len(args) - 1), out_s...]
  transfers between devices with their start and end apart: 10 -> 10, of which waited for: 7 -> 8; matrix products, arithmetic and copies ran while one was open for 0% -> 0% of each run, Pallas kernels for 15% -> 16%
where the time goes in v4:
time: 35.9 us; the launch traced here: 35.7 us
  waiting for transfers between devices  14.3 us (40%)
  starting transfers between devices  10.6 us (30%)
  Pallas kernels  6.79 us (19%)
  local copies, waits for them, and re-layouts  3.88 us (11%)
    ppermute x6, waiting for transfers between devices, along_bands(): lax.ppermute(block, 'band', [(i, (i + distance) % count) for i in range(c...  12.1 us
    ppermute x6, starting transfers between devices, along_bands(): lax.ppermute(block, 'band', [(i, (i + distance) % count) for i in range(c...  7.01 us
    pallas_call x7, Pallas kernels, call(): pl.pallas_call(kernel, in_specs=[first] + [VMEM] * (len(args) - 1), out_s...  5.61 us
    ppermute x3, starting transfers between devices, from_all_domains(): return [block] + [lax.ppermute(block, 'dom', route) for route in routes]  3.55 us
    unnamed x12, local copies, waits for them, and re-layouts  2.61 us
    ppermute x3, waiting for transfers between devices, from_all_domains(): return [block] + [lax.ppermute(block, 'dom', route) for route in routes]  2.26 us
    slice x1, local copies, waits for them, and re-layouts, on_device(): two_a = along_bands(orbitals[:cut], 2)  1.25 us
    pallas_call x1, Pallas kernels, finish(): pl.pallas_call(finish_kernel, in_specs=[VMEM] * len(args), out_specs=pl.B...  1.18 us
  transfers between devices with their start and end apart: 10, of which 8 were waited for; matrix products, arithmetic and copies ran while one was open for 0% of the time, Pallas kernels for 16%

profile of v4, /device:TPU:0, one launch (start us, length us, event | category | flops | bytes accessed | tf_op | source)
XLA Modules:
  0.0 35.7 jit_solution(5429887942321498394)
XLA Ops:
  0.0 0.0 slice-start
  0.0 1.3 %slice.6 = bf16[48,6144]{1,0:T(8,128)(2,1)S(1)} slice(bf16[64,6144]{1,0:T(8,128)(2,1)} %own.3), slice={[0:48], [0:6144]} | slice | bytes 1179648 | tf_op jit(solution)/shard_map/slice | solution.py:300
  1.3 3.1 %collective-permute-start = (bf16[48,6144]{1,0:T(8,128)(2,1)S(1)}, bf16[48,6144]{1,0:T(8,128)(2,1)S(1)}, u32[]{:S(2)}, u32[]{:S(2)}) collective-permute-start(bf16[48,6144]{1,0:T(8,128)(2,1)S(1)} %slice.6), channel_id=1, source_target_pairs={{0,8},{4,12},{8,16},{12,20},{16,24},{20,28},{24,0},{28,4},{1,9},{5... | collective-permute-start | bytes 1769480 | tf_op jit(solution)/shard_map/ppermute | solution.py:43
  4.3 0.0 copy-start.2
  4.3 0.9 %copy-done.2 = f32[16,16,16]{2,1,0:T(8,128)S(1)} copy-done((f32[16,16,16]{2,1,0:T(8,128)S(1)}, f32[16,16,16]{2,1,0:T(8,128)}, u32[]{:S(2)}) %copy-start.2) | copy-done | bytes 16408
  5.2 0.0 copy-start
  5.2 0.0 slice-start.1
  5.2 0.1 turn.1.turned_ref
  5.4 0.0 slice-done
  5.4 1.0 %copy-done = bf16[64,6144]{1,0:T(8,128)(2,1)S(1)} copy-done((bf16[64,6144]{1,0:T(8,128)(2,1)S(1)}, bf16[64,6144]{1,0:T(8,128)(2,1)}, u32[]{:S(2)}) %copy-start) | copy-done | bytes 786456
  6.4 0.7 %slice-done.1 = s8[2097152]{0:T(1024)(128)(4,1)S(1)} async-done(((s8[6291456]{0:T(1024)(128)(4,1)}), s8[2097152]{0:T(1024)(128)(4,1)S(1)}, s32[]{:S(2)}) %slice-start.1) | async-done | bytes 2097176
  7.1 0.0 copy-start.3
  7.1 1.8 %project.1.refs_0_ = bf16[80,512]{1,0:T(8,128)(2,1)S(1)} custom-call(bf16[64,6144]{1,0:T(8,128)(2,1)S(1)} %copy-done, bf16[512,6144]{1,0:T(8,128)(2,1)S(1)} %bitcast.4, bf16[16,512]{1,0:T(8,128)(2,1)S(1)} %turn.1.turned_ref), custom_call_target="tpu_custom_call" | custom-call | tf_op jit(solution)/shard_map/project/pallas_call | solution.py:29
  8.9 2.5 %collective-permute-start.4 = (bf16[80,512]{1,0:T(8,128)(2,1)S(1)}, bf16[80,512]{1,0:T(8,128)(2,1)S(1)}, u32[]{:S(2)}, u32[]{:S(2)}) collective-permute-start(bf16[80,512]{1,0:T(8,128)(2,1)S(1)} %project.1.refs_0_), channel_id=1, source_target_pairs={{0,3},{1,2},{2,1},{3,0},{4,7},{5,6},{6,5},{7,4},{8,11},{9,10},{10,... | collective-permute-start | bytes 245768 | tf_op jit(solution)/shard_map/ppermute | solution.py:64
  11.4 0.5 %collective-permute-start.3 = (bf16[80,512]{1,0:T(8,128)(2,1)S(1)}, bf16[80,512]{1,0:T(8,128)(2,1)S(1)}, u32[]{:S(2)}, u32[]{:S(2)}) collective-permute-start(bf16[80,512]{1,0:T(8,128)(2,1)S(1)} %project.1.refs_0_), channel_id=1, source_target_pairs={{0,2},{1,3},{2,0},{3,1},{4,6},{5,7},{6,4},{7,5},{8,10},{9,11},{10,... | collective-permute-start | bytes 245768 | tf_op jit(solution)/shard_map/ppermute | solution.py:64
  11.9 0.5 %collective-permute-start.2 = (bf16[80,512]{1,0:T(8,128)(2,1)S(1)}, bf16[80,512]{1,0:T(8,128)(2,1)S(1)}, u32[]{:S(2)}, u32[]{:S(2)}) collective-permute-start(bf16[80,512]{1,0:T(8,128)(2,1)S(1)} %project.1.refs_0_), channel_id=1, source_target_pairs={{0,1},{1,0},{2,3},{3,2},{4,5},{5,4},{6,7},{7,6},{8,9},{9,8},{10,11... | collective-permute-start | bytes 245768 | tf_op jit(solution)/shard_map/ppermute | solution.py:64
  12.5 1.6 %collective-permute-start.1 = (bf16[16,6144]{1,0:T(8,128)(2,1)S(1)}, bf16[16,6144]{1,0:T(8,128)(2,1)S(1)}, u32[]{:S(2)}, u32[]{:S(2)}) collective-permute-start(bf16[16,6144]{1,0:T(8,128)(2,1)S(1)} %slice.7), channel_id=1, source_target_pairs={{0,8},{4,12},{8,16},{12,20},{16,24},{20,28},{24,0},{28,4},{1,9},{5... | collective-permute-start | bytes 589832 | tf_op jit(solution)/shard_map/ppermute | solution.py:43
  14.1 0.3 collective-permute-done.4.refs_3_
  14.4 1.5 %collective-permute-done.3.refs_2_ = bf16[80,512]{1,0:T(8,128)(2,1)S(1)} collective-permute-done((bf16[80,512]{1,0:T(8,128)(2,1)S(1)}, bf16[80,512]{1,0:T(8,128)(2,1)S(1)}, u32[]{:S(2)}, u32[]{:S(2)}) %collective-permute-start.3) | collective-permute-done | bytes 81952 | tf_op jit(solution)/shard_map/ppermute | solution.py:64
  15.9 0.5 %collective-permute-done.2.refs_1_ = bf16[80,512]{1,0:T(8,128)(2,1)S(1)} collective-permute-done((bf16[80,512]{1,0:T(8,128)(2,1)S(1)}, bf16[80,512]{1,0:T(8,128)(2,1)S(1)}, u32[]{:S(2)}, u32[]{:S(2)}) %collective-permute-start.2) | collective-permute-done | bytes 81952 | tf_op jit(solution)/shard_map/ppermute | solution.py:64
  16.4 0.0 copy-done.3
  16.4 1.5 %couple.1.after_ref.mine = bf16[64,512]{1,0:T(8,128)(2,1)S(1)} custom-call(s32[4,32]{1,0:T(4,128)S(1)} %copy-done.3, bf16[80,512]{1,0:T(8,128)(2,1)S(1)} %project.1.refs_0_, bf16[80,512]{1,0:T(8,128)(2,1)S(1)} %collective-permute-done.2.refs_1_, bf16[80,512]{1,0:T(8,128)(2,1)S(1)} %collective-permute-done.3.refs_2_, ...), custom_call_target="tpu_custom_call" | custom-call | flops 2000000000 | tf_op jit(solution)/shard_map/couple/pallas_call | solution.py:29
  17.9 0.0 copy-start.1
  17.9 1.6 %collective-permute-start.6 = (bf16[64,512]{1,0:T(8,128)(2,1)S(1)}, bf16[64,512]{1,0:T(8,128)(2,1)S(1)}, u32[]{:S(2)}, u32[]{:S(2)}) collective-permute-start(bf16[64,512]{1,0:T(8,128)(2,1)S(1)} %couple.1.after_ref.mine), channel_id=1, source_target_pairs={{0,8},{4,12},{8,16},{12,20},{16,24},{20,28},{24,0},{28,4},{1,9},{5... | collective-permute-start | bytes 196616 | tf_op jit(solution)/shard_map/ppermute | solution.py:43
  19.6 1.0 %collective-permute-done.block_ref.two_a = bf16[48,6144]{1,0:T(8,128)(2,1)S(1)} collective-permute-done((bf16[48,6144]{1,0:T(8,128)(2,1)S(1)}, bf16[48,6144]{1,0:T(8,128)(2,1)S(1)}, u32[]{:S(2)}, u32[]{:S(2)}) %collective-permute-start) | collective-permute-done | bytes 589856 | tf_op jit(solution)/shard_map/ppermute | solution.py:43
  20.6 0.1 collective-permute-start.5
  20.6 4.7 %collective-permute-done.6.mine_two.two = bf16[64,512]{1,0:T(8,128)(2,1)S(1)} collective-permute-done((bf16[64,512]{1,0:T(8,128)(2,1)S(1)}, bf16[64,512]{1,0:T(8,128)(2,1)S(1)}, u32[]{:S(2)}, u32[]{:S(2)}) %collective-permute-start.6) | collective-permute-done | bytes 65568 | tf_op jit(solution)/shard_map/ppermute | solution.py:43
  25.3 0.0 collective-permute-done.1.two_b
  25.3 0.1 choose.1
  25.4 0.1 collective-permute-start.7
  25.5 0.5 %collective-permute-start.9 = (bf16[64,512]{1,0:T(8,128)(2,1)S(1)}, bf16[64,512]{1,0:T(8,128)(2,1)S(1)}, u32[]{:S(2)}, u32[]{:S(2)}) collective-permute-start(bf16[64,512]{1,0:T(8,128)(2,1)S(1)} %collective-permute-done.6.mine_two.two), channel_id=1, source_target_pairs={{0,4},{4,8},{8,12},{12,16},{16,20},{20,24},{24,28},{28,0},{1,5},{5... | collective-permute-start | bytes 196616 | tf_op jit(solution)/shard_map/ppermute | solution.py:43
  26.0 0.1 collective-permute-start.8
  26.1 5.6 %collective-permute-done.5.three_a = bf16[48,6144]{1,0:T(8,128)(2,1)S(1)} collective-permute-done((bf16[48,6144]{1,0:T(8,128)(2,1)S(1)}, bf16[48,6144]{1,0:T(8,128)(2,1)S(1)}, u32[]{:S(2)}, u32[]{:S(2)}) %collective-permute-start.5) | collective-permute-done | bytes 589856 | tf_op jit(solution)/shard_map/ppermute | solution.py:43
  31.7 0.0 copy-done.1
  31.7 0.6 %gather.1.after_ref.partial_ref = f32[64,6144]{1,0:T(8,128)S(1)} custom-call(bf16[64,256]{1,0:T(8,128)(2,1)S(1)} %copy-done.1, bf16[64,6144]{1,0:T(8,128)(2,1)S(1)} %copy-done, bf16[48,6144]{1,0:T(8,128)(2,1)S(1)} %collective-permute-done.block_ref.two_a, bf16[16,6144]{1,0:T(8,128)(2,1)S(1)} %collective-permute-done.1.two_b, ...), custom_call_target="tpu_custom_call" | custom-call | flops 4499999744 | tf_op jit(solution)/shard_map/gather/pallas_call | solution.py:29
  32.3 0.1 collective-permute-done.9.three
  32.4 0.0 collective-permute-done.7.swap_ref
  32.4 1.4 %apply.1.applied = f32[64,6144]{1,0:T(8,128)S(1)} custom-call(bf16[64,256]{1,0:T(8,128)(2,1)S(1)} %copy-done.1, bf16[64,512]{1,0:T(8,128)(2,1)S(1)} %couple.1.after_ref.mine, bf16[80,6144]{1,0:T(8,128)(2,1)S(1)} %collective-permute-done.7.swap_ref, bf16[64,512]{1,0:T(8,128)(2,1)S(1)} %collective-permute-done.6.mine_two.two, ...), custom_call_target="tpu_custom_call" | custom-call | flops 5000000000 | tf_op jit(solution)/shard_map/apply/pallas_call | solution.py:29
  33.9 0.7 %collective-permute-done.8.last_ref = bf16[16,6144]{1,0:T(8,128)(2,1)S(1)} collective-permute-done((bf16[16,6144]{1,0:T(8,128)(2,1)S(1)}, bf16[16,6144]{1,0:T(8,128)(2,1)S(1)}, u32[]{:S(2)}, u32[]{:S(2)}) %collective-permute-start.8) | collective-permute-done | bytes 196640 | tf_op jit(solution)/shard_map/ppermute | solution.py:43
  34.5 1.2 %finish.1 = bf16[64,6144]{1,0:T(8,128)(2,1)} custom-call(bf16[64,256]{1,0:T(8,128)(2,1)S(1)} %copy-done.1, f32[64,6144]{1,0:T(8,128)S(1)} %gather.1.after_ref.partial_ref, bf16[80,6144]{1,0:T(8,128)(2,1)S(1)} %collective-permute-done.7.swap_ref, bf16[16,6144]{1,0:T(8,128)(2,1)S(1)} %collective-permute-done.8.last_ref, f32[64,6144]{1,0:T(8,128)S(1)} %apply.1.applied), custom_call_target="tpu_custom_call" | custom-call | tf_op jit(solution)/shard_map/finish/pallas_call | solution.py:281
  (3 shorter events, 0.1 us)
Async XLA Ops:
  0.0 5.4 %slice-start = ((s8[6291456]{0:T(1024)(128)(4,1)}), s8[4194304]{0:T(1024)(128)(4,1)S(1)}, s32[]{:S(2)}) async-start(s8[6291456]{0:T(1024)(128)(4,1)} %bitcast.2), calls=%async_computation | async-start | bytes 8388608
  1.3 19.3 %collective-permute-start = (bf16[48,6144]{1,0:T(8,128)(2,1)S(1)}, bf16[48,6144]{1,0:T(8,128)(2,1)S(1)}, u32[]{:S(2)}, u32[]{:S(2)}) collective-permute-start(bf16[48,6144]{1,0:T(8,128)(2,1)S(1)} %slice.6), channel_id=1, source_target_pairs={{0,8},{4,12},{8,16},{12,20},{16,24},{20,28},{24,0},{28,4},{1,9},{5... | collective-permute-start | bytes 1769480 | tf_op jit(solution)/shard_map/ppermute | solution.py:43
  4.3 0.9 %copy-start.2 = (f32[16,16,16]{2,1,0:T(8,128)S(1)}, f32[16,16,16]{2,1,0:T(8,128)}, u32[]{:S(2)}) copy-start(f32[16,16,16]{2,1,0:T(8,128)} %param.8) | copy-start | bytes 49156
  5.2 1.1 %copy-start = (bf16[64,6144]{1,0:T(8,128)(2,1)S(1)}, bf16[64,6144]{1,0:T(8,128)(2,1)}, u32[]{:S(2)}) copy-start(bf16[64,6144]{1,0:T(8,128)(2,1)} %own.3) | copy-start | bytes 2359300
  5.2 1.8 %slice-start.1 = ((s8[6291456]{0:T(1024)(128)(4,1)}), s8[2097152]{0:T(1024)(128)(4,1)S(1)}, s32[]{:S(2)}) async-start(s8[6291456]{0:T(1024)(128)(4,1)} %bitcast.2), calls=%async_computation.1 | async-start | bytes 4194304
  7.1 9.3 %copy-start.3 = (s32[4,32]{1,0:T(4,128)S(1)}, s32[4,32]{1,0:T(4,128)}, u32[]{:S(2)}) copy-start(s32[4,32]{1,0:T(4,128)} %slot_ref.1) | copy-start | bytes 1540
  8.9 5.5 %collective-permute-start.4 = (bf16[80,512]{1,0:T(8,128)(2,1)S(1)}, bf16[80,512]{1,0:T(8,128)(2,1)S(1)}, u32[]{:S(2)}, u32[]{:S(2)}) collective-permute-start(bf16[80,512]{1,0:T(8,128)(2,1)S(1)} %project.1.refs_0_), channel_id=1, source_target_pairs={{0,3},{1,2},{2,1},{3,0},{4,7},{5,6},{6,5},{7,4},{8,11},{9,10},{10,... | collective-permute-start | bytes 245768 | tf_op jit(solution)/shard_map/ppermute | solution.py:64
  11.4 4.5 %collective-permute-start.3 = (bf16[80,512]{1,0:T(8,128)(2,1)S(1)}, bf16[80,512]{1,0:T(8,128)(2,1)S(1)}, u32[]{:S(2)}, u32[]{:S(2)}) collective-permute-start(bf16[80,512]{1,0:T(8,128)(2,1)S(1)} %project.1.refs_0_), channel_id=1, source_target_pairs={{0,2},{1,3},{2,0},{3,1},{4,6},{5,7},{6,4},{7,5},{8,10},{9,11},{10,... | collective-permute-start | bytes 245768 | tf_op jit(solution)/shard_map/ppermute | solution.py:64
  11.9 4.4 %collective-permute-start.2 = (bf16[80,512]{1,0:T(8,128)(2,1)S(1)}, bf16[80,512]{1,0:T(8,128)(2,1)S(1)}, u32[]{:S(2)}, u32[]{:S(2)}) collective-permute-start(bf16[80,512]{1,0:T(8,128)(2,1)S(1)} %project.1.refs_0_), channel_id=1, source_target_pairs={{0,1},{1,0},{2,3},{3,2},{4,5},{5,4},{6,7},{7,6},{8,9},{9,8},{10,11... | collective-permute-start | bytes 245768 | tf_op jit(solution)/shard_map/ppermute | solution.py:64
  12.5 12.8 %collective-permute-start.1 = (bf16[16,6144]{1,0:T(8,128)(2,1)S(1)}, bf16[16,6144]{1,0:T(8,128)(2,1)S(1)}, u32[]{:S(2)}, u32[]{:S(2)}) collective-permute-start(bf16[16,6144]{1,0:T(8,128)(2,1)S(1)} %slice.7), channel_id=1, source_target_pairs={{0,8},{4,12},{8,16},{12,20},{16,24},{20,28},{24,0},{28,4},{1,9},{5... | collective-permute-start | bytes 589832 | tf_op jit(solution)/shard_map/ppermute | solution.py:43
  17.9 13.8 %copy-start.1 = (bf16[64,256]{1,0:T(8,128)(2,1)S(1)}, bf16[64,256]{1,0:T(8,128)(2,1)}, u32[]{:S(2)}) copy-start(bf16[64,256]{1,0:T(8,128)(2,1)} %rot_ref.5) | copy-start | bytes 98308
  17.9 7.4 %collective-permute-start.6 = (bf16[64,512]{1,0:T(8,128)(2,1)S(1)}, bf16[64,512]{1,0:T(8,128)(2,1)S(1)}, u32[]{:S(2)}, u32[]{:S(2)}) collective-permute-start(bf16[64,512]{1,0:T(8,128)(2,1)S(1)} %couple.1.after_ref.mine), channel_id=1, source_target_pairs={{0,8},{4,12},{8,16},{12,20},{16,24},{20,28},{24,0},{28,4},{1,9},{5... | collective-permute-start | bytes 196616 | tf_op jit(solution)/shard_map/ppermute | solution.py:43
  20.6 11.2 %collective-permute-start.5 = (bf16[48,6144]{1,0:T(8,128)(2,1)S(1)}, bf16[48,6144]{1,0:T(8,128)(2,1)S(1)}, u32[]{:S(2)}, u32[]{:S(2)}) collective-permute-start(bf16[48,6144]{1,0:T(8,128)(2,1)S(1)} %hold.1), channel_id=1, source_target_pairs={{0,4},{4,8},{8,12},{12,16},{16,20},{20,24},{24,28},{28,0},{1,5},{5... | collective-permute-start | bytes 1769480 | tf_op jit(solution)/shard_map/ppermute | solution.py:43
  25.4 7.0 %collective-permute-start.7 = (bf16[80,6144]{1,0:T(8,128)(2,1)S(1)}, bf16[80,6144]{1,0:T(8,128)(2,1)S(1)}, u32[]{:S(2)}, u32[]{:S(2)}) collective-permute-start(bf16[80,6144]{1,0:T(8,128)(2,1)S(1)} %get-tuple-element.7), channel_id=1, source_target_pairs={{0,4},{4,0},{8,12},{12,8},{16,20},{20,16},{24,28},{28,24},{1,5},{5... | collective-permute-start | bytes 2949128 | tf_op jit(solution)/shard_map/ppermute | solution.py:48
  25.5 7.0 %collective-permute-start.9 = (bf16[64,512]{1,0:T(8,128)(2,1)S(1)}, bf16[64,512]{1,0:T(8,128)(2,1)S(1)}, u32[]{:S(2)}, u32[]{:S(2)}) collective-permute-start(bf16[64,512]{1,0:T(8,128)(2,1)S(1)} %collective-permute-done.6.mine_two.two), channel_id=1, source_target_pairs={{0,4},{4,8},{8,12},{12,16},{16,20},{20,24},{24,28},{28,0},{1,5},{5... | collective-permute-start | bytes 196616 | tf_op jit(solution)/shard_map/ppermute | solution.py:43
  26.0 8.6 %collective-permute-start.8 = (bf16[16,6144]{1,0:T(8,128)(2,1)S(1)}, bf16[16,6144]{1,0:T(8,128)(2,1)S(1)}, u32[]{:S(2)}, u32[]{:S(2)}) collective-permute-start(bf16[16,6144]{1,0:T(8,128)(2,1)S(1)} %get-tuple-element.8), channel_id=1, source_target_pairs={{0,4},{4,8},{8,12},{12,16},{16,20},{20,24},{24,28},{28,0},{1,5},{5... | collective-permute-start | bytes 589832 | tf_op jit(solution)/shard_map/ppermute | solution.py:43

commit v5 on v4

--- a/solution.py
+++ b/solution.py
@@ -7,7 +7,8 @@
 from jax.experimental.pallas import tpu as pltpu
 from jax.sharding import PartitionSpec as P
 
-TURN = 3 * 10**9
+TURN = 0 * 10**9
+CUT = 30 * 10**8
 COUPLE = 2 * 10**9
 APPLY = 50 * 10**8
 GATHER = 45 * 10**8
@@ -168,12 +169,27 @@
     )[0]
 
 
-def hold_kernel(block_ref, after_ref, out_ref):
-    out_ref[...] = block_ref[...]
-
-
-def hold(block, after):
-    return call(hold_kernel, "hold", [(block.shape, block.dtype)], [block, after])[0]
+def halves_kernel(block_ref, *refs):
+    upper_ref, lower_ref = refs[-2:]
+    half = upper_ref.shape[0]
+    upper_ref[...] = block_ref[:half, :]
+    lower_ref[...] = block_ref[half:, :]
+
+
+def halves(block, after, cost=0):
+    half = ((block.shape[0] // 2, block.shape[1]), block.dtype)
+    return call(halves_kernel, "halves", [half, half], [block, *after], cost=cost)
+
+
+def hold_kernel(upper_ref, lower_ref, after_ref, out_ref):
+    rows = upper_ref.shape[0]
+    out_ref[:rows, :] = upper_ref[...]
+    out_ref[rows:, :] = lower_ref[: out_ref.shape[0] - rows, :]
+
+
+def hold(upper, lower, rows, after):
+    shape = (rows, upper.shape[1])
+    return call(hold_kernel, "hold", [(shape, upper.dtype)], [upper, lower, after])[0]
 
 
 def packed(coef_shape, rows):
@@ -184,51 +200,64 @@
     ]
 
 
-def choose_kernel(mine, mine_two, own, two_a, two_b, swap_ref, held_ref):
-    width, cut = own.shape[0], two_a.shape[0]
+def choose_kernel(mine, mine_two, two, lower, swap_ref, held_ref):
+    width = two.shape[0]
     parts = packed(mine.shape, swap_ref.shape[0] - width)
+    swap_ref[:width, :] = two[...]
 
     @pl.when(on_even())
     def _():
-        swap_ref[:width, :] = own[...]
         for columns, rows in parts:
             swap_ref[width:, columns] = mine[rows, :]
 
     @pl.when(jnp.logical_not(on_even()))
     def _():
-        swap_ref[:cut, :] = two_a[...]
-        swap_ref[cut:width, :] = two_b[...]
         for columns, rows in parts:
             swap_ref[width:, columns] = mine_two[rows, :]
 
-    held_ref[...] = two_b[...]
-
-
-def choose(mine, mine_two, own, two_a, two_b):
-    args = [mine, mine_two, own, two_a, two_b]
-    width, points = own.shape
-    outs = [((width + width // 4, points), own.dtype), (two_b.shape, own.dtype)]
-    return call(choose_kernel, "choose", outs, args)
-
-
-def gather_kernel(rot_ref, own, two_a, two_b, three_a, out_ref, stack):
+    held_ref[...] = lower[lower.shape[0] - held_ref.shape[0] :, :]
+
+
+def choose(mine, mine_two, two, lower):
+    width, points = two.shape
+    part = width // 4
+    outs = [((width + part, points), two.dtype), ((part, points), two.dtype)]
+    return call(choose_kernel, "choose", outs, [mine, mine_two, two, lower])
+
+
+def where_even(tile, even):
+    here = on_even() if even else jnp.logical_not(on_even())
+    return jnp.where(here, tile.astype(F32), 0.0).astype(BF16)
+
+
+def gather_kernel(rot_ref, own, one, two, upper, lower, three_a, out_ref, stack):
     width, points = own.shape
     depth = stack.shape[0]
-    turn = jnp.concatenate([rot_ref[:, :width], rot_ref[:, 2 * width : width + depth]], axis=1)
+    turn = jnp.concatenate(
+        [rot_ref[:, : 3 * width], where_even(rot_ref[:, 3 * width : depth], True)], axis=1
+    )
+    stack[:width, :] = own[...]
+    stack[width : 2 * width, :] = one[...]
+    stack[3 * width :, :] = three_a[...]
+
+    @pl.when(on_even())
+    def _():
+        stack[2 * width : 3 * width, :] = two[...]
+
+    @pl.when(jnp.logical_not(on_even()))
+    def _():
+        stack[2 * width : 2 * width + upper.shape[0], :] = upper[...]
+        stack[2 * width + upper.shape[0] : 3 * width, :] = lower[...]
+
     tile = tile_of(points, 1024)
-    for i in range(points // tile):
-        here = slice(i * tile, (i + 1) * tile)
-        at = 0
-        for ref in (own, two_a, two_b, three_a):
-            stack[at : at + ref.shape[0], here] = ref[:, here]
-            at += ref.shape[0]
+    for at in range(0, points, tile):
+        here = slice(at, at + tile)
         out_ref[:, here] = jnp.dot(turn, stack[:, here], preferred_element_type=F32)
 
 
 def gather(rotation, *blocks):
-    width, points = blocks[0].shape
-    depth = sum(block.shape[0] for block in blocks)
-    scratch = [pltpu.VMEM((depth, points), BF16)]
+    (width, points), rows = blocks[0].shape, blocks[-1].shape[0]
+    scratch = [pltpu.VMEM((3 * width + rows, points), BF16)]
     return call(
         gather_kernel, "gather", [((width, points), F32)], [rotation, *blocks], scratch, cost=GATHER
     )[0]
@@ -259,7 +288,11 @@
     pieces = sems.shape[0]
     tile = points // pieces
     turn = jnp.concatenate(
-        [rot_ref[:, width : 2 * width], rot_ref[:, rot_ref.shape[1] - rows :]], axis=1
+        [
+            where_even(rot_ref[:, 3 * width : 4 * width], False),
+            where_even(rot_ref[:, 4 * width - rows : 4 * width], True),
+        ],
+        axis=1,
     )
     copies = []
     for i in range(pieces):
@@ -296,18 +329,19 @@
     owned = coupling.shape[0]
     proj = projectors.reshape(slot_count * rank, points)
 
-    cut = width * 3 // 4
-    two_a = along_bands(orbitals[:cut], 2)
-    two_b = along_bands(orbitals[cut:], 2)
+    one = along_bands(orbitals, 1)
+    upper, lower = [swapped(block) for block in halves(orbitals, [], CUT)]
+    two = along_bands(hold(upper, lower, width, upper), 1)
     loads = from_all_domains(project(orbitals, proj, coupling.reshape(owned * rank, rank)))
+    upper, lower = [swapped(block) for block in halves(one, loads[1:])]
     mine = couple(slot_atom, loads, width, owned)
     mine_two = along_bands(mine, 2)
-    three_a = along_bands(hold(two_a, mine), 1)
-    swap, held = choose(mine, mine_two, orbitals, two_a, two_b)
+    three_a = along_bands(hold(upper, lower, width * 3 // 4, mine), 1)
+    swap, held = choose(mine, mine_two, two, lower)
     mine_three = along_bands(mine_two, 1)
+    three_b = along_bands(held, 1)
     swap = swapped(swap)
-    three_b = along_bands(held, 1)
-    partial = gather(rotation, orbitals, two_a, two_b, three_a)
+    partial = gather(rotation, orbitals, one, two, upper, lower, three_a)
     applied = call(
         apply_kernel,
         "apply",

time: 35.9 us -> 36.2 us (level)
  waiting for transfers between devices: 14.3 us -> 17.4 us
  local copies, waits for them, and re-layouts: 3.88 us -> 1.17 us
  starting transfers between devices: 10.6 us -> 10.1 us
  Pallas kernels: 6.79 us -> 7.21 us
    ppermute x6, starting transfers between devices: 7.01 us -> 3.07 us  [along_bands(): lax.ppermute(block, 'band', [(i, (i + distance) % count) for i in range(c...]
    ppermute x1 -> x5, starting transfers between devices: 0.07 us -> 3.51 us  [swapped(): return lax.ppermute(block, 'band', [(i, i ^ 1) for i in range(count)])]
    ppermute x3, waiting for transfers between devices: 2.26 us -> 4.57 us  [from_all_domains(): return [block] + [lax.ppermute(block, 'dom', route) for route in routes]]
    ppermute x1 -> x5, waiting for transfers between devices: 0.01 us -> 1.84 us  [swapped(): return lax.ppermute(block, 'band', [(i, i ^ 1) for i in range(count)])]
    unnamed x12, local copies, waits for them, and re-layouts: 2.61 us -> 1.17 us
    slice x2 -> x0, local copies, waits for them, and re-layouts: 1.27 us -> none  [the longest x1 1.25 us: on_device(): two_a = along_bands(orbitals[:cut], 2)]
    ppermute x6, waiting for transfers between devices: 12.1 us -> 11 us  [along_bands(): lax.ppermute(block, 'band', [(i, (i + distance) % count) for i in range(c...]
    pallas_call x7 -> x10, Pallas kernels: 5.61 us -> 6.02 us  [call(): pl.pallas_call(kernel, in_specs=[first] + [VMEM] * (len(args) - 1), out_s...]
  transfers between devices with their start and end apart: 10 -> 14, of which waited for: 8 -> 8; matrix products, arithmetic and copies ran while one was open for 0% -> 0% of each run, Pallas kernels for 16% -> 17%
where the time goes in v5:
time: 36.2 us; the launch traced here: 36 us
  waiting for transfers between devices  17.4 us (48%)
  starting transfers between devices  10.1 us (28%)
  Pallas kernels  7.21 us (20%)
  local copies, waits for them, and re-layouts  1.17 us (3%)
    ppermute x6, waiting for transfers between devices, along_bands(): lax.ppermute(block, 'band', [(i, (i + distance) % count) for i in range(c...  11 us
    pallas_call x10, Pallas kernels, call(): pl.pallas_call(kernel, in_specs=[first] + [VMEM] * (len(args) - 1), out_s...  6.02 us
    ppermute x3, waiting for transfers between devices, from_all_domains(): return [block] + [lax.ppermute(block, 'dom', route) for route in routes]  4.57 us
    ppermute x3, starting transfers between devices, from_all_domains(): return [block] + [lax.ppermute(block, 'dom', route) for route in routes]  3.55 us
    ppermute x5, starting transfers between devices, swapped(): return lax.ppermute(block, 'band', [(i, i ^ 1) for i in range(count)])  3.51 us
    ppermute x6, starting transfers between devices, along_bands(): lax.ppermute(block, 'band', [(i, (i + distance) % count) for i in range(c...  3.07 us
    ppermute x5, waiting for transfers between devices, swapped(): return lax.ppermute(block, 'band', [(i, i ^ 1) for i in range(count)])  1.84 us
    pallas_call x1, Pallas kernels, finish(): pl.pallas_call(finish_kernel, in_specs=[VMEM] * len(args), out_specs=pl.B...  1.19 us
  transfers between devices with their start and end apart: 14, of which 8 were waited for; matrix products, arithmetic and copies ran while one was open for 0% of the time, Pallas kernels for 17%

profile of v5, /device:TPU:0, one launch (start us, length us, event | category | flops | bytes accessed | tf_op | source)
XLA Modules:
  0.0 36.0 jit_solution(12733816124958345173)
XLA Ops:
  0.0 0.5 %collective-permute-start = (bf16[64,6144]{1,0:T(8,128)(2,1)}, bf16[64,6144]{1,0:T(8,128)(2,1)S(1)}, u32[]{:S(2)}, u32[]{:S(2)}) collective-permute-start(bf16[64,6144]{1,0:T(8,128)(2,1)} %own.1), channel_id=1, source_target_pairs={{0,4},{4,8},{8,12},{12,16},{16,20},{20,24},{24,28},{28,0},{1,5},{5... | collective-permute-start | bytes 2359304 | tf_op jit(solution)/shard_map/ppermute | solution.py:44
  0.5 0.0 copy-start.1
  0.5 1.1 %copy-done.1 = bf16[64,6144]{1,0:T(8,128)(2,1)S(1)} copy-done((bf16[64,6144]{1,0:T(8,128)(2,1)S(1)}, bf16[64,6144]{1,0:T(8,128)(2,1)}, u32[]{:S(2)}) %copy-start.1) | copy-done | bytes 786456
  1.6 0.0 copy-start
  1.6 0.1 halves.2
  1.6 0.0 copy-start.3
  1.7 0.0 copy-start.2
  1.7 2.8 %collective-permute-start.1 = (bf16[32,6144]{1,0:T(8,128)(2,1)S(1)}, bf16[32,6144]{1,0:T(8,128)(2,1)S(1)}, u32[]{:S(2)}, u32[]{:S(2)}) collective-permute-start(bf16[32,6144]{1,0:T(8,128)(2,1)S(1)} %get-tuple-element.11), channel_id=1, source_target_pairs={{0,4},{4,0},{8,12},{12,8},{16,20},{20,16},{24,28},{28,24},{1,5},{5... | collective-permute-start | bytes 1179656 | tf_op jit(solution)/shard_map/ppermute | solution.py:49
  4.5 0.1 collective-permute-start.2
  4.5 1.3 %collective-permute-done.1.upper_ref.after_ref = bf16[32,6144]{1,0:T(8,128)(2,1)S(1)} collective-permute-done((bf16[32,6144]{1,0:T(8,128)(2,1)S(1)}, bf16[32,6144]{1,0:T(8,128)(2,1)S(1)}, u32[]{:S(2)}, u32[]{:S(2)}) %collective-permute-start.1) | collective-permute-done | bytes 393248 | tf_op jit(solution)/shard_map/ppermute | solution.py:49
  5.8 0.6 %collective-permute-done.2.lower_ref = bf16[32,6144]{1,0:T(8,128)(2,1)S(1)} collective-permute-done((bf16[32,6144]{1,0:T(8,128)(2,1)S(1)}, bf16[32,6144]{1,0:T(8,128)(2,1)S(1)}, u32[]{:S(2)}, u32[]{:S(2)}) %collective-permute-start.2) | collective-permute-done | bytes 393248 | tf_op jit(solution)/shard_map/ppermute | solution.py:49
  6.4 0.1 hold.2
  6.4 0.4 %collective-permute-start.3 = (bf16[64,6144]{1,0:T(8,128)(2,1)S(1)}, bf16[64,6144]{1,0:T(8,128)(2,1)S(1)}, u32[]{:S(2)}, u32[]{:S(2)}) collective-permute-start(bf16[64,6144]{1,0:T(8,128)(2,1)S(1)} %hold.2), channel_id=1, source_target_pairs={{0,4},{4,8},{8,12},{12,16},{16,20},{20,24},{24,28},{28,0},{1,5},{5... | collective-permute-start | bytes 2359304 | tf_op jit(solution)/shard_map/ppermute | solution.py:44
  6.8 0.0 copy-done.3
  6.9 0.1 turn.1.turned_ref
  7.0 0.0 copy-done
  7.0 0.0 copy-done.2
  7.0 0.0 copy-start.5
  7.0 1.8 %project.1.refs_0_ = bf16[80,512]{1,0:T(8,128)(2,1)S(1)} custom-call(bf16[64,6144]{1,0:T(8,128)(2,1)S(1)} %copy-done.2, bf16[512,6144]{1,0:T(8,128)(2,1)S(1)} %bitcast.2, bf16[16,512]{1,0:T(8,128)(2,1)S(1)} %turn.1.turned_ref), custom_call_target="tpu_custom_call" | custom-call | tf_op jit(solution)/shard_map/project/pallas_call | solution.py:30
  8.9 2.5 %collective-permute-start.6 = (bf16[80,512]{1,0:T(8,128)(2,1)S(1)}, bf16[80,512]{1,0:T(8,128)(2,1)S(1)}, u32[]{:S(2)}, u32[]{:S(2)}) collective-permute-start(bf16[80,512]{1,0:T(8,128)(2,1)S(1)} %project.1.refs_0_), channel_id=1, source_target_pairs={{0,3},{1,2},{2,1},{3,0},{4,7},{5,6},{6,5},{7,4},{8,11},{9,10},{10,... | collective-permute-start | bytes 245768 | tf_op jit(solution)/shard_map/ppermute | solution.py:65
  11.4 0.5 %collective-permute-start.5 = (bf16[80,512]{1,0:T(8,128)(2,1)S(1)}, bf16[80,512]{1,0:T(8,128)(2,1)S(1)}, u32[]{:S(2)}, u32[]{:S(2)}) collective-permute-start(bf16[80,512]{1,0:T(8,128)(2,1)S(1)} %project.1.refs_0_), channel_id=1, source_target_pairs={{0,2},{1,3},{2,0},{3,1},{4,6},{5,7},{6,4},{7,5},{8,10},{9,11},{10,... | collective-permute-start | bytes 245768 | tf_op jit(solution)/shard_map/ppermute | solution.py:65
  11.9 0.5 %collective-permute-start.4 = (bf16[80,512]{1,0:T(8,128)(2,1)S(1)}, bf16[80,512]{1,0:T(8,128)(2,1)S(1)}, u32[]{:S(2)}, u32[]{:S(2)}) collective-permute-start(bf16[80,512]{1,0:T(8,128)(2,1)S(1)} %project.1.refs_0_), channel_id=1, source_target_pairs={{0,1},{1,0},{2,3},{3,2},{4,5},{5,4},{6,7},{7,6},{8,9},{9,8},{10,11... | collective-permute-start | bytes 245768 | tf_op jit(solution)/shard_map/ppermute | solution.py:65
  12.4 2.4 %collective-permute-done.6.refs_2_.refs_3_ = bf16[80,512]{1,0:T(8,128)(2,1)S(1)} collective-permute-done((bf16[80,512]{1,0:T(8,128)(2,1)S(1)}, bf16[80,512]{1,0:T(8,128)(2,1)S(1)}, u32[]{:S(2)}, u32[]{:S(2)}) %collective-permute-start.6) | collective-permute-done | bytes 81952 | tf_op jit(solution)/shard_map/ppermute | solution.py:65
  14.8 2.1 %collective-permute-done.5.refs_1_.refs_2_ = bf16[80,512]{1,0:T(8,128)(2,1)S(1)} collective-permute-done((bf16[80,512]{1,0:T(8,128)(2,1)S(1)}, bf16[80,512]{1,0:T(8,128)(2,1)S(1)}, u32[]{:S(2)}, u32[]{:S(2)}) %collective-permute-start.5) | collective-permute-done | bytes 81952 | tf_op jit(solution)/shard_map/ppermute | solution.py:65
  16.9 0.1 collective-permute-done.4.refs_0_.refs_1_
  17.0 0.0 collective-permute-done.block_ref.one
  17.0 0.1 halves.3
  17.0 0.1 collective-permute-start.7
  17.1 0.5 %collective-permute-start.8 = (bf16[32,6144]{1,0:T(8,128)(2,1)S(1)}, bf16[32,6144]{1,0:T(8,128)(2,1)S(1)}, u32[]{:S(2)}, u32[]{:S(2)}) collective-permute-start(bf16[32,6144]{1,0:T(8,128)(2,1)S(1)} %get-tuple-element.14), channel_id=1, source_target_pairs={{0,4},{4,0},{8,12},{12,8},{16,20},{20,16},{24,28},{28,24},{1,5},{5... | collective-permute-start | bytes 1179656 | tf_op jit(solution)/shard_map/ppermute | solution.py:49
  17.6 0.0 copy-done.5
  17.6 1.5 %couple.1.after_ref.mine = bf16[64,512]{1,0:T(8,128)(2,1)S(1)} custom-call(s32[4,32]{1,0:T(4,128)S(1)} %copy-done.5, bf16[80,512]{1,0:T(8,128)(2,1)S(1)} %project.1.refs_0_, bf16[80,512]{1,0:T(8,128)(2,1)S(1)} %collective-permute-done.4.refs_0_.refs_1_, bf16[80,512]{1,0:T(8,128)(2,1)S(1)} %collective-permute-done.5.refs_1_.refs_2_, ...), custom_call_target="tpu_custom_call" | custom-call | flops 2000000000 | tf_op jit(solution)/shard_map/couple/pallas_call | solution.py:30
  19.2 0.0 copy-start.4
  19.2 1.6 %collective-permute-start.10 = (bf16[64,512]{1,0:T(8,128)(2,1)S(1)}, bf16[64,512]{1,0:T(8,128)(2,1)S(1)}, u32[]{:S(2)}, u32[]{:S(2)}) collective-permute-start(bf16[64,512]{1,0:T(8,128)(2,1)S(1)} %couple.1.after_ref.mine), channel_id=1, source_target_pairs={{0,8},{4,12},{8,16},{12,20},{16,24},{20,28},{24,0},{28,4},{1,9},{5... | collective-permute-start | bytes 196616 | tf_op jit(solution)/shard_map/ppermute | solution.py:44
  20.8 0.0 collective-permute-done.7.upper_ref.upper
  20.8 0.0 collective-permute-done.8.lower_ref.lower
  20.9 0.1 collective-permute-start.9
  20.9 4.4 %collective-permute-done.10.mine_two.two = bf16[64,512]{1,0:T(8,128)(2,1)S(1)} collective-permute-done((bf16[64,512]{1,0:T(8,128)(2,1)S(1)}, bf16[64,512]{1,0:T(8,128)(2,1)S(1)}, u32[]{:S(2)}, u32[]{:S(2)}) %collective-permute-start.10) | collective-permute-done | bytes 65568 | tf_op jit(solution)/shard_map/ppermute | solution.py:44
  25.3 0.0 collective-permute-done.3.two
  25.3 0.1 choose.1
  25.4 0.1 collective-permute-start.11
  25.5 0.5 %collective-permute-start.13 = (bf16[64,512]{1,0:T(8,128)(2,1)S(1)}, bf16[64,512]{1,0:T(8,128)(2,1)S(1)}, u32[]{:S(2)}, u32[]{:S(2)}) collective-permute-start(bf16[64,512]{1,0:T(8,128)(2,1)S(1)} %collective-permute-done.10.mine_two.two), channel_id=1, source_target_pairs={{0,4},{4,8},{8,12},{12,16},{16,20},{20,24},{24,28},{28,0},{1,5},{5... | collective-permute-start | bytes 196616 | tf_op jit(solution)/shard_map/ppermute | solution.py:44
  25.9 0.0 collective-permute-start.12
  26.0 6.1 %collective-permute-done.9.three_a = bf16[48,6144]{1,0:T(8,128)(2,1)S(1)} collective-permute-done((bf16[48,6144]{1,0:T(8,128)(2,1)S(1)}, bf16[48,6144]{1,0:T(8,128)(2,1)S(1)}, u32[]{:S(2)}, u32[]{:S(2)}) %collective-permute-start.9) | collective-permute-done | bytes 589856 | tf_op jit(solution)/shard_map/ppermute | solution.py:44
  32.0 0.0 copy-done.4
  32.0 0.8 %gather.1.after_ref.partial_ref = f32[64,6144]{1,0:T(8,128)S(1)} custom-call(bf16[64,256]{1,0:T(8,128)(2,1)S(1)} %copy-done.4, bf16[64,6144]{1,0:T(8,128)(2,1)S(1)} %copy-done.2, bf16[64,6144]{1,0:T(8,128)(2,1)S(1)} %collective-permute-done.block_ref.one, bf16[64,6144]{1,0:T(8,128)(2,1)S(1)} %collective-permute-done.3.two, ...), custom_call_target="tpu_custom_call" | custom-call | flops 4499999744 | tf_op jit(solution)/shard_map/gather/pallas_call | solution.py:30
  32.8 0.0 collective-permute-done.13.three
  32.9 0.0 collective-permute-done.11.swap_ref
  32.9 1.4 %apply.1.applied = f32[64,6144]{1,0:T(8,128)S(1)} custom-call(bf16[64,256]{1,0:T(8,128)(2,1)S(1)} %copy-done.4, bf16[64,512]{1,0:T(8,128)(2,1)S(1)} %couple.1.after_ref.mine, bf16[80,6144]{1,0:T(8,128)(2,1)S(1)} %collective-permute-done.11.swap_ref, bf16[64,512]{1,0:T(8,128)(2,1)S(1)} %collective-permute-done.10.mine_two.two, ...), custom_call_target="tpu_custom_call" | custom-call | flops 5000000000 | tf_op jit(solution)/shard_map/apply/pallas_call | solution.py:30
  34.3 0.5 %collective-permute-done.12.last_ref = bf16[16,6144]{1,0:T(8,128)(2,1)S(1)} collective-permute-done((bf16[16,6144]{1,0:T(8,128)(2,1)S(1)}, bf16[16,6144]{1,0:T(8,128)(2,1)S(1)}, u32[]{:S(2)}, u32[]{:S(2)}) %collective-permute-start.12) | collective-permute-done | bytes 196640 | tf_op jit(solution)/shard_map/ppermute | solution.py:44
  34.8 1.2 %finish.1 = bf16[64,6144]{1,0:T(8,128)(2,1)} custom-call(bf16[64,256]{1,0:T(8,128)(2,1)S(1)} %copy-done.4, f32[64,6144]{1,0:T(8,128)S(1)} %gather.1.after_ref.partial_ref, bf16[80,6144]{1,0:T(8,128)(2,1)S(1)} %collective-permute-done.11.swap_ref, bf16[16,6144]{1,0:T(8,128)(2,1)S(1)} %collective-permute-done.12.last_ref, f32[64,6144]{1,0:T(8,128)S(1)} %apply.1.applied), custom_call_target="tpu_custom_call" | custom-call | tf_op jit(solution)/shard_map/finish/pallas_call | solution.py:314
  (1 shorter events, 0.0 us)
Async XLA Ops:
  0.0 17.0 %collective-permute-start = (bf16[64,6144]{1,0:T(8,128)(2,1)}, bf16[64,6144]{1,0:T(8,128)(2,1)S(1)}, u32[]{:S(2)}, u32[]{:S(2)}) collective-permute-start(bf16[64,6144]{1,0:T(8,128)(2,1)} %own.1), channel_id=1, source_target_pairs={{0,4},{4,8},{8,12},{12,16},{16,20},{20,24},{24,28},{28,0},{1,5},{5... | collective-permute-start | bytes 2359304 | tf_op jit(solution)/shard_map/ppermute | solution.py:44
  0.5 1.1 %copy-start.1 = (bf16[64,6144]{1,0:T(8,128)(2,1)S(1)}, bf16[64,6144]{1,0:T(8,128)(2,1)}, u32[]{:S(2)}) copy-start(bf16[64,6144]{1,0:T(8,128)(2,1)} %own.1) | copy-start | bytes 2359300
  1.6 5.4 %copy-start = (bf16[32,16,6144]{2,1,0:T(8,128)(2,1)S(1)}, bf16[32,16,6144]{2,1,0:T(8,128)(2,1)}, u32[]{:S(2)}) copy-start(bf16[32,16,6144]{2,1,0:T(8,128)(2,1)} %param.7) | copy-start | bytes 18874372
  1.6 5.2 %copy-start.3 = (f32[16,16,16]{2,1,0:T(8,128)S(1)}, f32[16,16,16]{2,1,0:T(8,128)}, u32[]{:S(2)}) copy-start(f32[16,16,16]{2,1,0:T(8,128)} %param.8) | copy-start | bytes 49156
  1.7 5.3 %copy-start.2 = (bf16[64,6144]{1,0:T(8,128)(2,1)S(1)}, bf16[64,6144]{1,0:T(8,128)(2,1)}, u32[]{:S(2)}) copy-start(bf16[64,6144]{1,0:T(8,128)(2,1)} %own.1) | copy-start | bytes 2359300
  1.7 4.1 %collective-permute-start.1 = (bf16[32,6144]{1,0:T(8,128)(2,1)S(1)}, bf16[32,6144]{1,0:T(8,128)(2,1)S(1)}, u32[]{:S(2)}, u32[]{:S(2)}) collective-permute-start(bf16[32,6144]{1,0:T(8,128)(2,1)S(1)} %get-tuple-element.11), channel_id=1, source_target_pairs={{0,4},{4,0},{8,12},{12,8},{16,20},{20,16},{24,28},{28,24},{1,5},{5... | collective-permute-start | bytes 1179656 | tf_op jit(solution)/shard_map/ppermute | solution.py:49
  4.5 1.9 %collective-permute-start.2 = (bf16[32,6144]{1,0:T(8,128)(2,1)S(1)}, bf16[32,6144]{1,0:T(8,128)(2,1)S(1)}, u32[]{:S(2)}, u32[]{:S(2)}) collective-permute-start(bf16[32,6144]{1,0:T(8,128)(2,1)S(1)} %get-tuple-element.12), channel_id=1, source_target_pairs={{0,4},{4,0},{8,12},{12,8},{16,20},{20,16},{24,28},{28,24},{1,5},{5... | collective-permute-start | bytes 1179656 | tf_op jit(solution)/shard_map/ppermute | solution.py:49
  6.4 18.9 %collective-permute-start.3 = (bf16[64,6144]{1,0:T(8,128)(2,1)S(1)}, bf16[64,6144]{1,0:T(8,128)(2,1)S(1)}, u32[]{:S(2)}, u32[]{:S(2)}) collective-permute-start(bf16[64,6144]{1,0:T(8,128)(2,1)S(1)} %hold.2), channel_id=1, source_target_pairs={{0,4},{4,8},{8,12},{12,16},{16,20},{20,24},{24,28},{28,0},{1,5},{5... | collective-permute-start | bytes 2359304 | tf_op jit(solution)/shard_map/ppermute | solution.py:44
  7.0 10.6 %copy-start.5 = (s32[4,32]{1,0:T(4,128)S(1)}, s32[4,32]{1,0:T(4,128)}, u32[]{:S(2)}) copy-start(s32[4,32]{1,0:T(4,128)} %slot_ref.1) | copy-start | bytes 1540
  8.9 5.9 %collective-permute-start.6 = (bf16[80,512]{1,0:T(8,128)(2,1)S(1)}, bf16[80,512]{1,0:T(8,128)(2,1)S(1)}, u32[]{:S(2)}, u32[]{:S(2)}) collective-permute-start(bf16[80,512]{1,0:T(8,128)(2,1)S(1)} %project.1.refs_0_), channel_id=1, source_target_pairs={{0,3},{1,2},{2,1},{3,0},{4,7},{5,6},{6,5},{7,4},{8,11},{9,10},{10,... | collective-permute-start | bytes 245768 | tf_op jit(solution)/shard_map/ppermute | solution.py:65
  11.4 5.5 %collective-permute-start.5 = (bf16[80,512]{1,0:T(8,128)(2,1)S(1)}, bf16[80,512]{1,0:T(8,128)(2,1)S(1)}, u32[]{:S(2)}, u32[]{:S(2)}) collective-permute-start(bf16[80,512]{1,0:T(8,128)(2,1)S(1)} %project.1.refs_0_), channel_id=1, source_target_pairs={{0,2},{1,3},{2,0},{3,1},{4,6},{5,7},{6,4},{7,5},{8,10},{9,11},{10,... | collective-permute-start | bytes 245768 | tf_op jit(solution)/shard_map/ppermute | solution.py:65
  11.9 5.1 %collective-permute-start.4 = (bf16[80,512]{1,0:T(8,128)(2,1)S(1)}, bf16[80,512]{1,0:T(8,128)(2,1)S(1)}, u32[]{:S(2)}, u32[]{:S(2)}) collective-permute-start(bf16[80,512]{1,0:T(8,128)(2,1)S(1)} %project.1.refs_0_), channel_id=1, source_target_pairs={{0,1},{1,0},{2,3},{3,2},{4,5},{5,4},{6,7},{7,6},{8,9},{9,8},{10,11... | collective-permute-start | bytes 245768 | tf_op jit(solution)/shard_map/ppermute | solution.py:65
  17.0 3.8 %collective-permute-start.7 = (bf16[32,6144]{1,0:T(8,128)(2,1)S(1)}, bf16[32,6144]{1,0:T(8,128)(2,1)S(1)}, u32[]{:S(2)}, u32[]{:S(2)}) collective-permute-start(bf16[32,6144]{1,0:T(8,128)(2,1)S(1)} %get-tuple-element.13), channel_id=1, source_target_pairs={{0,4},{4,0},{8,12},{12,8},{16,20},{20,16},{24,28},{28,24},{1,5},{5... | collective-permute-start | bytes 1179656 | tf_op jit(solution)/shard_map/ppermute | solution.py:49
  17.1 3.7 %collective-permute-start.8 = (bf16[32,6144]{1,0:T(8,128)(2,1)S(1)}, bf16[32,6144]{1,0:T(8,128)(2,1)S(1)}, u32[]{:S(2)}, u32[]{:S(2)}) collective-permute-start(bf16[32,6144]{1,0:T(8,128)(2,1)S(1)} %get-tuple-element.14), channel_id=1, source_target_pairs={{0,4},{4,0},{8,12},{12,8},{16,20},{20,16},{24,28},{28,24},{1,5},{5... | collective-permute-start | bytes 1179656 | tf_op jit(solution)/shard_map/ppermute | solution.py:49
  19.2 12.9 %copy-start.4 = (bf16[64,256]{1,0:T(8,128)(2,1)S(1)}, bf16[64,256]{1,0:T(8,128)(2,1)}, u32[]{:S(2)}) copy-start(bf16[64,256]{1,0:T(8,128)(2,1)} %rot_ref.5) | copy-start | bytes 98308
  19.2 6.1 %collective-permute-start.10 = (bf16[64,512]{1,0:T(8,128)(2,1)S(1)}, bf16[64,512]{1,0:T(8,128)(2,1)S(1)}, u32[]{:S(2)}, u32[]{:S(2)}) collective-permute-start(bf16[64,512]{1,0:T(8,128)(2,1)S(1)} %couple.1.after_ref.mine), channel_id=1, source_target_pairs={{0,8},{4,12},{8,16},{12,20},{16,24},{20,28},{24,0},{28,4},{1,9},{5... | collective-permute-start | bytes 196616 | tf_op jit(solution)/shard_map/ppermute | solution.py:44
  20.9 11.2 %collective-permute-start.9 = (bf16[48,6144]{1,0:T(8,128)(2,1)S(1)}, bf16[48,6144]{1,0:T(8,128)(2,1)S(1)}, u32[]{:S(2)}, u32[]{:S(2)}) collective-permute-start(bf16[48,6144]{1,0:T(8,128)(2,1)S(1)} %hold.3), channel_id=1, source_target_pairs={{0,4},{4,8},{8,12},{12,16},{16,20},{20,24},{24,28},{28,0},{1,5},{5... | collective-permute-start | bytes 1769480 | tf_op jit(solution)/shard_map/ppermute | solution.py:44
  25.4 7.5 %collective-permute-start.11 = (bf16[80,6144]{1,0:T(8,128)(2,1)S(1)}, bf16[80,6144]{1,0:T(8,128)(2,1)S(1)}, u32[]{:S(2)}, u32[]{:S(2)}) collective-permute-start(bf16[80,6144]{1,0:T(8,128)(2,1)S(1)} %get-tuple-element.15), channel_id=1, source_target_pairs={{0,4},{4,0},{8,12},{12,8},{16,20},{20,16},{24,28},{28,24},{1,5},{5... | collective-permute-start | bytes 2949128 | tf_op jit(solution)/shard_map/ppermute | solution.py:49
  25.5 7.4 %collective-permute-start.13 = (bf16[64,512]{1,0:T(8,128)(2,1)S(1)}, bf16[64,512]{1,0:T(8,128)(2,1)S(1)}, u32[]{:S(2)}, u32[]{:S(2)}) collective-permute-start(bf16[64,512]{1,0:T(8,128)(2,1)S(1)} %collective-permute-done.10.mine_two.two), channel_id=1, source_target_pairs={{0,4},{4,8},{8,12},{12,16},{16,20},{20,24},{24,28},{28,0},{1,5},{5... | collective-permute-start | bytes 196616 | tf_op jit(solution)/shard_map/ppermute | solution.py:44
  25.9 8.9 %collective-permute-start.12 = (bf16[16,6144]{1,0:T(8,128)(2,1)S(1)}, bf16[16,6144]{1,0:T(8,128)(2,1)S(1)}, u32[]{:S(2)}, u32[]{:S(2)}) collective-permute-start(bf16[16,6144]{1,0:T(8,128)(2,1)S(1)} %get-tuple-element.16), channel_id=1, source_target_pairs={{0,4},{4,8},{8,12},{12,16},{16,20},{20,24},{24,28},{28,0},{1,5},{5... | collective-permute-start | bytes 589832 | tf_op jit(solution)/shard_map/ppermute | solution.py:44

commit v6 on v5

--- a/solution.py
+++ b/solution.py
@@ -9,7 +9,7 @@
 
 TURN = 0 * 10**9
 CUT = 30 * 10**8
-COUPLE = 2 * 10**9
+COUPLE = 4 * 10**9
 APPLY = 50 * 10**8
 GATHER = 45 * 10**8
 
@@ -333,7 +333,7 @@
     upper, lower = [swapped(block) for block in halves(orbitals, [], CUT)]
     two = along_bands(hold(upper, lower, width, upper), 1)
     loads = from_all_domains(project(orbitals, proj, coupling.reshape(owned * rank, rank)))
-    upper, lower = [swapped(block) for block in halves(one, loads[1:])]
+    upper, lower = [swapped(block) for block in halves(one, loads[-1:])]
     mine = couple(slot_atom, loads, width, owned)
     mine_two = along_bands(mine, 2)
     three_a = along_bands(hold(upper, lower, width * 3 // 4, mine), 1)

time: 36.2 us -> 35.5 us (0.981)
  waiting for transfers between devices: 17.4 us -> 16.7 us
    ppermute x3, waiting for transfers between devices: 4.57 us -> 3.91 us  [from_all_domains(): return [block] + [lax.ppermute(block, 'dom', route) for route in routes]]
where the time goes in v6:
time: 35.5 us; the launch traced here: 35.4 us
  waiting for transfers between devices  16.7 us (47%)
  starting transfers between devices  10.2 us (29%)
  Pallas kernels  7.21 us (20%)
  local copies, waits for them, and re-layouts  1.17 us (3%)
    ppermute x6, waiting for transfers between devices, along_bands(): lax.ppermute(block, 'band', [(i, (i + distance) % count) for i in range(c...  10.9 us
    pallas_call x10, Pallas kernels, call(): pl.pallas_call(kernel, in_specs=[first] + [VMEM] * (len(args) - 1), out_s...  6.03 us
    ppermute x3, waiting for transfers between devices, from_all_domains(): return [block] + [lax.ppermute(block, 'dom', route) for route in routes]  3.91 us
    ppermute x3, starting transfers between devices, from_all_domains(): return [block] + [lax.ppermute(block, 'dom', route) for route in routes]  3.55 us
    ppermute x5, starting transfers between devices, swapped(): return lax.ppermute(block, 'band', [(i, i ^ 1) for i in range(count)])  3.54 us
    ppermute x6, starting transfers between devices, along_bands(): lax.ppermute(block, 'band', [(i, (i + distance) % count) for i in range(c...  3.07 us
    ppermute x5, waiting for transfers between devices, swapped(): return lax.ppermute(block, 'band', [(i, i ^ 1) for i in range(count)])  1.84 us
    pallas_call x1, Pallas kernels, finish(): pl.pallas_call(finish_kernel, in_specs=[VMEM] * len(args), out_specs=pl.B...  1.18 us
  transfers between devices with their start and end apart: 14, of which 8 were waited for; matrix products, arithmetic and copies ran while one was open for 0% of the time, Pallas kernels for 17%

profile of v6, /device:TPU:0, one launch (start us, length us, event | category | flops | bytes accessed | tf_op | source)
XLA Modules:
  0.0 35.4 jit_solution(8514213116985880076)
XLA Ops:
  0.0 0.5 %collective-permute-start = (bf16[64,6144]{1,0:T(8,128)(2,1)}, bf16[64,6144]{1,0:T(8,128)(2,1)S(1)}, u32[]{:S(2)}, u32[]{:S(2)}) collective-permute-start(bf16[64,6144]{1,0:T(8,128)(2,1)} %own.1), channel_id=1, source_target_pairs={{0,4},{4,8},{8,12},{12,16},{16,20},{20,24},{24,28},{28,0},{1,5},{5... | collective-permute-start | bytes 2359304 | tf_op jit(solution)/shard_map/ppermute | solution.py:44
  0.5 0.0 copy-start.1
  0.5 1.1 %copy-done.1 = bf16[64,6144]{1,0:T(8,128)(2,1)S(1)} copy-done((bf16[64,6144]{1,0:T(8,128)(2,1)S(1)}, bf16[64,6144]{1,0:T(8,128)(2,1)}, u32[]{:S(2)}) %copy-start.1) | copy-done | bytes 786456
  1.6 0.0 copy-start
  1.6 0.1 halves.2
  1.6 0.0 copy-start.3
  1.7 0.0 copy-start.2
  1.7 2.8 %collective-permute-start.1 = (bf16[32,6144]{1,0:T(8,128)(2,1)S(1)}, bf16[32,6144]{1,0:T(8,128)(2,1)S(1)}, u32[]{:S(2)}, u32[]{:S(2)}) collective-permute-start(bf16[32,6144]{1,0:T(8,128)(2,1)S(1)} %get-tuple-element.11), channel_id=1, source_target_pairs={{0,4},{4,0},{8,12},{12,8},{16,20},{20,16},{24,28},{28,24},{1,5},{5... | collective-permute-start | bytes 1179656 | tf_op jit(solution)/shard_map/ppermute | solution.py:49
  4.5 0.1 collective-permute-start.2
  4.5 1.3 %collective-permute-done.1.upper_ref.after_ref = bf16[32,6144]{1,0:T(8,128)(2,1)S(1)} collective-permute-done((bf16[32,6144]{1,0:T(8,128)(2,1)S(1)}, bf16[32,6144]{1,0:T(8,128)(2,1)S(1)}, u32[]{:S(2)}, u32[]{:S(2)}) %collective-permute-start.1) | collective-permute-done | bytes 393248 | tf_op jit(solution)/shard_map/ppermute | solution.py:49
  5.8 0.6 %collective-permute-done.2.lower_ref = bf16[32,6144]{1,0:T(8,128)(2,1)S(1)} collective-permute-done((bf16[32,6144]{1,0:T(8,128)(2,1)S(1)}, bf16[32,6144]{1,0:T(8,128)(2,1)S(1)}, u32[]{:S(2)}, u32[]{:S(2)}) %collective-permute-start.2) | collective-permute-done | bytes 393248 | tf_op jit(solution)/shard_map/ppermute | solution.py:49
  6.4 0.1 hold.2
  6.4 0.4 %collective-permute-start.3 = (bf16[64,6144]{1,0:T(8,128)(2,1)S(1)}, bf16[64,6144]{1,0:T(8,128)(2,1)S(1)}, u32[]{:S(2)}, u32[]{:S(2)}) collective-permute-start(bf16[64,6144]{1,0:T(8,128)(2,1)S(1)} %hold.2), channel_id=1, source_target_pairs={{0,4},{4,8},{8,12},{12,16},{16,20},{20,24},{24,28},{28,0},{1,5},{5... | collective-permute-start | bytes 2359304 | tf_op jit(solution)/shard_map/ppermute | solution.py:44
  6.8 0.0 copy-done.3
  6.9 0.1 turn.1.turned_ref
  7.0 0.0 copy-done
  7.0 0.0 copy-done.2
  7.0 0.0 copy-start.5
  7.0 1.8 %project.1.refs_0_ = bf16[80,512]{1,0:T(8,128)(2,1)S(1)} custom-call(bf16[64,6144]{1,0:T(8,128)(2,1)S(1)} %copy-done.2, bf16[512,6144]{1,0:T(8,128)(2,1)S(1)} %bitcast.2, bf16[16,512]{1,0:T(8,128)(2,1)S(1)} %turn.1.turned_ref), custom_call_target="tpu_custom_call" | custom-call | tf_op jit(solution)/shard_map/project/pallas_call | solution.py:30
  8.9 2.5 %collective-permute-start.4 = (bf16[80,512]{1,0:T(8,128)(2,1)S(1)}, bf16[80,512]{1,0:T(8,128)(2,1)S(1)}, u32[]{:S(2)}, u32[]{:S(2)}) collective-permute-start(bf16[80,512]{1,0:T(8,128)(2,1)S(1)} %project.1.refs_0_), channel_id=1, source_target_pairs={{0,3},{1,2},{2,1},{3,0},{4,7},{5,6},{6,5},{7,4},{8,11},{9,10},{10,... | collective-permute-start | bytes 245768 | tf_op jit(solution)/shard_map/ppermute | solution.py:65
  11.4 0.5 %collective-permute-start.8 = (bf16[80,512]{1,0:T(8,128)(2,1)S(1)}, bf16[80,512]{1,0:T(8,128)(2,1)S(1)}, u32[]{:S(2)}, u32[]{:S(2)}) collective-permute-start(bf16[80,512]{1,0:T(8,128)(2,1)S(1)} %project.1.refs_0_), channel_id=1, source_target_pairs={{0,2},{1,3},{2,0},{3,1},{4,6},{5,7},{6,4},{7,5},{8,10},{9,11},{10,... | collective-permute-start | bytes 245768 | tf_op jit(solution)/shard_map/ppermute | solution.py:65
  11.9 0.5 %collective-permute-start.7 = (bf16[80,512]{1,0:T(8,128)(2,1)S(1)}, bf16[80,512]{1,0:T(8,128)(2,1)S(1)}, u32[]{:S(2)}, u32[]{:S(2)}) collective-permute-start(bf16[80,512]{1,0:T(8,128)(2,1)S(1)} %project.1.refs_0_), channel_id=1, source_target_pairs={{0,1},{1,0},{2,3},{3,2},{4,5},{5,4},{6,7},{7,6},{8,9},{9,8},{10,11... | collective-permute-start | bytes 245768 | tf_op jit(solution)/shard_map/ppermute | solution.py:65
  12.4 2.4 %collective-permute-done.4.refs_0_.refs_3_ = bf16[80,512]{1,0:T(8,128)(2,1)S(1)} collective-permute-done((bf16[80,512]{1,0:T(8,128)(2,1)S(1)}, bf16[80,512]{1,0:T(8,128)(2,1)S(1)}, u32[]{:S(2)}, u32[]{:S(2)}) %collective-permute-start.4) | collective-permute-done | bytes 81952 | tf_op jit(solution)/shard_map/ppermute | solution.py:65
  14.8 0.0 collective-permute-done.block_ref.one
  14.8 0.1 halves.3
  14.9 0.5 %collective-permute-start.5 = (bf16[32,6144]{1,0:T(8,128)(2,1)S(1)}, bf16[32,6144]{1,0:T(8,128)(2,1)S(1)}, u32[]{:S(2)}, u32[]{:S(2)}) collective-permute-start(bf16[32,6144]{1,0:T(8,128)(2,1)S(1)} %get-tuple-element.13), channel_id=1, source_target_pairs={{0,4},{4,0},{8,12},{12,8},{16,20},{20,16},{24,28},{28,24},{1,5},{5... | collective-permute-start | bytes 1179656 | tf_op jit(solution)/shard_map/ppermute | solution.py:49
  15.4 0.1 collective-permute-start.6
  15.5 1.4 %collective-permute-done.8.refs_2_ = bf16[80,512]{1,0:T(8,128)(2,1)S(1)} collective-permute-done((bf16[80,512]{1,0:T(8,128)(2,1)S(1)}, bf16[80,512]{1,0:T(8,128)(2,1)S(1)}, u32[]{:S(2)}, u32[]{:S(2)}) %collective-permute-start.8) | collective-permute-done | bytes 81952 | tf_op jit(solution)/shard_map/ppermute | solution.py:65
  16.9 0.1 collective-permute-done.7.refs_1_
  17.0 0.0 copy-done.5
  17.0 1.5 %couple.1.after_ref.mine = bf16[64,512]{1,0:T(8,128)(2,1)S(1)} custom-call(s32[4,32]{1,0:T(4,128)S(1)} %copy-done.5, bf16[80,512]{1,0:T(8,128)(2,1)S(1)} %project.1.refs_0_, bf16[80,512]{1,0:T(8,128)(2,1)S(1)} %collective-permute-done.7.refs_1_, bf16[80,512]{1,0:T(8,128)(2,1)S(1)} %collective-permute-done.8.refs_2_, ...), custom_call_target="tpu_custom_call" | custom-call | flops 4000000000 | tf_op jit(solution)/shard_map/couple/pallas_call | solution.py:30
  18.5 0.0 copy-start.4
  18.5 1.6 %collective-permute-start.10 = (bf16[64,512]{1,0:T(8,128)(2,1)S(1)}, bf16[64,512]{1,0:T(8,128)(2,1)S(1)}, u32[]{:S(2)}, u32[]{:S(2)}) collective-permute-start(bf16[64,512]{1,0:T(8,128)(2,1)S(1)} %couple.1.after_ref.mine), channel_id=1, source_target_pairs={{0,8},{4,12},{8,16},{12,20},{16,24},{20,28},{24,0},{28,4},{1,9},{5... | collective-permute-start | bytes 196616 | tf_op jit(solution)/shard_map/ppermute | solution.py:44
  20.2 0.0 collective-permute-done.5.upper_ref.upper
  20.2 0.0 collective-permute-done.6.lower_ref.lower
  20.2 0.1 collective-permute-start.9
  20.3 4.4 %collective-permute-done.10.mine_two.two = bf16[64,512]{1,0:T(8,128)(2,1)S(1)} collective-permute-done((bf16[64,512]{1,0:T(8,128)(2,1)S(1)}, bf16[64,512]{1,0:T(8,128)(2,1)S(1)}, u32[]{:S(2)}, u32[]{:S(2)}) %collective-permute-start.10) | collective-permute-done | bytes 65568 | tf_op jit(solution)/shard_map/ppermute | solution.py:44
  24.7 0.0 collective-permute-done.3.two
  24.7 0.1 choose.1
  24.7 0.1 collective-permute-start.11
  24.8 0.5 %collective-permute-start.13 = (bf16[64,512]{1,0:T(8,128)(2,1)S(1)}, bf16[64,512]{1,0:T(8,128)(2,1)S(1)}, u32[]{:S(2)}, u32[]{:S(2)}) collective-permute-start(bf16[64,512]{1,0:T(8,128)(2,1)S(1)} %collective-permute-done.10.mine_two.two), channel_id=1, source_target_pairs={{0,4},{4,8},{8,12},{12,16},{16,20},{20,24},{24,28},{28,0},{1,5},{5... | collective-permute-start | bytes 196616 | tf_op jit(solution)/shard_map/ppermute | solution.py:44
  25.3 0.0 collective-permute-start.12
  25.3 6.1 %collective-permute-done.9.three_a = bf16[48,6144]{1,0:T(8,128)(2,1)S(1)} collective-permute-done((bf16[48,6144]{1,0:T(8,128)(2,1)S(1)}, bf16[48,6144]{1,0:T(8,128)(2,1)S(1)}, u32[]{:S(2)}, u32[]{:S(2)}) %collective-permute-start.9) | collective-permute-done | bytes 589856 | tf_op jit(solution)/shard_map/ppermute | solution.py:44
  31.4 0.0 copy-done.4
  31.4 0.8 %gather.1.after_ref.partial_ref = f32[64,6144]{1,0:T(8,128)S(1)} custom-call(bf16[64,256]{1,0:T(8,128)(2,1)S(1)} %copy-done.4, bf16[64,6144]{1,0:T(8,128)(2,1)S(1)} %copy-done.2, bf16[64,6144]{1,0:T(8,128)(2,1)S(1)} %collective-permute-done.block_ref.one, bf16[64,6144]{1,0:T(8,128)(2,1)S(1)} %collective-permute-done.3.two, ...), custom_call_target="tpu_custom_call" | custom-call | flops 4499999744 | tf_op jit(solution)/shard_map/gather/pallas_call | solution.py:30
  32.2 0.0 collective-permute-done.13.three
  32.2 0.0 collective-permute-done.11.swap_ref
  32.2 1.4 %apply.1.applied = f32[64,6144]{1,0:T(8,128)S(1)} custom-call(bf16[64,256]{1,0:T(8,128)(2,1)S(1)} %copy-done.4, bf16[64,512]{1,0:T(8,128)(2,1)S(1)} %couple.1.after_ref.mine, bf16[80,6144]{1,0:T(8,128)(2,1)S(1)} %collective-permute-done.11.swap_ref, bf16[64,512]{1,0:T(8,128)(2,1)S(1)} %collective-permute-done.10.mine_two.two, ...), custom_call_target="tpu_custom_call" | custom-call | flops 5000000000 | tf_op jit(solution)/shard_map/apply/pallas_call | solution.py:30
  33.7 0.5 %collective-permute-done.12.last_ref = bf16[16,6144]{1,0:T(8,128)(2,1)S(1)} collective-permute-done((bf16[16,6144]{1,0:T(8,128)(2,1)S(1)}, bf16[16,6144]{1,0:T(8,128)(2,1)S(1)}, u32[]{:S(2)}, u32[]{:S(2)}) %collective-permute-start.12) | collective-permute-done | bytes 196640 | tf_op jit(solution)/shard_map/ppermute | solution.py:44
  34.2 1.2 %finish.1 = bf16[64,6144]{1,0:T(8,128)(2,1)} custom-call(bf16[64,256]{1,0:T(8,128)(2,1)S(1)} %copy-done.4, f32[64,6144]{1,0:T(8,128)S(1)} %gather.1.after_ref.partial_ref, bf16[80,6144]{1,0:T(8,128)(2,1)S(1)} %collective-permute-done.11.swap_ref, bf16[16,6144]{1,0:T(8,128)(2,1)S(1)} %collective-permute-done.12.last_ref, f32[64,6144]{1,0:T(8,128)S(1)} %apply.1.applied), custom_call_target="tpu_custom_call" | custom-call | tf_op jit(solution)/shard_map/finish/pallas_call | solution.py:314
  (1 shorter events, 0.0 us)
Async XLA Ops:
  0.0 14.8 %collective-permute-start = (bf16[64,6144]{1,0:T(8,128)(2,1)}, bf16[64,6144]{1,0:T(8,128)(2,1)S(1)}, u32[]{:S(2)}, u32[]{:S(2)}) collective-permute-start(bf16[64,6144]{1,0:T(8,128)(2,1)} %own.1), channel_id=1, source_target_pairs={{0,4},{4,8},{8,12},{12,16},{16,20},{20,24},{24,28},{28,0},{1,5},{5... | collective-permute-start | bytes 2359304 | tf_op jit(solution)/shard_map/ppermute | solution.py:44
  0.5 1.1 %copy-start.1 = (bf16[64,6144]{1,0:T(8,128)(2,1)S(1)}, bf16[64,6144]{1,0:T(8,128)(2,1)}, u32[]{:S(2)}) copy-start(bf16[64,6144]{1,0:T(8,128)(2,1)} %own.1) | copy-start | bytes 2359300
  1.6 5.4 %copy-start = (bf16[32,16,6144]{2,1,0:T(8,128)(2,1)S(1)}, bf16[32,16,6144]{2,1,0:T(8,128)(2,1)}, u32[]{:S(2)}) copy-start(bf16[32,16,6144]{2,1,0:T(8,128)(2,1)} %param.7) | copy-start | bytes 18874372
  1.6 5.2 %copy-start.3 = (f32[16,16,16]{2,1,0:T(8,128)S(1)}, f32[16,16,16]{2,1,0:T(8,128)}, u32[]{:S(2)}) copy-start(f32[16,16,16]{2,1,0:T(8,128)} %param.8) | copy-start | bytes 49156
  1.7 5.3 %copy-start.2 = (bf16[64,6144]{1,0:T(8,128)(2,1)S(1)}, bf16[64,6144]{1,0:T(8,128)(2,1)}, u32[]{:S(2)}) copy-start(bf16[64,6144]{1,0:T(8,128)(2,1)} %own.1) | copy-start | bytes 2359300
  1.7 4.1 %collective-permute-start.1 = (bf16[32,6144]{1,0:T(8,128)(2,1)S(1)}, bf16[32,6144]{1,0:T(8,128)(2,1)S(1)}, u32[]{:S(2)}, u32[]{:S(2)}) collective-permute-start(bf16[32,6144]{1,0:T(8,128)(2,1)S(1)} %get-tuple-element.11), channel_id=1, source_target_pairs={{0,4},{4,0},{8,12},{12,8},{16,20},{20,16},{24,28},{28,24},{1,5},{5... | collective-permute-start | bytes 1179656 | tf_op jit(solution)/shard_map/ppermute | solution.py:49
  4.5 1.9 %collective-permute-start.2 = (bf16[32,6144]{1,0:T(8,128)(2,1)S(1)}, bf16[32,6144]{1,0:T(8,128)(2,1)S(1)}, u32[]{:S(2)}, u32[]{:S(2)}) collective-permute-start(bf16[32,6144]{1,0:T(8,128)(2,1)S(1)} %get-tuple-element.12), channel_id=1, source_target_pairs={{0,4},{4,0},{8,12},{12,8},{16,20},{20,16},{24,28},{28,24},{1,5},{5... | collective-permute-start | bytes 1179656 | tf_op jit(solution)/shard_map/ppermute | solution.py:49
  6.4 18.2 %collective-permute-start.3 = (bf16[64,6144]{1,0:T(8,128)(2,1)S(1)}, bf16[64,6144]{1,0:T(8,128)(2,1)S(1)}, u32[]{:S(2)}, u32[]{:S(2)}) collective-permute-start(bf16[64,6144]{1,0:T(8,128)(2,1)S(1)} %hold.2), channel_id=1, source_target_pairs={{0,4},{4,8},{8,12},{12,16},{16,20},{20,24},{24,28},{28,0},{1,5},{5... | collective-permute-start | bytes 2359304 | tf_op jit(solution)/shard_map/ppermute | solution.py:44
  7.0 10.0 %copy-start.5 = (s32[4,32]{1,0:T(4,128)S(1)}, s32[4,32]{1,0:T(4,128)}, u32[]{:S(2)}) copy-start(s32[4,32]{1,0:T(4,128)} %slot_ref.1) | copy-start | bytes 1540
  8.9 5.9 %collective-permute-start.4 = (bf16[80,512]{1,0:T(8,128)(2,1)S(1)}, bf16[80,512]{1,0:T(8,128)(2,1)S(1)}, u32[]{:S(2)}, u32[]{:S(2)}) collective-permute-start(bf16[80,512]{1,0:T(8,128)(2,1)S(1)} %project.1.refs_0_), channel_id=1, source_target_pairs={{0,3},{1,2},{2,1},{3,0},{4,7},{5,6},{6,5},{7,4},{8,11},{9,10},{10,... | collective-permute-start | bytes 245768 | tf_op jit(solution)/shard_map/ppermute | solution.py:65
  11.4 5.5 %collective-permute-start.8 = (bf16[80,512]{1,0:T(8,128)(2,1)S(1)}, bf16[80,512]{1,0:T(8,128)(2,1)S(1)}, u32[]{:S(2)}, u32[]{:S(2)}) collective-permute-start(bf16[80,512]{1,0:T(8,128)(2,1)S(1)} %project.1.refs_0_), channel_id=1, source_target_pairs={{0,2},{1,3},{2,0},{3,1},{4,6},{5,7},{6,4},{7,5},{8,10},{9,11},{10,... | collective-permute-start | bytes 245768 | tf_op jit(solution)/shard_map/ppermute | solution.py:65
  11.9 5.1 %collective-permute-start.7 = (bf16[80,512]{1,0:T(8,128)(2,1)S(1)}, bf16[80,512]{1,0:T(8,128)(2,1)S(1)}, u32[]{:S(2)}, u32[]{:S(2)}) collective-permute-start(bf16[80,512]{1,0:T(8,128)(2,1)S(1)} %project.1.refs_0_), channel_id=1, source_target_pairs={{0,1},{1,0},{2,3},{3,2},{4,5},{5,4},{6,7},{7,6},{8,9},{9,8},{10,11... | collective-permute-start | bytes 245768 | tf_op jit(solution)/shard_map/ppermute | solution.py:65
  14.9 5.3 %collective-permute-start.5 = (bf16[32,6144]{1,0:T(8,128)(2,1)S(1)}, bf16[32,6144]{1,0:T(8,128)(2,1)S(1)}, u32[]{:S(2)}, u32[]{:S(2)}) collective-permute-start(bf16[32,6144]{1,0:T(8,128)(2,1)S(1)} %get-tuple-element.13), channel_id=1, source_target_pairs={{0,4},{4,0},{8,12},{12,8},{16,20},{20,16},{24,28},{28,24},{1,5},{5... | collective-permute-start | bytes 1179656 | tf_op jit(solution)/shard_map/ppermute | solution.py:49
  15.4 4.8 %collective-permute-start.6 = (bf16[32,6144]{1,0:T(8,128)(2,1)S(1)}, bf16[32,6144]{1,0:T(8,128)(2,1)S(1)}, u32[]{:S(2)}, u32[]{:S(2)}) collective-permute-start(bf16[32,6144]{1,0:T(8,128)(2,1)S(1)} %get-tuple-element.14), channel_id=1, source_target_pairs={{0,4},{4,0},{8,12},{12,8},{16,20},{20,16},{24,28},{28,24},{1,5},{5... | collective-permute-start | bytes 1179656 | tf_op jit(solution)/shard_map/ppermute | solution.py:49
  18.5 12.9 %copy-start.4 = (bf16[64,256]{1,0:T(8,128)(2,1)S(1)}, bf16[64,256]{1,0:T(8,128)(2,1)}, u32[]{:S(2)}) copy-start(bf16[64,256]{1,0:T(8,128)(2,1)} %rot_ref.5) | copy-start | bytes 98308
  18.5 6.1 %collective-permute-start.10 = (bf16[64,512]{1,0:T(8,128)(2,1)S(1)}, bf16[64,512]{1,0:T(8,128)(2,1)S(1)}, u32[]{:S(2)}, u32[]{:S(2)}) collective-permute-start(bf16[64,512]{1,0:T(8,128)(2,1)S(1)} %couple.1.after_ref.mine), channel_id=1, source_target_pairs={{0,8},{4,12},{8,16},{12,20},{16,24},{20,28},{24,0},{28,4},{1,9},{5... | collective-permute-start | bytes 196616 | tf_op jit(solution)/shard_map/ppermute | solution.py:44
  20.2 11.2 %collective-permute-start.9 = (bf16[48,6144]{1,0:T(8,128)(2,1)S(1)}, bf16[48,6144]{1,0:T(8,128)(2,1)S(1)}, u32[]{:S(2)}, u32[]{:S(2)}) collective-permute-start(bf16[48,6144]{1,0:T(8,128)(2,1)S(1)} %hold.3), channel_id=1, source_target_pairs={{0,4},{4,8},{8,12},{12,16},{16,20},{20,24},{24,28},{28,0},{1,5},{5... | collective-permute-start | bytes 1769480 | tf_op jit(solution)/shard_map/ppermute | solution.py:44
  24.7 7.5 %collective-permute-start.11 = (bf16[80,6144]{1,0:T(8,128)(2,1)S(1)}, bf16[80,6144]{1,0:T(8,128)(2,1)S(1)}, u32[]{:S(2)}, u32[]{:S(2)}) collective-permute-start(bf16[80,6144]{1,0:T(8,128)(2,1)S(1)} %get-tuple-element.15), channel_id=1, source_target_pairs={{0,4},{4,0},{8,12},{12,8},{16,20},{20,16},{24,28},{28,24},{1,5},{5... | collective-permute-start | bytes 2949128 | tf_op jit(solution)/shard_map/ppermute | solution.py:49
  24.8 7.4 %collective-permute-start.13 = (bf16[64,512]{1,0:T(8,128)(2,1)S(1)}, bf16[64,512]{1,0:T(8,128)(2,1)S(1)}, u32[]{:S(2)}, u32[]{:S(2)}) collective-permute-start(bf16[64,512]{1,0:T(8,128)(2,1)S(1)} %collective-permute-done.10.mine_two.two), channel_id=1, source_target_pairs={{0,4},{4,8},{8,12},{12,16},{16,20},{20,24},{24,28},{28,0},{1,5},{5... | collective-permute-start | bytes 196616 | tf_op jit(solution)/shard_map/ppermute | solution.py:44
  25.3 8.9 %collective-permute-start.12 = (bf16[16,6144]{1,0:T(8,128)(2,1)S(1)}, bf16[16,6144]{1,0:T(8,128)(2,1)S(1)}, u32[]{:S(2)}, u32[]{:S(2)}) collective-permute-start(bf16[16,6144]{1,0:T(8,128)(2,1)S(1)} %get-tuple-element.16), channel_id=1, source_target_pairs={{0,4},{4,8},{8,12},{12,16},{16,20},{20,24},{24,28},{28,0},{1,5},{5... | collective-permute-start | bytes 589832 | tf_op jit(solution)/shard_map/ppermute | solution.py:44

commit v7 on v6

--- a/solution.py
+++ b/solution.py
@@ -149,6 +149,77 @@
         term += jnp.dot(block, low_ref[...], preferred_element_type=F32)
         total = term if total is None else total + term
     out_ref[...] = total.astype(BF16)
+
+
+def match_kernel(count, slots, owned, slot_ref, *refs):
+    picks, matches = refs[:count], refs[count:]
+    flat = matches[0].shape[0]
+    rank = flat // slots
+    me = lax.axis_index("dom")
+    lanes = lax.broadcasted_iota(jnp.int32, (rank, flat), 1)
+    unit = lanes % rank == lax.broadcasted_iota(jnp.int32, (rank, flat), 0)
+    atoms = jnp.zeros((rank, flat), jnp.int32)
+    for k in range(slots):
+        atoms = jnp.where(lanes // rank == k, slot_ref[me, k], atoms)
+    for place in range(count):
+        domain = domain_at(place)
+        for a in range(owned):
+            hit = unit & (atoms == domain * owned + a)
+            rows = slice(a * rank, (a + 1) * rank)
+            picks[place][rows, :] = jnp.where(hit, 1.0, 0.0).astype(BF16)
+        for k in range(slots):
+            hit = unit & (atoms == slot_ref[domain, k])
+            rows = slice(k * rank, (k + 1) * rank)
+            matches[place][rows, :] = jnp.where(hit, 1.0, 0.0).astype(BF16)
+
+
+def match(slot_atom, owned, rank):
+    count, slots = slot_atom.shape
+    flat = slots * rank
+    outs = [((owned * rank, flat), BF16)] * count + [((flat, flat), BF16)] * count
+    kernel = functools.partial(match_kernel, count, slots, owned)
+    return call(kernel, "match", outs, [slot_atom], first=SMEM)
+
+
+def couple_matched_kernel(count, *refs):
+    loads, picks, matches = (refs[i * count : (i + 1) * count] for i in range(3))
+    out_ref, high_ref, low_ref = refs[3 * count :]
+    width, flat = out_ref.shape
+    rank = loads[0].shape[0] - width
+    size = picks[0].shape[0]
+
+    columns = None
+    for load, pick in zip(loads, picks):
+        parts = [load[width:, i * size : (i + 1) * size] for i in (0, 1)]
+        term = jnp.dot(jnp.concatenate(parts, 0), pick[...], preferred_element_type=F32)
+        columns = term if columns is None else columns + term
+    lane_slot = lax.broadcasted_iota(jnp.int32, (rank, flat), 1) // rank
+    for k in range(flat // rank):
+        rows = slice(k * rank, (k + 1) * rank)
+        high_ref[rows, :] = jnp.where(lane_slot == k, columns[:rank], 0.0).astype(BF16)
+        low_ref[rows, :] = jnp.where(lane_slot == k, columns[rank:], 0.0).astype(BF16)
+
+    total = sum(
+        jnp.dot(load[:width, :], x[...], preferred_element_type=F32)
+        for load, x in zip(loads, matches)
+    )
+    high = total.astype(BF16)
+    low = (total - high.astype(F32)).astype(BF16)
+    terms = ((high, high_ref), (low, high_ref), (high, low_ref))
+    coupled = sum(jnp.dot(x, y[...], preferred_element_type=F32) for x, y in terms)
+    out_ref[...] = coupled.astype(BF16)
+
+
+def couple_matched(loads, matched, width):
+    flat = loads[0].shape[1]
+    return call(
+        functools.partial(couple_matched_kernel, len(loads)),
+        "couple",
+        [((width, flat), BF16)],
+        [*loads, *matched],
+        [pltpu.VMEM((flat, flat), BF16)] * 2,
+        cost=COUPLE,
+    )[0]
 
 
 def couple(slot_atom, loads, width, owned):
@@ -333,8 +404,12 @@
     upper, lower = [swapped(block) for block in halves(orbitals, [], CUT)]
     two = along_bands(hold(upper, lower, width, upper), 1)
     loads = from_all_domains(project(orbitals, proj, coupling.reshape(owned * rank, rank)))
-    upper, lower = [swapped(block) for block in halves(one, loads[-1:])]
-    mine = couple(slot_atom, loads, width, owned)
+    matched = list(match(slot_atom, owned, rank)) if by_permutes() else []
+    upper, lower = [swapped(block) for block in halves(one, loads[-1:] + matched[:1])]
+    if by_permutes():
+        mine = couple_matched(loads, matched, width)
+    else:
+        mine = couple(slot_atom, loads, width, owned)
     mine_two = along_bands(mine, 2)
     three_a = along_bands(hold(upper, lower, width * 3 // 4, mine), 1)
     swap, held = choose(mine, mine_two, two, lower)

time: 35.5 us -> 34.9 us (0.983)
  waiting for transfers between devices: 16.7 us -> 15.5 us
  Pallas kernels: 7.21 us -> 7.73 us
    ppermute x3, waiting for transfers between devices: 3.91 us -> 2.77 us  [from_all_domains(): return [block] + [lax.ppermute(block, 'dom', route) for route in routes]]
    pallas_call x10 -> x11, Pallas kernels: 6.03 us -> 6.55 us  [call(): pl.pallas_call(kernel, in_specs=[first] + [VMEM] * (len(args) - 1), out_s...]
  transfers between devices with their start and end apart: 14 -> 14, of which waited for: 8 -> 8; matrix products, arithmetic and copies ran while one was open for 0% -> 0% of each run, Pallas kernels for 17% -> 19%
where the time goes in v7:
time: 34.9 us; the launch traced here: 34.8 us
  waiting for transfers between devices  15.5 us (44%)
  starting transfers between devices  10.2 us (29%)
  Pallas kernels  7.73 us (22%)
  local copies, waits for them, and re-layouts  1.17 us (3%)
    ppermute x6, waiting for transfers between devices, along_bands(): lax.ppermute(block, 'band', [(i, (i + distance) % count) for i in range(c...  10.9 us
    pallas_call x11, Pallas kernels, call(): pl.pallas_call(kernel, in_specs=[first] + [VMEM] * (len(args) - 1), out_s...  6.55 us
    ppermute x3, starting transfers between devices, from_all_domains(): return [block] + [lax.ppermute(block, 'dom', route) for route in routes]  3.55 us
    ppermute x5, starting transfers between devices, swapped(): return lax.ppermute(block, 'band', [(i, i ^ 1) for i in range(count)])  3.54 us
    ppermute x6, starting transfers between devices, along_bands(): lax.ppermute(block, 'band', [(i, (i + distance) % count) for i in range(c...  3.12 us
    ppermute x3, waiting for transfers between devices, from_all_domains(): return [block] + [lax.ppermute(block, 'dom', route) for route in routes]  2.77 us
    ppermute x5, waiting for transfers between devices, swapped(): return lax.ppermute(block, 'band', [(i, i ^ 1) for i in range(count)])  1.84 us
    pallas_call x1, Pallas kernels, finish(): pl.pallas_call(finish_kernel, in_specs=[VMEM] * len(args), out_specs=pl.B...  1.18 us
  transfers between devices with their start and end apart: 14, of which 8 were waited for; matrix products, arithmetic and copies ran while one was open for 0% of the time, Pallas kernels for 19%

profile of v7, /device:TPU:0, one launch (start us, length us, event | category | flops | bytes accessed | tf_op | source)
XLA Modules:
  0.0 34.8 jit_solution(12134084027761344631)
XLA Ops:
  0.0 0.5 %collective-permute-start = (bf16[64,6144]{1,0:T(8,128)(2,1)}, bf16[64,6144]{1,0:T(8,128)(2,1)S(1)}, u32[]{:S(2)}, u32[]{:S(2)}) collective-permute-start(bf16[64,6144]{1,0:T(8,128)(2,1)} %own.1), channel_id=1, source_target_pairs={{0,4},{4,8},{8,12},{12,16},{16,20},{20,24},{24,28},{28,0},{1,5},{5... | collective-permute-start | bytes 2359304 | tf_op jit(solution)/shard_map/ppermute | solution.py:44
  0.5 0.0 copy-start.1
  0.5 1.1 %copy-done.1 = bf16[64,6144]{1,0:T(8,128)(2,1)S(1)} copy-done((bf16[64,6144]{1,0:T(8,128)(2,1)S(1)}, bf16[64,6144]{1,0:T(8,128)(2,1)}, u32[]{:S(2)}) %copy-start.1) | copy-done | bytes 786456
  1.6 0.0 copy-start
  1.6 0.1 halves.2
  1.6 0.0 copy-start.3
  1.7 0.0 copy-start.2
  1.7 2.8 %collective-permute-start.1 = (bf16[32,6144]{1,0:T(8,128)(2,1)S(1)}, bf16[32,6144]{1,0:T(8,128)(2,1)S(1)}, u32[]{:S(2)}, u32[]{:S(2)}) collective-permute-start(bf16[32,6144]{1,0:T(8,128)(2,1)S(1)} %get-tuple-element.19), channel_id=1, source_target_pairs={{0,4},{4,0},{8,12},{12,8},{16,20},{20,16},{24,28},{28,24},{1,5},{5... | collective-permute-start | bytes 1179656 | tf_op jit(solution)/shard_map/ppermute | solution.py:49
  4.5 0.1 collective-permute-start.2
  4.5 1.3 %collective-permute-done.1.upper_ref.after_ref = bf16[32,6144]{1,0:T(8,128)(2,1)S(1)} collective-permute-done((bf16[32,6144]{1,0:T(8,128)(2,1)S(1)}, bf16[32,6144]{1,0:T(8,128)(2,1)S(1)}, u32[]{:S(2)}, u32[]{:S(2)}) %collective-permute-start.1) | collective-permute-done | bytes 393248 | tf_op jit(solution)/shard_map/ppermute | solution.py:49
  5.8 0.6 %collective-permute-done.2.lower_ref = bf16[32,6144]{1,0:T(8,128)(2,1)S(1)} collective-permute-done((bf16[32,6144]{1,0:T(8,128)(2,1)S(1)}, bf16[32,6144]{1,0:T(8,128)(2,1)S(1)}, u32[]{:S(2)}, u32[]{:S(2)}) %collective-permute-start.2) | collective-permute-done | bytes 393248 | tf_op jit(solution)/shard_map/ppermute | solution.py:49
  6.4 0.1 hold.2
  6.4 0.4 %collective-permute-start.3 = (bf16[64,6144]{1,0:T(8,128)(2,1)S(1)}, bf16[64,6144]{1,0:T(8,128)(2,1)S(1)}, u32[]{:S(2)}, u32[]{:S(2)}) collective-permute-start(bf16[64,6144]{1,0:T(8,128)(2,1)S(1)} %hold.2), channel_id=1, source_target_pairs={{0,4},{4,8},{8,12},{12,16},{16,20},{20,24},{24,28},{28,0},{1,5},{5... | collective-permute-start | bytes 2359304 | tf_op jit(solution)/shard_map/ppermute | solution.py:44
  6.8 0.0 copy-done.3
  6.9 0.1 turn.1.turned_ref
  7.0 0.0 copy-done
  7.0 0.0 copy-done.2
  7.0 0.0 copy-start.5
  7.0 1.8 %project.1.refs_0_ = bf16[80,512]{1,0:T(8,128)(2,1)S(1)} custom-call(bf16[64,6144]{1,0:T(8,128)(2,1)S(1)} %copy-done.2, bf16[512,6144]{1,0:T(8,128)(2,1)S(1)} %bitcast.2, bf16[16,512]{1,0:T(8,128)(2,1)S(1)} %turn.1.turned_ref), custom_call_target="tpu_custom_call" | custom-call | tf_op jit(solution)/shard_map/project/pallas_call | solution.py:30
  8.9 2.5 %collective-permute-start.4 = (bf16[80,512]{1,0:T(8,128)(2,1)S(1)}, bf16[80,512]{1,0:T(8,128)(2,1)S(1)}, u32[]{:S(2)}, u32[]{:S(2)}) collective-permute-start(bf16[80,512]{1,0:T(8,128)(2,1)S(1)} %project.1.refs_0_), channel_id=1, source_target_pairs={{0,3},{1,2},{2,1},{3,0},{4,7},{5,6},{6,5},{7,4},{8,11},{9,10},{10,... | collective-permute-start | bytes 245768 | tf_op jit(solution)/shard_map/ppermute | solution.py:65
  11.4 0.5 %collective-permute-start.8 = (bf16[80,512]{1,0:T(8,128)(2,1)S(1)}, bf16[80,512]{1,0:T(8,128)(2,1)S(1)}, u32[]{:S(2)}, u32[]{:S(2)}) collective-permute-start(bf16[80,512]{1,0:T(8,128)(2,1)S(1)} %project.1.refs_0_), channel_id=1, source_target_pairs={{0,2},{1,3},{2,0},{3,1},{4,6},{5,7},{6,4},{7,5},{8,10},{9,11},{10,... | collective-permute-start | bytes 245768 | tf_op jit(solution)/shard_map/ppermute | solution.py:65
  11.9 0.5 %collective-permute-start.7 = (bf16[80,512]{1,0:T(8,128)(2,1)S(1)}, bf16[80,512]{1,0:T(8,128)(2,1)S(1)}, u32[]{:S(2)}, u32[]{:S(2)}) collective-permute-start(bf16[80,512]{1,0:T(8,128)(2,1)S(1)} %project.1.refs_0_), channel_id=1, source_target_pairs={{0,1},{1,0},{2,3},{3,2},{4,5},{5,4},{6,7},{7,6},{8,9},{9,8},{10,11... | collective-permute-start | bytes 245768 | tf_op jit(solution)/shard_map/ppermute | solution.py:65
  12.4 0.0 copy-done.5
  12.4 1.1 %match.1 = (bf16[256,512]{1,0:T(8,128)(2,1)S(1)}, bf16[256,512]{1,0:T(8,128)(2,1)S(1)}, bf16[256,512]{1,0:T(8,128)(2,1)S(1)}, bf16[256,512]{1,0:T(8,128)(2,1)S(1...) custom-call(s32[4,32]{1,0:T(4,128)S(1)} %copy-done.5), custom_call_target="tpu_custom_call" | custom-call | tf_op jit(solution)/shard_map/match/pallas_call | solution.py:30
  13.6 1.2 %collective-permute-done.4.refs_0_.refs_3_ = bf16[80,512]{1,0:T(8,128)(2,1)S(1)} collective-permute-done((bf16[80,512]{1,0:T(8,128)(2,1)S(1)}, bf16[80,512]{1,0:T(8,128)(2,1)S(1)}, u32[]{:S(2)}, u32[]{:S(2)}) %collective-permute-start.4) | collective-permute-done | bytes 81952 | tf_op jit(solution)/shard_map/ppermute | solution.py:65
  14.8 0.0 collective-permute-done.block_ref.one
  14.8 0.1 halves.3
  14.9 0.5 %collective-permute-start.5 = (bf16[32,6144]{1,0:T(8,128)(2,1)S(1)}, bf16[32,6144]{1,0:T(8,128)(2,1)S(1)}, u32[]{:S(2)}, u32[]{:S(2)}) collective-permute-start(bf16[32,6144]{1,0:T(8,128)(2,1)S(1)} %get-tuple-element.22), channel_id=1, source_target_pairs={{0,4},{4,0},{8,12},{12,8},{16,20},{20,16},{24,28},{28,24},{1,5},{5... | collective-permute-start | bytes 1179656 | tf_op jit(solution)/shard_map/ppermute | solution.py:49
  15.4 0.1 collective-permute-start.6
  15.5 1.4 %collective-permute-done.8.refs_2_ = bf16[80,512]{1,0:T(8,128)(2,1)S(1)} collective-permute-done((bf16[80,512]{1,0:T(8,128)(2,1)S(1)}, bf16[80,512]{1,0:T(8,128)(2,1)S(1)}, u32[]{:S(2)}, u32[]{:S(2)}) %collective-permute-start.8) | collective-permute-done | bytes 81952 | tf_op jit(solution)/shard_map/ppermute | solution.py:65
  16.9 0.1 collective-permute-done.7.refs_1_
  17.0 0.9 %couple.1.after_ref.mine = bf16[64,512]{1,0:T(8,128)(2,1)S(1)} custom-call(bf16[80,512]{1,0:T(8,128)(2,1)S(1)} %project.1.refs_0_, bf16[80,512]{1,0:T(8,128)(2,1)S(1)} %collective-permute-done.7.refs_1_, bf16[80,512]{1,0:T(8,128)(2,1)S(1)} %collective-permute-done.8.refs_2_, bf16[80,512]{1,0:T(8,128)(2,1)S(1)} %collective-permute-done.4.refs_0_.refs_3_, ...), custom_call_target="tpu_custom_call" | custom-call | flops 4000000000 | tf_op jit(solution)/shard_map/couple/pallas_call | solution.py:30
  17.9 0.0 copy-start.4
  17.9 1.6 %collective-permute-start.10 = (bf16[64,512]{1,0:T(8,128)(2,1)S(1)}, bf16[64,512]{1,0:T(8,128)(2,1)S(1)}, u32[]{:S(2)}, u32[]{:S(2)}) collective-permute-start(bf16[64,512]{1,0:T(8,128)(2,1)S(1)} %couple.1.after_ref.mine), channel_id=1, source_target_pairs={{0,8},{4,12},{8,16},{12,20},{16,24},{20,28},{24,0},{28,4},{1,9},{5... | collective-permute-start | bytes 196616 | tf_op jit(solution)/shard_map/ppermute | solution.py:44
  19.6 0.0 collective-permute-done.5.upper_ref.upper
  19.6 0.0 collective-permute-done.6.lower_ref.lower
  19.6 0.1 collective-permute-start.9
  19.7 4.5 %collective-permute-done.10.mine_two.two = bf16[64,512]{1,0:T(8,128)(2,1)S(1)} collective-permute-done((bf16[64,512]{1,0:T(8,128)(2,1)S(1)}, bf16[64,512]{1,0:T(8,128)(2,1)S(1)}, u32[]{:S(2)}, u32[]{:S(2)}) %collective-permute-start.10) | collective-permute-done | bytes 65568 | tf_op jit(solution)/shard_map/ppermute | solution.py:44
  24.2 0.0 collective-permute-done.3.two
  24.2 0.1 choose.1
  24.3 0.1 collective-permute-start.11
  24.4 0.5 %collective-permute-start.13 = (bf16[64,512]{1,0:T(8,128)(2,1)S(1)}, bf16[64,512]{1,0:T(8,128)(2,1)S(1)}, u32[]{:S(2)}, u32[]{:S(2)}) collective-permute-start(bf16[64,512]{1,0:T(8,128)(2,1)S(1)} %collective-permute-done.10.mine_two.two), channel_id=1, source_target_pairs={{0,4},{4,8},{8,12},{12,16},{16,20},{20,24},{24,28},{28,0},{1,5},{5... | collective-permute-start | bytes 196616 | tf_op jit(solution)/shard_map/ppermute | solution.py:44
  24.9 0.1 collective-permute-start.12
  24.9 5.9 %collective-permute-done.9.three_a = bf16[48,6144]{1,0:T(8,128)(2,1)S(1)} collective-permute-done((bf16[48,6144]{1,0:T(8,128)(2,1)S(1)}, bf16[48,6144]{1,0:T(8,128)(2,1)S(1)}, u32[]{:S(2)}, u32[]{:S(2)}) %collective-permute-start.9) | collective-permute-done | bytes 589856 | tf_op jit(solution)/shard_map/ppermute | solution.py:44
  30.8 0.0 copy-done.4
  30.8 0.8 %gather.1.after_ref.partial_ref = f32[64,6144]{1,0:T(8,128)S(1)} custom-call(bf16[64,256]{1,0:T(8,128)(2,1)S(1)} %copy-done.4, bf16[64,6144]{1,0:T(8,128)(2,1)S(1)} %copy-done.2, bf16[64,6144]{1,0:T(8,128)(2,1)S(1)} %collective-permute-done.block_ref.one, bf16[64,6144]{1,0:T(8,128)(2,1)S(1)} %collective-permute-done.3.two, ...), custom_call_target="tpu_custom_call" | custom-call | flops 4499999744 | tf_op jit(solution)/shard_map/gather/pallas_call | solution.py:30
  31.6 0.0 collective-permute-done.13.three
  31.6 0.0 collective-permute-done.11.swap_ref
  31.6 1.4 %apply.1.applied = f32[64,6144]{1,0:T(8,128)S(1)} custom-call(bf16[64,256]{1,0:T(8,128)(2,1)S(1)} %copy-done.4, bf16[64,512]{1,0:T(8,128)(2,1)S(1)} %couple.1.after_ref.mine, bf16[80,6144]{1,0:T(8,128)(2,1)S(1)} %collective-permute-done.11.swap_ref, bf16[64,512]{1,0:T(8,128)(2,1)S(1)} %collective-permute-done.10.mine_two.two, ...), custom_call_target="tpu_custom_call" | custom-call | flops 5000000000 | tf_op jit(solution)/shard_map/apply/pallas_call | solution.py:30
  33.1 0.5 %collective-permute-done.12.last_ref = bf16[16,6144]{1,0:T(8,128)(2,1)S(1)} collective-permute-done((bf16[16,6144]{1,0:T(8,128)(2,1)S(1)}, bf16[16,6144]{1,0:T(8,128)(2,1)S(1)}, u32[]{:S(2)}, u32[]{:S(2)}) %collective-permute-start.12) | collective-permute-done | bytes 196640 | tf_op jit(solution)/shard_map/ppermute | solution.py:44
  33.6 1.2 %finish.1 = bf16[64,6144]{1,0:T(8,128)(2,1)} custom-call(bf16[64,256]{1,0:T(8,128)(2,1)S(1)} %copy-done.4, f32[64,6144]{1,0:T(8,128)S(1)} %gather.1.after_ref.partial_ref, bf16[80,6144]{1,0:T(8,128)(2,1)S(1)} %collective-permute-done.11.swap_ref, bf16[16,6144]{1,0:T(8,128)(2,1)S(1)} %collective-permute-done.12.last_ref, f32[64,6144]{1,0:T(8,128)S(1)} %apply.1.applied), custom_call_target="tpu_custom_call" | custom-call | tf_op jit(solution)/shard_map/finish/pallas_call | solution.py:385
  (1 shorter events, 0.0 us)
Async XLA Ops:
  0.0 14.8 %collective-permute-start = (bf16[64,6144]{1,0:T(8,128)(2,1)}, bf16[64,6144]{1,0:T(8,128)(2,1)S(1)}, u32[]{:S(2)}, u32[]{:S(2)}) collective-permute-start(bf16[64,6144]{1,0:T(8,128)(2,1)} %own.1), channel_id=1, source_target_pairs={{0,4},{4,8},{8,12},{12,16},{16,20},{20,24},{24,28},{28,0},{1,5},{5... | collective-permute-start | bytes 2359304 | tf_op jit(solution)/shard_map/ppermute | solution.py:44
  0.5 1.1 %copy-start.1 = (bf16[64,6144]{1,0:T(8,128)(2,1)S(1)}, bf16[64,6144]{1,0:T(8,128)(2,1)}, u32[]{:S(2)}) copy-start(bf16[64,6144]{1,0:T(8,128)(2,1)} %own.1) | copy-start | bytes 2359300
  1.6 5.4 %copy-start = (bf16[32,16,6144]{2,1,0:T(8,128)(2,1)S(1)}, bf16[32,16,6144]{2,1,0:T(8,128)(2,1)}, u32[]{:S(2)}) copy-start(bf16[32,16,6144]{2,1,0:T(8,128)(2,1)} %param.7) | copy-start | bytes 18874372
  1.6 5.2 %copy-start.3 = (f32[16,16,16]{2,1,0:T(8,128)S(1)}, f32[16,16,16]{2,1,0:T(8,128)}, u32[]{:S(2)}) copy-start(f32[16,16,16]{2,1,0:T(8,128)} %param.8) | copy-start | bytes 49156
  1.7 5.3 %copy-start.2 = (bf16[64,6144]{1,0:T(8,128)(2,1)S(1)}, bf16[64,6144]{1,0:T(8,128)(2,1)}, u32[]{:S(2)}) copy-start(bf16[64,6144]{1,0:T(8,128)(2,1)} %own.1) | copy-start | bytes 2359300
  1.7 4.1 %collective-permute-start.1 = (bf16[32,6144]{1,0:T(8,128)(2,1)S(1)}, bf16[32,6144]{1,0:T(8,128)(2,1)S(1)}, u32[]{:S(2)}, u32[]{:S(2)}) collective-permute-start(bf16[32,6144]{1,0:T(8,128)(2,1)S(1)} %get-tuple-element.19), channel_id=1, source_target_pairs={{0,4},{4,0},{8,12},{12,8},{16,20},{20,16},{24,28},{28,24},{1,5},{5... | collective-permute-start | bytes 1179656 | tf_op jit(solution)/shard_map/ppermute | solution.py:49
  4.5 1.9 %collective-permute-start.2 = (bf16[32,6144]{1,0:T(8,128)(2,1)S(1)}, bf16[32,6144]{1,0:T(8,128)(2,1)S(1)}, u32[]{:S(2)}, u32[]{:S(2)}) collective-permute-start(bf16[32,6144]{1,0:T(8,128)(2,1)S(1)} %get-tuple-element.20), channel_id=1, source_target_pairs={{0,4},{4,0},{8,12},{12,8},{16,20},{20,16},{24,28},{28,24},{1,5},{5... | collective-permute-start | bytes 1179656 | tf_op jit(solution)/shard_map/ppermute | solution.py:49
  6.4 17.8 %collective-permute-start.3 = (bf16[64,6144]{1,0:T(8,128)(2,1)S(1)}, bf16[64,6144]{1,0:T(8,128)(2,1)S(1)}, u32[]{:S(2)}, u32[]{:S(2)}) collective-permute-start(bf16[64,6144]{1,0:T(8,128)(2,1)S(1)} %hold.2), channel_id=1, source_target_pairs={{0,4},{4,8},{8,12},{12,16},{16,20},{20,24},{24,28},{28,0},{1,5},{5... | collective-permute-start | bytes 2359304 | tf_op jit(solution)/shard_map/ppermute | solution.py:44
  7.0 5.4 %copy-start.5 = (s32[4,32]{1,0:T(4,128)S(1)}, s32[4,32]{1,0:T(4,128)}, u32[]{:S(2)}) copy-start(s32[4,32]{1,0:T(4,128)} %slot_ref.1) | copy-start | bytes 1540
  8.9 5.9 %collective-permute-start.4 = (bf16[80,512]{1,0:T(8,128)(2,1)S(1)}, bf16[80,512]{1,0:T(8,128)(2,1)S(1)}, u32[]{:S(2)}, u32[]{:S(2)}) collective-permute-start(bf16[80,512]{1,0:T(8,128)(2,1)S(1)} %project.1.refs_0_), channel_id=1, source_target_pairs={{0,3},{1,2},{2,1},{3,0},{4,7},{5,6},{6,5},{7,4},{8,11},{9,10},{10,... | collective-permute-start | bytes 245768 | tf_op jit(solution)/shard_map/ppermute | solution.py:65
  11.4 5.5 %collective-permute-start.8 = (bf16[80,512]{1,0:T(8,128)(2,1)S(1)}, bf16[80,512]{1,0:T(8,128)(2,1)S(1)}, u32[]{:S(2)}, u32[]{:S(2)}) collective-permute-start(bf16[80,512]{1,0:T(8,128)(2,1)S(1)} %project.1.refs_0_), channel_id=1, source_target_pairs={{0,2},{1,3},{2,0},{3,1},{4,6},{5,7},{6,4},{7,5},{8,10},{9,11},{10,... | collective-permute-start | bytes 245768 | tf_op jit(solution)/shard_map/ppermute | solution.py:65
  11.9 5.1 %collective-permute-start.7 = (bf16[80,512]{1,0:T(8,128)(2,1)S(1)}, bf16[80,512]{1,0:T(8,128)(2,1)S(1)}, u32[]{:S(2)}, u32[]{:S(2)}) collective-permute-start(bf16[80,512]{1,0:T(8,128)(2,1)S(1)} %project.1.refs_0_), channel_id=1, source_target_pairs={{0,1},{1,0},{2,3},{3,2},{4,5},{5,4},{6,7},{7,6},{8,9},{9,8},{10,11... | collective-permute-start | bytes 245768 | tf_op jit(solution)/shard_map/ppermute | solution.py:65
  14.9 4.7 %collective-permute-start.5 = (bf16[32,6144]{1,0:T(8,128)(2,1)S(1)}, bf16[32,6144]{1,0:T(8,128)(2,1)S(1)}, u32[]{:S(2)}, u32[]{:S(2)}) collective-permute-start(bf16[32,6144]{1,0:T(8,128)(2,1)S(1)} %get-tuple-element.22), channel_id=1, source_target_pairs={{0,4},{4,0},{8,12},{12,8},{16,20},{20,16},{24,28},{28,24},{1,5},{5... | collective-permute-start | bytes 1179656 | tf_op jit(solution)/shard_map/ppermute | solution.py:49
  15.4 4.2 %collective-permute-start.6 = (bf16[32,6144]{1,0:T(8,128)(2,1)S(1)}, bf16[32,6144]{1,0:T(8,128)(2,1)S(1)}, u32[]{:S(2)}, u32[]{:S(2)}) collective-permute-start(bf16[32,6144]{1,0:T(8,128)(2,1)S(1)} %get-tuple-element.23), channel_id=1, source_target_pairs={{0,4},{4,0},{8,12},{12,8},{16,20},{20,16},{24,28},{28,24},{1,5},{5... | collective-permute-start | bytes 1179656 | tf_op jit(solution)/shard_map/ppermute | solution.py:49
  17.9 12.9 %copy-start.4 = (bf16[64,256]{1,0:T(8,128)(2,1)S(1)}, bf16[64,256]{1,0:T(8,128)(2,1)}, u32[]{:S(2)}) copy-start(bf16[64,256]{1,0:T(8,128)(2,1)} %rot_ref.5) | copy-start | bytes 98308
  17.9 6.3 %collective-permute-start.10 = (bf16[64,512]{1,0:T(8,128)(2,1)S(1)}, bf16[64,512]{1,0:T(8,128)(2,1)S(1)}, u32[]{:S(2)}, u32[]{:S(2)}) collective-permute-start(bf16[64,512]{1,0:T(8,128)(2,1)S(1)} %couple.1.after_ref.mine), channel_id=1, source_target_pairs={{0,8},{4,12},{8,16},{12,20},{16,24},{20,28},{24,0},{28,4},{1,9},{5... | collective-permute-start | bytes 196616 | tf_op jit(solution)/shard_map/ppermute | solution.py:44
  19.6 11.2 %collective-permute-start.9 = (bf16[48,6144]{1,0:T(8,128)(2,1)S(1)}, bf16[48,6144]{1,0:T(8,128)(2,1)S(1)}, u32[]{:S(2)}, u32[]{:S(2)}) collective-permute-start(bf16[48,6144]{1,0:T(8,128)(2,1)S(1)} %hold.3), channel_id=1, source_target_pairs={{0,4},{4,8},{8,12},{12,16},{16,20},{20,24},{24,28},{28,0},{1,5},{5... | collective-permute-start | bytes 1769480 | tf_op jit(solution)/shard_map/ppermute | solution.py:44
  24.3 7.3 %collective-permute-start.11 = (bf16[80,6144]{1,0:T(8,128)(2,1)S(1)}, bf16[80,6144]{1,0:T(8,128)(2,1)S(1)}, u32[]{:S(2)}, u32[]{:S(2)}) collective-permute-start(bf16[80,6144]{1,0:T(8,128)(2,1)S(1)} %get-tuple-element.31), channel_id=1, source_target_pairs={{0,4},{4,0},{8,12},{12,8},{16,20},{20,16},{24,28},{28,24},{1,5},{5... | collective-permute-start | bytes 2949128 | tf_op jit(solution)/shard_map/ppermute | solution.py:49
  24.4 7.2 %collective-permute-start.13 = (bf16[64,512]{1,0:T(8,128)(2,1)S(1)}, bf16[64,512]{1,0:T(8,128)(2,1)S(1)}, u32[]{:S(2)}, u32[]{:S(2)}) collective-permute-start(bf16[64,512]{1,0:T(8,128)(2,1)S(1)} %collective-permute-done.10.mine_two.two), channel_id=1, source_target_pairs={{0,4},{4,8},{8,12},{12,16},{16,20},{20,24},{24,28},{28,0},{1,5},{5... | collective-permute-start | bytes 196616 | tf_op jit(solution)/shard_map/ppermute | solution.py:44
  24.9 8.7 %collective-permute-start.12 = (bf16[16,6144]{1,0:T(8,128)(2,1)S(1)}, bf16[16,6144]{1,0:T(8,128)(2,1)S(1)}, u32[]{:S(2)}, u32[]{:S(2)}) collective-permute-start(bf16[16,6144]{1,0:T(8,128)(2,1)S(1)} %get-tuple-element.32), channel_id=1, source_target_pairs={{0,4},{4,8},{8,12},{12,16},{16,20},{20,24},{24,28},{28,0},{1,5},{5... | collective-permute-start | bytes 589832 | tf_op jit(solution)/shard_map/ppermute | solution.py:44

commit v8 on v7

--- a/solution.py
+++ b/solution.py
@@ -351,28 +351,30 @@
         )
 
 
+def tiles_of(points):
+    if points % 1024:
+        tile = tile_of(points, 1024)
+        return [(at, tile) for at in range(0, points, tile)]
+    ends = [0] + list(range(512, points, 1024)) + [points]
+    return [(at, end - at) for at, end in zip(ends, ends[1:])]
+
+
 def finish_kernel(
     rot_ref, partial_ref, swap_ref, last_ref, applied, out_hbm, out_ref, sems
 ):
     width, points = out_ref.shape
     rows = last_ref.shape[0]
-    pieces = sems.shape[0]
-    tile = points // pieces
-    turn = jnp.concatenate(
-        [
-            where_even(rot_ref[:, 3 * width : 4 * width], False),
-            where_even(rot_ref[:, 4 * width - rows : 4 * width], True),
-        ],
-        axis=1,
-    )
+    on_odd = where_even(rot_ref[:, 3 * width : 4 * width], False)
+    on_last = where_even(rot_ref[:, 4 * width - rows : 4 * width], True)
     copies = []
-    for i in range(pieces):
-        here = slice(i * tile, (i + 1) * tile)
-        last = jnp.concatenate([swap_ref[:width, here], last_ref[:, here]], axis=0)
-        rotated = partial_ref[:, here] + jnp.dot(turn, last, preferred_element_type=F32)
+    for i, (at, tile) in enumerate(tiles_of(points)):
+        here = slice(at, at + tile)
+        rotated = partial_ref[:, here]
+        rotated += jnp.dot(on_odd, swap_ref[:width, here], preferred_element_type=F32)
+        rotated += jnp.dot(on_last, last_ref[:, here], preferred_element_type=F32)
         added = rotated.astype(BF16).astype(F32) + applied[:, here]
         out_ref[:, here] = added.astype(out_ref.dtype)
-        part = (slice(None), pl.ds(i * tile, tile))
+        part = (slice(None), pl.ds(at, tile))
         copies.append(pltpu.make_async_copy(out_ref.at[part], out_hbm.at[part], sems.at[i]))
         copies[-1].start()
     for copy in copies:
@@ -381,7 +383,7 @@
 
 def finish(*args):
     width, points = args[-1].shape
-    pieces = points // tile_of(points, 1024)
+    pieces = len(tiles_of(points))
     return pl.pallas_call(
         finish_kernel,
         in_specs=[VMEM] * len(args),

time: 34.9 us -> 35.1 us (level)
  no operation moved by 1% of the time
where the time goes in v8:
time: 35.1 us; the launch traced here: 34.9 us
  waiting for transfers between devices  15.5 us (44%)
  starting transfers between devices  10.2 us (29%)
  Pallas kernels  7.88 us (22%)
  local copies, waits for them, and re-layouts  1.17 us (3%)
    ppermute x6, waiting for transfers between devices, along_bands(): lax.ppermute(block, 'band', [(i, (i + distance) % count) for i in range(c...  10.9 us
    pallas_call x11, Pallas kernels, call(): pl.pallas_call(kernel, in_specs=[first] + [VMEM] * (len(args) - 1), out_s...  6.55 us
    ppermute x3, starting transfers between devices, from_all_domains(): return [block] + [lax.ppermute(block, 'dom', route) for route in routes]  3.55 us
    ppermute x5, starting transfers between devices, swapped(): return lax.ppermute(block, 'band', [(i, i ^ 1) for i in range(count)])  3.54 us
    ppermute x6, starting transfers between devices, along_bands(): lax.ppermute(block, 'band', [(i, (i + distance) % count) for i in range(c...  3.12 us
    ppermute x3, waiting for transfers between devices, from_all_domains(): return [block] + [lax.ppermute(block, 'dom', route) for route in routes]  2.77 us
    ppermute x5, waiting for transfers between devices, swapped(): return lax.ppermute(block, 'band', [(i, i ^ 1) for i in range(count)])  1.84 us
    pallas_call x1, Pallas kernels, finish(): pl.pallas_call(finish_kernel, in_specs=[VMEM] * len(args), out_specs=pl.B...  1.33 us
  transfers between devices with their start and end apart: 14, of which 8 were waited for; matrix products, arithmetic and copies ran while one was open for 0% of the time, Pallas kernels for 19%

profile of v8, /device:TPU:0, one launch (start us, length us, event | category | flops | bytes accessed | tf_op | source)
XLA Modules:
  0.0 34.9 jit_solution(4982757074830109573)
XLA Ops:
  0.0 0.5 %collective-permute-start = (bf16[64,6144]{1,0:T(8,128)(2,1)}, bf16[64,6144]{1,0:T(8,128)(2,1)S(1)}, u32[]{:S(2)}, u32[]{:S(2)}) collective-permute-start(bf16[64,6144]{1,0:T(8,128)(2,1)} %own.1), channel_id=1, source_target_pairs={{0,4},{4,8},{8,12},{12,16},{16,20},{20,24},{24,28},{28,0},{1,5},{5... | collective-permute-start | bytes 2359304 | tf_op jit(solution)/shard_map/ppermute | solution.py:44
  0.5 0.0 copy-start.1
  0.5 1.1 %copy-done.1 = bf16[64,6144]{1,0:T(8,128)(2,1)S(1)} copy-done((bf16[64,6144]{1,0:T(8,128)(2,1)S(1)}, bf16[64,6144]{1,0:T(8,128)(2,1)}, u32[]{:S(2)}) %copy-start.1) | copy-done | bytes 786456
  1.6 0.0 copy-start
  1.6 0.1 halves.2
  1.6 0.0 copy-start.3
  1.7 0.0 copy-start.2
  1.7 2.8 %collective-permute-start.1 = (bf16[32,6144]{1,0:T(8,128)(2,1)S(1)}, bf16[32,6144]{1,0:T(8,128)(2,1)S(1)}, u32[]{:S(2)}, u32[]{:S(2)}) collective-permute-start(bf16[32,6144]{1,0:T(8,128)(2,1)S(1)} %get-tuple-element.19), channel_id=1, source_target_pairs={{0,4},{4,0},{8,12},{12,8},{16,20},{20,16},{24,28},{28,24},{1,5},{5... | collective-permute-start | bytes 1179656 | tf_op jit(solution)/shard_map/ppermute | solution.py:49
  4.5 0.1 collective-permute-start.2
  4.5 1.3 %collective-permute-done.1.upper_ref.after_ref = bf16[32,6144]{1,0:T(8,128)(2,1)S(1)} collective-permute-done((bf16[32,6144]{1,0:T(8,128)(2,1)S(1)}, bf16[32,6144]{1,0:T(8,128)(2,1)S(1)}, u32[]{:S(2)}, u32[]{:S(2)}) %collective-permute-start.1) | collective-permute-done | bytes 393248 | tf_op jit(solution)/shard_map/ppermute | solution.py:49
  5.8 0.6 %collective-permute-done.2.lower_ref = bf16[32,6144]{1,0:T(8,128)(2,1)S(1)} collective-permute-done((bf16[32,6144]{1,0:T(8,128)(2,1)S(1)}, bf16[32,6144]{1,0:T(8,128)(2,1)S(1)}, u32[]{:S(2)}, u32[]{:S(2)}) %collective-permute-start.2) | collective-permute-done | bytes 393248 | tf_op jit(solution)/shard_map/ppermute | solution.py:49
  6.4 0.1 hold.2
  6.4 0.4 %collective-permute-start.3 = (bf16[64,6144]{1,0:T(8,128)(2,1)S(1)}, bf16[64,6144]{1,0:T(8,128)(2,1)S(1)}, u32[]{:S(2)}, u32[]{:S(2)}) collective-permute-start(bf16[64,6144]{1,0:T(8,128)(2,1)S(1)} %hold.2), channel_id=1, source_target_pairs={{0,4},{4,8},{8,12},{12,16},{16,20},{20,24},{24,28},{28,0},{1,5},{5... | collective-permute-start | bytes 2359304 | tf_op jit(solution)/shard_map/ppermute | solution.py:44
  6.8 0.0 copy-done.3
  6.9 0.1 turn.1.turned_ref
  7.0 0.0 copy-done
  7.0 0.0 copy-done.2
  7.0 0.0 copy-start.5
  7.0 1.8 %project.1.refs_0_ = bf16[80,512]{1,0:T(8,128)(2,1)S(1)} custom-call(bf16[64,6144]{1,0:T(8,128)(2,1)S(1)} %copy-done.2, bf16[512,6144]{1,0:T(8,128)(2,1)S(1)} %bitcast.2, bf16[16,512]{1,0:T(8,128)(2,1)S(1)} %turn.1.turned_ref), custom_call_target="tpu_custom_call" | custom-call | tf_op jit(solution)/shard_map/project/pallas_call | solution.py:30
  8.9 2.5 %collective-permute-start.4 = (bf16[80,512]{1,0:T(8,128)(2,1)S(1)}, bf16[80,512]{1,0:T(8,128)(2,1)S(1)}, u32[]{:S(2)}, u32[]{:S(2)}) collective-permute-start(bf16[80,512]{1,0:T(8,128)(2,1)S(1)} %project.1.refs_0_), channel_id=1, source_target_pairs={{0,3},{1,2},{2,1},{3,0},{4,7},{5,6},{6,5},{7,4},{8,11},{9,10},{10,... | collective-permute-start | bytes 245768 | tf_op jit(solution)/shard_map/ppermute | solution.py:65
  11.4 0.5 %collective-permute-start.8 = (bf16[80,512]{1,0:T(8,128)(2,1)S(1)}, bf16[80,512]{1,0:T(8,128)(2,1)S(1)}, u32[]{:S(2)}, u32[]{:S(2)}) collective-permute-start(bf16[80,512]{1,0:T(8,128)(2,1)S(1)} %project.1.refs_0_), channel_id=1, source_target_pairs={{0,2},{1,3},{2,0},{3,1},{4,6},{5,7},{6,4},{7,5},{8,10},{9,11},{10,... | collective-permute-start | bytes 245768 | tf_op jit(solution)/shard_map/ppermute | solution.py:65
  11.9 0.5 %collective-permute-start.7 = (bf16[80,512]{1,0:T(8,128)(2,1)S(1)}, bf16[80,512]{1,0:T(8,128)(2,1)S(1)}, u32[]{:S(2)}, u32[]{:S(2)}) collective-permute-start(bf16[80,512]{1,0:T(8,128)(2,1)S(1)} %project.1.refs_0_), channel_id=1, source_target_pairs={{0,1},{1,0},{2,3},{3,2},{4,5},{5,4},{6,7},{7,6},{8,9},{9,8},{10,11... | collective-permute-start | bytes 245768 | tf_op jit(solution)/shard_map/ppermute | solution.py:65
  12.4 0.0 copy-done.5
  12.4 1.1 %match.1 = (bf16[256,512]{1,0:T(8,128)(2,1)S(1)}, bf16[256,512]{1,0:T(8,128)(2,1)S(1)}, bf16[256,512]{1,0:T(8,128)(2,1)S(1)}, bf16[256,512]{1,0:T(8,128)(2,1)S(1...) custom-call(s32[4,32]{1,0:T(4,128)S(1)} %copy-done.5), custom_call_target="tpu_custom_call" | custom-call | tf_op jit(solution)/shard_map/match/pallas_call | solution.py:30
  13.6 1.2 %collective-permute-done.4.refs_0_.refs_3_ = bf16[80,512]{1,0:T(8,128)(2,1)S(1)} collective-permute-done((bf16[80,512]{1,0:T(8,128)(2,1)S(1)}, bf16[80,512]{1,0:T(8,128)(2,1)S(1)}, u32[]{:S(2)}, u32[]{:S(2)}) %collective-permute-start.4) | collective-permute-done | bytes 81952 | tf_op jit(solution)/shard_map/ppermute | solution.py:65
  14.8 0.0 collective-permute-done.block_ref.one
  14.8 0.1 halves.3
  14.9 0.5 %collective-permute-start.5 = (bf16[32,6144]{1,0:T(8,128)(2,1)S(1)}, bf16[32,6144]{1,0:T(8,128)(2,1)S(1)}, u32[]{:S(2)}, u32[]{:S(2)}) collective-permute-start(bf16[32,6144]{1,0:T(8,128)(2,1)S(1)} %get-tuple-element.22), channel_id=1, source_target_pairs={{0,4},{4,0},{8,12},{12,8},{16,20},{20,16},{24,28},{28,24},{1,5},{5... | collective-permute-start | bytes 1179656 | tf_op jit(solution)/shard_map/ppermute | solution.py:49
  15.4 0.1 collective-permute-start.6
  15.5 1.4 %collective-permute-done.8.refs_2_ = bf16[80,512]{1,0:T(8,128)(2,1)S(1)} collective-permute-done((bf16[80,512]{1,0:T(8,128)(2,1)S(1)}, bf16[80,512]{1,0:T(8,128)(2,1)S(1)}, u32[]{:S(2)}, u32[]{:S(2)}) %collective-permute-start.8) | collective-permute-done | bytes 81952 | tf_op jit(solution)/shard_map/ppermute | solution.py:65
  16.9 0.1 collective-permute-done.7.refs_1_
  17.0 0.9 %couple.1.after_ref.mine = bf16[64,512]{1,0:T(8,128)(2,1)S(1)} custom-call(bf16[80,512]{1,0:T(8,128)(2,1)S(1)} %project.1.refs_0_, bf16[80,512]{1,0:T(8,128)(2,1)S(1)} %collective-permute-done.7.refs_1_, bf16[80,512]{1,0:T(8,128)(2,1)S(1)} %collective-permute-done.8.refs_2_, bf16[80,512]{1,0:T(8,128)(2,1)S(1)} %collective-permute-done.4.refs_0_.refs_3_, ...), custom_call_target="tpu_custom_call" | custom-call | flops 4000000000 | tf_op jit(solution)/shard_map/couple/pallas_call | solution.py:30
  17.9 0.0 copy-start.4
  17.9 1.6 %collective-permute-start.10 = (bf16[64,512]{1,0:T(8,128)(2,1)S(1)}, bf16[64,512]{1,0:T(8,128)(2,1)S(1)}, u32[]{:S(2)}, u32[]{:S(2)}) collective-permute-start(bf16[64,512]{1,0:T(8,128)(2,1)S(1)} %couple.1.after_ref.mine), channel_id=1, source_target_pairs={{0,8},{4,12},{8,16},{12,20},{16,24},{20,28},{24,0},{28,4},{1,9},{5... | collective-permute-start | bytes 196616 | tf_op jit(solution)/shard_map/ppermute | solution.py:44
  19.6 0.0 collective-permute-done.5.upper_ref.upper
  19.6 0.0 collective-permute-done.6.lower_ref.lower
  19.6 0.1 collective-permute-start.9
  19.7 4.5 %collective-permute-done.10.mine_two.two = bf16[64,512]{1,0:T(8,128)(2,1)S(1)} collective-permute-done((bf16[64,512]{1,0:T(8,128)(2,1)S(1)}, bf16[64,512]{1,0:T(8,128)(2,1)S(1)}, u32[]{:S(2)}, u32[]{:S(2)}) %collective-permute-start.10) | collective-permute-done | bytes 65568 | tf_op jit(solution)/shard_map/ppermute | solution.py:44
  24.2 0.0 collective-permute-done.3.two
  24.2 0.1 choose.1
  24.3 0.1 collective-permute-start.11
  24.4 0.5 %collective-permute-start.13 = (bf16[64,512]{1,0:T(8,128)(2,1)S(1)}, bf16[64,512]{1,0:T(8,128)(2,1)S(1)}, u32[]{:S(2)}, u32[]{:S(2)}) collective-permute-start(bf16[64,512]{1,0:T(8,128)(2,1)S(1)} %collective-permute-done.10.mine_two.two), channel_id=1, source_target_pairs={{0,4},{4,8},{8,12},{12,16},{16,20},{20,24},{24,28},{28,0},{1,5},{5... | collective-permute-start | bytes 196616 | tf_op jit(solution)/shard_map/ppermute | solution.py:44
  24.9 0.1 collective-permute-start.12
  24.9 5.9 %collective-permute-done.9.three_a = bf16[48,6144]{1,0:T(8,128)(2,1)S(1)} collective-permute-done((bf16[48,6144]{1,0:T(8,128)(2,1)S(1)}, bf16[48,6144]{1,0:T(8,128)(2,1)S(1)}, u32[]{:S(2)}, u32[]{:S(2)}) %collective-permute-start.9) | collective-permute-done | bytes 589856 | tf_op jit(solution)/shard_map/ppermute | solution.py:44
  30.8 0.0 copy-done.4
  30.8 0.8 %gather.1.after_ref.partial_ref = f32[64,6144]{1,0:T(8,128)S(1)} custom-call(bf16[64,256]{1,0:T(8,128)(2,1)S(1)} %copy-done.4, bf16[64,6144]{1,0:T(8,128)(2,1)S(1)} %copy-done.2, bf16[64,6144]{1,0:T(8,128)(2,1)S(1)} %collective-permute-done.block_ref.one, bf16[64,6144]{1,0:T(8,128)(2,1)S(1)} %collective-permute-done.3.two, ...), custom_call_target="tpu_custom_call" | custom-call | flops 4499999744 | tf_op jit(solution)/shard_map/gather/pallas_call | solution.py:30
  31.6 0.0 collective-permute-done.13.three
  31.6 0.0 collective-permute-done.11.swap_ref
  31.6 1.4 %apply.1.applied = f32[64,6144]{1,0:T(8,128)S(1)} custom-call(bf16[64,256]{1,0:T(8,128)(2,1)S(1)} %copy-done.4, bf16[64,512]{1,0:T(8,128)(2,1)S(1)} %couple.1.after_ref.mine, bf16[80,6144]{1,0:T(8,128)(2,1)S(1)} %collective-permute-done.11.swap_ref, bf16[64,512]{1,0:T(8,128)(2,1)S(1)} %collective-permute-done.10.mine_two.two, ...), custom_call_target="tpu_custom_call" | custom-call | flops 5000000000 | tf_op jit(solution)/shard_map/apply/pallas_call | solution.py:30
  33.1 0.5 %collective-permute-done.12.last_ref = bf16[16,6144]{1,0:T(8,128)(2,1)S(1)} collective-permute-done((bf16[16,6144]{1,0:T(8,128)(2,1)S(1)}, bf16[16,6144]{1,0:T(8,128)(2,1)S(1)}, u32[]{:S(2)}, u32[]{:S(2)}) %collective-permute-start.12) | collective-permute-done | bytes 196640 | tf_op jit(solution)/shard_map/ppermute | solution.py:44
  33.6 1.3 %finish.1 = bf16[64,6144]{1,0:T(8,128)(2,1)} custom-call(bf16[64,256]{1,0:T(8,128)(2,1)S(1)} %copy-done.4, f32[64,6144]{1,0:T(8,128)S(1)} %gather.1.after_ref.partial_ref, bf16[80,6144]{1,0:T(8,128)(2,1)S(1)} %collective-permute-done.11.swap_ref, bf16[16,6144]{1,0:T(8,128)(2,1)S(1)} %collective-permute-done.12.last_ref, f32[64,6144]{1,0:T(8,128)S(1)} %apply.1.applied), custom_call_target="tpu_custom_call" | custom-call | tf_op jit(solution)/shard_map/finish/pallas_call | solution.py:387
  (1 shorter events, 0.0 us)
Async XLA Ops:
  0.0 14.8 %collective-permute-start = (bf16[64,6144]{1,0:T(8,128)(2,1)}, bf16[64,6144]{1,0:T(8,128)(2,1)S(1)}, u32[]{:S(2)}, u32[]{:S(2)}) collective-permute-start(bf16[64,6144]{1,0:T(8,128)(2,1)} %own.1), channel_id=1, source_target_pairs={{0,4},{4,8},{8,12},{12,16},{16,20},{20,24},{24,28},{28,0},{1,5},{5... | collective-permute-start | bytes 2359304 | tf_op jit(solution)/shard_map/ppermute | solution.py:44
  0.5 1.1 %copy-start.1 = (bf16[64,6144]{1,0:T(8,128)(2,1)S(1)}, bf16[64,6144]{1,0:T(8,128)(2,1)}, u32[]{:S(2)}) copy-start(bf16[64,6144]{1,0:T(8,128)(2,1)} %own.1) | copy-start | bytes 2359300
  1.6 5.4 %copy-start = (bf16[32,16,6144]{2,1,0:T(8,128)(2,1)S(1)}, bf16[32,16,6144]{2,1,0:T(8,128)(2,1)}, u32[]{:S(2)}) copy-start(bf16[32,16,6144]{2,1,0:T(8,128)(2,1)} %param.7) | copy-start | bytes 18874372
  1.6 5.2 %copy-start.3 = (f32[16,16,16]{2,1,0:T(8,128)S(1)}, f32[16,16,16]{2,1,0:T(8,128)}, u32[]{:S(2)}) copy-start(f32[16,16,16]{2,1,0:T(8,128)} %param.8) | copy-start | bytes 49156
  1.7 5.3 %copy-start.2 = (bf16[64,6144]{1,0:T(8,128)(2,1)S(1)}, bf16[64,6144]{1,0:T(8,128)(2,1)}, u32[]{:S(2)}) copy-start(bf16[64,6144]{1,0:T(8,128)(2,1)} %own.1) | copy-start | bytes 2359300
  1.7 4.1 %collective-permute-start.1 = (bf16[32,6144]{1,0:T(8,128)(2,1)S(1)}, bf16[32,6144]{1,0:T(8,128)(2,1)S(1)}, u32[]{:S(2)}, u32[]{:S(2)}) collective-permute-start(bf16[32,6144]{1,0:T(8,128)(2,1)S(1)} %get-tuple-element.19), channel_id=1, source_target_pairs={{0,4},{4,0},{8,12},{12,8},{16,20},{20,16},{24,28},{28,24},{1,5},{5... | collective-permute-start | bytes 1179656 | tf_op jit(solution)/shard_map/ppermute | solution.py:49
  4.5 1.9 %collective-permute-start.2 = (bf16[32,6144]{1,0:T(8,128)(2,1)S(1)}, bf16[32,6144]{1,0:T(8,128)(2,1)S(1)}, u32[]{:S(2)}, u32[]{:S(2)}) collective-permute-start(bf16[32,6144]{1,0:T(8,128)(2,1)S(1)} %get-tuple-element.20), channel_id=1, source_target_pairs={{0,4},{4,0},{8,12},{12,8},{16,20},{20,16},{24,28},{28,24},{1,5},{5... | collective-permute-start | bytes 1179656 | tf_op jit(solution)/shard_map/ppermute | solution.py:49
  6.4 17.8 %collective-permute-start.3 = (bf16[64,6144]{1,0:T(8,128)(2,1)S(1)}, bf16[64,6144]{1,0:T(8,128)(2,1)S(1)}, u32[]{:S(2)}, u32[]{:S(2)}) collective-permute-start(bf16[64,6144]{1,0:T(8,128)(2,1)S(1)} %hold.2), channel_id=1, source_target_pairs={{0,4},{4,8},{8,12},{12,16},{16,20},{20,24},{24,28},{28,0},{1,5},{5... | collective-permute-start | bytes 2359304 | tf_op jit(solution)/shard_map/ppermute | solution.py:44
  7.0 5.4 %copy-start.5 = (s32[4,32]{1,0:T(4,128)S(1)}, s32[4,32]{1,0:T(4,128)}, u32[]{:S(2)}) copy-start(s32[4,32]{1,0:T(4,128)} %slot_ref.1) | copy-start | bytes 1540
  8.9 5.9 %collective-permute-start.4 = (bf16[80,512]{1,0:T(8,128)(2,1)S(1)}, bf16[80,512]{1,0:T(8,128)(2,1)S(1)}, u32[]{:S(2)}, u32[]{:S(2)}) collective-permute-start(bf16[80,512]{1,0:T(8,128)(2,1)S(1)} %project.1.refs_0_), channel_id=1, source_target_pairs={{0,3},{1,2},{2,1},{3,0},{4,7},{5,6},{6,5},{7,4},{8,11},{9,10},{10,... | collective-permute-start | bytes 245768 | tf_op jit(solution)/shard_map/ppermute | solution.py:65
  11.4 5.5 %collective-permute-start.8 = (bf16[80,512]{1,0:T(8,128)(2,1)S(1)}, bf16[80,512]{1,0:T(8,128)(2,1)S(1)}, u32[]{:S(2)}, u32[]{:S(2)}) collective-permute-start(bf16[80,512]{1,0:T(8,128)(2,1)S(1)} %project.1.refs_0_), channel_id=1, source_target_pairs={{0,2},{1,3},{2,0},{3,1},{4,6},{5,7},{6,4},{7,5},{8,10},{9,11},{10,... | collective-permute-start | bytes 245768 | tf_op jit(solution)/shard_map/ppermute | solution.py:65
  11.9 5.1 %collective-permute-start.7 = (bf16[80,512]{1,0:T(8,128)(2,1)S(1)}, bf16[80,512]{1,0:T(8,128)(2,1)S(1)}, u32[]{:S(2)}, u32[]{:S(2)}) collective-permute-start(bf16[80,512]{1,0:T(8,128)(2,1)S(1)} %project.1.refs_0_), channel_id=1, source_target_pairs={{0,1},{1,0},{2,3},{3,2},{4,5},{5,4},{6,7},{7,6},{8,9},{9,8},{10,11... | collective-permute-start | bytes 245768 | tf_op jit(solution)/shard_map/ppermute | solution.py:65
  14.9 4.7 %collective-permute-start.5 = (bf16[32,6144]{1,0:T(8,128)(2,1)S(1)}, bf16[32,6144]{1,0:T(8,128)(2,1)S(1)}, u32[]{:S(2)}, u32[]{:S(2)}) collective-permute-start(bf16[32,6144]{1,0:T(8,128)(2,1)S(1)} %get-tuple-element.22), channel_id=1, source_target_pairs={{0,4},{4,0},{8,12},{12,8},{16,20},{20,16},{24,28},{28,24},{1,5},{5... | collective-permute-start | bytes 1179656 | tf_op jit(solution)/shard_map/ppermute | solution.py:49
  15.4 4.2 %collective-permute-start.6 = (bf16[32,6144]{1,0:T(8,128)(2,1)S(1)}, bf16[32,6144]{1,0:T(8,128)(2,1)S(1)}, u32[]{:S(2)}, u32[]{:S(2)}) collective-permute-start(bf16[32,6144]{1,0:T(8,128)(2,1)S(1)} %get-tuple-element.23), channel_id=1, source_target_pairs={{0,4},{4,0},{8,12},{12,8},{16,20},{20,16},{24,28},{28,24},{1,5},{5... | collective-permute-start | bytes 1179656 | tf_op jit(solution)/shard_map/ppermute | solution.py:49
  17.9 12.9 %copy-start.4 = (bf16[64,256]{1,0:T(8,128)(2,1)S(1)}, bf16[64,256]{1,0:T(8,128)(2,1)}, u32[]{:S(2)}) copy-start(bf16[64,256]{1,0:T(8,128)(2,1)} %rot_ref.5) | copy-start | bytes 98308
  17.9 6.3 %collective-permute-start.10 = (bf16[64,512]{1,0:T(8,128)(2,1)S(1)}, bf16[64,512]{1,0:T(8,128)(2,1)S(1)}, u32[]{:S(2)}, u32[]{:S(2)}) collective-permute-start(bf16[64,512]{1,0:T(8,128)(2,1)S(1)} %couple.1.after_ref.mine), channel_id=1, source_target_pairs={{0,8},{4,12},{8,16},{12,20},{16,24},{20,28},{24,0},{28,4},{1,9},{5... | collective-permute-start | bytes 196616 | tf_op jit(solution)/shard_map/ppermute | solution.py:44
  19.6 11.2 %collective-permute-start.9 = (bf16[48,6144]{1,0:T(8,128)(2,1)S(1)}, bf16[48,6144]{1,0:T(8,128)(2,1)S(1)}, u32[]{:S(2)}, u32[]{:S(2)}) collective-permute-start(bf16[48,6144]{1,0:T(8,128)(2,1)S(1)} %hold.3), channel_id=1, source_target_pairs={{0,4},{4,8},{8,12},{12,16},{16,20},{20,24},{24,28},{28,0},{1,5},{5... | collective-permute-start | bytes 1769480 | tf_op jit(solution)/shard_map/ppermute | solution.py:44
  24.3 7.3 %collective-permute-start.11 = (bf16[80,6144]{1,0:T(8,128)(2,1)S(1)}, bf16[80,6144]{1,0:T(8,128)(2,1)S(1)}, u32[]{:S(2)}, u32[]{:S(2)}) collective-permute-start(bf16[80,6144]{1,0:T(8,128)(2,1)S(1)} %get-tuple-element.31), channel_id=1, source_target_pairs={{0,4},{4,0},{8,12},{12,8},{16,20},{20,16},{24,28},{28,24},{1,5},{5... | collective-permute-start | bytes 2949128 | tf_op jit(solution)/shard_map/ppermute | solution.py:49
  24.4 7.2 %collective-permute-start.13 = (bf16[64,512]{1,0:T(8,128)(2,1)S(1)}, bf16[64,512]{1,0:T(8,128)(2,1)S(1)}, u32[]{:S(2)}, u32[]{:S(2)}) collective-permute-start(bf16[64,512]{1,0:T(8,128)(2,1)S(1)} %collective-permute-done.10.mine_two.two), channel_id=1, source_target_pairs={{0,4},{4,8},{8,12},{12,16},{16,20},{20,24},{24,28},{28,0},{1,5},{5... | collective-permute-start | bytes 196616 | tf_op jit(solution)/shard_map/ppermute | solution.py:44
  24.9 8.7 %collective-permute-start.12 = (bf16[16,6144]{1,0:T(8,128)(2,1)S(1)}, bf16[16,6144]{1,0:T(8,128)(2,1)S(1)}, u32[]{:S(2)}, u32[]{:S(2)}) collective-permute-start(bf16[16,6144]{1,0:T(8,128)(2,1)S(1)} %get-tuple-element.32), channel_id=1, source_target_pairs={{0,4},{4,8},{8,12},{12,16},{16,20},{20,24},{24,28},{28,0},{1,5},{5... | collective-permute-start | bytes 589832 | tf_op jit(solution)/shard_map/ppermute | solution.py:44

commit v9 on v7

--- a/solution.py
+++ b/solution.py
@@ -351,25 +351,28 @@
         )
 
 
-def finish_kernel(
-    rot_ref, partial_ref, swap_ref, last_ref, applied, out_hbm, out_ref, sems
-):
+def add_kernel(rot_ref, partial_ref, swap_ref, applied, out_ref):
     width, points = out_ref.shape
-    rows = last_ref.shape[0]
+    turn = where_even(rot_ref[:, 3 * width : 4 * width], False)
+    tile = tile_of(points, 1024)
+    for at in range(0, points, tile):
+        here = slice(at, at + tile)
+        out_ref[:, here] = partial_ref[:, here] + jnp.dot(
+            turn, swap_ref[:width, here], preferred_element_type=F32
+        )
+
+
+def finish_kernel(rot_ref, partial_ref, last_ref, applied, out_hbm, out_ref, sems):
+    width, points = out_ref.shape
     pieces = sems.shape[0]
     tile = points // pieces
-    turn = jnp.concatenate(
-        [
-            where_even(rot_ref[:, 3 * width : 4 * width], False),
-            where_even(rot_ref[:, 4 * width - rows : 4 * width], True),
-        ],
-        axis=1,
-    )
+    turn = where_even(rot_ref[:, 4 * width - last_ref.shape[0] : 4 * width], True)
     copies = []
     for i in range(pieces):
         here = slice(i * tile, (i + 1) * tile)
-        last = jnp.concatenate([swap_ref[:width, here], last_ref[:, here]], axis=0)
-        rotated = partial_ref[:, here] + jnp.dot(turn, last, preferred_element_type=F32)
+        rotated = partial_ref[:, here] + jnp.dot(
+            turn, last_ref[:, here], preferred_element_type=F32
+        )
         added = rotated.astype(BF16).astype(F32) + applied[:, here]
         out_ref[:, here] = added.astype(out_ref.dtype)
         part = (slice(None), pl.ds(i * tile, tile))
@@ -424,7 +427,9 @@
         [rotation, mine, swap, mine_two, mine_three, proj, partial],
         cost=APPLY,
     )[0]
-    return finish(rotation, partial, swap, three_b, applied)
+    outs = [(partial.shape, F32)]
+    partial = call(add_kernel, "add", outs, [rotation, partial, swap, applied])[0]
+    return finish(rotation, partial, three_b, applied)
 
 
 def solution(mesh):

time: 34.9 us -> 34.9 us (level)
  Pallas kernels: 7.73 us -> 8.14 us
  waiting for transfers between devices: 15.5 us -> 15.1 us
    ppermute x6, waiting for transfers between devices: 10.9 us -> 10.5 us  [along_bands(): lax.ppermute(block, 'band', [(i, (i + distance) % count) for i in range(c...]
    pallas_call x11 -> x12, Pallas kernels: 6.55 us -> 6.98 us  [call(): pl.pallas_call(kernel, in_specs=[first] + [VMEM] * (len(args) - 1), out_s...]
  transfers between devices with their start and end apart: 14 -> 14, of which waited for: 8 -> 8; matrix products, arithmetic and copies ran while one was open for 0% -> 0% of each run, Pallas kernels for 19% -> 20%
where the time goes in v9:
time: 34.9 us; the launch traced here: 34.7 us
  waiting for transfers between devices  15.1 us (43%)
  starting transfers between devices  10.2 us (29%)
  Pallas kernels  8.14 us (23%)
  local copies, waits for them, and re-layouts  1.17 us (3%)
    ppermute x6, waiting for transfers between devices, along_bands(): lax.ppermute(block, 'band', [(i, (i + distance) % count) for i in range(c...  10.5 us
    pallas_call x12, Pallas kernels, call(): pl.pallas_call(kernel, in_specs=[first] + [VMEM] * (len(args) - 1), out_s...  6.98 us
    ppermute x3, starting transfers between devices, from_all_domains(): return [block] + [lax.ppermute(block, 'dom', route) for route in routes]  3.55 us
    ppermute x5, starting transfers between devices, swapped(): return lax.ppermute(block, 'band', [(i, i ^ 1) for i in range(count)])  3.54 us
    ppermute x6, starting transfers between devices, along_bands(): lax.ppermute(block, 'band', [(i, (i + distance) % count) for i in range(c...  3.13 us
    ppermute x3, waiting for transfers between devices, from_all_domains(): return [block] + [lax.ppermute(block, 'dom', route) for route in routes]  2.77 us
    ppermute x5, waiting for transfers between devices, swapped(): return lax.ppermute(block, 'band', [(i, i ^ 1) for i in range(count)])  1.84 us
    unnamed x12, local copies, waits for them, and re-layouts  1.17 us
  transfers between devices with their start and end apart: 14, of which 8 were waited for; matrix products, arithmetic and copies ran while one was open for 0% of the time, Pallas kernels for 20%

profile of v9, /device:TPU:0, one launch (start us, length us, event | category | flops | bytes accessed | tf_op | source)
XLA Modules:
  0.0 34.7 jit_solution(52091028269060756)
XLA Ops:
  0.0 0.5 %collective-permute-start = (bf16[64,6144]{1,0:T(8,128)(2,1)}, bf16[64,6144]{1,0:T(8,128)(2,1)S(1)}, u32[]{:S(2)}, u32[]{:S(2)}) collective-permute-start(bf16[64,6144]{1,0:T(8,128)(2,1)} %own.1), channel_id=1, source_target_pairs={{0,4},{4,8},{8,12},{12,16},{16,20},{20,24},{24,28},{28,0},{1,5},{5... | collective-permute-start | bytes 2359304 | tf_op jit(solution)/shard_map/ppermute | solution.py:44
  0.5 0.0 copy-start.1
  0.5 1.1 %copy-done.1 = bf16[64,6144]{1,0:T(8,128)(2,1)S(1)} copy-done((bf16[64,6144]{1,0:T(8,128)(2,1)S(1)}, bf16[64,6144]{1,0:T(8,128)(2,1)}, u32[]{:S(2)}) %copy-start.1) | copy-done | bytes 786456
  1.6 0.0 copy-start
  1.6 0.1 halves.2
  1.6 0.0 copy-start.4
  1.7 0.0 copy-start.2
  1.7 2.8 %collective-permute-start.1 = (bf16[32,6144]{1,0:T(8,128)(2,1)S(1)}, bf16[32,6144]{1,0:T(8,128)(2,1)S(1)}, u32[]{:S(2)}, u32[]{:S(2)}) collective-permute-start(bf16[32,6144]{1,0:T(8,128)(2,1)S(1)} %get-tuple-element.19), channel_id=1, source_target_pairs={{0,4},{4,0},{8,12},{12,8},{16,20},{20,16},{24,28},{28,24},{1,5},{5... | collective-permute-start | bytes 1179656 | tf_op jit(solution)/shard_map/ppermute | solution.py:49
  4.5 0.1 collective-permute-start.2
  4.5 1.3 %collective-permute-done.1.upper_ref.after_ref = bf16[32,6144]{1,0:T(8,128)(2,1)S(1)} collective-permute-done((bf16[32,6144]{1,0:T(8,128)(2,1)S(1)}, bf16[32,6144]{1,0:T(8,128)(2,1)S(1)}, u32[]{:S(2)}, u32[]{:S(2)}) %collective-permute-start.1) | collective-permute-done | bytes 393248 | tf_op jit(solution)/shard_map/ppermute | solution.py:49
  5.8 0.6 %collective-permute-done.2.lower_ref = bf16[32,6144]{1,0:T(8,128)(2,1)S(1)} collective-permute-done((bf16[32,6144]{1,0:T(8,128)(2,1)S(1)}, bf16[32,6144]{1,0:T(8,128)(2,1)S(1)}, u32[]{:S(2)}, u32[]{:S(2)}) %collective-permute-start.2) | collective-permute-done | bytes 393248 | tf_op jit(solution)/shard_map/ppermute | solution.py:49
  6.4 0.1 hold.2
  6.4 0.4 %collective-permute-start.3 = (bf16[64,6144]{1,0:T(8,128)(2,1)S(1)}, bf16[64,6144]{1,0:T(8,128)(2,1)S(1)}, u32[]{:S(2)}, u32[]{:S(2)}) collective-permute-start(bf16[64,6144]{1,0:T(8,128)(2,1)S(1)} %hold.2), channel_id=1, source_target_pairs={{0,4},{4,8},{8,12},{12,16},{16,20},{20,24},{24,28},{28,0},{1,5},{5... | collective-permute-start | bytes 2359304 | tf_op jit(solution)/shard_map/ppermute | solution.py:44
  6.8 0.0 copy-done.4
  6.9 0.1 turn.1.turned_ref
  7.0 0.0 copy-done
  7.0 0.0 copy-done.2
  7.0 0.0 copy-start.5
  7.0 1.8 %project.1.refs_0_ = bf16[80,512]{1,0:T(8,128)(2,1)S(1)} custom-call(bf16[64,6144]{1,0:T(8,128)(2,1)S(1)} %copy-done.2, bf16[512,6144]{1,0:T(8,128)(2,1)S(1)} %bitcast.2, bf16[16,512]{1,0:T(8,128)(2,1)S(1)} %turn.1.turned_ref), custom_call_target="tpu_custom_call" | custom-call | tf_op jit(solution)/shard_map/project/pallas_call | solution.py:30
  8.9 2.5 %collective-permute-start.4 = (bf16[80,512]{1,0:T(8,128)(2,1)S(1)}, bf16[80,512]{1,0:T(8,128)(2,1)S(1)}, u32[]{:S(2)}, u32[]{:S(2)}) collective-permute-start(bf16[80,512]{1,0:T(8,128)(2,1)S(1)} %project.1.refs_0_), channel_id=1, source_target_pairs={{0,3},{1,2},{2,1},{3,0},{4,7},{5,6},{6,5},{7,4},{8,11},{9,10},{10,... | collective-permute-start | bytes 245768 | tf_op jit(solution)/shard_map/ppermute | solution.py:65
  11.4 0.5 %collective-permute-start.8 = (bf16[80,512]{1,0:T(8,128)(2,1)S(1)}, bf16[80,512]{1,0:T(8,128)(2,1)S(1)}, u32[]{:S(2)}, u32[]{:S(2)}) collective-permute-start(bf16[80,512]{1,0:T(8,128)(2,1)S(1)} %project.1.refs_0_), channel_id=1, source_target_pairs={{0,2},{1,3},{2,0},{3,1},{4,6},{5,7},{6,4},{7,5},{8,10},{9,11},{10,... | collective-permute-start | bytes 245768 | tf_op jit(solution)/shard_map/ppermute | solution.py:65
  11.9 0.5 %collective-permute-start.7 = (bf16[80,512]{1,0:T(8,128)(2,1)S(1)}, bf16[80,512]{1,0:T(8,128)(2,1)S(1)}, u32[]{:S(2)}, u32[]{:S(2)}) collective-permute-start(bf16[80,512]{1,0:T(8,128)(2,1)S(1)} %project.1.refs_0_), channel_id=1, source_target_pairs={{0,1},{1,0},{2,3},{3,2},{4,5},{5,4},{6,7},{7,6},{8,9},{9,8},{10,11... | collective-permute-start | bytes 245768 | tf_op jit(solution)/shard_map/ppermute | solution.py:65
  12.4 0.0 copy-done.5
  12.4 1.1 %match.1 = (bf16[256,512]{1,0:T(8,128)(2,1)S(1)}, bf16[256,512]{1,0:T(8,128)(2,1)S(1)}, bf16[256,512]{1,0:T(8,128)(2,1)S(1)}, bf16[256,512]{1,0:T(8,128)(2,1)S(1...) custom-call(s32[4,32]{1,0:T(4,128)S(1)} %copy-done.5), custom_call_target="tpu_custom_call" | custom-call | tf_op jit(solution)/shard_map/match/pallas_call | solution.py:30
  13.6 1.2 %collective-permute-done.4.refs_0_.refs_3_ = bf16[80,512]{1,0:T(8,128)(2,1)S(1)} collective-permute-done((bf16[80,512]{1,0:T(8,128)(2,1)S(1)}, bf16[80,512]{1,0:T(8,128)(2,1)S(1)}, u32[]{:S(2)}, u32[]{:S(2)}) %collective-permute-start.4) | collective-permute-done | bytes 81952 | tf_op jit(solution)/shard_map/ppermute | solution.py:65
  14.8 0.0 collective-permute-done.block_ref.one
  14.8 0.1 halves.3
  14.9 0.5 %collective-permute-start.5 = (bf16[32,6144]{1,0:T(8,128)(2,1)S(1)}, bf16[32,6144]{1,0:T(8,128)(2,1)S(1)}, u32[]{:S(2)}, u32[]{:S(2)}) collective-permute-start(bf16[32,6144]{1,0:T(8,128)(2,1)S(1)} %get-tuple-element.22), channel_id=1, source_target_pairs={{0,4},{4,0},{8,12},{12,8},{16,20},{20,16},{24,28},{28,24},{1,5},{5... | collective-permute-start | bytes 1179656 | tf_op jit(solution)/shard_map/ppermute | solution.py:49
  15.4 0.1 collective-permute-start.6
  15.5 1.4 %collective-permute-done.8.refs_2_ = bf16[80,512]{1,0:T(8,128)(2,1)S(1)} collective-permute-done((bf16[80,512]{1,0:T(8,128)(2,1)S(1)}, bf16[80,512]{1,0:T(8,128)(2,1)S(1)}, u32[]{:S(2)}, u32[]{:S(2)}) %collective-permute-start.8) | collective-permute-done | bytes 81952 | tf_op jit(solution)/shard_map/ppermute | solution.py:65
  16.9 0.1 collective-permute-done.7.refs_1_
  17.0 0.9 %couple.1.after_ref.mine = bf16[64,512]{1,0:T(8,128)(2,1)S(1)} custom-call(bf16[80,512]{1,0:T(8,128)(2,1)S(1)} %project.1.refs_0_, bf16[80,512]{1,0:T(8,128)(2,1)S(1)} %collective-permute-done.7.refs_1_, bf16[80,512]{1,0:T(8,128)(2,1)S(1)} %collective-permute-done.8.refs_2_, bf16[80,512]{1,0:T(8,128)(2,1)S(1)} %collective-permute-done.4.refs_0_.refs_3_, ...), custom_call_target="tpu_custom_call" | custom-call | flops 4000000000 | tf_op jit(solution)/shard_map/couple/pallas_call | solution.py:30
  17.9 0.0 copy-start.3
  17.9 1.6 %collective-permute-start.10 = (bf16[64,512]{1,0:T(8,128)(2,1)S(1)}, bf16[64,512]{1,0:T(8,128)(2,1)S(1)}, u32[]{:S(2)}, u32[]{:S(2)}) collective-permute-start(bf16[64,512]{1,0:T(8,128)(2,1)S(1)} %couple.1.after_ref.mine), channel_id=1, source_target_pairs={{0,8},{4,12},{8,16},{12,20},{16,24},{20,28},{24,0},{28,4},{1,9},{5... | collective-permute-start | bytes 196616 | tf_op jit(solution)/shard_map/ppermute | solution.py:44
  19.6 0.0 collective-permute-done.5.upper_ref.upper
  19.6 0.0 collective-permute-done.6.lower_ref.lower
  19.6 0.1 collective-permute-start.9
  19.7 4.5 %collective-permute-done.10.mine_two.two = bf16[64,512]{1,0:T(8,128)(2,1)S(1)} collective-permute-done((bf16[64,512]{1,0:T(8,128)(2,1)S(1)}, bf16[64,512]{1,0:T(8,128)(2,1)S(1)}, u32[]{:S(2)}, u32[]{:S(2)}) %collective-permute-start.10) | collective-permute-done | bytes 65568 | tf_op jit(solution)/shard_map/ppermute | solution.py:44
  24.2 0.0 collective-permute-done.3.two
  24.2 0.1 choose.1
  24.3 0.1 collective-permute-start.11
  24.4 0.5 %collective-permute-start.12 = (bf16[64,512]{1,0:T(8,128)(2,1)S(1)}, bf16[64,512]{1,0:T(8,128)(2,1)S(1)}, u32[]{:S(2)}, u32[]{:S(2)}) collective-permute-start(bf16[64,512]{1,0:T(8,128)(2,1)S(1)} %collective-permute-done.10.mine_two.two), channel_id=1, source_target_pairs={{0,4},{4,8},{8,12},{12,16},{16,20},{20,24},{24,28},{28,0},{1,5},{5... | collective-permute-start | bytes 196616 | tf_op jit(solution)/shard_map/ppermute | solution.py:44
  24.9 0.1 collective-permute-start.13
  24.9 5.8 %collective-permute-done.9.three_a = bf16[48,6144]{1,0:T(8,128)(2,1)S(1)} collective-permute-done((bf16[48,6144]{1,0:T(8,128)(2,1)S(1)}, bf16[48,6144]{1,0:T(8,128)(2,1)S(1)}, u32[]{:S(2)}, u32[]{:S(2)}) %collective-permute-start.9) | collective-permute-done | bytes 589856 | tf_op jit(solution)/shard_map/ppermute | solution.py:44
  30.8 0.0 copy-done.3
  30.8 0.8 %gather.1.after_ref.partial_ref = f32[64,6144]{1,0:T(8,128)S(1)} custom-call(bf16[64,256]{1,0:T(8,128)(2,1)S(1)} %copy-done.3, bf16[64,6144]{1,0:T(8,128)(2,1)S(1)} %copy-done.2, bf16[64,6144]{1,0:T(8,128)(2,1)S(1)} %collective-permute-done.block_ref.one, bf16[64,6144]{1,0:T(8,128)(2,1)S(1)} %collective-permute-done.3.two, ...), custom_call_target="tpu_custom_call" | custom-call | flops 4499999744 | tf_op jit(solution)/shard_map/gather/pallas_call | solution.py:30
  31.6 0.0 collective-permute-done.12.three
  31.6 0.0 collective-permute-done.11.swap_ref
  31.6 1.4 %apply.1.applied = f32[64,6144]{1,0:T(8,128)S(1)} custom-call(bf16[64,256]{1,0:T(8,128)(2,1)S(1)} %copy-done.3, bf16[64,512]{1,0:T(8,128)(2,1)S(1)} %couple.1.after_ref.mine, bf16[80,6144]{1,0:T(8,128)(2,1)S(1)} %collective-permute-done.11.swap_ref, bf16[64,512]{1,0:T(8,128)(2,1)S(1)} %collective-permute-done.10.mine_two.two, ...), custom_call_target="tpu_custom_call" | custom-call | flops 5000000000 | tf_op jit(solution)/shard_map/apply/pallas_call | solution.py:30
  33.1 0.4 %add.1.partial_ref = f32[64,6144]{1,0:T(8,128)S(1)} custom-call(bf16[64,256]{1,0:T(8,128)(2,1)S(1)} %copy-done.3, f32[64,6144]{1,0:T(8,128)S(1)} %gather.1.after_ref.partial_ref, bf16[80,6144]{1,0:T(8,128)(2,1)S(1)} %collective-permute-done.11.swap_ref, f32[64,6144]{1,0:T(8,128)S(1)} %apply.1.applied), custom_call_target="tpu_custom_call" | custom-call | tf_op jit(solution)/shard_map/add/pallas_call | solution.py:30
  33.5 0.1 collective-permute-done.13.last_ref
  33.6 1.2 %finish.1 = bf16[64,6144]{1,0:T(8,128)(2,1)} custom-call(bf16[64,256]{1,0:T(8,128)(2,1)S(1)} %copy-done.3, f32[64,6144]{1,0:T(8,128)S(1)} %add.1.partial_ref, bf16[16,6144]{1,0:T(8,128)(2,1)S(1)} %collective-permute-done.13.last_ref, f32[64,6144]{1,0:T(8,128)S(1)} %apply.1.applied), custom_call_target="tpu_custom_call" | custom-call | tf_op jit(solution)/shard_map/finish/pallas_call | solution.py:388
  (1 shorter events, 0.0 us)
Async XLA Ops:
  0.0 14.8 %collective-permute-start = (bf16[64,6144]{1,0:T(8,128)(2,1)}, bf16[64,6144]{1,0:T(8,128)(2,1)S(1)}, u32[]{:S(2)}, u32[]{:S(2)}) collective-permute-start(bf16[64,6144]{1,0:T(8,128)(2,1)} %own.1), channel_id=1, source_target_pairs={{0,4},{4,8},{8,12},{12,16},{16,20},{20,24},{24,28},{28,0},{1,5},{5... | collective-permute-start | bytes 2359304 | tf_op jit(solution)/shard_map/ppermute | solution.py:44
  0.5 1.1 %copy-start.1 = (bf16[64,6144]{1,0:T(8,128)(2,1)S(1)}, bf16[64,6144]{1,0:T(8,128)(2,1)}, u32[]{:S(2)}) copy-start(bf16[64,6144]{1,0:T(8,128)(2,1)} %own.1) | copy-start | bytes 2359300
  1.6 5.4 %copy-start = (bf16[32,16,6144]{2,1,0:T(8,128)(2,1)S(1)}, bf16[32,16,6144]{2,1,0:T(8,128)(2,1)}, u32[]{:S(2)}) copy-start(bf16[32,16,6144]{2,1,0:T(8,128)(2,1)} %param.7) | copy-start | bytes 18874372
  1.6 5.2 %copy-start.4 = (f32[16,16,16]{2,1,0:T(8,128)S(1)}, f32[16,16,16]{2,1,0:T(8,128)}, u32[]{:S(2)}) copy-start(f32[16,16,16]{2,1,0:T(8,128)} %param.8) | copy-start | bytes 49156
  1.7 5.3 %copy-start.2 = (bf16[64,6144]{1,0:T(8,128)(2,1)S(1)}, bf16[64,6144]{1,0:T(8,128)(2,1)}, u32[]{:S(2)}) copy-start(bf16[64,6144]{1,0:T(8,128)(2,1)} %own.1) | copy-start | bytes 2359300
  1.7 4.1 %collective-permute-start.1 = (bf16[32,6144]{1,0:T(8,128)(2,1)S(1)}, bf16[32,6144]{1,0:T(8,128)(2,1)S(1)}, u32[]{:S(2)}, u32[]{:S(2)}) collective-permute-start(bf16[32,6144]{1,0:T(8,128)(2,1)S(1)} %get-tuple-element.19), channel_id=1, source_target_pairs={{0,4},{4,0},{8,12},{12,8},{16,20},{20,16},{24,28},{28,24},{1,5},{5... | collective-permute-start | bytes 1179656 | tf_op jit(solution)/shard_map/ppermute | solution.py:49
  4.5 1.9 %collective-permute-start.2 = (bf16[32,6144]{1,0:T(8,128)(2,1)S(1)}, bf16[32,6144]{1,0:T(8,128)(2,1)S(1)}, u32[]{:S(2)}, u32[]{:S(2)}) collective-permute-start(bf16[32,6144]{1,0:T(8,128)(2,1)S(1)} %get-tuple-element.20), channel_id=1, source_target_pairs={{0,4},{4,0},{8,12},{12,8},{16,20},{20,16},{24,28},{28,24},{1,5},{5... | collective-permute-start | bytes 1179656 | tf_op jit(solution)/shard_map/ppermute | solution.py:49
  6.4 17.8 %collective-permute-start.3 = (bf16[64,6144]{1,0:T(8,128)(2,1)S(1)}, bf16[64,6144]{1,0:T(8,128)(2,1)S(1)}, u32[]{:S(2)}, u32[]{:S(2)}) collective-permute-start(bf16[64,6144]{1,0:T(8,128)(2,1)S(1)} %hold.2), channel_id=1, source_target_pairs={{0,4},{4,8},{8,12},{12,16},{16,20},{20,24},{24,28},{28,0},{1,5},{5... | collective-permute-start | bytes 2359304 | tf_op jit(solution)/shard_map/ppermute | solution.py:44
  7.0 5.4 %copy-start.5 = (s32[4,32]{1,0:T(4,128)S(1)}, s32[4,32]{1,0:T(4,128)}, u32[]{:S(2)}) copy-start(s32[4,32]{1,0:T(4,128)} %slot_ref.1) | copy-start | bytes 1540
  8.9 5.9 %collective-permute-start.4 = (bf16[80,512]{1,0:T(8,128)(2,1)S(1)}, bf16[80,512]{1,0:T(8,128)(2,1)S(1)}, u32[]{:S(2)}, u32[]{:S(2)}) collective-permute-start(bf16[80,512]{1,0:T(8,128)(2,1)S(1)} %project.1.refs_0_), channel_id=1, source_target_pairs={{0,3},{1,2},{2,1},{3,0},{4,7},{5,6},{6,5},{7,4},{8,11},{9,10},{10,... | collective-permute-start | bytes 245768 | tf_op jit(solution)/shard_map/ppermute | solution.py:65
  11.4 5.5 %collective-permute-start.8 = (bf16[80,512]{1,0:T(8,128)(2,1)S(1)}, bf16[80,512]{1,0:T(8,128)(2,1)S(1)}, u32[]{:S(2)}, u32[]{:S(2)}) collective-permute-start(bf16[80,512]{1,0:T(8,128)(2,1)S(1)} %project.1.refs_0_), channel_id=1, source_target_pairs={{0,2},{1,3},{2,0},{3,1},{4,6},{5,7},{6,4},{7,5},{8,10},{9,11},{10,... | collective-permute-start | bytes 245768 | tf_op jit(solution)/shard_map/ppermute | solution.py:65
  11.9 5.1 %collective-permute-start.7 = (bf16[80,512]{1,0:T(8,128)(2,1)S(1)}, bf16[80,512]{1,0:T(8,128)(2,1)S(1)}, u32[]{:S(2)}, u32[]{:S(2)}) collective-permute-start(bf16[80,512]{1,0:T(8,128)(2,1)S(1)} %project.1.refs_0_), channel_id=1, source_target_pairs={{0,1},{1,0},{2,3},{3,2},{4,5},{5,4},{6,7},{7,6},{8,9},{9,8},{10,11... | collective-permute-start | bytes 245768 | tf_op jit(solution)/shard_map/ppermute | solution.py:65
  14.9 4.7 %collective-permute-start.5 = (bf16[32,6144]{1,0:T(8,128)(2,1)S(1)}, bf16[32,6144]{1,0:T(8,128)(2,1)S(1)}, u32[]{:S(2)}, u32[]{:S(2)}) collective-permute-start(bf16[32,6144]{1,0:T(8,128)(2,1)S(1)} %get-tuple-element.22), channel_id=1, source_target_pairs={{0,4},{4,0},{8,12},{12,8},{16,20},{20,16},{24,28},{28,24},{1,5},{5... | collective-permute-start | bytes 1179656 | tf_op jit(solution)/shard_map/ppermute | solution.py:49
  15.4 4.2 %collective-permute-start.6 = (bf16[32,6144]{1,0:T(8,128)(2,1)S(1)}, bf16[32,6144]{1,0:T(8,128)(2,1)S(1)}, u32[]{:S(2)}, u32[]{:S(2)}) collective-permute-start(bf16[32,6144]{1,0:T(8,128)(2,1)S(1)} %get-tuple-element.23), channel_id=1, source_target_pairs={{0,4},{4,0},{8,12},{12,8},{16,20},{20,16},{24,28},{28,24},{1,5},{5... | collective-permute-start | bytes 1179656 | tf_op jit(solution)/shard_map/ppermute | solution.py:49
  17.9 12.9 %copy-start.3 = (bf16[64,256]{1,0:T(8,128)(2,1)S(1)}, bf16[64,256]{1,0:T(8,128)(2,1)}, u32[]{:S(2)}) copy-start(bf16[64,256]{1,0:T(8,128)(2,1)} %rot_ref.7) | copy-start | bytes 98308
  17.9 6.3 %collective-permute-start.10 = (bf16[64,512]{1,0:T(8,128)(2,1)S(1)}, bf16[64,512]{1,0:T(8,128)(2,1)S(1)}, u32[]{:S(2)}, u32[]{:S(2)}) collective-permute-start(bf16[64,512]{1,0:T(8,128)(2,1)S(1)} %couple.1.after_ref.mine), channel_id=1, source_target_pairs={{0,8},{4,12},{8,16},{12,20},{16,24},{20,28},{24,0},{28,4},{1,9},{5... | collective-permute-start | bytes 196616 | tf_op jit(solution)/shard_map/ppermute | solution.py:44
  19.6 11.2 %collective-permute-start.9 = (bf16[48,6144]{1,0:T(8,128)(2,1)S(1)}, bf16[48,6144]{1,0:T(8,128)(2,1)S(1)}, u32[]{:S(2)}, u32[]{:S(2)}) collective-permute-start(bf16[48,6144]{1,0:T(8,128)(2,1)S(1)} %hold.3), channel_id=1, source_target_pairs={{0,4},{4,8},{8,12},{12,16},{16,20},{20,24},{24,28},{28,0},{1,5},{5... | collective-permute-start | bytes 1769480 | tf_op jit(solution)/shard_map/ppermute | solution.py:44
  24.3 7.3 %collective-permute-start.11 = (bf16[80,6144]{1,0:T(8,128)(2,1)S(1)}, bf16[80,6144]{1,0:T(8,128)(2,1)S(1)}, u32[]{:S(2)}, u32[]{:S(2)}) collective-permute-start(bf16[80,6144]{1,0:T(8,128)(2,1)S(1)} %get-tuple-element.31), channel_id=1, source_target_pairs={{0,4},{4,0},{8,12},{12,8},{16,20},{20,16},{24,28},{28,24},{1,5},{5... | collective-permute-start | bytes 2949128 | tf_op jit(solution)/shard_map/ppermute | solution.py:49
  24.4 7.2 %collective-permute-start.12 = (bf16[64,512]{1,0:T(8,128)(2,1)S(1)}, bf16[64,512]{1,0:T(8,128)(2,1)S(1)}, u32[]{:S(2)}, u32[]{:S(2)}) collective-permute-start(bf16[64,512]{1,0:T(8,128)(2,1)S(1)} %collective-permute-done.10.mine_two.two), channel_id=1, source_target_pairs={{0,4},{4,8},{8,12},{12,16},{16,20},{20,24},{24,28},{28,0},{1,5},{5... | collective-permute-start | bytes 196616 | tf_op jit(solution)/shard_map/ppermute | solution.py:44
  24.9 8.7 %collective-permute-start.13 = (bf16[16,6144]{1,0:T(8,128)(2,1)S(1)}, bf16[16,6144]{1,0:T(8,128)(2,1)S(1)}, u32[]{:S(2)}, u32[]{:S(2)}) collective-permute-start(bf16[16,6144]{1,0:T(8,128)(2,1)S(1)} %get-tuple-element.32), channel_id=1, source_target_pairs={{0,4},{4,8},{8,12},{12,16},{16,20},{20,24},{24,28},{28,0},{1,5},{5... | collective-permute-start | bytes 589832 | tf_op jit(solution)/shard_map/ppermute | solution.py:44

commit v10 on v7

--- a/solution.py
+++ b/solution.py
@@ -181,28 +181,37 @@
     return call(kernel, "match", outs, [slot_atom], first=SMEM)
 
 
-def couple_matched_kernel(count, *refs):
-    loads, picks, matches = (refs[i * count : (i + 1) * count] for i in range(3))
-    out_ref, high_ref, low_ref = refs[3 * count :]
+def matched_terms(width, loads, picks, matches):
+    size = picks[0].shape[0]
+    columns = total = None
+    for load, pick, same in zip(loads, picks, matches):
+        parts = [load[width:, i * size : (i + 1) * size] for i in (0, 1)]
+        rows = jnp.dot(jnp.concatenate(parts, 0), pick[...], preferred_element_type=F32)
+        coefs = jnp.dot(load[:width, :], same[...], preferred_element_type=F32)
+        columns = rows if columns is None else columns + rows
+        total = coefs if total is None else total + coefs
+    return columns, total
+
+
+def partly_kernel(count, *refs):
+    groups = [refs[i * count : (i + 1) * count] for i in range(3)]
+    columns_ref, total_ref = refs[3 * count :]
+    columns, total = matched_terms(total_ref.shape[0], *groups)
+    columns_ref[...] = columns
+    total_ref[...] = total
+
+
+def couple_matched_kernel(load, pick, same, columns_ref, total_ref, out_ref, high_ref, low_ref):
     width, flat = out_ref.shape
-    rank = loads[0].shape[0] - width
-    size = picks[0].shape[0]
-
-    columns = None
-    for load, pick in zip(loads, picks):
-        parts = [load[width:, i * size : (i + 1) * size] for i in (0, 1)]
-        term = jnp.dot(jnp.concatenate(parts, 0), pick[...], preferred_element_type=F32)
-        columns = term if columns is None else columns + term
+    rank = load.shape[0] - width
+    columns, total = matched_terms(width, [load], [pick], [same])
+    columns += columns_ref[...]
+    total += total_ref[...]
     lane_slot = lax.broadcasted_iota(jnp.int32, (rank, flat), 1) // rank
     for k in range(flat // rank):
         rows = slice(k * rank, (k + 1) * rank)
         high_ref[rows, :] = jnp.where(lane_slot == k, columns[:rank], 0.0).astype(BF16)
         low_ref[rows, :] = jnp.where(lane_slot == k, columns[rank:], 0.0).astype(BF16)
-
-    total = sum(
-        jnp.dot(load[:width, :], x[...], preferred_element_type=F32)
-        for load, x in zip(loads, matches)
-    )
     high = total.astype(BF16)
     low = (total - high.astype(F32)).astype(BF16)
     terms = ((high, high_ref), (low, high_ref), (high, low_ref))
@@ -211,12 +220,19 @@
 
 
 def couple_matched(loads, matched, width):
-    flat = loads[0].shape[1]
+    count, flat = len(loads), loads[0].shape[1]
+    picks, matches = matched[:count], matched[count:]
+    early = [i for i in range(count) if i != 1]
+    groups = [[x[i] for i in early] for x in (loads, picks, matches)]
+    rank = loads[0].shape[0] - width
+    outs = [((2 * rank, flat), F32), ((width, flat), F32)]
+    kernel = functools.partial(partly_kernel, len(early))
+    partly = call(kernel, "partly", outs, sum(groups, []))
     return call(
-        functools.partial(couple_matched_kernel, len(loads)),
+        couple_matched_kernel,
         "couple",
         [((width, flat), BF16)],
-        [*loads, *matched],
+        [loads[1], picks[1], matches[1], *partly],
         [pltpu.VMEM((flat, flat), BF16)] * 2,
         cost=COUPLE,
     )[0]

time: 34.9 us -> 35.3 us (1.011)
    pallas_call x11 -> x12, Pallas kernels: 6.55 us -> 6.66 us  [call(): pl.pallas_call(kernel, in_specs=[first] + [VMEM] * (len(args) - 1), out_s...]
  transfers between devices with their start and end apart: 14 -> 14, of which waited for: 8 -> 7; matrix products, arithmetic and copies ran while one was open for 0% -> 0% of each run, Pallas kernels for 19% -> 19%
where the time goes in v10:
time: 35.3 us; the launch traced here: 35.1 us
  waiting for transfers between devices  15.8 us (45%)
  starting transfers between devices  10.1 us (29%)
  Pallas kernels  7.85 us (22%)
  local copies, waits for them, and re-layouts  1.17 us (3%)
    ppermute x6, waiting for transfers between devices, along_bands(): lax.ppermute(block, 'band', [(i, (i + distance) % count) for i in range(c...  11 us
    pallas_call x12, Pallas kernels, call(): pl.pallas_call(kernel, in_specs=[first] + [VMEM] * (len(args) - 1), out_s...  6.66 us
    ppermute x3, starting transfers between devices, from_all_domains(): return [block] + [lax.ppermute(block, 'dom', route) for route in routes]  3.55 us
    ppermute x5, starting transfers between devices, swapped(): return lax.ppermute(block, 'band', [(i, i ^ 1) for i in range(count)])  3.51 us
    ppermute x6, starting transfers between devices, along_bands(): lax.ppermute(block, 'band', [(i, (i + distance) % count) for i in range(c...  3.07 us
    ppermute x3, waiting for transfers between devices, from_all_domains(): return [block] + [lax.ppermute(block, 'dom', route) for route in routes]  3.04 us
    ppermute x5, waiting for transfers between devices, swapped(): return lax.ppermute(block, 'band', [(i, i ^ 1) for i in range(count)])  1.84 us
    pallas_call x1, Pallas kernels, finish(): pl.pallas_call(finish_kernel, in_specs=[VMEM] * len(args), out_specs=pl.B...  1.19 us
  transfers between devices with their start and end apart: 14, of which 7 were waited for; matrix products, arithmetic and copies ran while one was open for 0% of the time, Pallas kernels for 19%

profile of v10, /device:TPU:0, one launch (start us, length us, event | category | flops | bytes accessed | tf_op | source)
XLA Modules:
  0.0 35.1 jit_solution(11415459834122881779)
XLA Ops:
  0.0 0.5 %collective-permute-start = (bf16[64,6144]{1,0:T(8,128)(2,1)}, bf16[64,6144]{1,0:T(8,128)(2,1)S(1)}, u32[]{:S(2)}, u32[]{:S(2)}) collective-permute-start(bf16[64,6144]{1,0:T(8,128)(2,1)} %own.1), channel_id=1, source_target_pairs={{0,4},{4,8},{8,12},{12,16},{16,20},{20,24},{24,28},{28,0},{1,5},{5... | collective-permute-start | bytes 2359304 | tf_op jit(solution)/shard_map/ppermute | solution.py:44
  0.5 0.0 copy-start.1
  0.5 1.1 %copy-done.1 = bf16[64,6144]{1,0:T(8,128)(2,1)S(1)} copy-done((bf16[64,6144]{1,0:T(8,128)(2,1)S(1)}, bf16[64,6144]{1,0:T(8,128)(2,1)}, u32[]{:S(2)}) %copy-start.1) | copy-done | bytes 786456
  1.6 0.0 copy-start
  1.6 0.1 halves.2
  1.6 0.0 copy-start.3
  1.7 0.0 copy-start.2
  1.7 2.8 %collective-permute-start.1 = (bf16[32,6144]{1,0:T(8,128)(2,1)S(1)}, bf16[32,6144]{1,0:T(8,128)(2,1)S(1)}, u32[]{:S(2)}, u32[]{:S(2)}) collective-permute-start(bf16[32,6144]{1,0:T(8,128)(2,1)S(1)} %get-tuple-element.21), channel_id=1, source_target_pairs={{0,4},{4,0},{8,12},{12,8},{16,20},{20,16},{24,28},{28,24},{1,5},{5... | collective-permute-start | bytes 1179656 | tf_op jit(solution)/shard_map/ppermute | solution.py:49
  4.5 0.1 collective-permute-start.2
  4.5 1.3 %collective-permute-done.1.upper_ref.after_ref = bf16[32,6144]{1,0:T(8,128)(2,1)S(1)} collective-permute-done((bf16[32,6144]{1,0:T(8,128)(2,1)S(1)}, bf16[32,6144]{1,0:T(8,128)(2,1)S(1)}, u32[]{:S(2)}, u32[]{:S(2)}) %collective-permute-start.1) | collective-permute-done | bytes 393248 | tf_op jit(solution)/shard_map/ppermute | solution.py:49
  5.8 0.6 %collective-permute-done.2.lower_ref = bf16[32,6144]{1,0:T(8,128)(2,1)S(1)} collective-permute-done((bf16[32,6144]{1,0:T(8,128)(2,1)S(1)}, bf16[32,6144]{1,0:T(8,128)(2,1)S(1)}, u32[]{:S(2)}, u32[]{:S(2)}) %collective-permute-start.2) | collective-permute-done | bytes 393248 | tf_op jit(solution)/shard_map/ppermute | solution.py:49
  6.4 0.1 hold.2
  6.4 0.4 %collective-permute-start.3 = (bf16[64,6144]{1,0:T(8,128)(2,1)S(1)}, bf16[64,6144]{1,0:T(8,128)(2,1)S(1)}, u32[]{:S(2)}, u32[]{:S(2)}) collective-permute-start(bf16[64,6144]{1,0:T(8,128)(2,1)S(1)} %hold.2), channel_id=1, source_target_pairs={{0,4},{4,8},{8,12},{12,16},{16,20},{20,24},{24,28},{28,0},{1,5},{5... | collective-permute-start | bytes 2359304 | tf_op jit(solution)/shard_map/ppermute | solution.py:44
  6.8 0.0 copy-done.3
  6.9 0.1 turn.1.turned_ref
  7.0 0.0 copy-done
  7.0 0.0 copy-done.2
  7.0 0.0 copy-start.5
  7.0 1.8 %project.1.refs_0_ = bf16[80,512]{1,0:T(8,128)(2,1)S(1)} custom-call(bf16[64,6144]{1,0:T(8,128)(2,1)S(1)} %copy-done.2, bf16[512,6144]{1,0:T(8,128)(2,1)S(1)} %bitcast.2, bf16[16,512]{1,0:T(8,128)(2,1)S(1)} %turn.1.turned_ref), custom_call_target="tpu_custom_call" | custom-call | tf_op jit(solution)/shard_map/project/pallas_call | solution.py:30
  8.9 1.6 %collective-permute-start.8 = (bf16[80,512]{1,0:T(8,128)(2,1)S(1)}, bf16[80,512]{1,0:T(8,128)(2,1)S(1)}, u32[]{:S(2)}, u32[]{:S(2)}) collective-permute-start(bf16[80,512]{1,0:T(8,128)(2,1)S(1)} %project.1.refs_0_), channel_id=1, source_target_pairs={{0,2},{1,3},{2,0},{3,1},{4,6},{5,7},{6,4},{7,5},{8,10},{9,11},{10,... | collective-permute-start | bytes 245768 | tf_op jit(solution)/shard_map/ppermute | solution.py:65
  10.4 1.4 %collective-permute-start.4 = (bf16[80,512]{1,0:T(8,128)(2,1)S(1)}, bf16[80,512]{1,0:T(8,128)(2,1)S(1)}, u32[]{:S(2)}, u32[]{:S(2)}) collective-permute-start(bf16[80,512]{1,0:T(8,128)(2,1)S(1)} %project.1.refs_0_), channel_id=1, source_target_pairs={{0,3},{1,2},{2,1},{3,0},{4,7},{5,6},{6,5},{7,4},{8,11},{9,10},{10,... | collective-permute-start | bytes 245768 | tf_op jit(solution)/shard_map/ppermute | solution.py:65
  11.9 0.5 %collective-permute-start.7 = (bf16[80,512]{1,0:T(8,128)(2,1)S(1)}, bf16[80,512]{1,0:T(8,128)(2,1)S(1)}, u32[]{:S(2)}, u32[]{:S(2)}) collective-permute-start(bf16[80,512]{1,0:T(8,128)(2,1)S(1)} %project.1.refs_0_), channel_id=1, source_target_pairs={{0,1},{1,0},{2,3},{3,2},{4,5},{5,4},{6,7},{7,6},{8,9},{9,8},{10,11... | collective-permute-start | bytes 245768 | tf_op jit(solution)/shard_map/ppermute | solution.py:65
  12.4 0.0 copy-done.5
  12.4 1.1 %match.1 = (bf16[256,512]{1,0:T(8,128)(2,1)S(1)}, bf16[256,512]{1,0:T(8,128)(2,1)S(1)}, bf16[256,512]{1,0:T(8,128)(2,1)S(1)}, bf16[256,512]{1,0:T(8,128)(2,1)S(1...) custom-call(s32[4,32]{1,0:T(4,128)S(1)} %copy-done.5), custom_call_target="tpu_custom_call" | custom-call | tf_op jit(solution)/shard_map/match/pallas_call | solution.py:30
  13.6 0.3 collective-permute-done.8.refs_1_
  13.9 2.7 %collective-permute-done.4.refs_0_.refs_2_ = bf16[80,512]{1,0:T(8,128)(2,1)S(1)} collective-permute-done((bf16[80,512]{1,0:T(8,128)(2,1)S(1)}, bf16[80,512]{1,0:T(8,128)(2,1)S(1)}, u32[]{:S(2)}, u32[]{:S(2)}) %collective-permute-start.4) | collective-permute-done | bytes 81952 | tf_op jit(solution)/shard_map/ppermute | solution.py:65
  16.6 0.5 %partly.1 = (f32[32,512]{1,0:T(8,128)S(1)}, f32[64,512]{1,0:T(8,128)S(1)}) custom-call(bf16[80,512]{1,0:T(8,128)(2,1)S(1)} %project.1.refs_0_, bf16[80,512]{1,0:T(8,128)(2,1)S(1)} %collective-permute-done.8.refs_1_, bf16[80,512]{1,0:T(8,128)(2,1)S(1)} %collective-permute-done.4.refs_0_.refs_2_, bf16[256,512]{1,0:T(8,128)(2,1)S(1)} %get-tuple-element.23.refs_1_.refs_3_, ...), custom_call_target="tpu_custom_call" | custom-call | tf_op jit(solution)/shard_map/partly/pallas_call | solution.py:30
  17.1 0.0 collective-permute-done.block_ref.one
  17.1 0.1 halves.3
  17.2 0.3 collective-permute-start.5
  17.5 0.3 collective-permute-start.6
  17.8 0.0 collective-permute-done.7.load
  17.8 0.5 %couple.1.after_ref.mine = bf16[64,512]{1,0:T(8,128)(2,1)S(1)} custom-call(bf16[80,512]{1,0:T(8,128)(2,1)S(1)} %collective-permute-done.7.load, bf16[256,512]{1,0:T(8,128)(2,1)S(1)} %get-tuple-element.26.pick, bf16[512,512]{1,0:T(8,128)(2,1)S(1)} %get-tuple-element.27.same, f32[32,512]{1,0:T(8,128)S(1)} %get-tuple-element.33.columns_ref, ...), custom_call_target="tpu_custom_call" | custom-call | flops 4000000000 | tf_op jit(solution)/shard_map/couple/pallas_call | solution.py:30
  18.3 0.0 copy-start.4
  18.3 1.6 %collective-permute-start.10 = (bf16[64,512]{1,0:T(8,128)(2,1)S(1)}, bf16[64,512]{1,0:T(8,128)(2,1)S(1)}, u32[]{:S(2)}, u32[]{:S(2)}) collective-permute-start(bf16[64,512]{1,0:T(8,128)(2,1)S(1)} %couple.1.after_ref.mine), channel_id=1, source_target_pairs={{0,8},{4,12},{8,16},{12,20},{16,24},{20,28},{24,0},{28,4},{1,9},{5... | collective-permute-start | bytes 196616 | tf_op jit(solution)/shard_map/ppermute | solution.py:44
  19.9 0.0 collective-permute-done.5.upper_ref.upper
  19.9 0.0 collective-permute-done.6.lower_ref.lower
  20.0 0.1 collective-permute-start.9
  20.1 4.4 %collective-permute-done.10.mine_two.two = bf16[64,512]{1,0:T(8,128)(2,1)S(1)} collective-permute-done((bf16[64,512]{1,0:T(8,128)(2,1)S(1)}, bf16[64,512]{1,0:T(8,128)(2,1)S(1)}, u32[]{:S(2)}, u32[]{:S(2)}) %collective-permute-start.10) | collective-permute-done | bytes 65568 | tf_op jit(solution)/shard_map/ppermute | solution.py:44
  24.4 0.0 collective-permute-done.3.two
  24.4 0.1 choose.1
  24.5 0.1 collective-permute-start.11
  24.6 0.5 %collective-permute-start.13 = (bf16[64,512]{1,0:T(8,128)(2,1)S(1)}, bf16[64,512]{1,0:T(8,128)(2,1)S(1)}, u32[]{:S(2)}, u32[]{:S(2)}) collective-permute-start(bf16[64,512]{1,0:T(8,128)(2,1)S(1)} %collective-permute-done.10.mine_two.two), channel_id=1, source_target_pairs={{0,4},{4,8},{8,12},{12,16},{16,20},{20,24},{24,28},{28,0},{1,5},{5... | collective-permute-start | bytes 196616 | tf_op jit(solution)/shard_map/ppermute | solution.py:44
  25.1 0.0 collective-permute-start.12
  25.1 6.1 %collective-permute-done.9.three_a = bf16[48,6144]{1,0:T(8,128)(2,1)S(1)} collective-permute-done((bf16[48,6144]{1,0:T(8,128)(2,1)S(1)}, bf16[48,6144]{1,0:T(8,128)(2,1)S(1)}, u32[]{:S(2)}, u32[]{:S(2)}) %collective-permute-start.9) | collective-permute-done | bytes 589856 | tf_op jit(solution)/shard_map/ppermute | solution.py:44
  31.1 0.0 copy-done.4
  31.1 0.8 %gather.1.after_ref.partial_ref = f32[64,6144]{1,0:T(8,128)S(1)} custom-call(bf16[64,256]{1,0:T(8,128)(2,1)S(1)} %copy-done.4, bf16[64,6144]{1,0:T(8,128)(2,1)S(1)} %copy-done.2, bf16[64,6144]{1,0:T(8,128)(2,1)S(1)} %collective-permute-done.block_ref.one, bf16[64,6144]{1,0:T(8,128)(2,1)S(1)} %collective-permute-done.3.two, ...), custom_call_target="tpu_custom_call" | custom-call | flops 4499999744 | tf_op jit(solution)/shard_map/gather/pallas_call | solution.py:30
  32.0 0.0 collective-permute-done.13.three
  32.0 0.0 collective-permute-done.11.swap_ref
  32.0 1.4 %apply.1.applied = f32[64,6144]{1,0:T(8,128)S(1)} custom-call(bf16[64,256]{1,0:T(8,128)(2,1)S(1)} %copy-done.4, bf16[64,512]{1,0:T(8,128)(2,1)S(1)} %couple.1.after_ref.mine, bf16[80,6144]{1,0:T(8,128)(2,1)S(1)} %collective-permute-done.11.swap_ref, bf16[64,512]{1,0:T(8,128)(2,1)S(1)} %collective-permute-done.10.mine_two.two, ...), custom_call_target="tpu_custom_call" | custom-call | flops 5000000000 | tf_op jit(solution)/shard_map/apply/pallas_call | solution.py:30
  33.4 0.5 %collective-permute-done.12.last_ref = bf16[16,6144]{1,0:T(8,128)(2,1)S(1)} collective-permute-done((bf16[16,6144]{1,0:T(8,128)(2,1)S(1)}, bf16[16,6144]{1,0:T(8,128)(2,1)S(1)}, u32[]{:S(2)}, u32[]{:S(2)}) %collective-permute-start.12) | collective-permute-done | bytes 196640 | tf_op jit(solution)/shard_map/ppermute | solution.py:44
  34.0 1.2 %finish.1 = bf16[64,6144]{1,0:T(8,128)(2,1)} custom-call(bf16[64,256]{1,0:T(8,128)(2,1)S(1)} %copy-done.4, f32[64,6144]{1,0:T(8,128)S(1)} %gather.1.after_ref.partial_ref, bf16[80,6144]{1,0:T(8,128)(2,1)S(1)} %collective-permute-done.11.swap_ref, bf16[16,6144]{1,0:T(8,128)(2,1)S(1)} %collective-permute-done.12.last_ref, f32[64,6144]{1,0:T(8,128)S(1)} %apply.1.applied), custom_call_target="tpu_custom_call" | custom-call | tf_op jit(solution)/shard_map/finish/pallas_call | solution.py:401
  (1 shorter events, 0.0 us)
Async XLA Ops:
  0.0 17.1 %collective-permute-start = (bf16[64,6144]{1,0:T(8,128)(2,1)}, bf16[64,6144]{1,0:T(8,128)(2,1)S(1)}, u32[]{:S(2)}, u32[]{:S(2)}) collective-permute-start(bf16[64,6144]{1,0:T(8,128)(2,1)} %own.1), channel_id=1, source_target_pairs={{0,4},{4,8},{8,12},{12,16},{16,20},{20,24},{24,28},{28,0},{1,5},{5... | collective-permute-start | bytes 2359304 | tf_op jit(solution)/shard_map/ppermute | solution.py:44
  0.5 1.1 %copy-start.1 = (bf16[64,6144]{1,0:T(8,128)(2,1)S(1)}, bf16[64,6144]{1,0:T(8,128)(2,1)}, u32[]{:S(2)}) copy-start(bf16[64,6144]{1,0:T(8,128)(2,1)} %own.1) | copy-start | bytes 2359300
  1.6 5.4 %copy-start = (bf16[32,16,6144]{2,1,0:T(8,128)(2,1)S(1)}, bf16[32,16,6144]{2,1,0:T(8,128)(2,1)}, u32[]{:S(2)}) copy-start(bf16[32,16,6144]{2,1,0:T(8,128)(2,1)} %param.7) | copy-start | bytes 18874372
  1.6 5.2 %copy-start.3 = (f32[16,16,16]{2,1,0:T(8,128)S(1)}, f32[16,16,16]{2,1,0:T(8,128)}, u32[]{:S(2)}) copy-start(f32[16,16,16]{2,1,0:T(8,128)} %param.8) | copy-start | bytes 49156
  1.7 5.3 %copy-start.2 = (bf16[64,6144]{1,0:T(8,128)(2,1)S(1)}, bf16[64,6144]{1,0:T(8,128)(2,1)}, u32[]{:S(2)}) copy-start(bf16[64,6144]{1,0:T(8,128)(2,1)} %own.1) | copy-start | bytes 2359300
  1.7 4.1 %collective-permute-start.1 = (bf16[32,6144]{1,0:T(8,128)(2,1)S(1)}, bf16[32,6144]{1,0:T(8,128)(2,1)S(1)}, u32[]{:S(2)}, u32[]{:S(2)}) collective-permute-start(bf16[32,6144]{1,0:T(8,128)(2,1)S(1)} %get-tuple-element.21), channel_id=1, source_target_pairs={{0,4},{4,0},{8,12},{12,8},{16,20},{20,16},{24,28},{28,24},{1,5},{5... | collective-permute-start | bytes 1179656 | tf_op jit(solution)/shard_map/ppermute | solution.py:49
  4.5 1.9 %collective-permute-start.2 = (bf16[32,6144]{1,0:T(8,128)(2,1)S(1)}, bf16[32,6144]{1,0:T(8,128)(2,1)S(1)}, u32[]{:S(2)}, u32[]{:S(2)}) collective-permute-start(bf16[32,6144]{1,0:T(8,128)(2,1)S(1)} %get-tuple-element.22), channel_id=1, source_target_pairs={{0,4},{4,0},{8,12},{12,8},{16,20},{20,16},{24,28},{28,24},{1,5},{5... | collective-permute-start | bytes 1179656 | tf_op jit(solution)/shard_map/ppermute | solution.py:49
  6.4 18.0 %collective-permute-start.3 = (bf16[64,6144]{1,0:T(8,128)(2,1)S(1)}, bf16[64,6144]{1,0:T(8,128)(2,1)S(1)}, u32[]{:S(2)}, u32[]{:S(2)}) collective-permute-start(bf16[64,6144]{1,0:T(8,128)(2,1)S(1)} %hold.2), channel_id=1, source_target_pairs={{0,4},{4,8},{8,12},{12,16},{16,20},{20,24},{24,28},{28,0},{1,5},{5... | collective-permute-start | bytes 2359304 | tf_op jit(solution)/shard_map/ppermute | solution.py:44
  7.0 5.4 %copy-start.5 = (s32[4,32]{1,0:T(4,128)S(1)}, s32[4,32]{1,0:T(4,128)}, u32[]{:S(2)}) copy-start(s32[4,32]{1,0:T(4,128)} %slot_ref.1) | copy-start | bytes 1540
  8.9 5.0 %collective-permute-start.8 = (bf16[80,512]{1,0:T(8,128)(2,1)S(1)}, bf16[80,512]{1,0:T(8,128)(2,1)S(1)}, u32[]{:S(2)}, u32[]{:S(2)}) collective-permute-start(bf16[80,512]{1,0:T(8,128)(2,1)S(1)} %project.1.refs_0_), channel_id=1, source_target_pairs={{0,2},{1,3},{2,0},{3,1},{4,6},{5,7},{6,4},{7,5},{8,10},{9,11},{10,... | collective-permute-start | bytes 245768 | tf_op jit(solution)/shard_map/ppermute | solution.py:65
  10.4 6.1 %collective-permute-start.4 = (bf16[80,512]{1,0:T(8,128)(2,1)S(1)}, bf16[80,512]{1,0:T(8,128)(2,1)S(1)}, u32[]{:S(2)}, u32[]{:S(2)}) collective-permute-start(bf16[80,512]{1,0:T(8,128)(2,1)S(1)} %project.1.refs_0_), channel_id=1, source_target_pairs={{0,3},{1,2},{2,1},{3,0},{4,7},{5,6},{6,5},{7,4},{8,11},{9,10},{10,... | collective-permute-start | bytes 245768 | tf_op jit(solution)/shard_map/ppermute | solution.py:65
  11.9 5.9 %collective-permute-start.7 = (bf16[80,512]{1,0:T(8,128)(2,1)S(1)}, bf16[80,512]{1,0:T(8,128)(2,1)S(1)}, u32[]{:S(2)}, u32[]{:S(2)}) collective-permute-start(bf16[80,512]{1,0:T(8,128)(2,1)S(1)} %project.1.refs_0_), channel_id=1, source_target_pairs={{0,1},{1,0},{2,3},{3,2},{4,5},{5,4},{6,7},{7,6},{8,9},{9,8},{10,11... | collective-permute-start | bytes 245768 | tf_op jit(solution)/shard_map/ppermute | solution.py:65
  17.2 2.8 %collective-permute-start.5 = (bf16[32,6144]{1,0:T(8,128)(2,1)S(1)}, bf16[32,6144]{1,0:T(8,128)(2,1)S(1)}, u32[]{:S(2)}, u32[]{:S(2)}) collective-permute-start(bf16[32,6144]{1,0:T(8,128)(2,1)S(1)} %get-tuple-element.24), channel_id=1, source_target_pairs={{0,4},{4,0},{8,12},{12,8},{16,20},{20,16},{24,28},{28,24},{1,5},{5... | collective-permute-start | bytes 1179656 | tf_op jit(solution)/shard_map/ppermute | solution.py:49
  17.5 2.4 %collective-permute-start.6 = (bf16[32,6144]{1,0:T(8,128)(2,1)S(1)}, bf16[32,6144]{1,0:T(8,128)(2,1)S(1)}, u32[]{:S(2)}, u32[]{:S(2)}) collective-permute-start(bf16[32,6144]{1,0:T(8,128)(2,1)S(1)} %get-tuple-element.25), channel_id=1, source_target_pairs={{0,4},{4,0},{8,12},{12,8},{16,20},{20,16},{24,28},{28,24},{1,5},{5... | collective-permute-start | bytes 1179656 | tf_op jit(solution)/shard_map/ppermute | solution.py:49
  18.3 12.9 %copy-start.4 = (bf16[64,256]{1,0:T(8,128)(2,1)S(1)}, bf16[64,256]{1,0:T(8,128)(2,1)}, u32[]{:S(2)}) copy-start(bf16[64,256]{1,0:T(8,128)(2,1)} %rot_ref.5) | copy-start | bytes 98308
  18.3 6.1 %collective-permute-start.10 = (bf16[64,512]{1,0:T(8,128)(2,1)S(1)}, bf16[64,512]{1,0:T(8,128)(2,1)S(1)}, u32[]{:S(2)}, u32[]{:S(2)}) collective-permute-start(bf16[64,512]{1,0:T(8,128)(2,1)S(1)} %couple.1.after_ref.mine), channel_id=1, source_target_pairs={{0,8},{4,12},{8,16},{12,20},{16,24},{20,28},{24,0},{28,4},{1,9},{5... | collective-permute-start | bytes 196616 | tf_op jit(solution)/shard_map/ppermute | solution.py:44
  20.0 11.2 %collective-permute-start.9 = (bf16[48,6144]{1,0:T(8,128)(2,1)S(1)}, bf16[48,6144]{1,0:T(8,128)(2,1)S(1)}, u32[]{:S(2)}, u32[]{:S(2)}) collective-permute-start(bf16[48,6144]{1,0:T(8,128)(2,1)S(1)} %hold.3), channel_id=1, source_target_pairs={{0,4},{4,8},{8,12},{12,16},{16,20},{20,24},{24,28},{28,0},{1,5},{5... | collective-permute-start | bytes 1769480 | tf_op jit(solution)/shard_map/ppermute | solution.py:44
  24.5 7.5 %collective-permute-start.11 = (bf16[80,6144]{1,0:T(8,128)(2,1)S(1)}, bf16[80,6144]{1,0:T(8,128)(2,1)S(1)}, u32[]{:S(2)}, u32[]{:S(2)}) collective-permute-start(bf16[80,6144]{1,0:T(8,128)(2,1)S(1)} %get-tuple-element.35), channel_id=1, source_target_pairs={{0,4},{4,0},{8,12},{12,8},{16,20},{20,16},{24,28},{28,24},{1,5},{5... | collective-permute-start | bytes 2949128 | tf_op jit(solution)/shard_map/ppermute | solution.py:49
  24.6 7.4 %collective-permute-start.13 = (bf16[64,512]{1,0:T(8,128)(2,1)S(1)}, bf16[64,512]{1,0:T(8,128)(2,1)S(1)}, u32[]{:S(2)}, u32[]{:S(2)}) collective-permute-start(bf16[64,512]{1,0:T(8,128)(2,1)S(1)} %collective-permute-done.10.mine_two.two), channel_id=1, source_target_pairs={{0,4},{4,8},{8,12},{12,16},{16,20},{20,24},{24,28},{28,0},{1,5},{5... | collective-permute-start | bytes 196616 | tf_op jit(solution)/shard_map/ppermute | solution.py:44
  25.1 8.9 %collective-permute-start.12 = (bf16[16,6144]{1,0:T(8,128)(2,1)S(1)}, bf16[16,6144]{1,0:T(8,128)(2,1)S(1)}, u32[]{:S(2)}, u32[]{:S(2)}) collective-permute-start(bf16[16,6144]{1,0:T(8,128)(2,1)S(1)} %get-tuple-element.36), channel_id=1, source_target_pairs={{0,4},{4,8},{8,12},{12,16},{16,20},{20,24},{24,28},{28,0},{1,5},{5... | collective-permute-start | bytes 589832 | tf_op jit(solution)/shard_map/ppermute | solution.py:44

commit v11 on v10

--- a/solution.py
+++ b/solution.py
@@ -201,12 +201,14 @@
     total_ref[...] = total
 
 
-def couple_matched_kernel(load, pick, same, columns_ref, total_ref, out_ref, high_ref, low_ref):
+def couple_matched_kernel(count, *refs):
+    groups = [refs[i * count : (i + 1) * count] for i in range(3)]
+    columns_ref, total_ref, out_ref, high_ref, low_ref = refs[3 * count :]
     width, flat = out_ref.shape
-    rank = load.shape[0] - width
-    columns, total = matched_terms(width, [load], [pick], [same])
+    columns, total = matched_terms(width, *groups)
     columns += columns_ref[...]
     total += total_ref[...]
+    rank = columns.shape[0] // 2
     lane_slot = lax.broadcasted_iota(jnp.int32, (rank, flat), 1) // rank
     for k in range(flat // rank):
         rows = slice(k * rank, (k + 1) * rank)
@@ -221,18 +223,17 @@
 
 def couple_matched(loads, matched, width):
     count, flat = len(loads), loads[0].shape[1]
-    picks, matches = matched[:count], matched[count:]
-    early = [i for i in range(count) if i != 1]
-    groups = [[x[i] for i in early] for x in (loads, picks, matches)]
+    lists = (loads, matched[:count], matched[count:])
+    early = sum([[x[0], x[-1]] for x in lists], [])
+    late = sum([x[1:-1] for x in lists], [])
     rank = loads[0].shape[0] - width
     outs = [((2 * rank, flat), F32), ((width, flat), F32)]
-    kernel = functools.partial(partly_kernel, len(early))
-    partly = call(kernel, "partly", outs, sum(groups, []))
+    partly = call(functools.partial(partly_kernel, 2), "partly", outs, early)
     return call(
-        couple_matched_kernel,
+        functools.partial(couple_matched_kernel, count - 2),
         "couple",
         [((width, flat), BF16)],
-        [loads[1], picks[1], matches[1], *partly],
+        [*late, *partly],
         [pltpu.VMEM((flat, flat), BF16)] * 2,
         cost=COUPLE,
     )[0]

time: 35.3 us -> 34.7 us (0.983)
  waiting for transfers between devices: 15.8 us -> 15.2 us
    ppermute x3, waiting for transfers between devices: 3.04 us -> 2.37 us  [from_all_domains(): return [block] + [lax.ppermute(block, 'dom', route) for route in routes]]
  transfers between devices with their start and end apart: 14 -> 14, of which waited for: 7 -> 8; matrix products, arithmetic and copies ran while one was open for 0% -> 0% of each run, Pallas kernels for 19% -> 19%
where the time goes in v11:
time: 34.7 us; the launch traced here: 34.5 us
  waiting for transfers between devices  15.2 us (44%)
  starting transfers between devices  10.2 us (29%)
  Pallas kernels  7.85 us (23%)
  local copies, waits for them, and re-layouts  1.17 us (3%)
    ppermute x6, waiting for transfers between devices, along_bands(): lax.ppermute(block, 'band', [(i, (i + distance) % count) for i in range(c...  11 us
    pallas_call x12, Pallas kernels, call(): pl.pallas_call(kernel, in_specs=[first] + [VMEM] * (len(args) - 1), out_s...  6.65 us
    ppermute x3, starting transfers between devices, from_all_domains(): return [block] + [lax.ppermute(block, 'dom', route) for route in routes]  3.55 us
    ppermute x5, starting transfers between devices, swapped(): return lax.ppermute(block, 'band', [(i, i ^ 1) for i in range(count)])  3.54 us
    ppermute x6, starting transfers between devices, along_bands(): lax.ppermute(block, 'band', [(i, (i + distance) % count) for i in range(c...  3.07 us
    ppermute x3, waiting for transfers between devices, from_all_domains(): return [block] + [lax.ppermute(block, 'dom', route) for route in routes]  2.37 us
    ppermute x5, waiting for transfers between devices, swapped(): return lax.ppermute(block, 'band', [(i, i ^ 1) for i in range(count)])  1.84 us
    pallas_call x1, Pallas kernels, finish(): pl.pallas_call(finish_kernel, in_specs=[VMEM] * len(args), out_specs=pl.B...  1.19 us
  transfers between devices with their start and end apart: 14, of which 8 were waited for; matrix products, arithmetic and copies ran while one was open for 0% of the time, Pallas kernels for 19%

profile of v11, /device:TPU:0, one launch (start us, length us, event | category | flops | bytes accessed | tf_op | source)
XLA Modules:
  0.0 34.5 jit_solution(8605380945628670411)
XLA Ops:
  0.0 0.5 %collective-permute-start = (bf16[64,6144]{1,0:T(8,128)(2,1)}, bf16[64,6144]{1,0:T(8,128)(2,1)S(1)}, u32[]{:S(2)}, u32[]{:S(2)}) collective-permute-start(bf16[64,6144]{1,0:T(8,128)(2,1)} %own.1), channel_id=1, source_target_pairs={{0,4},{4,8},{8,12},{12,16},{16,20},{20,24},{24,28},{28,0},{1,5},{5... | collective-permute-start | bytes 2359304 | tf_op jit(solution)/shard_map/ppermute | solution.py:44
  0.5 0.0 copy-start.1
  0.5 1.1 %copy-done.1 = bf16[64,6144]{1,0:T(8,128)(2,1)S(1)} copy-done((bf16[64,6144]{1,0:T(8,128)(2,1)S(1)}, bf16[64,6144]{1,0:T(8,128)(2,1)}, u32[]{:S(2)}) %copy-start.1) | copy-done | bytes 786456
  1.6 0.0 copy-start
  1.6 0.1 halves.2
  1.6 0.0 copy-start.3
  1.7 0.0 copy-start.2
  1.7 2.8 %collective-permute-start.1 = (bf16[32,6144]{1,0:T(8,128)(2,1)S(1)}, bf16[32,6144]{1,0:T(8,128)(2,1)S(1)}, u32[]{:S(2)}, u32[]{:S(2)}) collective-permute-start(bf16[32,6144]{1,0:T(8,128)(2,1)S(1)} %get-tuple-element.21), channel_id=1, source_target_pairs={{0,4},{4,0},{8,12},{12,8},{16,20},{20,16},{24,28},{28,24},{1,5},{5... | collective-permute-start | bytes 1179656 | tf_op jit(solution)/shard_map/ppermute | solution.py:49
  4.5 0.1 collective-permute-start.2
  4.5 1.3 %collective-permute-done.1.upper_ref.after_ref = bf16[32,6144]{1,0:T(8,128)(2,1)S(1)} collective-permute-done((bf16[32,6144]{1,0:T(8,128)(2,1)S(1)}, bf16[32,6144]{1,0:T(8,128)(2,1)S(1)}, u32[]{:S(2)}, u32[]{:S(2)}) %collective-permute-start.1) | collective-permute-done | bytes 393248 | tf_op jit(solution)/shard_map/ppermute | solution.py:49
  5.8 0.6 %collective-permute-done.2.lower_ref = bf16[32,6144]{1,0:T(8,128)(2,1)S(1)} collective-permute-done((bf16[32,6144]{1,0:T(8,128)(2,1)S(1)}, bf16[32,6144]{1,0:T(8,128)(2,1)S(1)}, u32[]{:S(2)}, u32[]{:S(2)}) %collective-permute-start.2) | collective-permute-done | bytes 393248 | tf_op jit(solution)/shard_map/ppermute | solution.py:49
  6.4 0.1 hold.2
  6.4 0.4 %collective-permute-start.3 = (bf16[64,6144]{1,0:T(8,128)(2,1)S(1)}, bf16[64,6144]{1,0:T(8,128)(2,1)S(1)}, u32[]{:S(2)}, u32[]{:S(2)}) collective-permute-start(bf16[64,6144]{1,0:T(8,128)(2,1)S(1)} %hold.2), channel_id=1, source_target_pairs={{0,4},{4,8},{8,12},{12,16},{16,20},{20,24},{24,28},{28,0},{1,5},{5... | collective-permute-start | bytes 2359304 | tf_op jit(solution)/shard_map/ppermute | solution.py:44
  6.8 0.0 copy-done.3
  6.9 0.1 turn.1.turned_ref
  7.0 0.0 copy-done
  7.0 0.0 copy-done.2
  7.0 0.0 copy-start.5
  7.0 1.8 %project.1.refs_0_ = bf16[80,512]{1,0:T(8,128)(2,1)S(1)} custom-call(bf16[64,6144]{1,0:T(8,128)(2,1)S(1)} %copy-done.2, bf16[512,6144]{1,0:T(8,128)(2,1)S(1)} %bitcast.2, bf16[16,512]{1,0:T(8,128)(2,1)S(1)} %turn.1.turned_ref), custom_call_target="tpu_custom_call" | custom-call | tf_op jit(solution)/shard_map/project/pallas_call | solution.py:30
  8.9 2.5 %collective-permute-start.4 = (bf16[80,512]{1,0:T(8,128)(2,1)S(1)}, bf16[80,512]{1,0:T(8,128)(2,1)S(1)}, u32[]{:S(2)}, u32[]{:S(2)}) collective-permute-start(bf16[80,512]{1,0:T(8,128)(2,1)S(1)} %project.1.refs_0_), channel_id=1, source_target_pairs={{0,3},{1,2},{2,1},{3,0},{4,7},{5,6},{6,5},{7,4},{8,11},{9,10},{10,... | collective-permute-start | bytes 245768 | tf_op jit(solution)/shard_map/ppermute | solution.py:65
  11.4 0.5 %collective-permute-start.8 = (bf16[80,512]{1,0:T(8,128)(2,1)S(1)}, bf16[80,512]{1,0:T(8,128)(2,1)S(1)}, u32[]{:S(2)}, u32[]{:S(2)}) collective-permute-start(bf16[80,512]{1,0:T(8,128)(2,1)S(1)} %project.1.refs_0_), channel_id=1, source_target_pairs={{0,2},{1,3},{2,0},{3,1},{4,6},{5,7},{6,4},{7,5},{8,10},{9,11},{10,... | collective-permute-start | bytes 245768 | tf_op jit(solution)/shard_map/ppermute | solution.py:65
  11.9 0.5 %collective-permute-start.7 = (bf16[80,512]{1,0:T(8,128)(2,1)S(1)}, bf16[80,512]{1,0:T(8,128)(2,1)S(1)}, u32[]{:S(2)}, u32[]{:S(2)}) collective-permute-start(bf16[80,512]{1,0:T(8,128)(2,1)S(1)} %project.1.refs_0_), channel_id=1, source_target_pairs={{0,1},{1,0},{2,3},{3,2},{4,5},{5,4},{6,7},{7,6},{8,9},{9,8},{10,11... | collective-permute-start | bytes 245768 | tf_op jit(solution)/shard_map/ppermute | solution.py:65
  12.4 0.0 copy-done.5
  12.4 1.1 %match.1 = (bf16[256,512]{1,0:T(8,128)(2,1)S(1)}, bf16[256,512]{1,0:T(8,128)(2,1)S(1)}, bf16[256,512]{1,0:T(8,128)(2,1)S(1)}, bf16[256,512]{1,0:T(8,128)(2,1)S(1...) custom-call(s32[4,32]{1,0:T(4,128)S(1)} %copy-done.5), custom_call_target="tpu_custom_call" | custom-call | tf_op jit(solution)/shard_map/match/pallas_call | solution.py:30
  13.6 1.2 %collective-permute-done.4.refs_0_.refs_1_ = bf16[80,512]{1,0:T(8,128)(2,1)S(1)} collective-permute-done((bf16[80,512]{1,0:T(8,128)(2,1)S(1)}, bf16[80,512]{1,0:T(8,128)(2,1)S(1)}, u32[]{:S(2)}, u32[]{:S(2)}) %collective-permute-start.4) | collective-permute-done | bytes 81952 | tf_op jit(solution)/shard_map/ppermute | solution.py:65
  14.8 0.4 %partly.1 = (f32[32,512]{1,0:T(8,128)S(1)}, f32[64,512]{1,0:T(8,128)S(1)}) custom-call(bf16[80,512]{1,0:T(8,128)(2,1)S(1)} %project.1.refs_0_, bf16[80,512]{1,0:T(8,128)(2,1)S(1)} %collective-permute-done.4.refs_0_.refs_1_, bf16[256,512]{1,0:T(8,128)(2,1)S(1)} %get-tuple-element.23.refs_1_.refs_2_, bf16[256,512]{1,0:T(8,128)(2,1)S(1)} %get-tuple-element.30.refs_3_, ...), custom_call_target="tpu_custom_call" | custom-call | tf_op jit(solution)/shard_map/partly/pallas_call | solution.py:30
  15.2 0.0 collective-permute-done.block_ref.one
  15.2 0.1 halves.3
  15.3 0.5 %collective-permute-start.5 = (bf16[32,6144]{1,0:T(8,128)(2,1)S(1)}, bf16[32,6144]{1,0:T(8,128)(2,1)S(1)}, u32[]{:S(2)}, u32[]{:S(2)}) collective-permute-start(bf16[32,6144]{1,0:T(8,128)(2,1)S(1)} %get-tuple-element.24), channel_id=1, source_target_pairs={{0,4},{4,0},{8,12},{12,8},{16,20},{20,16},{24,28},{28,24},{1,5},{5... | collective-permute-start | bytes 1179656 | tf_op jit(solution)/shard_map/ppermute | solution.py:49
  15.8 0.1 collective-permute-start.6
  15.9 1.0 %collective-permute-done.8.refs_1_ = bf16[80,512]{1,0:T(8,128)(2,1)S(1)} collective-permute-done((bf16[80,512]{1,0:T(8,128)(2,1)S(1)}, bf16[80,512]{1,0:T(8,128)(2,1)S(1)}, u32[]{:S(2)}, u32[]{:S(2)}) %collective-permute-start.8) | collective-permute-done | bytes 81952 | tf_op jit(solution)/shard_map/ppermute | solution.py:65
  16.9 0.1 collective-permute-done.7.refs_0_
  17.0 0.7 %couple.1.after_ref.mine = bf16[64,512]{1,0:T(8,128)(2,1)S(1)} custom-call(bf16[80,512]{1,0:T(8,128)(2,1)S(1)} %collective-permute-done.7.refs_0_, bf16[80,512]{1,0:T(8,128)(2,1)S(1)} %collective-permute-done.8.refs_1_, bf16[256,512]{1,0:T(8,128)(2,1)S(1)} %get-tuple-element.26.refs_2_, bf16[256,512]{1,0:T(8,128)(2,1)S(1)} %get-tuple-element.27.refs_3_, ...), custom_call_target="tpu_custom_call" | custom-call | flops 4000000000 | tf_op jit(solution)/shard_map/couple/pallas_call | solution.py:30
  17.7 0.0 copy-start.4
  17.7 1.6 %collective-permute-start.10 = (bf16[64,512]{1,0:T(8,128)(2,1)S(1)}, bf16[64,512]{1,0:T(8,128)(2,1)S(1)}, u32[]{:S(2)}, u32[]{:S(2)}) collective-permute-start(bf16[64,512]{1,0:T(8,128)(2,1)S(1)} %couple.1.after_ref.mine), channel_id=1, source_target_pairs={{0,8},{4,12},{8,16},{12,20},{16,24},{20,28},{24,0},{28,4},{1,9},{5... | collective-permute-start | bytes 196616 | tf_op jit(solution)/shard_map/ppermute | solution.py:44
  19.3 0.0 collective-permute-done.5.upper_ref.upper
  19.3 0.0 collective-permute-done.6.lower_ref.lower
  19.3 0.1 collective-permute-start.9
  19.4 4.8 %collective-permute-done.10.mine_two.two = bf16[64,512]{1,0:T(8,128)(2,1)S(1)} collective-permute-done((bf16[64,512]{1,0:T(8,128)(2,1)S(1)}, bf16[64,512]{1,0:T(8,128)(2,1)S(1)}, u32[]{:S(2)}, u32[]{:S(2)}) %collective-permute-start.10) | collective-permute-done | bytes 65568 | tf_op jit(solution)/shard_map/ppermute | solution.py:44
  24.2 0.0 collective-permute-done.3.two
  24.2 0.1 choose.1
  24.3 0.1 collective-permute-start.11
  24.4 0.5 %collective-permute-start.13 = (bf16[64,512]{1,0:T(8,128)(2,1)S(1)}, bf16[64,512]{1,0:T(8,128)(2,1)S(1)}, u32[]{:S(2)}, u32[]{:S(2)}) collective-permute-start(bf16[64,512]{1,0:T(8,128)(2,1)S(1)} %collective-permute-done.10.mine_two.two), channel_id=1, source_target_pairs={{0,4},{4,8},{8,12},{12,16},{16,20},{20,24},{24,28},{28,0},{1,5},{5... | collective-permute-start | bytes 196616 | tf_op jit(solution)/shard_map/ppermute | solution.py:44
  24.9 0.0 collective-permute-start.12
  24.9 5.7 %collective-permute-done.9.three_a = bf16[48,6144]{1,0:T(8,128)(2,1)S(1)} collective-permute-done((bf16[48,6144]{1,0:T(8,128)(2,1)S(1)}, bf16[48,6144]{1,0:T(8,128)(2,1)S(1)}, u32[]{:S(2)}, u32[]{:S(2)}) %collective-permute-start.9) | collective-permute-done | bytes 589856 | tf_op jit(solution)/shard_map/ppermute | solution.py:44
  30.5 0.0 copy-done.4
  30.5 0.8 %gather.1.after_ref.partial_ref = f32[64,6144]{1,0:T(8,128)S(1)} custom-call(bf16[64,256]{1,0:T(8,128)(2,1)S(1)} %copy-done.4, bf16[64,6144]{1,0:T(8,128)(2,1)S(1)} %copy-done.2, bf16[64,6144]{1,0:T(8,128)(2,1)S(1)} %collective-permute-done.block_ref.one, bf16[64,6144]{1,0:T(8,128)(2,1)S(1)} %collective-permute-done.3.two, ...), custom_call_target="tpu_custom_call" | custom-call | flops 4499999744 | tf_op jit(solution)/shard_map/gather/pallas_call | solution.py:30
  31.4 0.0 collective-permute-done.13.three
  31.4 0.0 collective-permute-done.11.swap_ref
  31.4 1.4 %apply.1.applied = f32[64,6144]{1,0:T(8,128)S(1)} custom-call(bf16[64,256]{1,0:T(8,128)(2,1)S(1)} %copy-done.4, bf16[64,512]{1,0:T(8,128)(2,1)S(1)} %couple.1.after_ref.mine, bf16[80,6144]{1,0:T(8,128)(2,1)S(1)} %collective-permute-done.11.swap_ref, bf16[64,512]{1,0:T(8,128)(2,1)S(1)} %collective-permute-done.10.mine_two.two, ...), custom_call_target="tpu_custom_call" | custom-call | flops 5000000000 | tf_op jit(solution)/shard_map/apply/pallas_call | solution.py:30
  32.8 0.5 %collective-permute-done.12.last_ref = bf16[16,6144]{1,0:T(8,128)(2,1)S(1)} collective-permute-done((bf16[16,6144]{1,0:T(8,128)(2,1)S(1)}, bf16[16,6144]{1,0:T(8,128)(2,1)S(1)}, u32[]{:S(2)}, u32[]{:S(2)}) %collective-permute-start.12) | collective-permute-done | bytes 196640 | tf_op jit(solution)/shard_map/ppermute | solution.py:44
  33.3 1.2 %finish.1 = bf16[64,6144]{1,0:T(8,128)(2,1)} custom-call(bf16[64,256]{1,0:T(8,128)(2,1)S(1)} %copy-done.4, f32[64,6144]{1,0:T(8,128)S(1)} %gather.1.after_ref.partial_ref, bf16[80,6144]{1,0:T(8,128)(2,1)S(1)} %collective-permute-done.11.swap_ref, bf16[16,6144]{1,0:T(8,128)(2,1)S(1)} %collective-permute-done.12.last_ref, f32[64,6144]{1,0:T(8,128)S(1)} %apply.1.applied), custom_call_target="tpu_custom_call" | custom-call | tf_op jit(solution)/shard_map/finish/pallas_call | solution.py:402
  (1 shorter events, 0.0 us)
Async XLA Ops:
  0.0 15.2 %collective-permute-start = (bf16[64,6144]{1,0:T(8,128)(2,1)}, bf16[64,6144]{1,0:T(8,128)(2,1)S(1)}, u32[]{:S(2)}, u32[]{:S(2)}) collective-permute-start(bf16[64,6144]{1,0:T(8,128)(2,1)} %own.1), channel_id=1, source_target_pairs={{0,4},{4,8},{8,12},{12,16},{16,20},{20,24},{24,28},{28,0},{1,5},{5... | collective-permute-start | bytes 2359304 | tf_op jit(solution)/shard_map/ppermute | solution.py:44
  0.5 1.1 %copy-start.1 = (bf16[64,6144]{1,0:T(8,128)(2,1)S(1)}, bf16[64,6144]{1,0:T(8,128)(2,1)}, u32[]{:S(2)}) copy-start(bf16[64,6144]{1,0:T(8,128)(2,1)} %own.1) | copy-start | bytes 2359300
  1.6 5.4 %copy-start = (bf16[32,16,6144]{2,1,0:T(8,128)(2,1)S(1)}, bf16[32,16,6144]{2,1,0:T(8,128)(2,1)}, u32[]{:S(2)}) copy-start(bf16[32,16,6144]{2,1,0:T(8,128)(2,1)} %param.7) | copy-start | bytes 18874372
  1.6 5.2 %copy-start.3 = (f32[16,16,16]{2,1,0:T(8,128)S(1)}, f32[16,16,16]{2,1,0:T(8,128)}, u32[]{:S(2)}) copy-start(f32[16,16,16]{2,1,0:T(8,128)} %param.8) | copy-start | bytes 49156
  1.7 5.3 %copy-start.2 = (bf16[64,6144]{1,0:T(8,128)(2,1)S(1)}, bf16[64,6144]{1,0:T(8,128)(2,1)}, u32[]{:S(2)}) copy-start(bf16[64,6144]{1,0:T(8,128)(2,1)} %own.1) | copy-start | bytes 2359300
  1.7 4.1 %collective-permute-start.1 = (bf16[32,6144]{1,0:T(8,128)(2,1)S(1)}, bf16[32,6144]{1,0:T(8,128)(2,1)S(1)}, u32[]{:S(2)}, u32[]{:S(2)}) collective-permute-start(bf16[32,6144]{1,0:T(8,128)(2,1)S(1)} %get-tuple-element.21), channel_id=1, source_target_pairs={{0,4},{4,0},{8,12},{12,8},{16,20},{20,16},{24,28},{28,24},{1,5},{5... | collective-permute-start | bytes 1179656 | tf_op jit(solution)/shard_map/ppermute | solution.py:49
  4.5 1.9 %collective-permute-start.2 = (bf16[32,6144]{1,0:T(8,128)(2,1)S(1)}, bf16[32,6144]{1,0:T(8,128)(2,1)S(1)}, u32[]{:S(2)}, u32[]{:S(2)}) collective-permute-start(bf16[32,6144]{1,0:T(8,128)(2,1)S(1)} %get-tuple-element.22), channel_id=1, source_target_pairs={{0,4},{4,0},{8,12},{12,8},{16,20},{20,16},{24,28},{28,24},{1,5},{5... | collective-permute-start | bytes 1179656 | tf_op jit(solution)/shard_map/ppermute | solution.py:49
  6.4 17.8 %collective-permute-start.3 = (bf16[64,6144]{1,0:T(8,128)(2,1)S(1)}, bf16[64,6144]{1,0:T(8,128)(2,1)S(1)}, u32[]{:S(2)}, u32[]{:S(2)}) collective-permute-start(bf16[64,6144]{1,0:T(8,128)(2,1)S(1)} %hold.2), channel_id=1, source_target_pairs={{0,4},{4,8},{8,12},{12,16},{16,20},{20,24},{24,28},{28,0},{1,5},{5... | collective-permute-start | bytes 2359304 | tf_op jit(solution)/shard_map/ppermute | solution.py:44
  7.0 5.4 %copy-start.5 = (s32[4,32]{1,0:T(4,128)S(1)}, s32[4,32]{1,0:T(4,128)}, u32[]{:S(2)}) copy-start(s32[4,32]{1,0:T(4,128)} %slot_ref.1) | copy-start | bytes 1540
  8.9 5.9 %collective-permute-start.4 = (bf16[80,512]{1,0:T(8,128)(2,1)S(1)}, bf16[80,512]{1,0:T(8,128)(2,1)S(1)}, u32[]{:S(2)}, u32[]{:S(2)}) collective-permute-start(bf16[80,512]{1,0:T(8,128)(2,1)S(1)} %project.1.refs_0_), channel_id=1, source_target_pairs={{0,3},{1,2},{2,1},{3,0},{4,7},{5,6},{6,5},{7,4},{8,11},{9,10},{10,... | collective-permute-start | bytes 245768 | tf_op jit(solution)/shard_map/ppermute | solution.py:65
  11.4 5.5 %collective-permute-start.8 = (bf16[80,512]{1,0:T(8,128)(2,1)S(1)}, bf16[80,512]{1,0:T(8,128)(2,1)S(1)}, u32[]{:S(2)}, u32[]{:S(2)}) collective-permute-start(bf16[80,512]{1,0:T(8,128)(2,1)S(1)} %project.1.refs_0_), channel_id=1, source_target_pairs={{0,2},{1,3},{2,0},{3,1},{4,6},{5,7},{6,4},{7,5},{8,10},{9,11},{10,... | collective-permute-start | bytes 245768 | tf_op jit(solution)/shard_map/ppermute | solution.py:65
  11.9 5.1 %collective-permute-start.7 = (bf16[80,512]{1,0:T(8,128)(2,1)S(1)}, bf16[80,512]{1,0:T(8,128)(2,1)S(1)}, u32[]{:S(2)}, u32[]{:S(2)}) collective-permute-start(bf16[80,512]{1,0:T(8,128)(2,1)S(1)} %project.1.refs_0_), channel_id=1, source_target_pairs={{0,1},{1,0},{2,3},{3,2},{4,5},{5,4},{6,7},{7,6},{8,9},{9,8},{10,11... | collective-permute-start | bytes 245768 | tf_op jit(solution)/shard_map/ppermute | solution.py:65
  15.3 4.0 %collective-permute-start.5 = (bf16[32,6144]{1,0:T(8,128)(2,1)S(1)}, bf16[32,6144]{1,0:T(8,128)(2,1)S(1)}, u32[]{:S(2)}, u32[]{:S(2)}) collective-permute-start(bf16[32,6144]{1,0:T(8,128)(2,1)S(1)} %get-tuple-element.24), channel_id=1, source_target_pairs={{0,4},{4,0},{8,12},{12,8},{16,20},{20,16},{24,28},{28,24},{1,5},{5... | collective-permute-start | bytes 1179656 | tf_op jit(solution)/shard_map/ppermute | solution.py:49
  15.8 3.5 %collective-permute-start.6 = (bf16[32,6144]{1,0:T(8,128)(2,1)S(1)}, bf16[32,6144]{1,0:T(8,128)(2,1)S(1)}, u32[]{:S(2)}, u32[]{:S(2)}) collective-permute-start(bf16[32,6144]{1,0:T(8,128)(2,1)S(1)} %get-tuple-element.25), channel_id=1, source_target_pairs={{0,4},{4,0},{8,12},{12,8},{16,20},{20,16},{24,28},{28,24},{1,5},{5... | collective-permute-start | bytes 1179656 | tf_op jit(solution)/shard_map/ppermute | solution.py:49
  17.7 12.9 %copy-start.4 = (bf16[64,256]{1,0:T(8,128)(2,1)S(1)}, bf16[64,256]{1,0:T(8,128)(2,1)}, u32[]{:S(2)}) copy-start(bf16[64,256]{1,0:T(8,128)(2,1)} %rot_ref.5) | copy-start | bytes 98308
  17.7 6.5 %collective-permute-start.10 = (bf16[64,512]{1,0:T(8,128)(2,1)S(1)}, bf16[64,512]{1,0:T(8,128)(2,1)S(1)}, u32[]{:S(2)}, u32[]{:S(2)}) collective-permute-start(bf16[64,512]{1,0:T(8,128)(2,1)S(1)} %couple.1.after_ref.mine), channel_id=1, source_target_pairs={{0,8},{4,12},{8,16},{12,20},{16,24},{20,28},{24,0},{28,4},{1,9},{5... | collective-permute-start | bytes 196616 | tf_op jit(solution)/shard_map/ppermute | solution.py:44
  19.3 11.2 %collective-permute-start.9 = (bf16[48,6144]{1,0:T(8,128)(2,1)S(1)}, bf16[48,6144]{1,0:T(8,128)(2,1)S(1)}, u32[]{:S(2)}, u32[]{:S(2)}) collective-permute-start(bf16[48,6144]{1,0:T(8,128)(2,1)S(1)} %hold.3), channel_id=1, source_target_pairs={{0,4},{4,8},{8,12},{12,16},{16,20},{20,24},{24,28},{28,0},{1,5},{5... | collective-permute-start | bytes 1769480 | tf_op jit(solution)/shard_map/ppermute | solution.py:44
  24.3 7.1 %collective-permute-start.11 = (bf16[80,6144]{1,0:T(8,128)(2,1)S(1)}, bf16[80,6144]{1,0:T(8,128)(2,1)S(1)}, u32[]{:S(2)}, u32[]{:S(2)}) collective-permute-start(bf16[80,6144]{1,0:T(8,128)(2,1)S(1)} %get-tuple-element.35), channel_id=1, source_target_pairs={{0,4},{4,0},{8,12},{12,8},{16,20},{20,16},{24,28},{28,24},{1,5},{5... | collective-permute-start | bytes 2949128 | tf_op jit(solution)/shard_map/ppermute | solution.py:49
  24.4 7.0 %collective-permute-start.13 = (bf16[64,512]{1,0:T(8,128)(2,1)S(1)}, bf16[64,512]{1,0:T(8,128)(2,1)S(1)}, u32[]{:S(2)}, u32[]{:S(2)}) collective-permute-start(bf16[64,512]{1,0:T(8,128)(2,1)S(1)} %collective-permute-done.10.mine_two.two), channel_id=1, source_target_pairs={{0,4},{4,8},{8,12},{12,16},{16,20},{20,24},{24,28},{28,0},{1,5},{5... | collective-permute-start | bytes 196616 | tf_op jit(solution)/shard_map/ppermute | solution.py:44
  24.9 8.5 %collective-permute-start.12 = (bf16[16,6144]{1,0:T(8,128)(2,1)S(1)}, bf16[16,6144]{1,0:T(8,128)(2,1)S(1)}, u32[]{:S(2)}, u32[]{:S(2)}) collective-permute-start(bf16[16,6144]{1,0:T(8,128)(2,1)S(1)} %get-tuple-element.36), channel_id=1, source_target_pairs={{0,4},{4,8},{8,12},{12,16},{16,20},{20,24},{24,28},{28,0},{1,5},{5... | collective-permute-start | bytes 589832 | tf_op jit(solution)/shard_map/ppermute | solution.py:44

commit v12 on v11

--- a/solution.py
+++ b/solution.py
@@ -368,25 +368,28 @@
         )
 
 
-def finish_kernel(
-    rot_ref, partial_ref, swap_ref, last_ref, applied, out_hbm, out_ref, sems
-):
+def add_kernel(rot_ref, partial_ref, swap_ref, applied, out_ref):
     width, points = out_ref.shape
-    rows = last_ref.shape[0]
+    turn = where_even(rot_ref[:, 3 * width : 4 * width], False)
+    tile = tile_of(points, 1024)
+    for at in range(0, points, tile):
+        here = slice(at, at + tile)
+        out_ref[:, here] = partial_ref[:, here] + jnp.dot(
+            turn, swap_ref[:width, here], preferred_element_type=F32
+        )
+
+
+def finish_kernel(rot_ref, partial_ref, last_ref, applied, out_hbm, out_ref, sems):
+    width, points = out_ref.shape
     pieces = sems.shape[0]
     tile = points // pieces
-    turn = jnp.concatenate(
-        [
-            where_even(rot_ref[:, 3 * width : 4 * width], False),
-            where_even(rot_ref[:, 4 * width - rows : 4 * width], True),
-        ],
-        axis=1,
-    )
+    turn = where_even(rot_ref[:, 4 * width - last_ref.shape[0] : 4 * width], True)
     copies = []
     for i in range(pieces):
         here = slice(i * tile, (i + 1) * tile)
-        last = jnp.concatenate([swap_ref[:width, here], last_ref[:, here]], axis=0)
-        rotated = partial_ref[:, here] + jnp.dot(turn, last, preferred_element_type=F32)
+        rotated = partial_ref[:, here] + jnp.dot(
+            turn, last_ref[:, here], preferred_element_type=F32
+        )
         added = rotated.astype(BF16).astype(F32) + applied[:, here]
         out_ref[:, here] = added.astype(out_ref.dtype)
         part = (slice(None), pl.ds(i * tile, tile))
@@ -398,7 +401,7 @@
 
 def finish(*args):
     width, points = args[-1].shape
-    pieces = points // tile_of(points, 1024)
+    pieces = points // tile_of(points, 1536)
     return pl.pallas_call(
         finish_kernel,
         in_specs=[VMEM] * len(args),
@@ -441,7 +444,9 @@
         [rotation, mine, swap, mine_two, mine_three, proj, partial],
         cost=APPLY,
     )[0]
-    return finish(rotation, partial, swap, three_b, applied)
+    outs = [(partial.shape, F32)]
+    partial = call(add_kernel, "add", outs, [rotation, partial, swap, applied])[0]
+    return finish(rotation, partial, three_b, applied)
 
 
 def solution(mesh):

time: 34.7 us -> 34.6 us (level)
  Pallas kernels: 7.85 us -> 8.25 us
  waiting for transfers between devices: 15.2 us -> 14.8 us
    ppermute x6, waiting for transfers between devices: 11 us -> 10.5 us  [along_bands(): lax.ppermute(block, 'band', [(i, (i + distance) % count) for i in range(c...]
    pallas_call x12 -> x13, Pallas kernels: 6.65 us -> 7.08 us  [call(): pl.pallas_call(kernel, in_specs=[first] + [VMEM] * (len(args) - 1), out_s...]
  transfers between devices with their start and end apart: 14 -> 14, of which waited for: 8 -> 8; matrix products, arithmetic and copies ran while one was open for 0% -> 0% of each run, Pallas kernels for 19% -> 21%
where the time goes in v12:
time: 34.6 us; the launch traced here: 34.5 us
  waiting for transfers between devices  14.8 us (43%)
  starting transfers between devices  10.2 us (29%)
  Pallas kernels  8.25 us (24%)
  local copies, waits for them, and re-layouts  1.17 us (3%)
    ppermute x6, waiting for transfers between devices, along_bands(): lax.ppermute(block, 'band', [(i, (i + distance) % count) for i in range(c...  10.5 us
    pallas_call x13, Pallas kernels, call(): pl.pallas_call(kernel, in_specs=[first] + [VMEM] * (len(args) - 1), out_s...  7.08 us
    ppermute x3, starting transfers between devices, from_all_domains(): return [block] + [lax.ppermute(block, 'dom', route) for route in routes]  3.55 us
    ppermute x5, starting transfers between devices, swapped(): return lax.ppermute(block, 'band', [(i, i ^ 1) for i in range(count)])  3.54 us
    ppermute x6, starting transfers between devices, along_bands(): lax.ppermute(block, 'band', [(i, (i + distance) % count) for i in range(c...  3.07 us
    ppermute x3, waiting for transfers between devices, from_all_domains(): return [block] + [lax.ppermute(block, 'dom', route) for route in routes]  2.37 us
    ppermute x5, waiting for transfers between devices, swapped(): return lax.ppermute(block, 'band', [(i, i ^ 1) for i in range(count)])  1.84 us
    unnamed x12, local copies, waits for them, and re-layouts  1.17 us
  transfers between devices with their start and end apart: 14, of which 8 were waited for; matrix products, arithmetic and copies ran while one was open for 0% of the time, Pallas kernels for 21%

profile of v12, /device:TPU:0, one launch (start us, length us, event | category | flops | bytes accessed | tf_op | source)
XLA Modules:
  0.0 34.5 jit_solution(17030588377265542460)
XLA Ops:
  0.0 0.5 %collective-permute-start = (bf16[64,6144]{1,0:T(8,128)(2,1)}, bf16[64,6144]{1,0:T(8,128)(2,1)S(1)}, u32[]{:S(2)}, u32[]{:S(2)}) collective-permute-start(bf16[64,6144]{1,0:T(8,128)(2,1)} %own.1), channel_id=1, source_target_pairs={{0,4},{4,8},{8,12},{12,16},{16,20},{20,24},{24,28},{28,0},{1,5},{5... | collective-permute-start | bytes 2359304 | tf_op jit(solution)/shard_map/ppermute | solution.py:44
  0.5 0.0 copy-start.1
  0.5 1.1 %copy-done.1 = bf16[64,6144]{1,0:T(8,128)(2,1)S(1)} copy-done((bf16[64,6144]{1,0:T(8,128)(2,1)S(1)}, bf16[64,6144]{1,0:T(8,128)(2,1)}, u32[]{:S(2)}) %copy-start.1) | copy-done | bytes 786456
  1.6 0.0 copy-start
  1.6 0.1 halves.2
  1.6 0.0 copy-start.4
  1.7 0.0 copy-start.2
  1.7 2.8 %collective-permute-start.1 = (bf16[32,6144]{1,0:T(8,128)(2,1)S(1)}, bf16[32,6144]{1,0:T(8,128)(2,1)S(1)}, u32[]{:S(2)}, u32[]{:S(2)}) collective-permute-start(bf16[32,6144]{1,0:T(8,128)(2,1)S(1)} %get-tuple-element.21), channel_id=1, source_target_pairs={{0,4},{4,0},{8,12},{12,8},{16,20},{20,16},{24,28},{28,24},{1,5},{5... | collective-permute-start | bytes 1179656 | tf_op jit(solution)/shard_map/ppermute | solution.py:49
  4.5 0.1 collective-permute-start.2
  4.5 1.3 %collective-permute-done.1.upper_ref.after_ref = bf16[32,6144]{1,0:T(8,128)(2,1)S(1)} collective-permute-done((bf16[32,6144]{1,0:T(8,128)(2,1)S(1)}, bf16[32,6144]{1,0:T(8,128)(2,1)S(1)}, u32[]{:S(2)}, u32[]{:S(2)}) %collective-permute-start.1) | collective-permute-done | bytes 393248 | tf_op jit(solution)/shard_map/ppermute | solution.py:49
  5.8 0.6 %collective-permute-done.2.lower_ref = bf16[32,6144]{1,0:T(8,128)(2,1)S(1)} collective-permute-done((bf16[32,6144]{1,0:T(8,128)(2,1)S(1)}, bf16[32,6144]{1,0:T(8,128)(2,1)S(1)}, u32[]{:S(2)}, u32[]{:S(2)}) %collective-permute-start.2) | collective-permute-done | bytes 393248 | tf_op jit(solution)/shard_map/ppermute | solution.py:49
  6.4 0.1 hold.2
  6.4 0.4 %collective-permute-start.3 = (bf16[64,6144]{1,0:T(8,128)(2,1)S(1)}, bf16[64,6144]{1,0:T(8,128)(2,1)S(1)}, u32[]{:S(2)}, u32[]{:S(2)}) collective-permute-start(bf16[64,6144]{1,0:T(8,128)(2,1)S(1)} %hold.2), channel_id=1, source_target_pairs={{0,4},{4,8},{8,12},{12,16},{16,20},{20,24},{24,28},{28,0},{1,5},{5... | collective-permute-start | bytes 2359304 | tf_op jit(solution)/shard_map/ppermute | solution.py:44
  6.8 0.0 copy-done.4
  6.9 0.1 turn.1.turned_ref
  7.0 0.0 copy-done
  7.0 0.0 copy-done.2
  7.0 0.0 copy-start.5
  7.0 1.8 %project.1.refs_0_ = bf16[80,512]{1,0:T(8,128)(2,1)S(1)} custom-call(bf16[64,6144]{1,0:T(8,128)(2,1)S(1)} %copy-done.2, bf16[512,6144]{1,0:T(8,128)(2,1)S(1)} %bitcast.2, bf16[16,512]{1,0:T(8,128)(2,1)S(1)} %turn.1.turned_ref), custom_call_target="tpu_custom_call" | custom-call | tf_op jit(solution)/shard_map/project/pallas_call | solution.py:30
  8.9 2.5 %collective-permute-start.4 = (bf16[80,512]{1,0:T(8,128)(2,1)S(1)}, bf16[80,512]{1,0:T(8,128)(2,1)S(1)}, u32[]{:S(2)}, u32[]{:S(2)}) collective-permute-start(bf16[80,512]{1,0:T(8,128)(2,1)S(1)} %project.1.refs_0_), channel_id=1, source_target_pairs={{0,3},{1,2},{2,1},{3,0},{4,7},{5,6},{6,5},{7,4},{8,11},{9,10},{10,... | collective-permute-start | bytes 245768 | tf_op jit(solution)/shard_map/ppermute | solution.py:65
  11.4 0.5 %collective-permute-start.8 = (bf16[80,512]{1,0:T(8,128)(2,1)S(1)}, bf16[80,512]{1,0:T(8,128)(2,1)S(1)}, u32[]{:S(2)}, u32[]{:S(2)}) collective-permute-start(bf16[80,512]{1,0:T(8,128)(2,1)S(1)} %project.1.refs_0_), channel_id=1, source_target_pairs={{0,2},{1,3},{2,0},{3,1},{4,6},{5,7},{6,4},{7,5},{8,10},{9,11},{10,... | collective-permute-start | bytes 245768 | tf_op jit(solution)/shard_map/ppermute | solution.py:65
  11.9 0.5 %collective-permute-start.7 = (bf16[80,512]{1,0:T(8,128)(2,1)S(1)}, bf16[80,512]{1,0:T(8,128)(2,1)S(1)}, u32[]{:S(2)}, u32[]{:S(2)}) collective-permute-start(bf16[80,512]{1,0:T(8,128)(2,1)S(1)} %project.1.refs_0_), channel_id=1, source_target_pairs={{0,1},{1,0},{2,3},{3,2},{4,5},{5,4},{6,7},{7,6},{8,9},{9,8},{10,11... | collective-permute-start | bytes 245768 | tf_op jit(solution)/shard_map/ppermute | solution.py:65
  12.4 0.0 copy-done.5
  12.4 1.1 %match.1 = (bf16[256,512]{1,0:T(8,128)(2,1)S(1)}, bf16[256,512]{1,0:T(8,128)(2,1)S(1)}, bf16[256,512]{1,0:T(8,128)(2,1)S(1)}, bf16[256,512]{1,0:T(8,128)(2,1)S(1...) custom-call(s32[4,32]{1,0:T(4,128)S(1)} %copy-done.5), custom_call_target="tpu_custom_call" | custom-call | tf_op jit(solution)/shard_map/match/pallas_call | solution.py:30
  13.6 1.2 %collective-permute-done.4.refs_0_.refs_1_ = bf16[80,512]{1,0:T(8,128)(2,1)S(1)} collective-permute-done((bf16[80,512]{1,0:T(8,128)(2,1)S(1)}, bf16[80,512]{1,0:T(8,128)(2,1)S(1)}, u32[]{:S(2)}, u32[]{:S(2)}) %collective-permute-start.4) | collective-permute-done | bytes 81952 | tf_op jit(solution)/shard_map/ppermute | solution.py:65
  14.8 0.4 %partly.1 = (f32[32,512]{1,0:T(8,128)S(1)}, f32[64,512]{1,0:T(8,128)S(1)}) custom-call(bf16[80,512]{1,0:T(8,128)(2,1)S(1)} %project.1.refs_0_, bf16[80,512]{1,0:T(8,128)(2,1)S(1)} %collective-permute-done.4.refs_0_.refs_1_, bf16[256,512]{1,0:T(8,128)(2,1)S(1)} %get-tuple-element.23.refs_1_.refs_2_, bf16[256,512]{1,0:T(8,128)(2,1)S(1)} %get-tuple-element.30.refs_3_, ...), custom_call_target="tpu_custom_call" | custom-call | tf_op jit(solution)/shard_map/partly/pallas_call | solution.py:30
  15.2 0.0 collective-permute-done.block_ref.one
  15.2 0.1 halves.3
  15.3 0.5 %collective-permute-start.5 = (bf16[32,6144]{1,0:T(8,128)(2,1)S(1)}, bf16[32,6144]{1,0:T(8,128)(2,1)S(1)}, u32[]{:S(2)}, u32[]{:S(2)}) collective-permute-start(bf16[32,6144]{1,0:T(8,128)(2,1)S(1)} %get-tuple-element.24), channel_id=1, source_target_pairs={{0,4},{4,0},{8,12},{12,8},{16,20},{20,16},{24,28},{28,24},{1,5},{5... | collective-permute-start | bytes 1179656 | tf_op jit(solution)/shard_map/ppermute | solution.py:49
  15.8 0.1 collective-permute-start.6
  15.9 1.0 %collective-permute-done.8.refs_1_ = bf16[80,512]{1,0:T(8,128)(2,1)S(1)} collective-permute-done((bf16[80,512]{1,0:T(8,128)(2,1)S(1)}, bf16[80,512]{1,0:T(8,128)(2,1)S(1)}, u32[]{:S(2)}, u32[]{:S(2)}) %collective-permute-start.8) | collective-permute-done | bytes 81952 | tf_op jit(solution)/shard_map/ppermute | solution.py:65
  16.9 0.1 collective-permute-done.7.refs_0_
  17.0 0.7 %couple.1.after_ref.mine = bf16[64,512]{1,0:T(8,128)(2,1)S(1)} custom-call(bf16[80,512]{1,0:T(8,128)(2,1)S(1)} %collective-permute-done.7.refs_0_, bf16[80,512]{1,0:T(8,128)(2,1)S(1)} %collective-permute-done.8.refs_1_, bf16[256,512]{1,0:T(8,128)(2,1)S(1)} %get-tuple-element.26.refs_2_, bf16[256,512]{1,0:T(8,128)(2,1)S(1)} %get-tuple-element.27.refs_3_, ...), custom_call_target="tpu_custom_call" | custom-call | flops 4000000000 | tf_op jit(solution)/shard_map/couple/pallas_call | solution.py:30
  17.7 0.0 copy-start.3
  17.7 1.6 %collective-permute-start.10 = (bf16[64,512]{1,0:T(8,128)(2,1)S(1)}, bf16[64,512]{1,0:T(8,128)(2,1)S(1)}, u32[]{:S(2)}, u32[]{:S(2)}) collective-permute-start(bf16[64,512]{1,0:T(8,128)(2,1)S(1)} %couple.1.after_ref.mine), channel_id=1, source_target_pairs={{0,8},{4,12},{8,16},{12,20},{16,24},{20,28},{24,0},{28,4},{1,9},{5... | collective-permute-start | bytes 196616 | tf_op jit(solution)/shard_map/ppermute | solution.py:44
  19.3 0.0 collective-permute-done.5.upper_ref.upper
  19.3 0.0 collective-permute-done.6.lower_ref.lower
  19.3 0.1 collective-permute-start.9
  19.4 4.8 %collective-permute-done.10.mine_two.two = bf16[64,512]{1,0:T(8,128)(2,1)S(1)} collective-permute-done((bf16[64,512]{1,0:T(8,128)(2,1)S(1)}, bf16[64,512]{1,0:T(8,128)(2,1)S(1)}, u32[]{:S(2)}, u32[]{:S(2)}) %collective-permute-start.10) | collective-permute-done | bytes 65568 | tf_op jit(solution)/shard_map/ppermute | solution.py:44
  24.2 0.0 collective-permute-done.3.two
  24.2 0.1 choose.1
  24.3 0.1 collective-permute-start.11
  24.4 0.5 %collective-permute-start.12 = (bf16[64,512]{1,0:T(8,128)(2,1)S(1)}, bf16[64,512]{1,0:T(8,128)(2,1)S(1)}, u32[]{:S(2)}, u32[]{:S(2)}) collective-permute-start(bf16[64,512]{1,0:T(8,128)(2,1)S(1)} %collective-permute-done.10.mine_two.two), channel_id=1, source_target_pairs={{0,4},{4,8},{8,12},{12,16},{16,20},{20,24},{24,28},{28,0},{1,5},{5... | collective-permute-start | bytes 196616 | tf_op jit(solution)/shard_map/ppermute | solution.py:44
  24.9 0.0 collective-permute-start.13
  24.9 5.7 %collective-permute-done.9.three_a = bf16[48,6144]{1,0:T(8,128)(2,1)S(1)} collective-permute-done((bf16[48,6144]{1,0:T(8,128)(2,1)S(1)}, bf16[48,6144]{1,0:T(8,128)(2,1)S(1)}, u32[]{:S(2)}, u32[]{:S(2)}) %collective-permute-start.9) | collective-permute-done | bytes 589856 | tf_op jit(solution)/shard_map/ppermute | solution.py:44
  30.5 0.0 copy-done.3
  30.5 0.8 %gather.1.after_ref.partial_ref = f32[64,6144]{1,0:T(8,128)S(1)} custom-call(bf16[64,256]{1,0:T(8,128)(2,1)S(1)} %copy-done.3, bf16[64,6144]{1,0:T(8,128)(2,1)S(1)} %copy-done.2, bf16[64,6144]{1,0:T(8,128)(2,1)S(1)} %collective-permute-done.block_ref.one, bf16[64,6144]{1,0:T(8,128)(2,1)S(1)} %collective-permute-done.3.two, ...), custom_call_target="tpu_custom_call" | custom-call | flops 4499999744 | tf_op jit(solution)/shard_map/gather/pallas_call | solution.py:30
  31.4 0.0 collective-permute-done.12.three
  31.4 0.0 collective-permute-done.11.swap_ref
  31.4 1.4 %apply.1.applied = f32[64,6144]{1,0:T(8,128)S(1)} custom-call(bf16[64,256]{1,0:T(8,128)(2,1)S(1)} %copy-done.3, bf16[64,512]{1,0:T(8,128)(2,1)S(1)} %couple.1.after_ref.mine, bf16[80,6144]{1,0:T(8,128)(2,1)S(1)} %collective-permute-done.11.swap_ref, bf16[64,512]{1,0:T(8,128)(2,1)S(1)} %collective-permute-done.10.mine_two.two, ...), custom_call_target="tpu_custom_call" | custom-call | flops 5000000000 | tf_op jit(solution)/shard_map/apply/pallas_call | solution.py:30
  32.8 0.4 %add.1.partial_ref = f32[64,6144]{1,0:T(8,128)S(1)} custom-call(bf16[64,256]{1,0:T(8,128)(2,1)S(1)} %copy-done.3, f32[64,6144]{1,0:T(8,128)S(1)} %gather.1.after_ref.partial_ref, bf16[80,6144]{1,0:T(8,128)(2,1)S(1)} %collective-permute-done.11.swap_ref, f32[64,6144]{1,0:T(8,128)S(1)} %apply.1.applied), custom_call_target="tpu_custom_call" | custom-call | tf_op jit(solution)/shard_map/add/pallas_call | solution.py:30
  33.2 0.1 collective-permute-done.13.last_ref
  33.3 1.2 %finish.1 = bf16[64,6144]{1,0:T(8,128)(2,1)} custom-call(bf16[64,256]{1,0:T(8,128)(2,1)S(1)} %copy-done.3, f32[64,6144]{1,0:T(8,128)S(1)} %add.1.partial_ref, bf16[16,6144]{1,0:T(8,128)(2,1)S(1)} %collective-permute-done.13.last_ref, f32[64,6144]{1,0:T(8,128)S(1)} %apply.1.applied), custom_call_target="tpu_custom_call" | custom-call | tf_op jit(solution)/shard_map/finish/pallas_call | solution.py:405
  (1 shorter events, 0.0 us)
Async XLA Ops:
  0.0 15.2 %collective-permute-start = (bf16[64,6144]{1,0:T(8,128)(2,1)}, bf16[64,6144]{1,0:T(8,128)(2,1)S(1)}, u32[]{:S(2)}, u32[]{:S(2)}) collective-permute-start(bf16[64,6144]{1,0:T(8,128)(2,1)} %own.1), channel_id=1, source_target_pairs={{0,4},{4,8},{8,12},{12,16},{16,20},{20,24},{24,28},{28,0},{1,5},{5... | collective-permute-start | bytes 2359304 | tf_op jit(solution)/shard_map/ppermute | solution.py:44
  0.5 1.1 %copy-start.1 = (bf16[64,6144]{1,0:T(8,128)(2,1)S(1)}, bf16[64,6144]{1,0:T(8,128)(2,1)}, u32[]{:S(2)}) copy-start(bf16[64,6144]{1,0:T(8,128)(2,1)} %own.1) | copy-start | bytes 2359300
  1.6 5.4 %copy-start = (bf16[32,16,6144]{2,1,0:T(8,128)(2,1)S(1)}, bf16[32,16,6144]{2,1,0:T(8,128)(2,1)}, u32[]{:S(2)}) copy-start(bf16[32,16,6144]{2,1,0:T(8,128)(2,1)} %param.7) | copy-start | bytes 18874372
  1.6 5.2 %copy-start.4 = (f32[16,16,16]{2,1,0:T(8,128)S(1)}, f32[16,16,16]{2,1,0:T(8,128)}, u32[]{:S(2)}) copy-start(f32[16,16,16]{2,1,0:T(8,128)} %param.8) | copy-start | bytes 49156
  1.7 5.3 %copy-start.2 = (bf16[64,6144]{1,0:T(8,128)(2,1)S(1)}, bf16[64,6144]{1,0:T(8,128)(2,1)}, u32[]{:S(2)}) copy-start(bf16[64,6144]{1,0:T(8,128)(2,1)} %own.1) | copy-start | bytes 2359300
  1.7 4.1 %collective-permute-start.1 = (bf16[32,6144]{1,0:T(8,128)(2,1)S(1)}, bf16[32,6144]{1,0:T(8,128)(2,1)S(1)}, u32[]{:S(2)}, u32[]{:S(2)}) collective-permute-start(bf16[32,6144]{1,0:T(8,128)(2,1)S(1)} %get-tuple-element.21), channel_id=1, source_target_pairs={{0,4},{4,0},{8,12},{12,8},{16,20},{20,16},{24,28},{28,24},{1,5},{5... | collective-permute-start | bytes 1179656 | tf_op jit(solution)/shard_map/ppermute | solution.py:49
  4.5 1.9 %collective-permute-start.2 = (bf16[32,6144]{1,0:T(8,128)(2,1)S(1)}, bf16[32,6144]{1,0:T(8,128)(2,1)S(1)}, u32[]{:S(2)}, u32[]{:S(2)}) collective-permute-start(bf16[32,6144]{1,0:T(8,128)(2,1)S(1)} %get-tuple-element.22), channel_id=1, source_target_pairs={{0,4},{4,0},{8,12},{12,8},{16,20},{20,16},{24,28},{28,24},{1,5},{5... | collective-permute-start | bytes 1179656 | tf_op jit(solution)/shard_map/ppermute | solution.py:49
  6.4 17.8 %collective-permute-start.3 = (bf16[64,6144]{1,0:T(8,128)(2,1)S(1)}, bf16[64,6144]{1,0:T(8,128)(2,1)S(1)}, u32[]{:S(2)}, u32[]{:S(2)}) collective-permute-start(bf16[64,6144]{1,0:T(8,128)(2,1)S(1)} %hold.2), channel_id=1, source_target_pairs={{0,4},{4,8},{8,12},{12,16},{16,20},{20,24},{24,28},{28,0},{1,5},{5... | collective-permute-start | bytes 2359304 | tf_op jit(solution)/shard_map/ppermute | solution.py:44
  7.0 5.4 %copy-start.5 = (s32[4,32]{1,0:T(4,128)S(1)}, s32[4,32]{1,0:T(4,128)}, u32[]{:S(2)}) copy-start(s32[4,32]{1,0:T(4,128)} %slot_ref.1) | copy-start | bytes 1540
  8.9 5.9 %collective-permute-start.4 = (bf16[80,512]{1,0:T(8,128)(2,1)S(1)}, bf16[80,512]{1,0:T(8,128)(2,1)S(1)}, u32[]{:S(2)}, u32[]{:S(2)}) collective-permute-start(bf16[80,512]{1,0:T(8,128)(2,1)S(1)} %project.1.refs_0_), channel_id=1, source_target_pairs={{0,3},{1,2},{2,1},{3,0},{4,7},{5,6},{6,5},{7,4},{8,11},{9,10},{10,... | collective-permute-start | bytes 245768 | tf_op jit(solution)/shard_map/ppermute | solution.py:65
  11.4 5.5 %collective-permute-start.8 = (bf16[80,512]{1,0:T(8,128)(2,1)S(1)}, bf16[80,512]{1,0:T(8,128)(2,1)S(1)}, u32[]{:S(2)}, u32[]{:S(2)}) collective-permute-start(bf16[80,512]{1,0:T(8,128)(2,1)S(1)} %project.1.refs_0_), channel_id=1, source_target_pairs={{0,2},{1,3},{2,0},{3,1},{4,6},{5,7},{6,4},{7,5},{8,10},{9,11},{10,... | collective-permute-start | bytes 245768 | tf_op jit(solution)/shard_map/ppermute | solution.py:65
  11.9 5.1 %collective-permute-start.7 = (bf16[80,512]{1,0:T(8,128)(2,1)S(1)}, bf16[80,512]{1,0:T(8,128)(2,1)S(1)}, u32[]{:S(2)}, u32[]{:S(2)}) collective-permute-start(bf16[80,512]{1,0:T(8,128)(2,1)S(1)} %project.1.refs_0_), channel_id=1, source_target_pairs={{0,1},{1,0},{2,3},{3,2},{4,5},{5,4},{6,7},{7,6},{8,9},{9,8},{10,11... | collective-permute-start | bytes 245768 | tf_op jit(solution)/shard_map/ppermute | solution.py:65
  15.3 4.0 %collective-permute-start.5 = (bf16[32,6144]{1,0:T(8,128)(2,1)S(1)}, bf16[32,6144]{1,0:T(8,128)(2,1)S(1)}, u32[]{:S(2)}, u32[]{:S(2)}) collective-permute-start(bf16[32,6144]{1,0:T(8,128)(2,1)S(1)} %get-tuple-element.24), channel_id=1, source_target_pairs={{0,4},{4,0},{8,12},{12,8},{16,20},{20,16},{24,28},{28,24},{1,5},{5... | collective-permute-start | bytes 1179656 | tf_op jit(solution)/shard_map/ppermute | solution.py:49
  15.8 3.5 %collective-permute-start.6 = (bf16[32,6144]{1,0:T(8,128)(2,1)S(1)}, bf16[32,6144]{1,0:T(8,128)(2,1)S(1)}, u32[]{:S(2)}, u32[]{:S(2)}) collective-permute-start(bf16[32,6144]{1,0:T(8,128)(2,1)S(1)} %get-tuple-element.25), channel_id=1, source_target_pairs={{0,4},{4,0},{8,12},{12,8},{16,20},{20,16},{24,28},{28,24},{1,5},{5... | collective-permute-start | bytes 1179656 | tf_op jit(solution)/shard_map/ppermute | solution.py:49
  17.7 12.9 %copy-start.3 = (bf16[64,256]{1,0:T(8,128)(2,1)S(1)}, bf16[64,256]{1,0:T(8,128)(2,1)}, u32[]{:S(2)}) copy-start(bf16[64,256]{1,0:T(8,128)(2,1)} %rot_ref.7) | copy-start | bytes 98308
  17.7 6.5 %collective-permute-start.10 = (bf16[64,512]{1,0:T(8,128)(2,1)S(1)}, bf16[64,512]{1,0:T(8,128)(2,1)S(1)}, u32[]{:S(2)}, u32[]{:S(2)}) collective-permute-start(bf16[64,512]{1,0:T(8,128)(2,1)S(1)} %couple.1.after_ref.mine), channel_id=1, source_target_pairs={{0,8},{4,12},{8,16},{12,20},{16,24},{20,28},{24,0},{28,4},{1,9},{5... | collective-permute-start | bytes 196616 | tf_op jit(solution)/shard_map/ppermute | solution.py:44
  19.3 11.2 %collective-permute-start.9 = (bf16[48,6144]{1,0:T(8,128)(2,1)S(1)}, bf16[48,6144]{1,0:T(8,128)(2,1)S(1)}, u32[]{:S(2)}, u32[]{:S(2)}) collective-permute-start(bf16[48,6144]{1,0:T(8,128)(2,1)S(1)} %hold.3), channel_id=1, source_target_pairs={{0,4},{4,8},{8,12},{12,16},{16,20},{20,24},{24,28},{28,0},{1,5},{5... | collective-permute-start | bytes 1769480 | tf_op jit(solution)/shard_map/ppermute | solution.py:44
  24.3 7.1 %collective-permute-start.11 = (bf16[80,6144]{1,0:T(8,128)(2,1)S(1)}, bf16[80,6144]{1,0:T(8,128)(2,1)S(1)}, u32[]{:S(2)}, u32[]{:S(2)}) collective-permute-start(bf16[80,6144]{1,0:T(8,128)(2,1)S(1)} %get-tuple-element.35), channel_id=1, source_target_pairs={{0,4},{4,0},{8,12},{12,8},{16,20},{20,16},{24,28},{28,24},{1,5},{5... | collective-permute-start | bytes 2949128 | tf_op jit(solution)/shard_map/ppermute | solution.py:49
  24.4 7.0 %collective-permute-start.12 = (bf16[64,512]{1,0:T(8,128)(2,1)S(1)}, bf16[64,512]{1,0:T(8,128)(2,1)S(1)}, u32[]{:S(2)}, u32[]{:S(2)}) collective-permute-start(bf16[64,512]{1,0:T(8,128)(2,1)S(1)} %collective-permute-done.10.mine_two.two), channel_id=1, source_target_pairs={{0,4},{4,8},{8,12},{12,16},{16,20},{20,24},{24,28},{28,0},{1,5},{5... | collective-permute-start | bytes 196616 | tf_op jit(solution)/shard_map/ppermute | solution.py:44
  24.9 8.5 %collective-permute-start.13 = (bf16[16,6144]{1,0:T(8,128)(2,1)S(1)}, bf16[16,6144]{1,0:T(8,128)(2,1)S(1)}, u32[]{:S(2)}, u32[]{:S(2)}) collective-permute-start(bf16[16,6144]{1,0:T(8,128)(2,1)S(1)} %get-tuple-element.36), channel_id=1, source_target_pairs={{0,4},{4,8},{8,12},{12,16},{16,20},{20,24},{24,28},{28,0},{1,5},{5... | collective-permute-start | bytes 589832 | tf_op jit(solution)/shard_map/ppermute | solution.py:44

commit v13 on v12

--- a/solution.py
+++ b/solution.py
@@ -401,7 +401,7 @@
 
 def finish(*args):
     width, points = args[-1].shape
-    pieces = points // tile_of(points, 1536)
+    pieces = points // tile_of(points, 2048)
     return pl.pallas_call(
         finish_kernel,
         in_specs=[VMEM] * len(args),

time: 34.6 us -> 34.7 us (level)
  no operation moved by 1% of the time
where the time goes in v13:
time: 34.7 us; the launch traced here: 34.5 us
  waiting for transfers between devices  14.8 us (43%)
  starting transfers between devices  10.2 us (29%)
  Pallas kernels  8.26 us (24%)
  local copies, waits for them, and re-layouts  1.17 us (3%)
    ppermute x6, waiting for transfers between devices, along_bands(): lax.ppermute(block, 'band', [(i, (i + distance) % count) for i in range(c...  10.5 us
    pallas_call x13, Pallas kernels, call(): pl.pallas_call(kernel, in_specs=[first] + [VMEM] * (len(args) - 1), out_s...  7.08 us
    ppermute x3, starting transfers between devices, from_all_domains(): return [block] + [lax.ppermute(block, 'dom', route) for route in routes]  3.55 us
    ppermute x5, starting transfers between devices, swapped(): return lax.ppermute(block, 'band', [(i, i ^ 1) for i in range(count)])  3.54 us
    ppermute x6, starting transfers between devices, along_bands(): lax.ppermute(block, 'band', [(i, (i + distance) % count) for i in range(c...  3.07 us
    ppermute x3, waiting for transfers between devices, from_all_domains(): return [block] + [lax.ppermute(block, 'dom', route) for route in routes]  2.37 us
    ppermute x5, waiting for transfers between devices, swapped(): return lax.ppermute(block, 'band', [(i, i ^ 1) for i in range(count)])  1.84 us
    pallas_call x1, Pallas kernels, finish(): pl.pallas_call(finish_kernel, in_specs=[VMEM] * len(args), out_specs=pl.B...  1.18 us
  transfers between devices with their start and end apart: 14, of which 8 were waited for; matrix products, arithmetic and copies ran while one was open for 0% of the time, Pallas kernels for 21%

profile of v13, /device:TPU:0, one launch (start us, length us, event | category | flops | bytes accessed | tf_op | source)
XLA Modules:
  0.0 34.5 jit_solution(350412075358828286)
XLA Ops:
  0.0 0.5 %collective-permute-start = (bf16[64,6144]{1,0:T(8,128)(2,1)}, bf16[64,6144]{1,0:T(8,128)(2,1)S(1)}, u32[]{:S(2)}, u32[]{:S(2)}) collective-permute-start(bf16[64,6144]{1,0:T(8,128)(2,1)} %own.1), channel_id=1, source_target_pairs={{0,4},{4,8},{8,12},{12,16},{16,20},{20,24},{24,28},{28,0},{1,5},{5... | collective-permute-start | bytes 2359304 | tf_op jit(solution)/shard_map/ppermute | solution.py:44
  0.5 0.0 copy-start.1
  0.5 1.1 %copy-done.1 = bf16[64,6144]{1,0:T(8,128)(2,1)S(1)} copy-done((bf16[64,6144]{1,0:T(8,128)(2,1)S(1)}, bf16[64,6144]{1,0:T(8,128)(2,1)}, u32[]{:S(2)}) %copy-start.1) | copy-done | bytes 786456
  1.6 0.0 copy-start
  1.6 0.1 halves.2
  1.6 0.0 copy-start.4
  1.7 0.0 copy-start.2
  1.7 2.8 %collective-permute-start.1 = (bf16[32,6144]{1,0:T(8,128)(2,1)S(1)}, bf16[32,6144]{1,0:T(8,128)(2,1)S(1)}, u32[]{:S(2)}, u32[]{:S(2)}) collective-permute-start(bf16[32,6144]{1,0:T(8,128)(2,1)S(1)} %get-tuple-element.21), channel_id=1, source_target_pairs={{0,4},{4,0},{8,12},{12,8},{16,20},{20,16},{24,28},{28,24},{1,5},{5... | collective-permute-start | bytes 1179656 | tf_op jit(solution)/shard_map/ppermute | solution.py:49
  4.5 0.1 collective-permute-start.2
  4.5 1.3 %collective-permute-done.1.upper_ref.after_ref = bf16[32,6144]{1,0:T(8,128)(2,1)S(1)} collective-permute-done((bf16[32,6144]{1,0:T(8,128)(2,1)S(1)}, bf16[32,6144]{1,0:T(8,128)(2,1)S(1)}, u32[]{:S(2)}, u32[]{:S(2)}) %collective-permute-start.1) | collective-permute-done | bytes 393248 | tf_op jit(solution)/shard_map/ppermute | solution.py:49
  5.8 0.6 %collective-permute-done.2.lower_ref = bf16[32,6144]{1,0:T(8,128)(2,1)S(1)} collective-permute-done((bf16[32,6144]{1,0:T(8,128)(2,1)S(1)}, bf16[32,6144]{1,0:T(8,128)(2,1)S(1)}, u32[]{:S(2)}, u32[]{:S(2)}) %collective-permute-start.2) | collective-permute-done | bytes 393248 | tf_op jit(solution)/shard_map/ppermute | solution.py:49
  6.4 0.1 hold.2
  6.4 0.4 %collective-permute-start.3 = (bf16[64,6144]{1,0:T(8,128)(2,1)S(1)}, bf16[64,6144]{1,0:T(8,128)(2,1)S(1)}, u32[]{:S(2)}, u32[]{:S(2)}) collective-permute-start(bf16[64,6144]{1,0:T(8,128)(2,1)S(1)} %hold.2), channel_id=1, source_target_pairs={{0,4},{4,8},{8,12},{12,16},{16,20},{20,24},{24,28},{28,0},{1,5},{5... | collective-permute-start | bytes 2359304 | tf_op jit(solution)/shard_map/ppermute | solution.py:44
  6.8 0.0 copy-done.4
  6.9 0.1 turn.1.turned_ref
  7.0 0.0 copy-done
  7.0 0.0 copy-done.2
  7.0 0.0 copy-start.5
  7.0 1.8 %project.1.refs_0_ = bf16[80,512]{1,0:T(8,128)(2,1)S(1)} custom-call(bf16[64,6144]{1,0:T(8,128)(2,1)S(1)} %copy-done.2, bf16[512,6144]{1,0:T(8,128)(2,1)S(1)} %bitcast.2, bf16[16,512]{1,0:T(8,128)(2,1)S(1)} %turn.1.turned_ref), custom_call_target="tpu_custom_call" | custom-call | tf_op jit(solution)/shard_map/project/pallas_call | solution.py:30
  8.9 2.5 %collective-permute-start.4 = (bf16[80,512]{1,0:T(8,128)(2,1)S(1)}, bf16[80,512]{1,0:T(8,128)(2,1)S(1)}, u32[]{:S(2)}, u32[]{:S(2)}) collective-permute-start(bf16[80,512]{1,0:T(8,128)(2,1)S(1)} %project.1.refs_0_), channel_id=1, source_target_pairs={{0,3},{1,2},{2,1},{3,0},{4,7},{5,6},{6,5},{7,4},{8,11},{9,10},{10,... | collective-permute-start | bytes 245768 | tf_op jit(solution)/shard_map/ppermute | solution.py:65
  11.4 0.5 %collective-permute-start.8 = (bf16[80,512]{1,0:T(8,128)(2,1)S(1)}, bf16[80,512]{1,0:T(8,128)(2,1)S(1)}, u32[]{:S(2)}, u32[]{:S(2)}) collective-permute-start(bf16[80,512]{1,0:T(8,128)(2,1)S(1)} %project.1.refs_0_), channel_id=1, source_target_pairs={{0,2},{1,3},{2,0},{3,1},{4,6},{5,7},{6,4},{7,5},{8,10},{9,11},{10,... | collective-permute-start | bytes 245768 | tf_op jit(solution)/shard_map/ppermute | solution.py:65
  11.9 0.5 %collective-permute-start.7 = (bf16[80,512]{1,0:T(8,128)(2,1)S(1)}, bf16[80,512]{1,0:T(8,128)(2,1)S(1)}, u32[]{:S(2)}, u32[]{:S(2)}) collective-permute-start(bf16[80,512]{1,0:T(8,128)(2,1)S(1)} %project.1.refs_0_), channel_id=1, source_target_pairs={{0,1},{1,0},{2,3},{3,2},{4,5},{5,4},{6,7},{7,6},{8,9},{9,8},{10,11... | collective-permute-start | bytes 245768 | tf_op jit(solution)/shard_map/ppermute | solution.py:65
  12.4 0.0 copy-done.5
  12.4 1.1 %match.1 = (bf16[256,512]{1,0:T(8,128)(2,1)S(1)}, bf16[256,512]{1,0:T(8,128)(2,1)S(1)}, bf16[256,512]{1,0:T(8,128)(2,1)S(1)}, bf16[256,512]{1,0:T(8,128)(2,1)S(1...) custom-call(s32[4,32]{1,0:T(4,128)S(1)} %copy-done.5), custom_call_target="tpu_custom_call" | custom-call | tf_op jit(solution)/shard_map/match/pallas_call | solution.py:30
  13.6 1.2 %collective-permute-done.4.refs_0_.refs_1_ = bf16[80,512]{1,0:T(8,128)(2,1)S(1)} collective-permute-done((bf16[80,512]{1,0:T(8,128)(2,1)S(1)}, bf16[80,512]{1,0:T(8,128)(2,1)S(1)}, u32[]{:S(2)}, u32[]{:S(2)}) %collective-permute-start.4) | collective-permute-done | bytes 81952 | tf_op jit(solution)/shard_map/ppermute | solution.py:65
  14.8 0.4 %partly.1 = (f32[32,512]{1,0:T(8,128)S(1)}, f32[64,512]{1,0:T(8,128)S(1)}) custom-call(bf16[80,512]{1,0:T(8,128)(2,1)S(1)} %project.1.refs_0_, bf16[80,512]{1,0:T(8,128)(2,1)S(1)} %collective-permute-done.4.refs_0_.refs_1_, bf16[256,512]{1,0:T(8,128)(2,1)S(1)} %get-tuple-element.23.refs_1_.refs_2_, bf16[256,512]{1,0:T(8,128)(2,1)S(1)} %get-tuple-element.30.refs_3_, ...), custom_call_target="tpu_custom_call" | custom-call | tf_op jit(solution)/shard_map/partly/pallas_call | solution.py:30
  15.2 0.0 collective-permute-done.block_ref.one
  15.2 0.1 halves.3
  15.3 0.5 %collective-permute-start.5 = (bf16[32,6144]{1,0:T(8,128)(2,1)S(1)}, bf16[32,6144]{1,0:T(8,128)(2,1)S(1)}, u32[]{:S(2)}, u32[]{:S(2)}) collective-permute-start(bf16[32,6144]{1,0:T(8,128)(2,1)S(1)} %get-tuple-element.24), channel_id=1, source_target_pairs={{0,4},{4,0},{8,12},{12,8},{16,20},{20,16},{24,28},{28,24},{1,5},{5... | collective-permute-start | bytes 1179656 | tf_op jit(solution)/shard_map/ppermute | solution.py:49
  15.8 0.1 collective-permute-start.6
  15.9 1.0 %collective-permute-done.8.refs_1_ = bf16[80,512]{1,0:T(8,128)(2,1)S(1)} collective-permute-done((bf16[80,512]{1,0:T(8,128)(2,1)S(1)}, bf16[80,512]{1,0:T(8,128)(2,1)S(1)}, u32[]{:S(2)}, u32[]{:S(2)}) %collective-permute-start.8) | collective-permute-done | bytes 81952 | tf_op jit(solution)/shard_map/ppermute | solution.py:65
  16.9 0.1 collective-permute-done.7.refs_0_
  17.0 0.7 %couple.1.after_ref.mine = bf16[64,512]{1,0:T(8,128)(2,1)S(1)} custom-call(bf16[80,512]{1,0:T(8,128)(2,1)S(1)} %collective-permute-done.7.refs_0_, bf16[80,512]{1,0:T(8,128)(2,1)S(1)} %collective-permute-done.8.refs_1_, bf16[256,512]{1,0:T(8,128)(2,1)S(1)} %get-tuple-element.26.refs_2_, bf16[256,512]{1,0:T(8,128)(2,1)S(1)} %get-tuple-element.27.refs_3_, ...), custom_call_target="tpu_custom_call" | custom-call | flops 4000000000 | tf_op jit(solution)/shard_map/couple/pallas_call | solution.py:30
  17.7 0.0 copy-start.3
  17.7 1.6 %collective-permute-start.10 = (bf16[64,512]{1,0:T(8,128)(2,1)S(1)}, bf16[64,512]{1,0:T(8,128)(2,1)S(1)}, u32[]{:S(2)}, u32[]{:S(2)}) collective-permute-start(bf16[64,512]{1,0:T(8,128)(2,1)S(1)} %couple.1.after_ref.mine), channel_id=1, source_target_pairs={{0,8},{4,12},{8,16},{12,20},{16,24},{20,28},{24,0},{28,4},{1,9},{5... | collective-permute-start | bytes 196616 | tf_op jit(solution)/shard_map/ppermute | solution.py:44
  19.3 0.0 collective-permute-done.5.upper_ref.upper
  19.3 0.0 collective-permute-done.6.lower_ref.lower
  19.3 0.1 collective-permute-start.9
  19.4 4.8 %collective-permute-done.10.mine_two.two = bf16[64,512]{1,0:T(8,128)(2,1)S(1)} collective-permute-done((bf16[64,512]{1,0:T(8,128)(2,1)S(1)}, bf16[64,512]{1,0:T(8,128)(2,1)S(1)}, u32[]{:S(2)}, u32[]{:S(2)}) %collective-permute-start.10) | collective-permute-done | bytes 65568 | tf_op jit(solution)/shard_map/ppermute | solution.py:44
  24.2 0.0 collective-permute-done.3.two
  24.2 0.1 choose.1
  24.3 0.1 collective-permute-start.11
  24.4 0.5 %collective-permute-start.12 = (bf16[64,512]{1,0:T(8,128)(2,1)S(1)}, bf16[64,512]{1,0:T(8,128)(2,1)S(1)}, u32[]{:S(2)}, u32[]{:S(2)}) collective-permute-start(bf16[64,512]{1,0:T(8,128)(2,1)S(1)} %collective-permute-done.10.mine_two.two), channel_id=1, source_target_pairs={{0,4},{4,8},{8,12},{12,16},{16,20},{20,24},{24,28},{28,0},{1,5},{5... | collective-permute-start | bytes 196616 | tf_op jit(solution)/shard_map/ppermute | solution.py:44
  24.9 0.0 collective-permute-start.13
  24.9 5.7 %collective-permute-done.9.three_a = bf16[48,6144]{1,0:T(8,128)(2,1)S(1)} collective-permute-done((bf16[48,6144]{1,0:T(8,128)(2,1)S(1)}, bf16[48,6144]{1,0:T(8,128)(2,1)S(1)}, u32[]{:S(2)}, u32[]{:S(2)}) %collective-permute-start.9) | collective-permute-done | bytes 589856 | tf_op jit(solution)/shard_map/ppermute | solution.py:44
  30.5 0.0 copy-done.3
  30.5 0.8 %gather.1.after_ref.partial_ref = f32[64,6144]{1,0:T(8,128)S(1)} custom-call(bf16[64,256]{1,0:T(8,128)(2,1)S(1)} %copy-done.3, bf16[64,6144]{1,0:T(8,128)(2,1)S(1)} %copy-done.2, bf16[64,6144]{1,0:T(8,128)(2,1)S(1)} %collective-permute-done.block_ref.one, bf16[64,6144]{1,0:T(8,128)(2,1)S(1)} %collective-permute-done.3.two, ...), custom_call_target="tpu_custom_call" | custom-call | flops 4499999744 | tf_op jit(solution)/shard_map/gather/pallas_call | solution.py:30
  31.4 0.0 collective-permute-done.12.three
  31.4 0.0 collective-permute-done.11.swap_ref
  31.4 1.4 %apply.1.applied = f32[64,6144]{1,0:T(8,128)S(1)} custom-call(bf16[64,256]{1,0:T(8,128)(2,1)S(1)} %copy-done.3, bf16[64,512]{1,0:T(8,128)(2,1)S(1)} %couple.1.after_ref.mine, bf16[80,6144]{1,0:T(8,128)(2,1)S(1)} %collective-permute-done.11.swap_ref, bf16[64,512]{1,0:T(8,128)(2,1)S(1)} %collective-permute-done.10.mine_two.two, ...), custom_call_target="tpu_custom_call" | custom-call | flops 5000000000 | tf_op jit(solution)/shard_map/apply/pallas_call | solution.py:30
  32.8 0.4 %add.1.partial_ref = f32[64,6144]{1,0:T(8,128)S(1)} custom-call(bf16[64,256]{1,0:T(8,128)(2,1)S(1)} %copy-done.3, f32[64,6144]{1,0:T(8,128)S(1)} %gather.1.after_ref.partial_ref, bf16[80,6144]{1,0:T(8,128)(2,1)S(1)} %collective-permute-done.11.swap_ref, f32[64,6144]{1,0:T(8,128)S(1)} %apply.1.applied), custom_call_target="tpu_custom_call" | custom-call | tf_op jit(solution)/shard_map/add/pallas_call | solution.py:30
  33.2 0.1 collective-permute-done.13.last_ref
  33.3 1.2 %finish.1 = bf16[64,6144]{1,0:T(8,128)(2,1)} custom-call(bf16[64,256]{1,0:T(8,128)(2,1)S(1)} %copy-done.3, f32[64,6144]{1,0:T(8,128)S(1)} %add.1.partial_ref, bf16[16,6144]{1,0:T(8,128)(2,1)S(1)} %collective-permute-done.13.last_ref, f32[64,6144]{1,0:T(8,128)S(1)} %apply.1.applied), custom_call_target="tpu_custom_call" | custom-call | tf_op jit(solution)/shard_map/finish/pallas_call | solution.py:405
  (1 shorter events, 0.0 us)
Async XLA Ops:
  0.0 15.2 %collective-permute-start = (bf16[64,6144]{1,0:T(8,128)(2,1)}, bf16[64,6144]{1,0:T(8,128)(2,1)S(1)}, u32[]{:S(2)}, u32[]{:S(2)}) collective-permute-start(bf16[64,6144]{1,0:T(8,128)(2,1)} %own.1), channel_id=1, source_target_pairs={{0,4},{4,8},{8,12},{12,16},{16,20},{20,24},{24,28},{28,0},{1,5},{5... | collective-permute-start | bytes 2359304 | tf_op jit(solution)/shard_map/ppermute | solution.py:44
  0.5 1.1 %copy-start.1 = (bf16[64,6144]{1,0:T(8,128)(2,1)S(1)}, bf16[64,6144]{1,0:T(8,128)(2,1)}, u32[]{:S(2)}) copy-start(bf16[64,6144]{1,0:T(8,128)(2,1)} %own.1) | copy-start | bytes 2359300
  1.6 5.4 %copy-start = (bf16[32,16,6144]{2,1,0:T(8,128)(2,1)S(1)}, bf16[32,16,6144]{2,1,0:T(8,128)(2,1)}, u32[]{:S(2)}) copy-start(bf16[32,16,6144]{2,1,0:T(8,128)(2,1)} %param.7) | copy-start | bytes 18874372
  1.6 5.2 %copy-start.4 = (f32[16,16,16]{2,1,0:T(8,128)S(1)}, f32[16,16,16]{2,1,0:T(8,128)}, u32[]{:S(2)}) copy-start(f32[16,16,16]{2,1,0:T(8,128)} %param.8) | copy-start | bytes 49156
  1.7 5.3 %copy-start.2 = (bf16[64,6144]{1,0:T(8,128)(2,1)S(1)}, bf16[64,6144]{1,0:T(8,128)(2,1)}, u32[]{:S(2)}) copy-start(bf16[64,6144]{1,0:T(8,128)(2,1)} %own.1) | copy-start | bytes 2359300
  1.7 4.1 %collective-permute-start.1 = (bf16[32,6144]{1,0:T(8,128)(2,1)S(1)}, bf16[32,6144]{1,0:T(8,128)(2,1)S(1)}, u32[]{:S(2)}, u32[]{:S(2)}) collective-permute-start(bf16[32,6144]{1,0:T(8,128)(2,1)S(1)} %get-tuple-element.21), channel_id=1, source_target_pairs={{0,4},{4,0},{8,12},{12,8},{16,20},{20,16},{24,28},{28,24},{1,5},{5... | collective-permute-start | bytes 1179656 | tf_op jit(solution)/shard_map/ppermute | solution.py:49
  4.5 1.9 %collective-permute-start.2 = (bf16[32,6144]{1,0:T(8,128)(2,1)S(1)}, bf16[32,6144]{1,0:T(8,128)(2,1)S(1)}, u32[]{:S(2)}, u32[]{:S(2)}) collective-permute-start(bf16[32,6144]{1,0:T(8,128)(2,1)S(1)} %get-tuple-element.22), channel_id=1, source_target_pairs={{0,4},{4,0},{8,12},{12,8},{16,20},{20,16},{24,28},{28,24},{1,5},{5... | collective-permute-start | bytes 1179656 | tf_op jit(solution)/shard_map/ppermute | solution.py:49
  6.4 17.8 %collective-permute-start.3 = (bf16[64,6144]{1,0:T(8,128)(2,1)S(1)}, bf16[64,6144]{1,0:T(8,128)(2,1)S(1)}, u32[]{:S(2)}, u32[]{:S(2)}) collective-permute-start(bf16[64,6144]{1,0:T(8,128)(2,1)S(1)} %hold.2), channel_id=1, source_target_pairs={{0,4},{4,8},{8,12},{12,16},{16,20},{20,24},{24,28},{28,0},{1,5},{5... | collective-permute-start | bytes 2359304 | tf_op jit(solution)/shard_map/ppermute | solution.py:44
  7.0 5.4 %copy-start.5 = (s32[4,32]{1,0:T(4,128)S(1)}, s32[4,32]{1,0:T(4,128)}, u32[]{:S(2)}) copy-start(s32[4,32]{1,0:T(4,128)} %slot_ref.1) | copy-start | bytes 1540
  8.9 5.9 %collective-permute-start.4 = (bf16[80,512]{1,0:T(8,128)(2,1)S(1)}, bf16[80,512]{1,0:T(8,128)(2,1)S(1)}, u32[]{:S(2)}, u32[]{:S(2)}) collective-permute-start(bf16[80,512]{1,0:T(8,128)(2,1)S(1)} %project.1.refs_0_), channel_id=1, source_target_pairs={{0,3},{1,2},{2,1},{3,0},{4,7},{5,6},{6,5},{7,4},{8,11},{9,10},{10,... | collective-permute-start | bytes 245768 | tf_op jit(solution)/shard_map/ppermute | solution.py:65
  11.4 5.5 %collective-permute-start.8 = (bf16[80,512]{1,0:T(8,128)(2,1)S(1)}, bf16[80,512]{1,0:T(8,128)(2,1)S(1)}, u32[]{:S(2)}, u32[]{:S(2)}) collective-permute-start(bf16[80,512]{1,0:T(8,128)(2,1)S(1)} %project.1.refs_0_), channel_id=1, source_target_pairs={{0,2},{1,3},{2,0},{3,1},{4,6},{5,7},{6,4},{7,5},{8,10},{9,11},{10,... | collective-permute-start | bytes 245768 | tf_op jit(solution)/shard_map/ppermute | solution.py:65
  11.9 5.1 %collective-permute-start.7 = (bf16[80,512]{1,0:T(8,128)(2,1)S(1)}, bf16[80,512]{1,0:T(8,128)(2,1)S(1)}, u32[]{:S(2)}, u32[]{:S(2)}) collective-permute-start(bf16[80,512]{1,0:T(8,128)(2,1)S(1)} %project.1.refs_0_), channel_id=1, source_target_pairs={{0,1},{1,0},{2,3},{3,2},{4,5},{5,4},{6,7},{7,6},{8,9},{9,8},{10,11... | collective-permute-start | bytes 245768 | tf_op jit(solution)/shard_map/ppermute | solution.py:65
  15.3 4.0 %collective-permute-start.5 = (bf16[32,6144]{1,0:T(8,128)(2,1)S(1)}, bf16[32,6144]{1,0:T(8,128)(2,1)S(1)}, u32[]{:S(2)}, u32[]{:S(2)}) collective-permute-start(bf16[32,6144]{1,0:T(8,128)(2,1)S(1)} %get-tuple-element.24), channel_id=1, source_target_pairs={{0,4},{4,0},{8,12},{12,8},{16,20},{20,16},{24,28},{28,24},{1,5},{5... | collective-permute-start | bytes 1179656 | tf_op jit(solution)/shard_map/ppermute | solution.py:49
  15.8 3.5 %collective-permute-start.6 = (bf16[32,6144]{1,0:T(8,128)(2,1)S(1)}, bf16[32,6144]{1,0:T(8,128)(2,1)S(1)}, u32[]{:S(2)}, u32[]{:S(2)}) collective-permute-start(bf16[32,6144]{1,0:T(8,128)(2,1)S(1)} %get-tuple-element.25), channel_id=1, source_target_pairs={{0,4},{4,0},{8,12},{12,8},{16,20},{20,16},{24,28},{28,24},{1,5},{5... | collective-permute-start | bytes 1179656 | tf_op jit(solution)/shard_map/ppermute | solution.py:49
  17.7 12.9 %copy-start.3 = (bf16[64,256]{1,0:T(8,128)(2,1)S(1)}, bf16[64,256]{1,0:T(8,128)(2,1)}, u32[]{:S(2)}) copy-start(bf16[64,256]{1,0:T(8,128)(2,1)} %rot_ref.7) | copy-start | bytes 98308
  17.7 6.5 %collective-permute-start.10 = (bf16[64,512]{1,0:T(8,128)(2,1)S(1)}, bf16[64,512]{1,0:T(8,128)(2,1)S(1)}, u32[]{:S(2)}, u32[]{:S(2)}) collective-permute-start(bf16[64,512]{1,0:T(8,128)(2,1)S(1)} %couple.1.after_ref.mine), channel_id=1, source_target_pairs={{0,8},{4,12},{8,16},{12,20},{16,24},{20,28},{24,0},{28,4},{1,9},{5... | collective-permute-start | bytes 196616 | tf_op jit(solution)/shard_map/ppermute | solution.py:44
  19.3 11.2 %collective-permute-start.9 = (bf16[48,6144]{1,0:T(8,128)(2,1)S(1)}, bf16[48,6144]{1,0:T(8,128)(2,1)S(1)}, u32[]{:S(2)}, u32[]{:S(2)}) collective-permute-start(bf16[48,6144]{1,0:T(8,128)(2,1)S(1)} %hold.3), channel_id=1, source_target_pairs={{0,4},{4,8},{8,12},{12,16},{16,20},{20,24},{24,28},{28,0},{1,5},{5... | collective-permute-start | bytes 1769480 | tf_op jit(solution)/shard_map/ppermute | solution.py:44
  24.3 7.1 %collective-permute-start.11 = (bf16[80,6144]{1,0:T(8,128)(2,1)S(1)}, bf16[80,6144]{1,0:T(8,128)(2,1)S(1)}, u32[]{:S(2)}, u32[]{:S(2)}) collective-permute-start(bf16[80,6144]{1,0:T(8,128)(2,1)S(1)} %get-tuple-element.35), channel_id=1, source_target_pairs={{0,4},{4,0},{8,12},{12,8},{16,20},{20,16},{24,28},{28,24},{1,5},{5... | collective-permute-start | bytes 2949128 | tf_op jit(solution)/shard_map/ppermute | solution.py:49
  24.4 7.0 %collective-permute-start.12 = (bf16[64,512]{1,0:T(8,128)(2,1)S(1)}, bf16[64,512]{1,0:T(8,128)(2,1)S(1)}, u32[]{:S(2)}, u32[]{:S(2)}) collective-permute-start(bf16[64,512]{1,0:T(8,128)(2,1)S(1)} %collective-permute-done.10.mine_two.two), channel_id=1, source_target_pairs={{0,4},{4,8},{8,12},{12,16},{16,20},{20,24},{24,28},{28,0},{1,5},{5... | collective-permute-start | bytes 196616 | tf_op jit(solution)/shard_map/ppermute | solution.py:44
  24.9 8.5 %collective-permute-start.13 = (bf16[16,6144]{1,0:T(8,128)(2,1)S(1)}, bf16[16,6144]{1,0:T(8,128)(2,1)S(1)}, u32[]{:S(2)}, u32[]{:S(2)}) collective-permute-start(bf16[16,6144]{1,0:T(8,128)(2,1)S(1)} %get-tuple-element.36), channel_id=1, source_target_pairs={{0,4},{4,8},{8,12},{12,16},{16,20},{20,24},{24,28},{28,0},{1,5},{5... | collective-permute-start | bytes 589832 | tf_op jit(solution)/shard_map/ppermute | solution.py:44

commit v14 on v12

--- a/solution.py
+++ b/solution.py
@@ -361,7 +361,7 @@
         for s, block in enumerate(blocks)
     )
     mixed = mixed.astype(BF16)
-    tile = tile_of(points, 1024)
+    tile = tile_of(points, 2048)
     for at in range(0, points, tile):
         out_ref[:, at : at + tile] = jnp.dot(
             mixed, proj_ref[:, at : at + tile], preferred_element_type=F32
@@ -371,7 +371,7 @@
 def add_kernel(rot_ref, partial_ref, swap_ref, applied, out_ref):
     width, points = out_ref.shape
     turn = where_even(rot_ref[:, 3 * width : 4 * width], False)
-    tile = tile_of(points, 1024)
+    tile = tile_of(points, 2048)
     for at in range(0, points, tile):
         here = slice(at, at + tile)
         out_ref[:, here] = partial_ref[:, here] + jnp.dot(

time: 34.6 us -> 34.6 us (level)
  no operation moved by 1% of the time
where the time goes in v14:
time: 34.6 us; the launch traced here: 34.5 us
  waiting for transfers between devices  14.8 us (43%)
  starting transfers between devices  10.2 us (29%)
  Pallas kernels  8.25 us (24%)
  local copies, waits for them, and re-layouts  1.17 us (3%)
    ppermute x6, waiting for transfers between devices, along_bands(): lax.ppermute(block, 'band', [(i, (i + distance) % count) for i in range(c...  10.5 us
    pallas_call x13, Pallas kernels, call(): pl.pallas_call(kernel, in_specs=[first] + [VMEM] * (len(args) - 1), out_s...  7.08 us
    ppermute x3, starting transfers between devices, from_all_domains(): return [block] + [lax.ppermute(block, 'dom', route) for route in routes]  3.55 us
    ppermute x5, starting transfers between devices, swapped(): return lax.ppermute(block, 'band', [(i, i ^ 1) for i in range(count)])  3.54 us
    ppermute x6, starting transfers between devices, along_bands(): lax.ppermute(block, 'band', [(i, (i + distance) % count) for i in range(c...  3.07 us
    ppermute x3, waiting for transfers between devices, from_all_domains(): return [block] + [lax.ppermute(block, 'dom', route) for route in routes]  2.37 us
    ppermute x5, waiting for transfers between devices, swapped(): return lax.ppermute(block, 'band', [(i, i ^ 1) for i in range(count)])  1.84 us
    unnamed x12, local copies, waits for them, and re-layouts  1.17 us
  transfers between devices with their start and end apart: 14, of which 8 were waited for; matrix products, arithmetic and copies ran while one was open for 0% of the time, Pallas kernels for 21%

profile of v14, /device:TPU:0, one launch (start us, length us, event | category | flops | bytes accessed | tf_op | source)
XLA Modules:
  0.0 34.5 jit_solution(17030588377265542460)
XLA Ops:
  0.0 0.5 %collective-permute-start = (bf16[64,6144]{1,0:T(8,128)(2,1)}, bf16[64,6144]{1,0:T(8,128)(2,1)S(1)}, u32[]{:S(2)}, u32[]{:S(2)}) collective-permute-start(bf16[64,6144]{1,0:T(8,128)(2,1)} %own.1), channel_id=1, source_target_pairs={{0,4},{4,8},{8,12},{12,16},{16,20},{20,24},{24,28},{28,0},{1,5},{5... | collective-permute-start | bytes 2359304 | tf_op jit(solution)/shard_map/ppermute | solution.py:44
  0.5 0.0 copy-start.1
  0.5 1.1 %copy-done.1 = bf16[64,6144]{1,0:T(8,128)(2,1)S(1)} copy-done((bf16[64,6144]{1,0:T(8,128)(2,1)S(1)}, bf16[64,6144]{1,0:T(8,128)(2,1)}, u32[]{:S(2)}) %copy-start.1) | copy-done | bytes 786456
  1.6 0.0 copy-start
  1.6 0.1 halves.2
  1.6 0.0 copy-start.4
  1.7 0.0 copy-start.2
  1.7 2.8 %collective-permute-start.1 = (bf16[32,6144]{1,0:T(8,128)(2,1)S(1)}, bf16[32,6144]{1,0:T(8,128)(2,1)S(1)}, u32[]{:S(2)}, u32[]{:S(2)}) collective-permute-start(bf16[32,6144]{1,0:T(8,128)(2,1)S(1)} %get-tuple-element.21), channel_id=1, source_target_pairs={{0,4},{4,0},{8,12},{12,8},{16,20},{20,16},{24,28},{28,24},{1,5},{5... | collective-permute-start | bytes 1179656 | tf_op jit(solution)/shard_map/ppermute | solution.py:49
  4.5 0.1 collective-permute-start.2
  4.5 1.3 %collective-permute-done.1.upper_ref.after_ref = bf16[32,6144]{1,0:T(8,128)(2,1)S(1)} collective-permute-done((bf16[32,6144]{1,0:T(8,128)(2,1)S(1)}, bf16[32,6144]{1,0:T(8,128)(2,1)S(1)}, u32[]{:S(2)}, u32[]{:S(2)}) %collective-permute-start.1) | collective-permute-done | bytes 393248 | tf_op jit(solution)/shard_map/ppermute | solution.py:49
  5.8 0.6 %collective-permute-done.2.lower_ref = bf16[32,6144]{1,0:T(8,128)(2,1)S(1)} collective-permute-done((bf16[32,6144]{1,0:T(8,128)(2,1)S(1)}, bf16[32,6144]{1,0:T(8,128)(2,1)S(1)}, u32[]{:S(2)}, u32[]{:S(2)}) %collective-permute-start.2) | collective-permute-done | bytes 393248 | tf_op jit(solution)/shard_map/ppermute | solution.py:49
  6.4 0.1 hold.2
  6.4 0.4 %collective-permute-start.3 = (bf16[64,6144]{1,0:T(8,128)(2,1)S(1)}, bf16[64,6144]{1,0:T(8,128)(2,1)S(1)}, u32[]{:S(2)}, u32[]{:S(2)}) collective-permute-start(bf16[64,6144]{1,0:T(8,128)(2,1)S(1)} %hold.2), channel_id=1, source_target_pairs={{0,4},{4,8},{8,12},{12,16},{16,20},{20,24},{24,28},{28,0},{1,5},{5... | collective-permute-start | bytes 2359304 | tf_op jit(solution)/shard_map/ppermute | solution.py:44
  6.8 0.0 copy-done.4
  6.9 0.1 turn.1.turned_ref
  7.0 0.0 copy-done
  7.0 0.0 copy-done.2
  7.0 0.0 copy-start.5
  7.0 1.8 %project.1.refs_0_ = bf16[80,512]{1,0:T(8,128)(2,1)S(1)} custom-call(bf16[64,6144]{1,0:T(8,128)(2,1)S(1)} %copy-done.2, bf16[512,6144]{1,0:T(8,128)(2,1)S(1)} %bitcast.2, bf16[16,512]{1,0:T(8,128)(2,1)S(1)} %turn.1.turned_ref), custom_call_target="tpu_custom_call" | custom-call | tf_op jit(solution)/shard_map/project/pallas_call | solution.py:30
  8.9 2.5 %collective-permute-start.4 = (bf16[80,512]{1,0:T(8,128)(2,1)S(1)}, bf16[80,512]{1,0:T(8,128)(2,1)S(1)}, u32[]{:S(2)}, u32[]{:S(2)}) collective-permute-start(bf16[80,512]{1,0:T(8,128)(2,1)S(1)} %project.1.refs_0_), channel_id=1, source_target_pairs={{0,3},{1,2},{2,1},{3,0},{4,7},{5,6},{6,5},{7,4},{8,11},{9,10},{10,... | collective-permute-start | bytes 245768 | tf_op jit(solution)/shard_map/ppermute | solution.py:65
  11.4 0.5 %collective-permute-start.8 = (bf16[80,512]{1,0:T(8,128)(2,1)S(1)}, bf16[80,512]{1,0:T(8,128)(2,1)S(1)}, u32[]{:S(2)}, u32[]{:S(2)}) collective-permute-start(bf16[80,512]{1,0:T(8,128)(2,1)S(1)} %project.1.refs_0_), channel_id=1, source_target_pairs={{0,2},{1,3},{2,0},{3,1},{4,6},{5,7},{6,4},{7,5},{8,10},{9,11},{10,... | collective-permute-start | bytes 245768 | tf_op jit(solution)/shard_map/ppermute | solution.py:65
  11.9 0.5 %collective-permute-start.7 = (bf16[80,512]{1,0:T(8,128)(2,1)S(1)}, bf16[80,512]{1,0:T(8,128)(2,1)S(1)}, u32[]{:S(2)}, u32[]{:S(2)}) collective-permute-start(bf16[80,512]{1,0:T(8,128)(2,1)S(1)} %project.1.refs_0_), channel_id=1, source_target_pairs={{0,1},{1,0},{2,3},{3,2},{4,5},{5,4},{6,7},{7,6},{8,9},{9,8},{10,11... | collective-permute-start | bytes 245768 | tf_op jit(solution)/shard_map/ppermute | solution.py:65
  12.4 0.0 copy-done.5
  12.4 1.1 %match.1 = (bf16[256,512]{1,0:T(8,128)(2,1)S(1)}, bf16[256,512]{1,0:T(8,128)(2,1)S(1)}, bf16[256,512]{1,0:T(8,128)(2,1)S(1)}, bf16[256,512]{1,0:T(8,128)(2,1)S(1...) custom-call(s32[4,32]{1,0:T(4,128)S(1)} %copy-done.5), custom_call_target="tpu_custom_call" | custom-call | tf_op jit(solution)/shard_map/match/pallas_call | solution.py:30
  13.6 1.2 %collective-permute-done.4.refs_0_.refs_1_ = bf16[80,512]{1,0:T(8,128)(2,1)S(1)} collective-permute-done((bf16[80,512]{1,0:T(8,128)(2,1)S(1)}, bf16[80,512]{1,0:T(8,128)(2,1)S(1)}, u32[]{:S(2)}, u32[]{:S(2)}) %collective-permute-start.4) | collective-permute-done | bytes 81952 | tf_op jit(solution)/shard_map/ppermute | solution.py:65
  14.8 0.4 %partly.1 = (f32[32,512]{1,0:T(8,128)S(1)}, f32[64,512]{1,0:T(8,128)S(1)}) custom-call(bf16[80,512]{1,0:T(8,128)(2,1)S(1)} %project.1.refs_0_, bf16[80,512]{1,0:T(8,128)(2,1)S(1)} %collective-permute-done.4.refs_0_.refs_1_, bf16[256,512]{1,0:T(8,128)(2,1)S(1)} %get-tuple-element.23.refs_1_.refs_2_, bf16[256,512]{1,0:T(8,128)(2,1)S(1)} %get-tuple-element.30.refs_3_, ...), custom_call_target="tpu_custom_call" | custom-call | tf_op jit(solution)/shard_map/partly/pallas_call | solution.py:30
  15.2 0.0 collective-permute-done.block_ref.one
  15.2 0.1 halves.3
  15.3 0.5 %collective-permute-start.5 = (bf16[32,6144]{1,0:T(8,128)(2,1)S(1)}, bf16[32,6144]{1,0:T(8,128)(2,1)S(1)}, u32[]{:S(2)}, u32[]{:S(2)}) collective-permute-start(bf16[32,6144]{1,0:T(8,128)(2,1)S(1)} %get-tuple-element.24), channel_id=1, source_target_pairs={{0,4},{4,0},{8,12},{12,8},{16,20},{20,16},{24,28},{28,24},{1,5},{5... | collective-permute-start | bytes 1179656 | tf_op jit(solution)/shard_map/ppermute | solution.py:49
  15.8 0.1 collective-permute-start.6
  15.9 1.0 %collective-permute-done.8.refs_1_ = bf16[80,512]{1,0:T(8,128)(2,1)S(1)} collective-permute-done((bf16[80,512]{1,0:T(8,128)(2,1)S(1)}, bf16[80,512]{1,0:T(8,128)(2,1)S(1)}, u32[]{:S(2)}, u32[]{:S(2)}) %collective-permute-start.8) | collective-permute-done | bytes 81952 | tf_op jit(solution)/shard_map/ppermute | solution.py:65
  16.9 0.1 collective-permute-done.7.refs_0_
  17.0 0.7 %couple.1.after_ref.mine = bf16[64,512]{1,0:T(8,128)(2,1)S(1)} custom-call(bf16[80,512]{1,0:T(8,128)(2,1)S(1)} %collective-permute-done.7.refs_0_, bf16[80,512]{1,0:T(8,128)(2,1)S(1)} %collective-permute-done.8.refs_1_, bf16[256,512]{1,0:T(8,128)(2,1)S(1)} %get-tuple-element.26.refs_2_, bf16[256,512]{1,0:T(8,128)(2,1)S(1)} %get-tuple-element.27.refs_3_, ...), custom_call_target="tpu_custom_call" | custom-call | flops 4000000000 | tf_op jit(solution)/shard_map/couple/pallas_call | solution.py:30
  17.7 0.0 copy-start.3
  17.7 1.6 %collective-permute-start.10 = (bf16[64,512]{1,0:T(8,128)(2,1)S(1)}, bf16[64,512]{1,0:T(8,128)(2,1)S(1)}, u32[]{:S(2)}, u32[]{:S(2)}) collective-permute-start(bf16[64,512]{1,0:T(8,128)(2,1)S(1)} %couple.1.after_ref.mine), channel_id=1, source_target_pairs={{0,8},{4,12},{8,16},{12,20},{16,24},{20,28},{24,0},{28,4},{1,9},{5... | collective-permute-start | bytes 196616 | tf_op jit(solution)/shard_map/ppermute | solution.py:44
  19.3 0.0 collective-permute-done.5.upper_ref.upper
  19.3 0.0 collective-permute-done.6.lower_ref.lower
  19.3 0.1 collective-permute-start.9
  19.4 4.8 %collective-permute-done.10.mine_two.two = bf16[64,512]{1,0:T(8,128)(2,1)S(1)} collective-permute-done((bf16[64,512]{1,0:T(8,128)(2,1)S(1)}, bf16[64,512]{1,0:T(8,128)(2,1)S(1)}, u32[]{:S(2)}, u32[]{:S(2)}) %collective-permute-start.10) | collective-permute-done | bytes 65568 | tf_op jit(solution)/shard_map/ppermute | solution.py:44
  24.2 0.0 collective-permute-done.3.two
  24.2 0.1 choose.1
  24.3 0.1 collective-permute-start.11
  24.4 0.5 %collective-permute-start.12 = (bf16[64,512]{1,0:T(8,128)(2,1)S(1)}, bf16[64,512]{1,0:T(8,128)(2,1)S(1)}, u32[]{:S(2)}, u32[]{:S(2)}) collective-permute-start(bf16[64,512]{1,0:T(8,128)(2,1)S(1)} %collective-permute-done.10.mine_two.two), channel_id=1, source_target_pairs={{0,4},{4,8},{8,12},{12,16},{16,20},{20,24},{24,28},{28,0},{1,5},{5... | collective-permute-start | bytes 196616 | tf_op jit(solution)/shard_map/ppermute | solution.py:44
  24.9 0.0 collective-permute-start.13
  24.9 5.7 %collective-permute-done.9.three_a = bf16[48,6144]{1,0:T(8,128)(2,1)S(1)} collective-permute-done((bf16[48,6144]{1,0:T(8,128)(2,1)S(1)}, bf16[48,6144]{1,0:T(8,128)(2,1)S(1)}, u32[]{:S(2)}, u32[]{:S(2)}) %collective-permute-start.9) | collective-permute-done | bytes 589856 | tf_op jit(solution)/shard_map/ppermute | solution.py:44
  30.5 0.0 copy-done.3
  30.5 0.8 %gather.1.after_ref.partial_ref = f32[64,6144]{1,0:T(8,128)S(1)} custom-call(bf16[64,256]{1,0:T(8,128)(2,1)S(1)} %copy-done.3, bf16[64,6144]{1,0:T(8,128)(2,1)S(1)} %copy-done.2, bf16[64,6144]{1,0:T(8,128)(2,1)S(1)} %collective-permute-done.block_ref.one, bf16[64,6144]{1,0:T(8,128)(2,1)S(1)} %collective-permute-done.3.two, ...), custom_call_target="tpu_custom_call" | custom-call | flops 4499999744 | tf_op jit(solution)/shard_map/gather/pallas_call | solution.py:30
  31.4 0.0 collective-permute-done.12.three
  31.4 0.0 collective-permute-done.11.swap_ref
  31.4 1.4 %apply.1.applied = f32[64,6144]{1,0:T(8,128)S(1)} custom-call(bf16[64,256]{1,0:T(8,128)(2,1)S(1)} %copy-done.3, bf16[64,512]{1,0:T(8,128)(2,1)S(1)} %couple.1.after_ref.mine, bf16[80,6144]{1,0:T(8,128)(2,1)S(1)} %collective-permute-done.11.swap_ref, bf16[64,512]{1,0:T(8,128)(2,1)S(1)} %collective-permute-done.10.mine_two.two, ...), custom_call_target="tpu_custom_call" | custom-call | flops 5000000000 | tf_op jit(solution)/shard_map/apply/pallas_call | solution.py:30
  32.8 0.4 %add.1.partial_ref = f32[64,6144]{1,0:T(8,128)S(1)} custom-call(bf16[64,256]{1,0:T(8,128)(2,1)S(1)} %copy-done.3, f32[64,6144]{1,0:T(8,128)S(1)} %gather.1.after_ref.partial_ref, bf16[80,6144]{1,0:T(8,128)(2,1)S(1)} %collective-permute-done.11.swap_ref, f32[64,6144]{1,0:T(8,128)S(1)} %apply.1.applied), custom_call_target="tpu_custom_call" | custom-call | tf_op jit(solution)/shard_map/add/pallas_call | solution.py:30
  33.2 0.1 collective-permute-done.13.last_ref
  33.3 1.2 %finish.1 = bf16[64,6144]{1,0:T(8,128)(2,1)} custom-call(bf16[64,256]{1,0:T(8,128)(2,1)S(1)} %copy-done.3, f32[64,6144]{1,0:T(8,128)S(1)} %add.1.partial_ref, bf16[16,6144]{1,0:T(8,128)(2,1)S(1)} %collective-permute-done.13.last_ref, f32[64,6144]{1,0:T(8,128)S(1)} %apply.1.applied), custom_call_target="tpu_custom_call" | custom-call | tf_op jit(solution)/shard_map/finish/pallas_call | solution.py:405
  (1 shorter events, 0.0 us)
Async XLA Ops:
  0.0 15.2 %collective-permute-start = (bf16[64,6144]{1,0:T(8,128)(2,1)}, bf16[64,6144]{1,0:T(8,128)(2,1)S(1)}, u32[]{:S(2)}, u32[]{:S(2)}) collective-permute-start(bf16[64,6144]{1,0:T(8,128)(2,1)} %own.1), channel_id=1, source_target_pairs={{0,4},{4,8},{8,12},{12,16},{16,20},{20,24},{24,28},{28,0},{1,5},{5... | collective-permute-start | bytes 2359304 | tf_op jit(solution)/shard_map/ppermute | solution.py:44
  0.5 1.1 %copy-start.1 = (bf16[64,6144]{1,0:T(8,128)(2,1)S(1)}, bf16[64,6144]{1,0:T(8,128)(2,1)}, u32[]{:S(2)}) copy-start(bf16[64,6144]{1,0:T(8,128)(2,1)} %own.1) | copy-start | bytes 2359300
  1.6 5.4 %copy-start = (bf16[32,16,6144]{2,1,0:T(8,128)(2,1)S(1)}, bf16[32,16,6144]{2,1,0:T(8,128)(2,1)}, u32[]{:S(2)}) copy-start(bf16[32,16,6144]{2,1,0:T(8,128)(2,1)} %param.7) | copy-start | bytes 18874372
  1.6 5.2 %copy-start.4 = (f32[16,16,16]{2,1,0:T(8,128)S(1)}, f32[16,16,16]{2,1,0:T(8,128)}, u32[]{:S(2)}) copy-start(f32[16,16,16]{2,1,0:T(8,128)} %param.8) | copy-start | bytes 49156
  1.7 5.3 %copy-start.2 = (bf16[64,6144]{1,0:T(8,128)(2,1)S(1)}, bf16[64,6144]{1,0:T(8,128)(2,1)}, u32[]{:S(2)}) copy-start(bf16[64,6144]{1,0:T(8,128)(2,1)} %own.1) | copy-start | bytes 2359300
  1.7 4.1 %collective-permute-start.1 = (bf16[32,6144]{1,0:T(8,128)(2,1)S(1)}, bf16[32,6144]{1,0:T(8,128)(2,1)S(1)}, u32[]{:S(2)}, u32[]{:S(2)}) collective-permute-start(bf16[32,6144]{1,0:T(8,128)(2,1)S(1)} %get-tuple-element.21), channel_id=1, source_target_pairs={{0,4},{4,0},{8,12},{12,8},{16,20},{20,16},{24,28},{28,24},{1,5},{5... | collective-permute-start | bytes 1179656 | tf_op jit(solution)/shard_map/ppermute | solution.py:49
  4.5 1.9 %collective-permute-start.2 = (bf16[32,6144]{1,0:T(8,128)(2,1)S(1)}, bf16[32,6144]{1,0:T(8,128)(2,1)S(1)}, u32[]{:S(2)}, u32[]{:S(2)}) collective-permute-start(bf16[32,6144]{1,0:T(8,128)(2,1)S(1)} %get-tuple-element.22), channel_id=1, source_target_pairs={{0,4},{4,0},{8,12},{12,8},{16,20},{20,16},{24,28},{28,24},{1,5},{5... | collective-permute-start | bytes 1179656 | tf_op jit(solution)/shard_map/ppermute | solution.py:49
  6.4 17.8 %collective-permute-start.3 = (bf16[64,6144]{1,0:T(8,128)(2,1)S(1)}, bf16[64,6144]{1,0:T(8,128)(2,1)S(1)}, u32[]{:S(2)}, u32[]{:S(2)}) collective-permute-start(bf16[64,6144]{1,0:T(8,128)(2,1)S(1)} %hold.2), channel_id=1, source_target_pairs={{0,4},{4,8},{8,12},{12,16},{16,20},{20,24},{24,28},{28,0},{1,5},{5... | collective-permute-start | bytes 2359304 | tf_op jit(solution)/shard_map/ppermute | solution.py:44
  7.0 5.4 %copy-start.5 = (s32[4,32]{1,0:T(4,128)S(1)}, s32[4,32]{1,0:T(4,128)}, u32[]{:S(2)}) copy-start(s32[4,32]{1,0:T(4,128)} %slot_ref.1) | copy-start | bytes 1540
  8.9 5.9 %collective-permute-start.4 = (bf16[80,512]{1,0:T(8,128)(2,1)S(1)}, bf16[80,512]{1,0:T(8,128)(2,1)S(1)}, u32[]{:S(2)}, u32[]{:S(2)}) collective-permute-start(bf16[80,512]{1,0:T(8,128)(2,1)S(1)} %project.1.refs_0_), channel_id=1, source_target_pairs={{0,3},{1,2},{2,1},{3,0},{4,7},{5,6},{6,5},{7,4},{8,11},{9,10},{10,... | collective-permute-start | bytes 245768 | tf_op jit(solution)/shard_map/ppermute | solution.py:65
  11.4 5.5 %collective-permute-start.8 = (bf16[80,512]{1,0:T(8,128)(2,1)S(1)}, bf16[80,512]{1,0:T(8,128)(2,1)S(1)}, u32[]{:S(2)}, u32[]{:S(2)}) collective-permute-start(bf16[80,512]{1,0:T(8,128)(2,1)S(1)} %project.1.refs_0_), channel_id=1, source_target_pairs={{0,2},{1,3},{2,0},{3,1},{4,6},{5,7},{6,4},{7,5},{8,10},{9,11},{10,... | collective-permute-start | bytes 245768 | tf_op jit(solution)/shard_map/ppermute | solution.py:65
  11.9 5.1 %collective-permute-start.7 = (bf16[80,512]{1,0:T(8,128)(2,1)S(1)}, bf16[80,512]{1,0:T(8,128)(2,1)S(1)}, u32[]{:S(2)}, u32[]{:S(2)}) collective-permute-start(bf16[80,512]{1,0:T(8,128)(2,1)S(1)} %project.1.refs_0_), channel_id=1, source_target_pairs={{0,1},{1,0},{2,3},{3,2},{4,5},{5,4},{6,7},{7,6},{8,9},{9,8},{10,11... | collective-permute-start | bytes 245768 | tf_op jit(solution)/shard_map/ppermute | solution.py:65
  15.3 4.0 %collective-permute-start.5 = (bf16[32,6144]{1,0:T(8,128)(2,1)S(1)}, bf16[32,6144]{1,0:T(8,128)(2,1)S(1)}, u32[]{:S(2)}, u32[]{:S(2)}) collective-permute-start(bf16[32,6144]{1,0:T(8,128)(2,1)S(1)} %get-tuple-element.24), channel_id=1, source_target_pairs={{0,4},{4,0},{8,12},{12,8},{16,20},{20,16},{24,28},{28,24},{1,5},{5... | collective-permute-start | bytes 1179656 | tf_op jit(solution)/shard_map/ppermute | solution.py:49
  15.8 3.5 %collective-permute-start.6 = (bf16[32,6144]{1,0:T(8,128)(2,1)S(1)}, bf16[32,6144]{1,0:T(8,128)(2,1)S(1)}, u32[]{:S(2)}, u32[]{:S(2)}) collective-permute-start(bf16[32,6144]{1,0:T(8,128)(2,1)S(1)} %get-tuple-element.25), channel_id=1, source_target_pairs={{0,4},{4,0},{8,12},{12,8},{16,20},{20,16},{24,28},{28,24},{1,5},{5... | collective-permute-start | bytes 1179656 | tf_op jit(solution)/shard_map/ppermute | solution.py:49
  17.7 12.9 %copy-start.3 = (bf16[64,256]{1,0:T(8,128)(2,1)S(1)}, bf16[64,256]{1,0:T(8,128)(2,1)}, u32[]{:S(2)}) copy-start(bf16[64,256]{1,0:T(8,128)(2,1)} %rot_ref.7) | copy-start | bytes 98308
  17.7 6.5 %collective-permute-start.10 = (bf16[64,512]{1,0:T(8,128)(2,1)S(1)}, bf16[64,512]{1,0:T(8,128)(2,1)S(1)}, u32[]{:S(2)}, u32[]{:S(2)}) collective-permute-start(bf16[64,512]{1,0:T(8,128)(2,1)S(1)} %couple.1.after_ref.mine), channel_id=1, source_target_pairs={{0,8},{4,12},{8,16},{12,20},{16,24},{20,28},{24,0},{28,4},{1,9},{5... | collective-permute-start | bytes 196616 | tf_op jit(solution)/shard_map/ppermute | solution.py:44
  19.3 11.2 %collective-permute-start.9 = (bf16[48,6144]{1,0:T(8,128)(2,1)S(1)}, bf16[48,6144]{1,0:T(8,128)(2,1)S(1)}, u32[]{:S(2)}, u32[]{:S(2)}) collective-permute-start(bf16[48,6144]{1,0:T(8,128)(2,1)S(1)} %hold.3), channel_id=1, source_target_pairs={{0,4},{4,8},{8,12},{12,16},{16,20},{20,24},{24,28},{28,0},{1,5},{5... | collective-permute-start | bytes 1769480 | tf_op jit(solution)/shard_map/ppermute | solution.py:44
  24.3 7.1 %collective-permute-start.11 = (bf16[80,6144]{1,0:T(8,128)(2,1)S(1)}, bf16[80,6144]{1,0:T(8,128)(2,1)S(1)}, u32[]{:S(2)}, u32[]{:S(2)}) collective-permute-start(bf16[80,6144]{1,0:T(8,128)(2,1)S(1)} %get-tuple-element.35), channel_id=1, source_target_pairs={{0,4},{4,0},{8,12},{12,8},{16,20},{20,16},{24,28},{28,24},{1,5},{5... | collective-permute-start | bytes 2949128 | tf_op jit(solution)/shard_map/ppermute | solution.py:49
  24.4 7.0 %collective-permute-start.12 = (bf16[64,512]{1,0:T(8,128)(2,1)S(1)}, bf16[64,512]{1,0:T(8,128)(2,1)S(1)}, u32[]{:S(2)}, u32[]{:S(2)}) collective-permute-start(bf16[64,512]{1,0:T(8,128)(2,1)S(1)} %collective-permute-done.10.mine_two.two), channel_id=1, source_target_pairs={{0,4},{4,8},{8,12},{12,16},{16,20},{20,24},{24,28},{28,0},{1,5},{5... | collective-permute-start | bytes 196616 | tf_op jit(solution)/shard_map/ppermute | solution.py:44
  24.9 8.5 %collective-permute-start.13 = (bf16[16,6144]{1,0:T(8,128)(2,1)S(1)}, bf16[16,6144]{1,0:T(8,128)(2,1)S(1)}, u32[]{:S(2)}, u32[]{:S(2)}) collective-permute-start(bf16[16,6144]{1,0:T(8,128)(2,1)S(1)} %get-tuple-element.36), channel_id=1, source_target_pairs={{0,4},{4,8},{8,12},{12,16},{16,20},{20,24},{24,28},{28,0},{1,5},{5... | collective-permute-start | bytes 589832 | tf_op jit(solution)/shard_map/ppermute | solution.py:44
